TPU v7x, 128 devices: a whole 4x4x4 slice. The times are simulated.
128 devices in a mesh: seq: 64 (over y, z, x_lo, core), tensor: 2 (over x_hi).
Axes of the slice: x: 4 (x_hi: 2, x_lo: 2; x = x_hi * 2 + x_lo), y: 4, z: 4, core: 2. Of those that a mesh axis runs over, the one named last changes fastest.
Arguments:
- tokens: bfloat16 [16384, 1024], P('seq'), may hold values from -6 to 6
- starts: int32 [64], P('seq'), may hold values from 2 to 256, as said below
- gain_one: float32 [1024], replicated, may hold values from 0.1 to 1.9
- in_weight: bfloat16 [1024, 3, 1024], P(None, None, 'tensor'), may hold values from -0.1875 to 0.1875
- conv_weight: float32 [3, 1024], P(None, 'tensor'), may hold values from -3 to 3
- out_weight: bfloat16 [1024, 1024], P('tensor'), may hold values from -0.1875 to 0.1875
- gain_two: float32 [1024], replicated, may hold values from 0.1 to 1.9
- gate_weight: bfloat16 [1024, 4608], P(None, 'tensor'), may hold values from -0.1875 to 0.1875
- up_weight: bfloat16 [1024, 4608], P(None, 'tensor'), may hold values from -0.1875 to 0.1875
- down_weight: bfloat16 [4608, 1024], P('tensor'), may hold values from -0.125 to 0.125
- cotangent: bfloat16 [16384, 1024], P('seq'), may hold values from -16 to 16
Outputs:
- mixed: bfloat16 [16384, 1024], P('seq')
- tokens_grad: float32 [16384, 1024], P('seq')
- gain_one_grad: float32 [1024], replicated
- in_grad: float32 [1024, 3, 1024], P('seq', None, 'tensor')
- conv_grad: float32 [3, 1024], P(None, 'tensor')
- out_grad: float32 [1024, 1024], P('tensor', 'seq')
- gain_two_grad: float32 [1024], replicated
- gate_grad: float32 [1024, 4608], P('seq', 'tensor')
- up_grad: float32 [1024, 4608], P('seq', 'tensor')
- down_grad: float32 [4608, 1024], P('tensor', 'seq')
Inputs may be any that keep to these rules, and one draw needn't show every extreme that they name: `starts`: entry j is the offset inside shard j of the only segment start in it, or 256 where the shard has none; shard 0 has none, and the shards that have one lie 16 apart, at a position drawn from the seed.
All inputs are finite; a program needn't handle non-finite values.
Results may differ from a plain program's by a relative error of at most 0.014.
Values may be sent and summed in bfloat16 or wider, within the bound.
No kernel may reach another device: no remote copies, remote signals or barrier semaphores. Data moves between devices by JAX's collectives and lax.ppermute only.
A program may use at most 128 MiB of HBM per device.

v0:
```python
import jax
import jax.numpy as jnp
from jax import lax
from jax.sharding import PartitionSpec as P

EPS = 1e-05


def from_behind(value, axis, steps):
    count = lax.axis_size(axis)
    leading, last = (max(0, -steps), min(count, count - steps))
    return lax.ppermute(value, axis, [(source, source + steps) for source in range(leading, last)])


def norm_scale(values):
    return lax.rsqrt(jnp.mean(values * values, axis=1, keepdims=True) + EPS)


def norm_backward(out_grad_rows, values, scale_rows, gain):
    scaled = out_grad_rows * gain
    gain_part = jnp.sum(out_grad_rows * values * scale_rows, axis=0)
    inner = jnp.mean(scaled * values, axis=1, keepdims=True)
    return (scale_rows * (scaled - values * scale_rows * scale_rows * inner), gain_part)


def on_device(
    tokens,
    starts,
    gain_one,
    in_weight,
    conv_weight,
    out_weight,
    gain_two,
    gate_weight,
    up_weight,
    down_weight,
    cotangent,
):
    count_rows = tokens.shape[0]
    inputs = tokens.astype(jnp.float32)
    scale_one = norm_scale(inputs)
    normed_one = (inputs * scale_one * gain_one).astype(jnp.bfloat16)
    projected = jnp.einsum("td,dkc->tkc", normed_one, in_weight, preferred_element_type=jnp.float32)
    b_part, c_part, x_part = (projected[:, 0], projected[:, 1], projected[:, 2])
    gated = (b_part * x_part).astype(jnp.bfloat16)
    offset = starts[0]
    positions = jnp.arange(count_rows, dtype=jnp.int32)
    tail_positions = positions[count_rows - 2 :]
    keep_mask = jnp.logical_not((tail_positions < offset) & (offset < count_rows)).astype(
        jnp.float32
    )[:, None]
    tail = (gated[count_rows - 2 :].astype(jnp.float32) * keep_mask).astype(jnp.bfloat16)
    incoming = from_behind(tail, "seq", 1)
    extended = jnp.concatenate([incoming, gated], 0).astype(jnp.float32)
    valid = [jnp.ones((count_rows, 1), jnp.float32)]
    for shift_lag in (1, 2):
        valid.append(
            jnp.logical_not((offset <= positions) & (offset > positions - shift_lag)).astype(
                jnp.float32
            )[:, None]
        )
    conv = jnp.zeros_like(b_part)
    for shift_lag in range(3):
        conv = (
            conv
            + conv_weight[shift_lag]
            * extended[2 - shift_lag : 2 - shift_lag + count_rows]
            * valid[shift_lag]
        )
    ymix = (c_part * conv).astype(jnp.bfloat16)
    branch = lax.psum(jnp.dot(ymix, out_weight, preferred_element_type=jnp.float32), "tensor")
    resid = inputs + branch
    scale_two = norm_scale(resid)
    normed_two = (resid * scale_two * gain_two).astype(jnp.bfloat16)
    gate_act = jnp.dot(normed_two, gate_weight, preferred_element_type=jnp.float32)
    up_act = jnp.dot(normed_two, up_weight, preferred_element_type=jnp.float32)
    sigmoid_gate = jax.nn.sigmoid(gate_act)
    swish = gate_act * sigmoid_gate
    hidden = (swish * up_act).astype(jnp.bfloat16)
    down_sum = lax.psum(
        jnp.dot(hidden, down_weight, preferred_element_type=jnp.float32).astype(jnp.bfloat16),
        "tensor",
    ).astype(jnp.float32)
    mixed = (resid + down_sum).astype(jnp.bfloat16)
    upstream = cotangent.astype(jnp.float32)
    down_g = jnp.einsum("tf,td->fd", hidden, cotangent, preferred_element_type=jnp.float32)
    hidden_grad = jnp.einsum(
        "td,fd->tf", cotangent, down_weight, preferred_element_type=jnp.float32
    )
    swish_slope = sigmoid_gate * (1.0 + gate_act * (1.0 - sigmoid_gate))
    gate_back = (hidden_grad * up_act * swish_slope).astype(jnp.bfloat16)
    up_back = (hidden_grad * swish).astype(jnp.bfloat16)
    gate_g = jnp.einsum("td,tf->df", normed_two, gate_back, preferred_element_type=jnp.float32)
    up_g = jnp.einsum("td,tf->df", normed_two, up_back, preferred_element_type=jnp.float32)
    norm_two_part = jnp.einsum(
        "tf,df->td", gate_back, gate_weight, preferred_element_type=jnp.float32
    )
    norm_two_part = norm_two_part + jnp.einsum(
        "tf,df->td", up_back, up_weight, preferred_element_type=jnp.float32
    )
    norm_two_back = lax.psum(norm_two_part.astype(jnp.bfloat16), "tensor").astype(jnp.float32)
    resid_norm_grad, gain_two_g = norm_backward(norm_two_back, resid, scale_two, gain_two)
    resid_grad = upstream + resid_norm_grad
    resid_low = resid_grad.astype(jnp.bfloat16)
    out_g = jnp.einsum("tc,td->cd", ymix, resid_low, preferred_element_type=jnp.float32)
    ymix_back = jnp.einsum("td,cd->tc", resid_low, out_weight, preferred_element_type=jnp.float32)
    c_back = ymix_back * conv
    conv_back = ymix_back * c_part
    extended_grad = jnp.zeros_like(extended)
    tap_grads = []
    for shift_lag in range(3):
        lag_term = conv_back * valid[shift_lag]
        tap_grads.append(
            jnp.sum(lag_term * extended[2 - shift_lag : 2 - shift_lag + count_rows], axis=0)
        )
        extended_grad = extended_grad + jnp.pad(
            lag_term * conv_weight[shift_lag], ((2 - shift_lag, shift_lag), (0, 0))
        )
    conv_g = jnp.stack(tap_grads, 0)
    returned = from_behind(extended_grad[:2], "seq", -1)
    gated_back = extended_grad[2:] + jnp.pad(returned * keep_mask, ((count_rows - 2, 0), (0, 0)))
    proj_back = jnp.stack([gated_back * x_part, c_back, gated_back * b_part], 1).astype(
        jnp.bfloat16
    )
    in_g = jnp.einsum("td,tkc->dkc", normed_one, proj_back, preferred_element_type=jnp.float32)
    norm_one_back = lax.psum(
        jnp.einsum("tkc,dkc->td", proj_back, in_weight, preferred_element_type=jnp.float32).astype(
            jnp.bfloat16
        ),
        "tensor",
    ).astype(jnp.float32)
    input_norm_grad, gain_one_g = norm_backward(norm_one_back, inputs, scale_one, gain_one)
    tokens_grad = resid_grad + input_norm_grad
    conv_g, gain_one_g, gain_two_g = lax.psum((conv_g, gain_one_g, gain_two_g), "seq")
    in_g, out_g, gate_g, up_g, down_g = (
        lax.psum_scatter(in_g, "seq", scatter_dimension=0, tiled=True),
        lax.psum_scatter(out_g, "seq", scatter_dimension=1, tiled=True),
        lax.psum_scatter(gate_g, "seq", scatter_dimension=0, tiled=True),
        lax.psum_scatter(up_g, "seq", scatter_dimension=0, tiled=True),
        lax.psum_scatter(down_g, "seq", scatter_dimension=1, tiled=True),
    )
    return (mixed, tokens_grad, gain_one_g, in_g, conv_g, out_g, gain_two_g, gate_g, up_g, down_g)


def solution(mesh):
    return jax.shard_map(
        on_device,
        mesh=mesh,
        in_specs=(
            P("seq", None),
            P("seq"),
            P(),
            P(None, None, "tensor"),
            P(None, "tensor"),
            P("tensor", None),
            P(),
            P(None, "tensor"),
            P(None, "tensor"),
            P("tensor", None),
            P("seq", None),
        ),
        out_specs=(
            P("seq", None),
            P("seq", None),
            P(),
            P("seq", None, "tensor"),
            P(None, "tensor"),
            P("tensor", "seq"),
            P(),
            P("seq", "tensor"),
            P("seq", "tensor"),
            P("tensor", "seq"),
        ),
        check_vma=False,
    )
```

profile of v0, /device:TPU:1, one launch (start us, length us, event | category | flops | bytes accessed | tf_op | source)
XLA Modules:
  0.0 1676.9 jit_solution(13281826637792076185)
XLA Ops:
  9.4 2.1 fusion.25
  12.9 4.6 collective-permute-start
  19.2 2.1 multiply_convert_fusion.7
  22.8 52.0 %all-reduce.10.cloned.1.call-done = f32[256,1024]{1,0:T(8,128)} async-done(((f32[256,1024]{1,0:T(8,128)}), f32[256,1024]{1,0:T(8,128)}) %all-reduce.10.cloned.1.call-update) | async-done | bytes 1048592 | tf_op jit(solution)/shard_map/psum | solution.py:71
  77.5 4.0 fusion.40
  83.1 3.4 multiply_convert_fusion
  87.9 2.2 fusion.2
  90.2 4.9 convolution_convert_fusion
  95.1 31.3 %all-reduce.12.cloned.1.call-done = bf16[256,1024]{1,0:T(8,128)(2,1)} async-done(((bf16[256,1024]{1,0:T(8,128)(2,1)}), bf16[256,1024]{1,0:T(8,128)(2,1)}) %all-reduce.12.cloned.1.call-update) | async-done | bytes 524304 | tf_op jit(solution)/shard_map/psum | solution.py:101
  132.3 2.8 collective-permute-start.1
  140.2 3.1 fusion.30
  143.4 3.8 fusion.23
  148.6 5.1 fusion.43
  155.0 5.1 fusion.42
  161.5 5.1 fusion.44
  166.7 23.6 %all-reduce.14.cloned.1.call-done = (bf16[256,1024]{1,0:T(8,128)(2,1)}, bf16[256,1024]{1,0:T(8,128)(2,1)}) async-done(((bf16[256,1024]{1,0:T(8,128)(2,1)}, bf16[256,1024]{1,0:T(8,128)(2,1)}), (bf16[256,1024]{1,0:T(8,128)(2,1)}, bf16[256,1024]{1,0:T(8,128)(2,1)})) %all-reduce.14.cloned.1.call-update) | async-done | bytes 1048592 | tf_op jit(solution)/shard_map/psum | solution.py:80
  191.7 273.8 %all-reduce.4 = (f32[1024]{0:T(1024)}, f32[3,512]{1,0:T(4,128)}, f32[1024]{0:T(1024)}) all-reduce(f32[1024]{0:T(1024)S(1)} %get-tuple-element.15, f32[3,512]{1,0:T(4,128)S(1)} %pad_maximum_fusion.3, f32[1024]{0:T(1024)S(1)} %get-tuple-element.10), channel_id=1, replica_groups=mesh['seq'=64,'tensor'=2] {'seq'}, use_global_device_ids=true, to_apply=%region_9.10 | all-reduce | flops 3584 | bytes 28672 | tf_op jit(solution)/shard_map/psum | solution.py:134
  465.5 2.4 add_convert_fusion
  468.0 2.7 fusion.11
  470.6 3.2 reduce-scatter.8.cloned.1.call-done
  473.9 294.2 %reduce-scatter.6.cloned.1.call-done = f32[16,3,512]{2,0,1:T(8,128)} async-done(((f32[1024,3,512]{2,0,1:T(8,128)}), f32[16,3,512]{2,0,1:T(8,128)}) %reduce-scatter.6.cloned.1.call-update) | async-done | bytes 98320 | tf_op jit(solution)/shard_map/reduce_scatter | solution.py:136
  768.1 301.3 %reduce-scatter.12.cloned.1.call-done = f32[16,2304]{1,0:T(8,128)} async-done(((f32[1024,2304]{1,0:T(8,128)}), f32[16,2304]{1,0:T(8,128)}) %reduce-scatter.12.cloned.1.call-update) | async-done | bytes 147472 | tf_op jit(solution)/shard_map/reduce_scatter | solution.py:139
  1069.4 299.6 %reduce-scatter.10.cloned.1.call-done = f32[16,2304]{1,0:T(8,128)} async-done(((f32[1024,2304]{1,0:T(8,128)}), f32[16,2304]{1,0:T(8,128)}) %reduce-scatter.10.cloned.1.call-update) | async-done | bytes 147472 | tf_op jit(solution)/shard_map/reduce_scatter | solution.py:138
  1369.0 301.0 %reduce-scatter.14.cloned.1.call-done = f32[2304,16]{0,1:T(8,128)} async-done(((f32[2304,1024]{0,1:T(8,128)}), f32[2304,16]{0,1:T(8,128)}) %reduce-scatter.14.cloned.1.call-update) | async-done | bytes 147472 | tf_op jit(solution)/shard_map/reduce_scatter | solution.py:140
  (124 shorter events, 27.9 us)
Async XLA Ops:
  7.2 67.6 %all-reduce.10.cloned.1.call-start = ((), (), s32[]{:S(2)}) async-start(), calls=%async_computation.5 | async-start | bytes 2097152 | tf_op jit(solution)/shard_map/psum | solution.py:71
  9.4 8.2 copy-start.30
  12.8 8.5 copy-start.11
  12.9 5.4 collective-permute-start
  22.7 54.6 %copy-start.29 = (f32[1024]{0:T(1024)S(1)}, f32[1024]{0:T(1024)}, u32[]{:S(2)}) copy-start(f32[1024]{0:T(1024)} %param.17) | copy-start | bytes 12292
  22.7 103.8 %all-reduce.12.cloned.1.call-start = ((), (), s32[]{:S(2)}) async-start(), calls=%async_computation.6 | async-start | bytes 1048576 | tf_op jit(solution)/shard_map/psum | solution.py:101
  77.3 4.2 slice-start
  77.5 4.1 copy-start.9
  77.5 4.1 slice-start.1
  77.5 5.6 slice-start.4
  81.6 6.3 slice-start.2
  83.1 4.8 slice-start.3
  90.2 100.1 %all-reduce.14.cloned.1.call-start = ((), (), s32[]{:S(2)}) async-start(), calls=%async_computation.12 | async-start | bytes 2097152 | tf_op jit(solution)/shard_map/psum | solution.py:80
  126.5 4.9 copy-start.12
  128.2 3.6 copy-start.8
  128.2 3.6 copy-start.15
  132.1 5.4 copy-start.26
  132.3 4.9 collective-permute-start.1
  140.2 333.7 %reduce-scatter.8.cloned.1.call-start = ((), (), s32[]{:S(2)}) async-start(), calls=%async_computation.8 | async-start | bytes 2129920 | tf_op jit(solution)/shard_map/reduce_scatter | solution.py:137
  143.3 624.7 %reduce-scatter.6.cloned.1.call-start = ((), (), s32[]{:S(2)}) async-start(), calls=%async_computation.7 | async-start | bytes 6389760 | tf_op jit(solution)/shard_map/reduce_scatter | solution.py:136
  147.2 922.2 %reduce-scatter.12.cloned.1.call-start = ((), (), s32[]{:S(2)}) async-start(), calls=%async_computation.10 | async-start | bytes 9584640 | tf_op jit(solution)/shard_map/reduce_scatter | solution.py:139
  153.8 1215.2 %reduce-scatter.10.cloned.1.call-start = ((), (), s32[]{:S(2)}) async-start(), calls=%async_computation.9 | async-start | bytes 9584640 | tf_op jit(solution)/shard_map/reduce_scatter | solution.py:138
  160.1 1509.9 %reduce-scatter.14.cloned.1.call-start = ((), (), s32[]{:S(2)}) async-start(), calls=%async_computation.11 | async-start | bytes 9584640 | tf_op jit(solution)/shard_map/reduce_scatter | solution.py:140
  465.5 1204.5 %copy-start.1 = (bf16[1024,3,512]{2,0,1:T(8,128)(2,1)S(1)}, bf16[1024,3,512]{2,0,1:T(8,128)(2,1)}, u32[]{:S(2)}) copy-start(bf16[1024,3,512]{2,0,1:T(8,128)(2,1)} %param.14) | copy-start | bytes 9437188
  (23 other events, 42.1 us)
Sparse Core Ops, SparseCore 0:
  22.8 51.8 all-reduce.9
  90.3 36.0 all-reduce.11
  140.3 50.0 all-reduce.13
  193.2 280.6 reduce-scatter.7
  476.7 291.3 reduce-scatter.5
  771.0 298.3 reduce-scatter.11
  1072.5 296.4 reduce-scatter.9
  1372.1 297.8 reduce-scatter.13
where the time goes:
time: 1680 us
  waiting for transfers between devices  1310 us (78%)
  blocking collectives  274 us (16%)
  matrix products  45.3 us (3%)
    reduce_scatter x1, waiting for transfers between devices, on_device(): lax.psum_scatter(up_g, 'seq', scatter_dimension=0, tiled=True)  301 us
    reduce_scatter x1, waiting for transfers between devices, on_device(): lax.psum_scatter(down_g, 'seq', scatter_dimension=1, tiled=True)  301 us
    reduce_scatter x1, waiting for transfers between devices, on_device(): lax.psum_scatter(gate_g, 'seq', scatter_dimension=0, tiled=True)  300 us
    reduce_scatter x1, waiting for transfers between devices, on_device(): lax.psum_scatter(in_g, 'seq', scatter_dimension=0, tiled=True)  294 us
    psum x1, blocking collectives, on_device(): lax.psum((conv_g, gain_one_g, gain_two_g), 'seq')  274 us
    psum x1, waiting for transfers between devices, on_device(): lax.psum(jnp.dot(ymix, out_weight, preferred_element_type=jnp.float32), '...  52 us
  transfers between devices with their start and end apart: 10, of which 10 were waited for; matrix products, arithmetic and copies ran while one was open for 2% of the time, Pallas kernels for 0%

commit v1 on v0

v1 whole, which is shorter than its diff:
```python
import functools

import jax
import jax.numpy as jnp
from jax import lax
from jax.experimental import pallas as pl
from jax.experimental.pallas import tpu as pltpu
from jax.sharding import PartitionSpec as P

EPS = 1e-05
AXES = ("seq", "tensor")
BF16 = jnp.bfloat16
F32 = jnp.float32


def device_pairs(move):
    def number(y, z, x, core):
        return ((((y % 4) * 4 + z % 4) * 2 + x % 2) * 2 + core) * 2 + (x % 4) // 2

    return [
        (number(y, z, x, core), number(*move(y, z, x, core)))
        for y in range(4)
        for z in range(4)
        for x in range(4)
        for core in range(2)
    ]


ACROSS = device_pairs(lambda y, z, x, core: (y, z, (x + 2) % 4, core))
BESIDE = device_pairs(lambda y, z, x, core: (y, z, x ^ 1, core))
CORES = device_pairs(lambda y, z, x, core: (y, z, x, 1 - core))


def peer(at, pairing):
    return (at ^ 1, 3 - at, at ^ 2)[pairing]


SETS = (("y", 0), ("y", 1), ("y", 2), ("z", 0), ("z", 1), ("z", 2))
FIRST = (("y", 0), ("y", 1), ("z", 0), ("z", 1))
SECOND = (("y", 1), ("y", 0), ("z", 1), ("z", 0))
PAIRS = {
    (axis, pairing): device_pairs(
        functools.partial(
            lambda axis, pairing, y, z, x, core: (peer(y, pairing), z, x, core)
            if axis == "y"
            else (y, peer(z, pairing), x, core),
            axis,
            pairing,
        )
    )
    for axis, pairing in SETS
}
WIDE = (7, 7, 7, 6)
NARROW = (2, 2, 2, 2)
WIDE_COLUMNS = 1152
CUT = 896
BLOCK = (64, 128)
TILES = sum(WIDE) + sum(NARROW)
OTHER_AXIS = {"y": "z", "z": "y"}


def layouts():
    one, two = [], []
    for axis, pairing in SETS:
        entries, total = {}, 0
        for kind in range(4):
            if SECOND[kind] == (axis, pairing):
                entries["wide", kind] = total
                total += 4 * WIDE[kind]
        for kind in range(4):
            if FIRST[kind][0] == axis:
                entries["narrow", kind] = total
                total += 4 * NARROW[kind]
        if axis == "y":
            entries["small"] = total
            total += 1
        one.append((entries, total))
        entries, total = {}, 0
        for family, tiles in (("wide", WIDE), ("narrow", NARROW)):
            for kind in range(4):
                if FIRST[kind][0] != axis:
                    entries[family, kind] = total
                    total += tiles[kind]
        if axis == "z":
            entries["small"] = total
            total += 1
        two.append((entries, total))
    return one, two


ROUND_ONE, ROUND_TWO = layouts()


def swap(value, pairs):
    return lax.ppermute(value, AXES, pairs)


def from_behind(value, axis, steps):
    count = lax.axis_size(axis)
    leading, last = (max(0, -steps), min(count, count - steps))
    return lax.ppermute(value, axis, [(source, source + steps) for source in range(leading, last)])


def norm_scale(values):
    return lax.rsqrt(jnp.mean(values * values, axis=1, keepdims=True) + EPS)


def norm_backward(out_grad_rows, values, scale_rows, gain):
    scaled = out_grad_rows * gain
    inner = jnp.mean(scaled * values, axis=1, keepdims=True)
    return scale_rows * (scaled - values * scale_rows * scale_rows * inner)


def like(shape, dtype):
    return jax.ShapeDtypeStruct(shape, dtype)


def call(body, *, scalars, operands, outs, scratch=()):
    size = sum(v.size * v.dtype.itemsize for v in list(operands) + list(outs))
    whole = pl.BlockSpec(memory_space=pltpu.VMEM)
    return pl.pallas_call(
        body,
        out_shape=tuple(outs),
        in_specs=[pl.BlockSpec(memory_space=pltpu.SMEM)] + [whole] * len(operands),
        out_specs=tuple(whole for _ in outs),
        scratch_shapes=list(scratch),
        compiler_params=pltpu.CompilerParams(vmem_limit_bytes=min(size + 14 * 2**20, 48 * 2**20)),
        cost_estimate=pl.CostEstimate(flops=0, bytes_accessed=0, transcendentals=0),
    )(scalars, *operands)


def dot(left, right):
    return jnp.dot(left, right, preferred_element_type=F32)


def dot_rows(left, right):
    return lax.dot_general(left, right, (((1,), (1,)), ((), ())), preferred_element_type=F32)


def row_numbers(shape, first=0):
    return lax.broadcasted_iota(jnp.int32, shape, 0) + first


def valid_rows(offset, lag, shape):
    row = row_numbers(shape)
    return jnp.where((offset <= row) & (offset > row - lag), 0.0, 1.0)


def linked_rows(offset, shape, first, count):
    return jnp.where((row_numbers(shape, first) < offset) & (offset < count), 0.0, 1.0)


def tail_kernel(scalars, tokens, gain, weight, tail):
    rows = tokens.shape[0]
    values = tokens[rows - 16 :].astype(F32)
    normed = (values * norm_scale(values) * gain[...]).astype(BF16)
    gated = (dot(normed, weight[0]) * dot(normed, weight[2])).astype(BF16).astype(F32)
    tail[...] = (gated * linked_rows(scalars[4], gated.shape, rows - 16, rows)).astype(BF16)


def project_kernel(scalars, tokens, gain, weight, normed, parts, gated):
    values = tokens[...].astype(F32)
    normed[...] = (values * norm_scale(values) * gain[...]).astype(BF16)
    for k in range(3):
        parts[k] = dot(normed[...], weight[k])
    gated[...] = (parts[0] * parts[2]).astype(BF16)


def behind(gated, incoming, lag):
    moved = pltpu.roll(gated, lag, 0)
    row = row_numbers(gated.shape)
    for at in range(lag):
        moved = jnp.where(row == at, incoming[16 - lag + at : 17 - lag + at], moved)
    return moved


def mix_kernel(scalars, gated, incoming, parts, taps, weight, conv, ymix, ymix_away, branch):
    values = gated[...].astype(F32)
    before = incoming[...].astype(F32)
    total = taps[0:1] * values
    for lag in (1, 2):
        total = total + taps[lag : lag + 1] * behind(values, before, lag) * valid_rows(
            scalars[4], lag, values.shape
        )
    conv[...] = total
    ymix[...] = (parts[1] * total).astype(BF16)
    ymix_away[...] = away_half(ymix[...], scalars[3])
    branch[...] = dot(ymix[...], weight[...]).astype(BF16)


def away_half(value, core):
    half = value.shape[-1] // 2
    return jnp.where(core == 0, value[..., half:], value[..., :half])


def second_norm(part, other, resid, gain, cot):
    back = part.astype(F32) + other.astype(F32)
    scale = norm_scale(resid)
    return back, scale, cot.astype(F32) + norm_backward(back, resid, scale, gain)


def edge_kernel(scalars, part, other, resid, gain, cot, weight, parts, taps, edge):
    top = slice(0, 16)
    _, _, grad = second_norm(part[top], other[top], resid[top], gain[...], cot[top])
    conv_back = dot_rows(grad.astype(BF16), weight[...]) * parts[1, top]
    one = conv_back * valid_rows(scalars[4], 1, conv_back.shape) * taps[1:2]
    two = conv_back * valid_rows(scalars[4], 2, conv_back.shape) * taps[2:3]
    row = row_numbers((8, conv_back.shape[1]))
    edge[...] = jnp.where(row == 6, two[0:1], 0.0) + jnp.where(row == 7, one[0:1] + two[1:2], 0.0)


def middle_kernel(
    scalars, part, other, resid, gain, cot, weight, parts, taps, conv, gated, incoming, grad, low, gain_grad, c_back, gated_back, tap_grads
):
    back, scale, resid_grad = second_norm(part[...], other[...], resid[...], gain[...], cot[...])
    gain_grad[...] = jnp.sum(back * resid[...] * scale, axis=0, keepdims=True)
    grad[...] = resid_grad
    low[...] = resid_grad.astype(BF16)
    ymix_back = dot_rows(low[...], weight[...])
    c_back[...] = (ymix_back * conv[...]).astype(BF16)
    conv_back = ymix_back * parts[1]
    values, before = gated[...].astype(F32), incoming[...].astype(F32)
    rows = values.shape[0]
    tap_grads[0:1] = jnp.sum(conv_back * values, axis=0, keepdims=True)
    total = conv_back * taps[0:1]
    row = row_numbers(values.shape)
    for lag in (1, 2):
        term = conv_back * valid_rows(scalars[4], lag, values.shape)
        tap_grads[lag : lag + 1] = jnp.sum(term * behind(values, before, lag), axis=0, keepdims=True)
        moved = pltpu.roll(term * taps[lag : lag + 1], rows - lag, 0)
        total = total + jnp.where(row < rows - lag, moved, 0.0)
    gated_back[...] = total


def last_kernel(
    scalars, gated_back, returned, parts, c_back, weight, tokens, gain_two_grad, tap_grads, backs, backs_away, low, small
):
    rows = gated_back.shape[0]
    links = linked_rows(scalars[4], returned.shape, rows - 8, rows)
    end = gated_back[rows - 8 :] + returned[...] * links
    total = jnp.concatenate([gated_back[: rows - 8], end], 0)
    backs[0] = (total * parts[2]).astype(BF16)
    backs[1] = c_back[...]
    backs[2] = (total * parts[0]).astype(BF16)
    for k in range(3):
        backs_away[k] = away_half(backs[k], scalars[3])
    grad = dot_rows(backs[0], weight[0]) + dot_rows(backs[1], weight[1]) + dot_rows(backs[2], weight[2])
    low[...] = grad.astype(BF16)
    values = tokens[...].astype(F32)
    gain_grad = jnp.sum(grad * values * norm_scale(values), axis=0, keepdims=True)
    for at in range(8):
        lanes = slice(at * 128, at * 128 + 128)
        small[at : at + 1] = gain_grad[:, lanes]
        small[8 + at : 9 + at] = gain_two_grad[:, lanes]
    for lag in range(3):
        for at in range(4):
            row = 16 + 4 * lag + at
            small[row : row + 1] = tap_grads[lag : lag + 1, at * 128 : at * 128 + 128]
    small[28:32] = jnp.zeros((4, 128), F32)


def fill_transposed(left, own, other):
    for at in range(0, own.shape[1], 256):
        left[at : at + 256, :256] = own[:, at : at + 256].T
        left[at : at + 256, 256:] = other[:, at : at + 256].T


def chunk_rows(left, axis, chunk):
    if axis == "y":
        return left[pl.ds(pl.multiple_of(chunk * 256, 256), 256)]
    return jnp.concatenate(
        [left[pl.ds(pl.multiple_of(at * 256 + chunk * 64, 64), 64)] for at in range(4)], 0
    )


def store_blocks(value, target, base, tiles, tile):
    value = value.astype(BF16)
    for chunk in range(4):
        for column in range(value.shape[1] // 128):
            target[base + chunk * tiles + tile + column] = value[
                chunk * 64 : chunk * 64 + 64, column * 128 : column * 128 + 128
            ]


def position(scalars, axis):
    return scalars[0 if axis == "y" else 1]


def wide_kernel(scalars, two, two_other, cot, cot_other, *refs):
    own, other, sends, keeps = refs[:3], refs[3:6], refs[6:10], refs[10:14]
    left_two, left_cot = refs[14:]
    fill_transposed(left_cot, cot, cot_other)
    fill_transposed(left_two, two, two_other)
    core = scalars[3]
    runs = [(k, k, at, min(256, CUT - at), at // 128) for k in range(3) for at in range(0, CUT, 256)]
    runs += [(3, k, CUT, WIDE_COLUMNS - CUT, 2 * k) for k in range(3)]
    for kind, (axis, pairing) in enumerate(FIRST):
        at = position(scalars, axis)
        first, second = peer(at, pairing), peer(at, 1 - pairing)
        chunks = (at, second, first, peer(first, 1 - pairing))
        for slot, chunk in enumerate(chunks):
            target = keeps[kind] if slot < 2 else sends[kind]
            rows = {}
            for run_kind, matrix, column, width, tile in runs:
                if run_kind != kind:
                    continue
                if (matrix == 0) not in rows:
                    rows[matrix == 0] = chunk_rows(left_cot if matrix == 0 else left_two, axis, chunk)
                left = rows[matrix == 0]
                mine = pl.ds(pl.multiple_of(core * WIDE_COLUMNS + column, 128), width)
                value = dot(left[:, :256], own[matrix][:, mine])
                value = value + dot(left[:, 256:], other[matrix][:, column : column + width])
                store_blocks(value, target, (slot % 2) * 4 * WIDE[kind], WIDE[kind], tile)


def split_small(value, target, at):
    high = value.astype(BF16)
    target[at, :32] = high
    target[at, 32:] = (value - high.astype(F32)).astype(BF16)


def join_small(source, at):
    return source[at, :32].astype(F32) + source[at, 32:].astype(F32)


def rounded_small(value):
    high = value.astype(BF16)
    return high.astype(F32) + (value - high.astype(F32)).astype(BF16).astype(F32)


def sum_small(value, gots, layout, axis):
    near, far, cross = (
        join_small(gots[SETS.index((axis, p))], layout[SETS.index((axis, p))][0]["small"]) for p in range(3)
    )
    return (rounded_small(value) + cross) + (near + far)


def take(refs, *counts):
    out, at = [], 0
    for count in counts:
        out.append(refs[at : at + count])
        at += count
    return out


def first_kernel(scalars, *refs):
    gots, keeps, operands, (small,), sends, wide_keeps, narrow_keeps, lefts = take(refs, 4, 4, 8, 1, 6, 4, 4, 2)
    one, one_other, low, low_other, backs, backs_other, ymix, ymix_other = operands
    left_one, left_low = lefts
    fill_transposed(left_one, one, one_other)
    fill_transposed(left_low, low, low_other)
    mine = pl.ds(pl.multiple_of(scalars[3] * 256, 256), 256)
    for kind in range(4):
        axis = FIRST[kind][0]
        at = position(scalars, axis)
        left, own, other = (
            (left_one, backs[kind, :, mine], backs_other[kind])
            if kind < 3
            else (left_low, ymix[:, mine], ymix_other[...])
        )
        for pairing in (0, 1, 2, None):
            rows = chunk_rows(left, axis, at if pairing is None else peer(at, pairing))
            value = dot(rows[:, :256], own) + dot(rows[:, 256:], other)
            if pairing is None:
                store_blocks(value, narrow_keeps[kind], 0, 2, 0)
            else:
                place = SETS.index((axis, pairing))
                store_blocks(value, sends[place], ROUND_ONE[place][0]["narrow", kind], 2, 0)
    for kind in range(4):
        half = 4 * WIDE[kind]
        place = SETS.index(SECOND[kind])
        base = ROUND_ONE[place][0]["wide", kind]
        wide_keeps[kind][...] = (keeps[kind][:half].astype(F32) + gots[kind][:half].astype(F32)).astype(BF16)
        sends[place][base : base + half] = (
            keeps[kind][half:].astype(F32) + gots[kind][half:].astype(F32)
        ).astype(BF16)
    for pairing in range(3):
        place = SETS.index(("y", pairing))
        split_small(small[...], sends[place], ROUND_ONE[place][0]["small"])


def second_kernel(scalars, *refs):
    gots, wide_in, narrow_in, (small,), sends, wide_keeps, narrow_keeps, (new_small,) = take(refs, 6, 4, 4, 1, 6, 4, 4, 1)
    for family, tiles, keeps, new_keeps in (
        ("narrow", NARROW, narrow_in, narrow_keeps),
        ("wide", WIDE, wide_in, wide_keeps),
    ):
        for kind in range(4):
            axis, count = FIRST[kind][0], tiles[kind]
            came = [SECOND[kind]] if family == "wide" else [(axis, p) for p in range(3)]
            came = [SETS.index(entry) for entry in came]

            def total(chunk):
                value = keeps[kind][pl.ds(chunk * count, count)].astype(F32)
                for place in came:
                    base = ROUND_ONE[place][0][family, kind]
                    value = value + gots[place][pl.ds(base + chunk * count, count)].astype(F32)
                return value.astype(BF16)

            at = position(scalars, OTHER_AXIS[axis])
            new_keeps[kind][...] = total(at)
            for pairing in range(3):
                place = SETS.index((OTHER_AXIS[axis], pairing))
                base = ROUND_TWO[place][0][family, kind]
                sends[place][base : base + count] = total(peer(at, pairing))
    value = sum_small(small[...], gots, ROUND_ONE, "y")
    new_small[...] = value
    for pairing in range(3):
        place = SETS.index(("z", pairing))
        split_small(value, sends[place], ROUND_TWO[place][0]["small"])


def third_kernel(scalars, *refs):
    gots, wide_in, narrow_in, (small,), (send, keep) = take(refs, 6, 4, 4, 1, 2)
    here = scalars[2]
    tile = 0
    for family, tiles, keeps in (("wide", WIDE, wide_in), ("narrow", NARROW, narrow_in)):
        for kind in range(4):
            count = tiles[kind]
            value = keeps[kind][...].astype(F32)
            for pairing in range(3):
                place = SETS.index((OTHER_AXIS[FIRST[kind][0]], pairing))
                base = ROUND_TWO[place][0][family, kind]
                value = value + gots[place][base : base + count].astype(F32)
            zero, one = value[:, :32], value[:, 32:]
            keep[tile : tile + count] = jnp.where(here == 0, zero, one)
            send[tile : tile + count] = jnp.where(here == 0, one, zero).astype(BF16)
            tile += count
    value = sum_small(small[...], gots, ROUND_TWO, "z")
    high = value.astype(BF16)
    low = (value - high.astype(F32)).astype(BF16)
    send[TILES] = high
    send[TILES + 1] = low
    keep[TILES] = high.astype(F32)
    keep[TILES + 1] = low.astype(F32)


def cores_kernel(scalars, keep, got, mine, away):
    core = scalars[3]
    total = keep[:TILES] + got[:TILES].astype(F32)
    zero, one = total[:, :16], total[:, 16:]
    mine[:TILES] = jnp.where(core == 0, zero, one)
    away[:TILES] = jnp.where(core == 0, one, zero)
    small = (keep[TILES] + keep[TILES + 1]) + (got[TILES].astype(F32) + got[TILES + 1].astype(F32))
    for at in range(2):
        mine[TILES + at] = small[at * 16 : at * 16 + 16]
        away[TILES + at] = small[at * 16 : at * 16 + 16]


def outputs_kernel(scalars, mine, got, down, gate, up, inner, out, small):
    core = scalars[3]

    def place(target, tile, column, columns):
        zero, one = jnp.where(core == 0, mine[tile], got[tile]), jnp.where(core == 0, got[tile], mine[tile])
        target[:, column : column + 128] = zero
        target[:, columns + column : columns + column + 128] = one

    for matrix, target in enumerate((down, gate, up)):
        for column in range(0, WIDE_COLUMNS, 128):
            tile = 7 * matrix + column // 128 if column < CUT else 21 + 2 * matrix + (column - CUT) // 128
            place(target, tile, column, WIDE_COLUMNS)
    for kind in range(4):
        for column in range(2):
            place(inner.at[kind] if kind < 3 else out, 27 + 2 * kind + column, column * 128, 256)
    small[:16] = mine[TILES] + got[TILES]
    small[16:] = mine[TILES + 1] + got[TILES + 1]


def swap_round(sends, sets):
    return [swap(value, PAIRS[entry]) for value, entry in zip(sends, sets)]


def blocks(counts):
    return [like((count, *BLOCK), BF16) for count in counts]


def on_device(
    tokens,
    starts,
    gain_one,
    in_weight,
    conv_weight,
    out_weight,
    gain_two,
    gate_weight,
    up_weight,
    down_weight,
    cotangent,
):
    at = lax.axis_index("seq")
    core = at % 2
    scalars = jnp.stack([at // 16, (at // 4) % 4, (at // 2) % 2, core, starts[0]]).astype(jnp.int32)
    run = functools.partial(call, scalars=scalars)
    rows, width = tokens.shape
    channels = conv_weight.shape[1]
    in_parts = in_weight.transpose(1, 0, 2)
    gain_one_row, gain_two_row = gain_one.reshape(1, -1), gain_two.reshape(1, -1)

    def share(value):
        return swap(value, CORES)

    tail = run(tail_kernel, operands=[tokens, gain_one_row, in_parts], outs=[like((16, channels), BF16)])[0]
    incoming = from_behind(tail, "seq", 1)
    normed_one, parts, gated = run(
        project_kernel,
        operands=[tokens, gain_one_row, in_parts],
        outs=[like((rows, width), BF16), like((3, rows, channels), F32), like((rows, channels), BF16)],
    )
    conv, ymix, ymix_away, branch = run(
        mix_kernel,
        operands=[gated, incoming, parts, conv_weight, out_weight],
        outs=[
            like((rows, channels), F32),
            like((rows, channels), BF16),
            like((rows, channels // 2), BF16),
            like((rows, width), BF16),
        ],
    )
    branch_other = swap(branch, ACROSS)
    hidden_grad = jnp.einsum("td,fd->tf", cotangent, down_weight, preferred_element_type=F32)
    cotangent_other = share(cotangent)
    normed_one_other = share(normed_one)
    ymix_other = share(ymix_away)
    resid = tokens.astype(F32) + (branch.astype(F32) + branch_other.astype(F32))
    normed_two = (resid * norm_scale(resid) * gain_two).astype(BF16)
    gate_act = jnp.dot(normed_two, gate_weight, preferred_element_type=F32)
    up_act = jnp.dot(normed_two, up_weight, preferred_element_type=F32)
    sigmoid_gate = jax.nn.sigmoid(gate_act)
    swish = gate_act * sigmoid_gate
    hidden = (swish * up_act).astype(BF16)
    swish_slope = sigmoid_gate * (1.0 + gate_act * (1.0 - sigmoid_gate))
    gate_back = (hidden_grad * up_act * swish_slope).astype(BF16)
    up_back = (hidden_grad * swish).astype(BF16)
    norm_two_part = jnp.einsum("tf,df->td", gate_back, gate_weight, preferred_element_type=F32)
    norm_two_part = norm_two_part + jnp.einsum(
        "tf,df->td", up_back, up_weight, preferred_element_type=F32
    )
    norm_two_part = norm_two_part.astype(BF16)
    norm_two_other = swap(norm_two_part, ACROSS)

    results = run(
        wide_kernel,
        operands=[normed_two, share(normed_two), cotangent, cotangent_other, hidden, gate_back, up_back]
        + [share(away_half(value, core)) for value in (hidden, gate_back, up_back)],
        outs=blocks([8 * count for count in WIDE] * 2),
        scratch=[pltpu.VMEM((width, 2 * rows), BF16)] * 2,
    )
    sends, keeps = list(results[:4]), list(results[4:])
    norm_two_other, keeps[3] = lax.optimization_barrier((norm_two_other, keeps[3]))
    gots = swap_round(sends, FIRST)

    edge_operands = [norm_two_part, norm_two_other, resid, gain_two_row, cotangent, out_weight, parts, conv_weight]
    edge = run(edge_kernel, operands=edge_operands, outs=[like((8, channels), F32)])[0]
    returned = from_behind(edge, "seq", -1)
    resid_grad, resid_low, gain_two_grad, c_back, gated_back, tap_grads = run(
        middle_kernel,
        operands=edge_operands + [conv, gated, incoming],
        outs=[
            like((rows, width), F32),
            like((rows, width), BF16),
            like((1, width), F32),
            like((rows, channels), BF16),
            like((rows, channels), F32),
            like((3, channels), F32),
        ],
    )
    resid_low_other = share(resid_low)
    backs, backs_away, norm_one_low, small = run(
        last_kernel,
        operands=[gated_back, returned, parts, c_back, in_parts, tokens, gain_two_grad, tap_grads],
        outs=[
            like((3, rows, channels), BF16),
            like((3, rows, channels // 2), BF16),
            like((rows, width), BF16),
            like((32, 128), F32),
        ],
    )
    norm_one_other = swap(norm_one_low, ACROSS)
    results = run(
        first_kernel,
        operands=gots
        + keeps
        + [normed_one, normed_one_other, resid_low, resid_low_other, backs, share(backs_away), ymix, ymix_other]
        + [small],
        outs=blocks([total for _, total in ROUND_ONE])
        + blocks([4 * count for count in WIDE])
        + blocks([4 * count for count in NARROW]),
        scratch=[pltpu.VMEM((width, 2 * rows), BF16)] * 2,
    )
    sends, keeps = list(results[:6]), list(results[6:])
    gots = swap_round(sends, SETS)
    gots[0], norm_one_other = lax.optimization_barrier((gots[0], norm_one_other))
    results = run(
        second_kernel,
        operands=gots + keeps + [small],
        outs=blocks([total for _, total in ROUND_TWO]) + blocks(WIDE) + blocks(NARROW) + [like((32, 128), F32)],
    )
    sends, keeps, small = list(results[:6]), list(results[6:14]), results[14]
    down_part = jnp.dot(hidden, down_weight, preferred_element_type=F32).astype(BF16)
    norm_one_other, down_part = lax.optimization_barrier((norm_one_other, down_part))
    down_other = swap(down_part, ACROSS)
    gots = swap_round(sends, SETS)
    gots[0], down_other = lax.optimization_barrier((gots[0], down_other))
    beside, kept = run(
        third_kernel,
        operands=gots + keeps + [small],
        outs=[like((TILES + 2, 32, 128), BF16), like((TILES + 2, 32, 128), F32)],
    )
    mine, away = run(
        cores_kernel,
        operands=[kept, swap(beside, BESIDE)],
        outs=[like((TILES + 2, 16, 128), F32)] * 2,
    )
    down_g, gate_g, up_g, in_g, out_g, small = run(
        outputs_kernel,
        operands=[mine, swap(away, CORES)],
        outs=[like((16, 2 * WIDE_COLUMNS), F32)] * 3
        + [like((3, 16, channels), F32), like((16, channels), F32), like((32, 128), F32)],
    )
    in_g = in_g.transpose(1, 0, 2)
    gain_one_g = (small[:8] + swap(small[:8], ACROSS)).reshape(-1)
    gain_two_g = small[8:16].reshape(-1)
    conv_g = small[16:28].reshape(3, -1)

    mixed = (resid + (down_part.astype(F32) + down_other.astype(F32))).astype(BF16)
    inputs = tokens.astype(F32)
    norm_one_back = norm_one_low.astype(F32) + norm_one_other.astype(F32)
    tokens_grad = resid_grad + norm_backward(norm_one_back, inputs, norm_scale(inputs), gain_one)
    return (mixed, tokens_grad, gain_one_g, in_g, conv_g, out_g.T, gain_two_g, gate_g, up_g, down_g.T)


def solution(mesh):
    return jax.shard_map(
        on_device,
        mesh=mesh,
        in_specs=(
            P("seq", None),
            P("seq"),
            P(),
            P(None, None, "tensor"),
            P(None, "tensor"),
            P("tensor", None),
            P(),
            P(None, "tensor"),
            P(None, "tensor"),
            P("tensor", None),
            P("seq", None),
        ),
        out_specs=(
            P("seq", None),
            P("seq", None),
            P(),
            P("seq", None, "tensor"),
            P(None, "tensor"),
            P("tensor", "seq"),
            P(),
            P("seq", "tensor"),
            P("seq", "tensor"),
            P("tensor", "seq"),
        ),
        check_vma=False,
    )
```

time: 1680 us -> 171 us (0.10)
  waiting for transfers between devices: 1310 us -> 60.5 us
  blocking collectives: 274 us -> 0 us
  starting transfers between devices: 7.72 us -> 55.3 us
  matrix products: 45.3 us -> 14.3 us
  Pallas kernels: 0 us -> 24.4 us
    reduce_scatter x5 -> x0, waiting for transfers between devices: 1200 us -> none  [the longest x1 301 us: on_device(): lax.psum_scatter(up_g, 'seq', scatter_dimension=0, tiled=True)]
    psum x1 -> x0, blocking collectives: 274 us -> none  [on_device(): lax.psum((conv_g, gain_one_g, gain_two_g), 'seq')]
    psum x3 -> x0, waiting for transfers between devices: 107 us -> none  [the longest x1 52 us: on_device(): lax.psum(jnp.dot(ymix, out_weight, preferred_element_type=jnp.float32), '...]
    ppermute x0 -> x32, waiting for transfers between devices: none -> 59.6 us  [swap(): return lax.ppermute(value, AXES, pairs)]
    ppermute x0 -> x32, starting transfers between devices: none -> 47.9 us  [swap(): return lax.ppermute(value, AXES, pairs)]
    dot_general x15 -> x6, matrix products: 45.3 us -> 14.3 us  [the longest x1 3.97 us: on_device(): jnp.einsum('td,fd->tf', cotangent, down_weight, preferred_element_type=F32)]
    pallas_call x0 -> x12, Pallas kernels: none -> 24.4 us  [call(): pl.pallas_call(body, out_shape=tuple(outs), in_specs=[pl.BlockSpec(memory...]
  transfers between devices with their start and end apart: 10 -> 34, of which waited for: 10 -> 14; matrix products, arithmetic and copies ran while one was open for 2% -> 12% of each run, Pallas kernels for 0% -> 9%
where the time goes in v1:
time: 171 us; the launch traced here: 170 us
  waiting for transfers between devices  60.5 us (35%)
  starting transfers between devices  55.3 us (32%)
  Pallas kernels  24.4 us (14%)
  matrix products  14.3 us (8%)
  local copies, waits for them, and re-layouts  8.53 us (5%)
  other arithmetic  5.33 us (3%)
  between operations  1.78 us (1%)
    ppermute x32, waiting for transfers between devices, swap(): return lax.ppermute(value, AXES, pairs)  59.6 us
    ppermute x32, starting transfers between devices, swap(): return lax.ppermute(value, AXES, pairs)  47.9 us
    pallas_call x12, Pallas kernels, call(): pl.pallas_call(body, out_shape=tuple(outs), in_specs=[pl.BlockSpec(memory...  24.4 us
    unnamed x54, local copies, waits for them, and re-layouts  7.83 us
    ppermute x2, starting transfers between devices, from_behind(): lax.ppermute(value, axis, [(source, source + steps) for source in range(l...  7.42 us
    dot_general x1, matrix products, on_device(): jnp.einsum('td,fd->tf', cotangent, down_weight, preferred_element_type=F32)  3.97 us
    dot_general x1, matrix products, on_device(): up_act = jnp.dot(normed_two, up_weight, preferred_element_type=F32)  3.88 us
  transfers between devices with their start and end apart: 34, of which 14 were waited for; matrix products, arithmetic and copies ran while one was open for 12% of the time, Pallas kernels for 9%

profile of v1, /device:TPU:1, one launch (start us, length us, event | category | flops | bytes accessed | tf_op | source)
XLA Modules:
  0.0 170.2 jit_solution(793383731000157972)
XLA Ops:
  6.1 4.6 %collective-permute-start = (bf16[16,512]{1,0:T(8,128)(2,1)S(1)}, bf16[16,512]{1,0:T(8,128)(2,1)S(1)}, u32[]{:S(2)}, u32[]{:S(2)}) collective-permute-start(bf16[16,512]{1,0:T(8,128)(2,1)S(1)} %shard_map.187), channel_id=1, source_target_pairs={{0,2},{2,4},{4,6},{6,8},{8,10},{10,12},{12,14},{14,16},{16,18},{18... | collective-permute-start | bytes 49160 | tf_op jit(solution)/shard_map/ppermute | solution.py:101
  18.5 2.5 %collective-permute-start.1 = (bf16[256,1024]{1,0:T(8,128)(2,1)}, bf16[256,1024]{1,0:T(8,128)(2,1)}, u32[]{:S(2)}, u32[]{:S(2)}) collective-permute-start(bf16[256,1024]{1,0:T(8,128)(2,1)} %get-tuple-element.84), channel_id=1, source_target_pairs={{0,1},{2,3},{4,5},{6,7},{1,0},{3,2},{5,4},{7,6},{8,9},{10,11},{12,... | collective-permute-start | bytes 1572872 | tf_op jit(solution)/shard_map/ppermute | solution.py:95
  21.0 4.0 %fusion.10 = f32[256,2304]{1,0:T(8,128)S(1)} fusion(bf16[256,1024]{1,0:T(8,128)(2,1)} %cot.5, bf16[2304,1024]{1,0:T(8,128)(2,1)} %param.20), kind=kOutput, calls=%fused_computation.32 | convolution fusion | flops 1207959552 | bytes 7602176 | tf_op jit(solution)/shard_map/td,fd->tf/dot_general | solution.py:520
  25.0 7.7 %collective-permute-done.1 = bf16[256,1024]{1,0:T(8,128)(2,1)} collective-permute-done((bf16[256,1024]{1,0:T(8,128)(2,1)}, bf16[256,1024]{1,0:T(8,128)(2,1)}, u32[]{:S(2)}, u32[]{:S(2)}) %collective-permute-start.1) | collective-permute-done | bytes 524320 | tf_op jit(solution)/shard_map/ppermute | solution.py:95
  34.5 3.9 %fusion.9 = f32[256,2304]{1,0:T(8,128)S(1)} fusion(bf16[256,1024]{1,0:T(8,128)(2,1)S(1)} %multiply_convert_fusion.3.two, bf16[1024,2304]{1,0:T(8,128)(2,1)} %param.19), kind=kOutput, calls=%fused_computation.31 | convolution fusion | flops 1207959552 | bytes 7602176 | tf_op jit(solution)/shard_map/dot_general | solution.py:527
  38.4 2.3 %multiply_convert_fusion = (bf16[256,2304]{1,0:T(8,128)(2,1)S(1)}, bf16[256,2304]{1,0:T(8,128)(2,1)S(1)}, bf16[256,2304]{1,0:T(8,128)(2,1)S(1)}) fusion(f32[256,2304]{1,0:T(8,128)S(1)} %fusion.10, f32[256,2304]{1,0:T(8,128)S(1)} %fusion.9, bf16[256,1024]{1,0:T(8,128)(2,1)S(1)} %multiply_convert_fusion.3.two, bf16[1024,2304]{1,0:T(8,128)(2,1)S(1)} %bitcast.34), kind=kOutput, calls=%fused_computation | convolution fusion | flops 1216806912 | bytes 13500416 | tf_op jit(solution)/shard_map/dot_general | solution.py:526
  45.2 3.1 %collective-permute-start.11 = (bf16[256,1024]{1,0:T(8,128)(2,1)S(1)}, bf16[256,1024]{1,0:T(8,128)(2,1)S(1)}, u32[]{:S(2)}, u32[]{:S(2)}) collective-permute-start(bf16[256,1024]{1,0:T(8,128)(2,1)S(1)} %fusion.1.part), channel_id=1, source_target_pairs={{0,1},{2,3},{4,5},{6,7},{1,0},{3,2},{5,4},{7,6},{8,9},{10,11},{12,... | collective-permute-start | bytes 1572872 | tf_op jit(solution)/shard_map/ppermute | solution.py:95
  49.2 6.0 %shard_map.189 = (bf16[56,64,128]{2,1,0:T(8,128)(2,1)S(1)}, bf16[56,64,128]{2,1,0:T(8,128)(2,1)S(1)}, bf16[56,64,128]{2,1,0:T(8,128)(2,1)S(1)}, bf16[48,64,128]{...) custom-call(s32[5]{0:T(128)S(1)} %stack.19.scalars, ...), custom_call_target="tpu_custom_call" | custom-call | tf_op jit(solution)/shard_map/pallas_call | solution.py:121
  55.2 5.2 %collective-permute-done.11.other = bf16[256,1024]{1,0:T(8,128)(2,1)S(1)} collective-permute-done((bf16[256,1024]{1,0:T(8,128)(2,1)S(1)}, bf16[256,1024]{1,0:T(8,128)(2,1)S(1)}, u32[]{:S(2)}, u32[]{:S(2)}) %collective-permute-start.11) | collective-permute-done | bytes 524320 | tf_op jit(solution)/shard_map/ppermute | solution.py:95
  61.9 2.8 %collective-permute-start.14 = (f32[8,512]{1,0:T(8,128)S(1)}, f32[8,512]{1,0:T(8,128)S(1)}, u32[]{:S(2)}, u32[]{:S(2)}) collective-permute-start(f32[8,512]{1,0:T(8,128)S(1)} %shard_map.191), channel_id=1, source_target_pairs={{2,0},{4,2},{6,4},{8,6},{10,8},{12,10},{14,12},{16,14},{18,16},{20... | collective-permute-start | bytes 49160 | tf_op jit(solution)/shard_map/ppermute | solution.py:101
  64.7 2.7 %shard_map.190 = (f32[256,1024]{1,0:T(8,128)S(1)}, bf16[256,1024]{1,0:T(8,128)(2,1)S(1)}, f32[1,1024]{1,0:T(1,128)S(1)}, bf16[256,512]{1,0:T(8,128)(2,1)S(1)}, f...) custom-call(s32[5]{0:T(128)S(1)} %stack.19.scalars, bf16[256,1024]{1,0:T(8,128)(2,1)S(1)} %fusion.1.part, ...), custom_call_target="tpu_custom_call" | custom-call | tf_op jit(solution)/shard_map/pallas_call | solution.py:121
  70.2 4.0 %collective-permute-start.7 = (bf16[56,64,128]{2,1,0:T(8,128)(2,1)S(1)}, bf16[56,64,128]{2,1,0:T(8,128)(2,1)S(1)}, u32[]{:S(2)}, u32[]{:S(2)}) collective-permute-start(bf16[56,64,128]{2,1,0:T(8,128)(2,1)S(1)} %get-tuple-element.85), channel_id=1, source_target_pairs={{0,32},{2,34},{4,36},{6,38},{1,33},{3,35},{5,37},{7,39},{8,40},{10... | collective-permute-start | bytes 2752520 | tf_op jit(solution)/shard_map/ppermute | solution.py:95
  80.6 15.2 %collective-permute-done.10.refs_3_ = bf16[48,64,128]{2,1,0:T(8,128)(2,1)S(1)} collective-permute-done((bf16[48,64,128]{2,1,0:T(8,128)(2,1)S(1)}, bf16[48,64,128]{2,1,0:T(8,128)(2,1)S(1)}, u32[]{:S(2)}, u32[]{:S(2)}) %collective-permute-start.10) | collective-permute-done | bytes 786464 | tf_op jit(solution)/shard_map/ppermute | solution.py:95
  97.3 3.8 %shard_map.193 = (bf16[45,64,128]{2,1,0:T(8,128)(2,1)S(1)}, bf16[45,64,128]{2,1,0:T(8,128)(2,1)S(1)}, bf16[17,64,128]{2,1,0:T(8,128)(2,1)S(1)}, bf16[40,64,128]{...) custom-call(s32[5]{0:T(128)S(1)} %stack.19.scalars, ...), custom_call_target="tpu_custom_call" | custom-call | tf_op jit(solution)/shard_map/pallas_call | solution.py:121
  101.6 2.7 %collective-permute-start.18 = (bf16[256,1024]{1,0:T(8,128)(2,1)S(1)}, bf16[256,1024]{1,0:T(8,128)(2,1)S(1)}, u32[]{:S(2)}, u32[]{:S(2)}) collective-permute-start(bf16[256,1024]{1,0:T(8,128)(2,1)S(1)} %get-tuple-element.108), channel_id=1, source_target_pairs={{0,1},{2,3},{4,5},{6,7},{1,0},{3,2},{5,4},{7,6},{8,9},{10,11},{12,... | collective-permute-start | bytes 1572872 | tf_op jit(solution)/shard_map/ppermute | solution.py:95
  107.4 7.4 %collective-permute-done.18 = bf16[256,1024]{1,0:T(8,128)(2,1)S(1)} collective-permute-done((bf16[256,1024]{1,0:T(8,128)(2,1)S(1)}, bf16[256,1024]{1,0:T(8,128)(2,1)S(1)}, u32[]{:S(2)}, u32[]{:S(2)}) %collective-permute-start.18) | collective-permute-done | bytes 524320 | tf_op jit(solution)/shard_map/ppermute | solution.py:95
  114.7 2.7 %collective-permute-start.20 = (bf16[17,64,128]{2,1,0:T(8,128)(2,1)S(1)}, bf16[17,64,128]{2,1,0:T(8,128)(2,1)S(1)}, u32[]{:S(2)}, u32[]{:S(2)}) collective-permute-start(bf16[17,64,128]{2,1,0:T(8,128)(2,1)S(1)} %get-tuple-element.113), channel_id=1, source_target_pairs={{0,64},{2,66},{4,68},{6,70},{1,65},{3,67},{5,69},{7,71},{8,72},{10... | collective-permute-start | bytes 835592 | tf_op jit(solution)/shard_map/ppermute | solution.py:95
  119.7 2.8 %collective-permute-start.25 = (bf16[256,1024]{1,0:T(8,128)(2,1)S(1)}, bf16[256,1024]{1,0:T(8,128)(2,1)S(1)}, u32[]{:S(2)}, u32[]{:S(2)}) collective-permute-start(bf16[256,1024]{1,0:T(8,128)(2,1)S(1)} %convolution_convert_fusion), channel_id=1, source_target_pairs={{0,1},{2,3},{4,5},{6,7},{1,0},{3,2},{5,4},{7,6},{8,9},{10,11},{12,... | collective-permute-start | bytes 1572872 | tf_op jit(solution)/shard_map/ppermute | solution.py:95
  122.6 2.8 %collective-permute-done.20.refs_2_ = bf16[17,64,128]{2,1,0:T(8,128)(2,1)S(1)} collective-permute-done((bf16[17,64,128]{2,1,0:T(8,128)(2,1)S(1)}, bf16[17,64,128]{2,1,0:T(8,128)(2,1)S(1)}, u32[]{:S(2)}, u32[]{:S(2)}) %collective-permute-start.20) | collective-permute-done | bytes 278560 | tf_op jit(solution)/shard_map/ppermute | solution.py:95
  125.3 5.2 %collective-permute-done.21.refs_3_ = bf16[40,64,128]{2,1,0:T(8,128)(2,1)S(1)} collective-permute-done((bf16[40,64,128]{2,1,0:T(8,128)(2,1)S(1)}, bf16[40,64,128]{2,1,0:T(8,128)(2,1)S(1)}, u32[]{:S(2)}, u32[]{:S(2)}) %collective-permute-start.21) | collective-permute-done | bytes 655392 | tf_op jit(solution)/shard_map/ppermute | solution.py:95
  140.4 6.7 %collective-permute-done.26.refs_1_ = bf16[17,64,128]{2,1,0:T(8,128)(2,1)S(1)} collective-permute-done((bf16[17,64,128]{2,1,0:T(8,128)(2,1)S(1)}, bf16[17,64,128]{2,1,0:T(8,128)(2,1)S(1)}, u32[]{:S(2)}, u32[]{:S(2)}) %collective-permute-start.26) | collective-permute-done | bytes 278560 | tf_op jit(solution)/shard_map/ppermute | solution.py:95
  148.6 5.2 %collective-permute-done.31.got = bf16[37,32,128]{2,1,0:T(8,128)(2,1)S(1)} collective-permute-done((bf16[37,32,128]{2,1,0:T(8,128)(2,1)S(1)}, bf16[37,32,128]{2,1,0:T(8,128)(2,1)S(1)}, u32[]{:S(2)}, u32[]{:S(2)}) %collective-permute-start.31) | collective-permute-done | bytes 303136 | tf_op jit(solution)/shard_map/ppermute | solution.py:95
  154.4 8.0 %collective-permute-start.32 = (f32[37,16,128]{2,1,0:T(8,128)S(1)}, f32[37,16,128]{2,1,0:T(8,128)S(1)}, u32[]{:S(2)}, u32[]{:S(2)}) collective-permute-start(f32[37,16,128]{2,1,0:T(8,128)S(1)} %get-tuple-element.147), channel_id=1, source_target_pairs={{0,2},{2,0},{4,6},{6,4},{1,3},{3,1},{5,7},{7,5},{8,10},{10,8},{12,... | collective-permute-start | bytes 909320 | tf_op jit(solution)/shard_map/ppermute | solution.py:95
  165.2 2.7 %collective-permute-start.33 = (f32[8,128]{1,0:T(8,128)S(1)}, f32[8,128]{1,0:T(8,128)S(1)}, u32[]{:S(2)}, u32[]{:S(2)}) collective-permute-start(f32[8,128]{1,0:T(8,128)S(1)} %slice.34), channel_id=1, source_target_pairs={{0,1},{2,3},{4,5},{6,7},{1,0},{3,2},{5,4},{7,6},{8,9},{10,11},{12,... | collective-permute-start | bytes 12296 | tf_op jit(solution)/shard_map/ppermute | solution.py:95
  (134 shorter events, 54.3 us)
Async XLA Ops:
  18.5 14.2 %collective-permute-start.1 = (bf16[256,1024]{1,0:T(8,128)(2,1)}, bf16[256,1024]{1,0:T(8,128)(2,1)}, u32[]{:S(2)}, u32[]{:S(2)}) collective-permute-start(bf16[256,1024]{1,0:T(8,128)(2,1)} %get-tuple-element.84), channel_id=1, source_target_pairs={{0,1},{2,3},{4,5},{6,7},{1,0},{3,2},{5,4},{7,6},{8,9},{10,11},{12,... | collective-permute-start | bytes 1572872 | tf_op jit(solution)/shard_map/ppermute | solution.py:95
  21.0 24.2 %collective-permute-start.3 = (bf16[256,1024]{1,0:T(8,128)(2,1)}, bf16[256,1024]{1,0:T(8,128)(2,1)}, u32[]{:S(2)}, u32[]{:S(2)}) collective-permute-start(bf16[256,1024]{1,0:T(8,128)(2,1)} %cot.5), channel_id=1, source_target_pairs={{0,2},{2,0},{4,6},{6,4},{1,3},{3,1},{5,7},{7,5},{8,10},{10,8},{12,... | collective-permute-start | bytes 1572872 | tf_op jit(solution)/shard_map/ppermute | solution.py:95
  34.4 13.9 %collective-permute-start.2 = (bf16[256,1024]{1,0:T(8,128)(2,1)S(1)}, bf16[256,1024]{1,0:T(8,128)(2,1)S(1)}, u32[]{:S(2)}, u32[]{:S(2)}) collective-permute-start(bf16[256,1024]{1,0:T(8,128)(2,1)S(1)} %multiply_convert_fusion.3.two), channel_id=1, source_target_pairs={{0,2},{2,0},{4,6},{6,4},{1,3},{3,1},{5,7},{7,5},{8,10},{10,8},{12,... | collective-permute-start | bytes 1572872 | tf_op jit(solution)/shard_map/ppermute | solution.py:95
  45.2 15.2 %collective-permute-start.11 = (bf16[256,1024]{1,0:T(8,128)(2,1)S(1)}, bf16[256,1024]{1,0:T(8,128)(2,1)S(1)}, u32[]{:S(2)}, u32[]{:S(2)}) collective-permute-start(bf16[256,1024]{1,0:T(8,128)(2,1)S(1)} %fusion.1.part), channel_id=1, source_target_pairs={{0,1},{2,3},{4,5},{6,7},{1,0},{3,2},{5,4},{7,6},{8,9},{10,11},{12,... | collective-permute-start | bytes 1572872 | tf_op jit(solution)/shard_map/ppermute | solution.py:95
  48.4 27.7 %collective-permute-start.12 = (bf16[256,1024]{1,0:T(8,128)(2,1)S(1)}, bf16[256,1024]{1,0:T(8,128)(2,1)S(1)}, u32[]{:S(2)}, u32[]{:S(2)}) collective-permute-start(bf16[256,1024]{1,0:T(8,128)(2,1)S(1)} %copy-done.12), channel_id=1, source_target_pairs={{0,2},{2,0},{4,6},{6,4},{1,3},{3,1},{5,7},{7,5},{8,10},{10,8},{12,... | collective-permute-start | bytes 1572872 | tf_op jit(solution)/shard_map/ppermute | solution.py:95
  48.9 27.2 %collective-permute-start.16 = (bf16[256,256]{1,0:T(8,128)(2,1)S(1)}, bf16[256,256]{1,0:T(8,128)(2,1)S(1)}, u32[]{:S(2)}, u32[]{:S(2)}) collective-permute-start(bf16[256,256]{1,0:T(8,128)(2,1)S(1)} %copy-done.20), channel_id=1, source_target_pairs={{0,2},{2,0},{4,6},{6,4},{1,3},{3,1},{5,7},{7,5},{8,10},{10,8},{12,... | collective-permute-start | bytes 393224 | tf_op jit(solution)/shard_map/ppermute | solution.py:95
  70.2 25.7 %collective-permute-start.7 = (bf16[56,64,128]{2,1,0:T(8,128)(2,1)S(1)}, bf16[56,64,128]{2,1,0:T(8,128)(2,1)S(1)}, u32[]{:S(2)}, u32[]{:S(2)}) collective-permute-start(bf16[56,64,128]{2,1,0:T(8,128)(2,1)S(1)} %get-tuple-element.85), channel_id=1, source_target_pairs={{0,32},{2,34},{4,36},{6,38},{1,33},{3,35},{5,37},{7,39},{8,40},{10... | collective-permute-start | bytes 2752520 | tf_op jit(solution)/shard_map/ppermute | solution.py:95
  74.2 22.8 %collective-permute-start.8 = (bf16[56,64,128]{2,1,0:T(8,128)(2,1)S(1)}, bf16[56,64,128]{2,1,0:T(8,128)(2,1)S(1)}, u32[]{:S(2)}, u32[]{:S(2)}) collective-permute-start(bf16[56,64,128]{2,1,0:T(8,128)(2,1)S(1)} %get-tuple-element.86), channel_id=1, source_target_pairs={{0,96},{2,98},{4,100},{6,102},{1,97},{3,99},{5,101},{7,103},{8,104... | collective-permute-start | bytes 2752520 | tf_op jit(solution)/shard_map/ppermute | solution.py:95
  76.1 21.3 %collective-permute-start.9 = (bf16[56,64,128]{2,1,0:T(8,128)(2,1)S(1)}, bf16[56,64,128]{2,1,0:T(8,128)(2,1)S(1)}, u32[]{:S(2)}, u32[]{:S(2)}) collective-permute-start(bf16[56,64,128]{2,1,0:T(8,128)(2,1)S(1)} %get-tuple-element.87), channel_id=1, source_target_pairs={{0,8},{2,10},{4,12},{6,14},{1,9},{3,11},{5,13},{7,15},{8,0},{10,2}... | collective-permute-start | bytes 2752520 | tf_op jit(solution)/shard_map/ppermute | solution.py:95
  76.1 19.7 %collective-permute-start.10 = (bf16[48,64,128]{2,1,0:T(8,128)(2,1)S(1)}, bf16[48,64,128]{2,1,0:T(8,128)(2,1)S(1)}, u32[]{:S(2)}, u32[]{:S(2)}) collective-permute-start(bf16[48,64,128]{2,1,0:T(8,128)(2,1)S(1)} %get-tuple-element.88), channel_id=1, source_target_pairs={{0,24},{2,26},{4,28},{6,30},{1,25},{3,27},{5,29},{7,31},{8,16},{10... | collective-permute-start | bytes 2359304 | tf_op jit(solution)/shard_map/ppermute | solution.py:95
  101.1 16.6 %collective-permute-start.17 = (bf16[45,64,128]{2,1,0:T(8,128)(2,1)S(1)}, bf16[45,64,128]{2,1,0:T(8,128)(2,1)S(1)}, u32[]{:S(2)}, u32[]{:S(2)}) collective-permute-start(bf16[45,64,128]{2,1,0:T(8,128)(2,1)S(1)} %get-tuple-element.107), channel_id=1, source_target_pairs={{0,32},{2,34},{4,36},{6,38},{1,33},{3,35},{5,37},{7,39},{8,40},{10... | collective-permute-start | bytes 2211848 | tf_op jit(solution)/shard_map/ppermute | solution.py:95
  101.6 13.2 %collective-permute-start.18 = (bf16[256,1024]{1,0:T(8,128)(2,1)S(1)}, bf16[256,1024]{1,0:T(8,128)(2,1)S(1)}, u32[]{:S(2)}, u32[]{:S(2)}) collective-permute-start(bf16[256,1024]{1,0:T(8,128)(2,1)S(1)} %get-tuple-element.108), channel_id=1, source_target_pairs={{0,1},{2,3},{4,5},{6,7},{1,0},{3,2},{5,4},{7,6},{8,9},{10,11},{12,... | collective-permute-start | bytes 1572872 | tf_op jit(solution)/shard_map/ppermute | solution.py:95
  104.3 26.2 %collective-permute-start.19 = (bf16[45,64,128]{2,1,0:T(8,128)(2,1)S(1)}, bf16[45,64,128]{2,1,0:T(8,128)(2,1)S(1)}, u32[]{:S(2)}, u32[]{:S(2)}) collective-permute-start(bf16[45,64,128]{2,1,0:T(8,128)(2,1)S(1)} %get-tuple-element.112), channel_id=1, source_target_pairs={{0,96},{2,98},{4,100},{6,102},{1,97},{3,99},{5,101},{7,103},{8,104... | collective-permute-start | bytes 2211848 | tf_op jit(solution)/shard_map/ppermute | solution.py:95
  105.8 24.7 %collective-permute-start.22 = (bf16[44,64,128]{2,1,0:T(8,128)(2,1)S(1)}, bf16[44,64,128]{2,1,0:T(8,128)(2,1)S(1)}, u32[]{:S(2)}, u32[]{:S(2)}) collective-permute-start(bf16[44,64,128]{2,1,0:T(8,128)(2,1)S(1)} %get-tuple-element.115), channel_id=1, source_target_pairs={{0,24},{2,26},{4,28},{6,30},{1,25},{3,27},{5,29},{7,31},{8,16},{10... | collective-permute-start | bytes 2162696 | tf_op jit(solution)/shard_map/ppermute | solution.py:95
  107.0 12.7 %collective-permute-start.23 = (bf16[16,64,128]{2,1,0:T(8,128)(2,1)S(1)}, bf16[16,64,128]{2,1,0:T(8,128)(2,1)S(1)}, u32[]{:S(2)}, u32[]{:S(2)}) collective-permute-start(bf16[16,64,128]{2,1,0:T(8,128)(2,1)S(1)} %get-tuple-element.116), channel_id=1, source_target_pairs={{0,16},{2,18},{4,20},{6,22},{1,17},{3,19},{5,21},{7,23},{8,24},{10... | collective-permute-start | bytes 786440 | tf_op jit(solution)/shard_map/ppermute | solution.py:95
  114.7 10.6 %collective-permute-start.20 = (bf16[17,64,128]{2,1,0:T(8,128)(2,1)S(1)}, bf16[17,64,128]{2,1,0:T(8,128)(2,1)S(1)}, u32[]{:S(2)}, u32[]{:S(2)}) collective-permute-start(bf16[17,64,128]{2,1,0:T(8,128)(2,1)S(1)} %get-tuple-element.113), channel_id=1, source_target_pairs={{0,64},{2,66},{4,68},{6,70},{1,65},{3,67},{5,69},{7,71},{8,72},{10... | collective-permute-start | bytes 835592 | tf_op jit(solution)/shard_map/ppermute | solution.py:95
  117.7 12.9 %collective-permute-start.21 = (bf16[40,64,128]{2,1,0:T(8,128)(2,1)S(1)}, bf16[40,64,128]{2,1,0:T(8,128)(2,1)S(1)}, u32[]{:S(2)}, u32[]{:S(2)}) collective-permute-start(bf16[40,64,128]{2,1,0:T(8,128)(2,1)S(1)} %get-tuple-element.114), channel_id=1, source_target_pairs={{0,8},{2,10},{4,12},{6,14},{1,9},{3,11},{5,13},{7,15},{8,0},{10,2}... | collective-permute-start | bytes 1966088 | tf_op jit(solution)/shard_map/ppermute | solution.py:95
  119.7 19.0 %collective-permute-start.25 = (bf16[256,1024]{1,0:T(8,128)(2,1)S(1)}, bf16[256,1024]{1,0:T(8,128)(2,1)S(1)}, u32[]{:S(2)}, u32[]{:S(2)}) collective-permute-start(bf16[256,1024]{1,0:T(8,128)(2,1)S(1)} %convolution_convert_fusion), channel_id=1, source_target_pairs={{0,1},{2,3},{4,5},{6,7},{1,0},{3,2},{5,4},{7,6},{8,9},{10,11},{12,... | collective-permute-start | bytes 1572872 | tf_op jit(solution)/shard_map/ppermute | solution.py:95
  133.2 13.9 %collective-permute-start.28 = (bf16[19,64,128]{2,1,0:T(8,128)(2,1)S(1)}, bf16[19,64,128]{2,1,0:T(8,128)(2,1)S(1)}, u32[]{:S(2)}, u32[]{:S(2)}) collective-permute-start(bf16[19,64,128]{2,1,0:T(8,128)(2,1)S(1)} %get-tuple-element.132), channel_id=1, source_target_pairs={{0,8},{2,10},{4,12},{6,14},{1,9},{3,11},{5,13},{7,15},{8,0},{10,2}... | collective-permute-start | bytes 933896 | tf_op jit(solution)/shard_map/ppermute | solution.py:95
  133.5 13.7 %collective-permute-start.29 = (bf16[19,64,128]{2,1,0:T(8,128)(2,1)S(1)}, bf16[19,64,128]{2,1,0:T(8,128)(2,1)S(1)}, u32[]{:S(2)}, u32[]{:S(2)}) collective-permute-start(bf16[19,64,128]{2,1,0:T(8,128)(2,1)S(1)} %get-tuple-element.133), channel_id=1, source_target_pairs={{0,24},{2,26},{4,28},{6,30},{1,25},{3,27},{5,29},{7,31},{8,16},{10... | collective-permute-start | bytes 933896 | tf_op jit(solution)/shard_map/ppermute | solution.py:95
  135.0 12.1 %collective-permute-start.30 = (bf16[19,64,128]{2,1,0:T(8,128)(2,1)S(1)}, bf16[19,64,128]{2,1,0:T(8,128)(2,1)S(1)}, u32[]{:S(2)}, u32[]{:S(2)}) collective-permute-start(bf16[19,64,128]{2,1,0:T(8,128)(2,1)S(1)} %get-tuple-element.134), channel_id=1, source_target_pairs={{0,16},{2,18},{4,20},{6,22},{1,17},{3,19},{5,21},{7,23},{8,24},{10... | collective-permute-start | bytes 933896 | tf_op jit(solution)/shard_map/ppermute | solution.py:95
  137.3 9.9 %collective-permute-start.26 = (bf16[17,64,128]{2,1,0:T(8,128)(2,1)S(1)}, bf16[17,64,128]{2,1,0:T(8,128)(2,1)S(1)}, u32[]{:S(2)}, u32[]{:S(2)}) collective-permute-start(bf16[17,64,128]{2,1,0:T(8,128)(2,1)S(1)} %get-tuple-element.130), channel_id=1, source_target_pairs={{0,96},{2,98},{4,100},{6,102},{1,97},{3,99},{5,101},{7,103},{8,104... | collective-permute-start | bytes 835592 | tf_op jit(solution)/shard_map/ppermute | solution.py:95
  138.8 8.4 %collective-permute-start.27 = (bf16[17,64,128]{2,1,0:T(8,128)(2,1)S(1)}, bf16[17,64,128]{2,1,0:T(8,128)(2,1)S(1)}, u32[]{:S(2)}, u32[]{:S(2)}) collective-permute-start(bf16[17,64,128]{2,1,0:T(8,128)(2,1)S(1)} %get-tuple-element.131), channel_id=1, source_target_pairs={{0,64},{2,66},{4,68},{6,70},{1,65},{3,67},{5,69},{7,71},{8,72},{10... | collective-permute-start | bytes 835592 | tf_op jit(solution)/shard_map/ppermute | solution.py:95
  154.4 9.4 %collective-permute-start.32 = (f32[37,16,128]{2,1,0:T(8,128)S(1)}, f32[37,16,128]{2,1,0:T(8,128)S(1)}, u32[]{:S(2)}, u32[]{:S(2)}) collective-permute-start(f32[37,16,128]{2,1,0:T(8,128)S(1)} %get-tuple-element.147), channel_id=1, source_target_pairs={{0,2},{2,0},{4,6},{6,4},{1,3},{3,1},{5,7},{7,5},{8,10},{10,8},{12,... | collective-permute-start | bytes 909320 | tf_op jit(solution)/shard_map/ppermute | solution.py:95
  (37 other events, 276.0 us)

commit v2 on v1

--- a/solution.py
+++ b/solution.py
@@ -28,6 +28,7 @@
 
 ACROSS = device_pairs(lambda y, z, x, core: (y, z, (x + 2) % 4, core))
 BESIDE = device_pairs(lambda y, z, x, core: (y, z, x ^ 1, core))
+SKEW = device_pairs(lambda y, z, x, core: (y, z, (x ^ 1) ^ 2, core))
 CORES = device_pairs(lambda y, z, x, core: (y, z, x, 1 - core))
 
 
@@ -116,7 +117,6 @@
 
 
 def call(body, *, scalars, operands, outs, scratch=()):
-    size = sum(v.size * v.dtype.itemsize for v in list(operands) + list(outs))
     whole = pl.BlockSpec(memory_space=pltpu.VMEM)
     return pl.pallas_call(
         body,
@@ -124,7 +124,7 @@
         in_specs=[pl.BlockSpec(memory_space=pltpu.SMEM)] + [whole] * len(operands),
         out_specs=tuple(whole for _ in outs),
         scratch_shapes=list(scratch),
-        compiler_params=pltpu.CompilerParams(vmem_limit_bytes=min(size + 14 * 2**20, 48 * 2**20)),
+        compiler_params=pltpu.CompilerParams(vmem_limit_bytes=16 * 2**20),
         cost_estimate=pl.CostEstimate(flops=0, bytes_accessed=0, transcendentals=0),
     )(scalars, *operands)
 
@@ -174,7 +174,7 @@
     return moved
 
 
-def mix_kernel(scalars, gated, incoming, parts, taps, weight, conv, ymix, ymix_away, branch):
+def mix_kernel(scalars, gated, incoming, parts, taps, weight, normed, conv, ymix, shared, branch):
     values = gated[...].astype(F32)
     before = incoming[...].astype(F32)
     total = taps[0:1] * values
@@ -184,7 +184,8 @@
         )
     conv[...] = total
     ymix[...] = (parts[1] * total).astype(BF16)
-    ymix_away[...] = away_half(ymix[...], scalars[3])
+    shared[:, : normed.shape[1]] = normed[...]
+    shared[:, normed.shape[1] :] = away_half(ymix[...], scalars[3])
     branch[...] = dot(ymix[...], weight[...]).astype(BF16)
 
 
@@ -233,7 +234,21 @@
 
 
 def last_kernel(
-    scalars, gated_back, returned, parts, c_back, weight, tokens, gain_two_grad, tap_grads, backs, backs_away, low, small
+    scalars,
+    gated_back,
+    returned,
+    parts,
+    c_back,
+    weight,
+    tokens,
+    gain_two_grad,
+    tap_grads,
+    resid_low,
+    down_part,
+    backs,
+    shared,
+    sums,
+    small,
 ):
     rows = gated_back.shape[0]
     links = linked_rows(scalars[4], returned.shape, rows - 8, rows)
@@ -243,9 +258,12 @@
     backs[1] = c_back[...]
     backs[2] = (total * parts[0]).astype(BF16)
     for k in range(3):
-        backs_away[k] = away_half(backs[k], scalars[3])
+        shared[4 + k] = away_half(backs[k], scalars[3])
+    for at in range(4):
+        shared[at] = resid_low[:, at * 256 : at * 256 + 256]
     grad = dot_rows(backs[0], weight[0]) + dot_rows(backs[1], weight[1]) + dot_rows(backs[2], weight[2])
-    low[...] = grad.astype(BF16)
+    sums[0] = grad.astype(BF16)
+    sums[1] = down_part[...]
     values = tokens[...].astype(F32)
     gain_grad = jnp.sum(grad * values * norm_scale(values), axis=0, keepdims=True)
     for at in range(8):
@@ -344,19 +362,23 @@
 
 
 def first_kernel(scalars, *refs):
-    gots, keeps, operands, (small,), sends, wide_keeps, narrow_keeps, lefts = take(refs, 4, 4, 8, 1, 6, 4, 4, 2)
-    one, one_other, low, low_other, backs, backs_other, ymix, ymix_other = operands
+    gots, keeps, operands, (small,), sends, wide_keeps, narrow_keeps, lefts = take(refs, 4, 4, 6, 1, 6, 4, 4, 2)
+    one, one_other, low, late_other, backs, ymix = operands
     left_one, left_low = lefts
-    fill_transposed(left_one, one, one_other)
-    fill_transposed(left_low, low, low_other)
+    width = one.shape[1]
+    for at in range(0, width, 256):
+        left_one[at : at + 256, :256] = one[:, at : at + 256].T
+        left_one[at : at + 256, 256:] = one_other[:, at : at + 256].T
+        left_low[at : at + 256, :256] = low[:, at : at + 256].T
+        left_low[at : at + 256, 256:] = late_other[at // 256].T
     mine = pl.ds(pl.multiple_of(scalars[3] * 256, 256), 256)
     for kind in range(4):
         axis = FIRST[kind][0]
         at = position(scalars, axis)
         left, own, other = (
-            (left_one, backs[kind, :, mine], backs_other[kind])
+            (left_one, backs[kind, :, mine], late_other[4 + kind])
             if kind < 3
-            else (left_low, ymix[:, mine], ymix_other[...])
+            else (left_low, ymix[:, mine], one_other[:, width:])
         )
         for pairing in (0, 1, 2, None):
             rows = chunk_rows(left, axis, at if pairing is None else peer(at, pairing))
@@ -411,7 +433,7 @@
 
 
 def third_kernel(scalars, *refs):
-    gots, wide_in, narrow_in, (small,), (send, keep) = take(refs, 6, 4, 4, 1, 2)
+    gots, wide_in, narrow_in, (small,), (send, keep, gain_sum) = take(refs, 6, 4, 4, 1, 3)
     here = scalars[2]
     tile = 0
     for family, tiles, keeps in (("wide", WIDE, wide_in), ("narrow", NARROW, narrow_in)):
@@ -431,23 +453,28 @@
     low = (value - high.astype(F32)).astype(BF16)
     send[TILES] = high
     send[TILES + 1] = low
+    gain_sum[...] = high[:8].astype(F32) + low[:8].astype(F32)
     keep[TILES] = high.astype(F32)
     keep[TILES + 1] = low.astype(F32)
 
 
-def cores_kernel(scalars, keep, got, mine, away):
+def cores_kernel(scalars, keep, across, skew, got, mine, away):
     core = scalars[3]
     total = keep[:TILES] + got[:TILES].astype(F32)
     zero, one = total[:, :16], total[:, 16:]
     mine[:TILES] = jnp.where(core == 0, zero, one)
     away[:TILES] = jnp.where(core == 0, one, zero)
-    small = (keep[TILES] + keep[TILES + 1]) + (got[TILES].astype(F32) + got[TILES + 1].astype(F32))
-    for at in range(2):
-        mine[TILES + at] = small[at * 16 : at * 16 + 16]
-        away[TILES + at] = small[at * 16 : at * 16 + 16]
-
-
-def outputs_kernel(scalars, mine, got, down, gate, up, inner, out, small):
+    here = keep[TILES] + keep[TILES + 1]
+    there = got[TILES].astype(F32) + got[TILES + 1].astype(F32)
+    both = here + there
+    gain = (here[:8] + across[...]) + (there[:8] + skew[...])
+    for target in (mine, away):
+        target[TILES, :8] = gain
+        target[TILES, 8:] = both[8:16]
+        target[TILES + 1] = both[16:]
+
+
+def outputs_kernel(scalars, mine, got, down, gate, up, inner, out, gain_one, gain_two, taps):
     core = scalars[3]
 
     def place(target, tile, column, columns):
@@ -462,8 +489,16 @@
     for kind in range(4):
         for column in range(2):
             place(inner.at[kind] if kind < 3 else out, 27 + 2 * kind + column, column * 128, 256)
-    small[:16] = mine[TILES] + got[TILES]
-    small[16:] = mine[TILES + 1] + got[TILES + 1]
+    gains = mine[TILES] + got[TILES]
+    rest = mine[TILES + 1] + got[TILES + 1]
+    for at in range(8):
+        lanes = slice(at * 128, at * 128 + 128)
+        gain_one[:, lanes] = gains[at : at + 1]
+        gain_two[:, lanes] = gains[8 + at : 9 + at]
+    for lag in range(3):
+        for at in range(4):
+            row = 4 * lag + at
+            taps[lag : lag + 1, at * 128 : at * 128 + 128] = rest[row : row + 1]
 
 
 def swap_round(sends, sets):
@@ -506,21 +541,23 @@
         operands=[tokens, gain_one_row, in_parts],
         outs=[like((rows, width), BF16), like((3, rows, channels), F32), like((rows, channels), BF16)],
     )
-    conv, ymix, ymix_away, branch = run(
+    conv, ymix, shared, branch = run(
         mix_kernel,
-        operands=[gated, incoming, parts, conv_weight, out_weight],
+        operands=[gated, incoming, parts, conv_weight, out_weight, normed_one],
         outs=[
             like((rows, channels), F32),
             like((rows, channels), BF16),
-            like((rows, channels // 2), BF16),
+            like((rows, width + channels // 2), BF16),
             like((rows, width), BF16),
         ],
     )
     branch_other = swap(branch, ACROSS)
     hidden_grad = jnp.einsum("td,fd->tf", cotangent, down_weight, preferred_element_type=F32)
     cotangent_other = share(cotangent)
-    normed_one_other = share(normed_one)
-    ymix_other = share(ymix_away)
+    shared_other = share(shared)
+    branch_other, cotangent_other, shared_other, hidden_grad = lax.optimization_barrier(
+        (branch_other, cotangent_other, shared_other, hidden_grad)
+    )
     resid = tokens.astype(F32) + (branch.astype(F32) + branch_other.astype(F32))
     normed_two = (resid * norm_scale(resid) * gain_two).astype(BF16)
     gate_act = jnp.dot(normed_two, gate_weight, preferred_element_type=F32)
@@ -546,7 +583,8 @@
         scratch=[pltpu.VMEM((width, 2 * rows), BF16)] * 2,
     )
     sends, keeps = list(results[:4]), list(results[4:])
-    norm_two_other, keeps[3] = lax.optimization_barrier((norm_two_other, keeps[3]))
+    down_part = jnp.dot(hidden, down_weight, preferred_element_type=F32).astype(BF16)
+    norm_two_other, keeps[3], down_part = lax.optimization_barrier((norm_two_other, keeps[3], down_part))
     gots = swap_round(sends, FIRST)
 
     edge_operands = [norm_two_part, norm_two_other, resid, gain_two_row, cotangent, out_weight, parts, conv_weight]
@@ -564,23 +602,22 @@
             like((3, channels), F32),
         ],
     )
-    resid_low_other = share(resid_low)
-    backs, backs_away, norm_one_low, small = run(
+    backs, shared, sums, small = run(
         last_kernel,
-        operands=[gated_back, returned, parts, c_back, in_parts, tokens, gain_two_grad, tap_grads],
+        operands=[gated_back, returned, parts, c_back, in_parts, tokens, gain_two_grad, tap_grads]
+        + [resid_low, down_part],
         outs=[
             like((3, rows, channels), BF16),
-            like((3, rows, channels // 2), BF16),
-            like((rows, width), BF16),
+            like((7, rows, 256), BF16),
+            like((2, rows, width), BF16),
             like((32, 128), F32),
         ],
     )
-    norm_one_other = swap(norm_one_low, ACROSS)
     results = run(
         first_kernel,
         operands=gots
         + keeps
-        + [normed_one, normed_one_other, resid_low, resid_low_other, backs, share(backs_away), ymix, ymix_other]
+        + [normed_one, shared_other, resid_low, share(shared), backs, ymix]
         + [small],
         outs=blocks([total for _, total in ROUND_ONE])
         + blocks([4 * count for count in WIDE])
@@ -589,43 +626,40 @@
     )
     sends, keeps = list(results[:6]), list(results[6:])
     gots = swap_round(sends, SETS)
-    gots[0], norm_one_other = lax.optimization_barrier((gots[0], norm_one_other))
+    sums_other = swap(sums, ACROSS)
+    gots[0], sums_other = lax.optimization_barrier((gots[0], sums_other))
     results = run(
         second_kernel,
         operands=gots + keeps + [small],
         outs=blocks([total for _, total in ROUND_TWO]) + blocks(WIDE) + blocks(NARROW) + [like((32, 128), F32)],
     )
     sends, keeps, small = list(results[:6]), list(results[6:14]), results[14]
-    down_part = jnp.dot(hidden, down_weight, preferred_element_type=F32).astype(BF16)
-    norm_one_other, down_part = lax.optimization_barrier((norm_one_other, down_part))
-    down_other = swap(down_part, ACROSS)
     gots = swap_round(sends, SETS)
-    gots[0], down_other = lax.optimization_barrier((gots[0], down_other))
-    beside, kept = run(
+    beside, kept, gain_sum = run(
         third_kernel,
         operands=gots + keeps + [small],
-        outs=[like((TILES + 2, 32, 128), BF16), like((TILES + 2, 32, 128), F32)],
-    )
+        outs=[like((TILES + 2, 32, 128), BF16), like((TILES + 2, 32, 128), F32), like((8, 128), F32)],
+    )
+    gots = [swap(gain_sum, ACROSS), swap(gain_sum, SKEW), swap(beside, BESIDE)]
+    mixed = (resid + (sums[1].astype(F32) + sums_other[1].astype(F32))).astype(BF16)
+    inputs = tokens.astype(F32)
+    norm_one_back = sums[0].astype(F32) + sums_other[0].astype(F32)
+    tokens_grad = resid_grad + norm_backward(norm_one_back, inputs, norm_scale(inputs), gain_one)
+    gots[0], mixed, tokens_grad = lax.optimization_barrier((gots[0], mixed, tokens_grad))
     mine, away = run(
         cores_kernel,
-        operands=[kept, swap(beside, BESIDE)],
+        operands=[kept] + gots,
         outs=[like((TILES + 2, 16, 128), F32)] * 2,
     )
-    down_g, gate_g, up_g, in_g, out_g, small = run(
+    down_g, gate_g, up_g, in_g, out_g, gain_one_g, gain_two_g, conv_g = run(
         outputs_kernel,
         operands=[mine, swap(away, CORES)],
         outs=[like((16, 2 * WIDE_COLUMNS), F32)] * 3
-        + [like((3, 16, channels), F32), like((16, channels), F32), like((32, 128), F32)],
-    )
-    in_g = in_g.transpose(1, 0, 2)
-    gain_one_g = (small[:8] + swap(small[:8], ACROSS)).reshape(-1)
-    gain_two_g = small[8:16].reshape(-1)
-    conv_g = small[16:28].reshape(3, -1)
-
-    mixed = (resid + (down_part.astype(F32) + down_other.astype(F32))).astype(BF16)
-    inputs = tokens.astype(F32)
-    norm_one_back = norm_one_low.astype(F32) + norm_one_other.astype(F32)
-    tokens_grad = resid_grad + norm_backward(norm_one_back, inputs, norm_scale(inputs), gain_one)
+        + [like((3, 16, channels), F32), like((16, channels), F32)]
+        + [like((1, width), F32)] * 2
+        + [like((3, channels), F32)],
+    )
+    in_g, gain_one_g, gain_two_g = in_g.transpose(1, 0, 2), gain_one_g.reshape(-1), gain_two_g.reshape(-1)
     return (mixed, tokens_grad, gain_one_g, in_g, conv_g, out_g.T, gain_two_g, gate_g, up_g, down_g.T)
 
 

time: 171 us -> 158 us (0.924)
  waiting for transfers between devices: 60.5 us -> 48.5 us
  starting transfers between devices: 55.3 us -> 58.9 us
  local copies, waits for them, and re-layouts: 8.53 us -> 6 us
    ppermute x32 -> x30, waiting for transfers between devices: 59.6 us -> 48.5 us  [swap(): return lax.ppermute(value, AXES, pairs)]
    ppermute x32 -> x30, starting transfers between devices: 47.9 us -> 51.5 us  [swap(): return lax.ppermute(value, AXES, pairs)]
    dot_general x1, matrix products: 3.88 us -> 1.42 us  [on_device(): up_act = jnp.dot(normed_two, up_weight, preferred_element_type=F32)]
    unnamed x54 -> x44, local copies, waits for them, and re-layouts: 7.83 us -> 5.92 us
    dot_general x1, matrix products: 2.29 us -> 4.03 us  [on_device(): gate_act = jnp.dot(normed_two, gate_weight, preferred_element_type=F32)]
  transfers between devices with their start and end apart: 34 -> 32, of which waited for: 14 -> 15; matrix products, arithmetic and copies ran while one was open for 12% -> 11% of each run, Pallas kernels for 9% -> 11%
where the time goes in v2:
time: 158 us
  starting transfers between devices  58.9 us (37%)
  waiting for transfers between devices  48.5 us (31%)
  Pallas kernels  23.9 us (15%)
  matrix products  13.5 us (9%)
  local copies, waits for them, and re-layouts  6 us (4%)
  other arithmetic  5.61 us (4%)
  between operations  1.75 us (1%)
    ppermute x30, starting transfers between devices, swap(): return lax.ppermute(value, AXES, pairs)  51.5 us
    ppermute x30, waiting for transfers between devices, swap(): return lax.ppermute(value, AXES, pairs)  48.5 us
    pallas_call x12, Pallas kernels, call(): pl.pallas_call(body, out_shape=tuple(outs), in_specs=[pl.BlockSpec(memory...  23.9 us
    ppermute x2, starting transfers between devices, from_behind(): lax.ppermute(value, axis, [(source, source + steps) for source in range(l...  7.35 us
    unnamed x44, local copies, waits for them, and re-layouts  5.92 us
    dot_general x1, matrix products, on_device(): gate_act = jnp.dot(normed_two, gate_weight, preferred_element_type=F32)  4.03 us
    dot_general x1, matrix products, on_device(): jnp.einsum('td,fd->tf', cotangent, down_weight, preferred_element_type=F32)  3.81 us
  transfers between devices with their start and end apart: 32, of which 15 were waited for; matrix products, arithmetic and copies ran while one was open for 11% of the time, Pallas kernels for 11%

profile of v2, /device:TPU:1, one launch (start us, length us, event | category | flops | bytes accessed | tf_op | source)
XLA Modules:
  0.0 158.1 jit_solution(8516867519051592998)
XLA Ops:
  6.1 4.6 %collective-permute-start = (bf16[16,512]{1,0:T(8,128)(2,1)S(1)}, bf16[16,512]{1,0:T(8,128)(2,1)S(1)}, u32[]{:S(2)}, u32[]{:S(2)}) collective-permute-start(bf16[16,512]{1,0:T(8,128)(2,1)S(1)} %shard_map.187), channel_id=1, source_target_pairs={{0,2},{2,4},{4,6},{6,8},{8,10},{10,12},{12,14},{14,16},{16,18},{18... | collective-permute-start | bytes 49160 | tf_op jit(solution)/shard_map/ppermute | solution.py:102
  16.6 2.5 %collective-permute-start.1 = (bf16[256,1024]{1,0:T(8,128)(2,1)}, bf16[256,1024]{1,0:T(8,128)(2,1)}, u32[]{:S(2)}, u32[]{:S(2)}) collective-permute-start(bf16[256,1024]{1,0:T(8,128)(2,1)} %get-tuple-element.92), channel_id=1, source_target_pairs={{0,1},{2,3},{4,5},{6,7},{1,0},{3,2},{5,4},{7,6},{8,9},{10,11},{12,... | collective-permute-start | bytes 1572872 | tf_op jit(solution)/shard_map/ppermute | solution.py:96
  19.1 3.8 %fusion.10 = f32[256,2304]{1,0:T(8,128)S(1)} fusion(bf16[256,1024]{1,0:T(8,128)(2,1)S(1)} %copy-done.5, bf16[2304,1024]{1,0:T(8,128)(2,1)} %param.20), kind=kOutput, calls=%fused_computation.30 | convolution fusion | flops 1207959552 | bytes 7602176 | tf_op jit(solution)/shard_map/td,fd->tf/dot_general | solution.py:555
  22.9 9.0 %collective-permute-done.1 = bf16[256,1024]{1,0:T(8,128)(2,1)} collective-permute-done((bf16[256,1024]{1,0:T(8,128)(2,1)}, bf16[256,1024]{1,0:T(8,128)(2,1)}, u32[]{:S(2)}, u32[]{:S(2)}) %collective-permute-start.1) | collective-permute-done | bytes 524320 | tf_op jit(solution)/shard_map/ppermute | solution.py:96
  34.6 4.0 %fusion.11 = f32[256,2304]{1,0:T(8,128)S(1)} fusion(bf16[256,1024]{1,0:T(8,128)(2,1)S(1)} %multiply_convert_fusion.3.two, bf16[1024,2304]{1,0:T(8,128)(2,1)} %param.18), kind=kOutput, calls=%fused_computation.31 | convolution fusion | flops 1207959552 | bytes 7602176 | tf_op jit(solution)/shard_map/dot_general | solution.py:563
  46.3 2.7 %collective-permute-start.12 = (bf16[256,1024]{1,0:T(8,128)(2,1)S(1)}, bf16[256,1024]{1,0:T(8,128)(2,1)S(1)}, u32[]{:S(2)}, u32[]{:S(2)}) collective-permute-start(bf16[256,1024]{1,0:T(8,128)(2,1)S(1)} %fusion.1.part), channel_id=1, source_target_pairs={{0,1},{2,3},{4,5},{6,7},{1,0},{3,2},{5,4},{7,6},{8,9},{10,11},{12,... | collective-permute-start | bytes 1572872 | tf_op jit(solution)/shard_map/ppermute | solution.py:96
  49.0 5.8 %shard_map.189 = (bf16[56,64,128]{2,1,0:T(8,128)(2,1)S(1)}, bf16[56,64,128]{2,1,0:T(8,128)(2,1)S(1)}, bf16[56,64,128]{2,1,0:T(8,128)(2,1)S(1)}, bf16[48,64,128]{...) custom-call(s32[5]{0:T(128)S(1)} %stack.19.scalars, ...), custom_call_target="tpu_custom_call" | custom-call | tf_op jit(solution)/shard_map/pallas_call | solution.py:121
  54.8 4.6 %collective-permute-start.11 = (bf16[48,64,128]{2,1,0:T(8,128)(2,1)S(1)}, bf16[48,64,128]{2,1,0:T(8,128)(2,1)S(1)}, u32[]{:S(2)}, u32[]{:S(2)}) collective-permute-start(bf16[48,64,128]{2,1,0:T(8,128)(2,1)S(1)} %get-tuple-element.100), channel_id=1, source_target_pairs={{0,24},{2,26},{4,28},{6,30},{1,25},{3,27},{5,29},{7,31},{8,16},{10... | collective-permute-start | bytes 2359304 | tf_op jit(solution)/shard_map/ppermute | solution.py:96
  62.6 2.7 %collective-permute-start.13 = (f32[8,512]{1,0:T(8,128)S(1)}, f32[8,512]{1,0:T(8,128)S(1)}, u32[]{:S(2)}, u32[]{:S(2)}) collective-permute-start(f32[8,512]{1,0:T(8,128)S(1)} %shard_map.191), channel_id=1, source_target_pairs={{2,0},{4,2},{6,4},{8,6},{10,8},{12,10},{14,12},{16,14},{18,16},{20... | collective-permute-start | bytes 49160 | tf_op jit(solution)/shard_map/ppermute | solution.py:102
  65.3 4.0 %collective-permute-start.8 = (bf16[56,64,128]{2,1,0:T(8,128)(2,1)S(1)}, bf16[56,64,128]{2,1,0:T(8,128)(2,1)S(1)}, u32[]{:S(2)}, u32[]{:S(2)}) collective-permute-start(bf16[56,64,128]{2,1,0:T(8,128)(2,1)S(1)} %get-tuple-element.97), channel_id=1, source_target_pairs={{0,32},{2,34},{4,36},{6,38},{1,33},{3,35},{5,37},{7,39},{8,40},{10... | collective-permute-start | bytes 2752520 | tf_op jit(solution)/shard_map/ppermute | solution.py:96
  71.2 2.2 %shard_map.190 = (f32[256,1024]{1,0:T(8,128)S(1)}, bf16[256,1024]{1,0:T(8,128)(2,1)S(1)}, f32[1,1024]{1,0:T(1,128)S(1)}, bf16[256,512]{1,0:T(8,128)(2,1)S(1)}, f...) custom-call(s32[5]{0:T(128)S(1)} %stack.19.scalars, bf16[256,1024]{1,0:T(8,128)(2,1)S(1)} %fusion.1.part, ...), custom_call_target="tpu_custom_call" | custom-call | tf_op jit(solution)/shard_map/pallas_call | solution.py:121
  77.1 2.2 %collective-permute-start.16 = (bf16[2,256,1024]{2,1,0:T(8,128)(2,1)S(1)}, bf16[2,256,1024]{2,1,0:T(8,128)(2,1)S(1)}, u32[]{:S(2)}, u32[]{:S(2)}) collective-permute-start(bf16[2,256,1024]{2,1,0:T(8,128)(2,1)S(1)} %get-tuple-element.120), channel_id=1, source_target_pairs={{0,1},{2,3},{4,5},{6,7},{1,0},{3,2},{5,4},{7,6},{8,9},{10,11},{12,... | collective-permute-start | bytes 3145736 | tf_op jit(solution)/shard_map/ppermute | solution.py:96
  79.2 9.8 %collective-permute-done.8.refs_0_ = bf16[56,64,128]{2,1,0:T(8,128)(2,1)S(1)} collective-permute-done((bf16[56,64,128]{2,1,0:T(8,128)(2,1)S(1)}, bf16[56,64,128]{2,1,0:T(8,128)(2,1)S(1)}, u32[]{:S(2)}, u32[]{:S(2)}) %collective-permute-start.8) | collective-permute-done | bytes 917536 | tf_op jit(solution)/shard_map/ppermute | solution.py:96
  91.5 4.4 %shard_map.193 = (bf16[45,64,128]{2,1,0:T(8,128)(2,1)S(1)}, bf16[45,64,128]{2,1,0:T(8,128)(2,1)S(1)}, bf16[17,64,128]{2,1,0:T(8,128)(2,1)S(1)}, bf16[40,64,128]{...) custom-call(s32[5]{0:T(128)S(1)} %stack.19.scalars, ...), custom_call_target="tpu_custom_call" | custom-call | tf_op jit(solution)/shard_map/pallas_call | solution.py:121
  97.6 2.7 %collective-permute-start.20 = (bf16[44,64,128]{2,1,0:T(8,128)(2,1)S(1)}, bf16[44,64,128]{2,1,0:T(8,128)(2,1)S(1)}, u32[]{:S(2)}, u32[]{:S(2)}) collective-permute-start(bf16[44,64,128]{2,1,0:T(8,128)(2,1)S(1)} %get-tuple-element.125), channel_id=1, source_target_pairs={{0,24},{2,26},{4,28},{6,30},{1,25},{3,27},{5,29},{7,31},{8,16},{10... | collective-permute-start | bytes 2162696 | tf_op jit(solution)/shard_map/ppermute | solution.py:96
  102.3 3.3 %collective-permute-start.18 = (bf16[17,64,128]{2,1,0:T(8,128)(2,1)S(1)}, bf16[17,64,128]{2,1,0:T(8,128)(2,1)S(1)}, u32[]{:S(2)}, u32[]{:S(2)}) collective-permute-start(bf16[17,64,128]{2,1,0:T(8,128)(2,1)S(1)} %get-tuple-element.123), channel_id=1, source_target_pairs={{0,64},{2,66},{4,68},{6,70},{1,65},{3,67},{5,69},{7,71},{8,72},{10... | collective-permute-start | bytes 835592 | tf_op jit(solution)/shard_map/ppermute | solution.py:96
  105.6 5.9 %collective-permute-done.15.refs_0_ = bf16[45,64,128]{2,1,0:T(8,128)(2,1)S(1)} collective-permute-done((bf16[45,64,128]{2,1,0:T(8,128)(2,1)S(1)}, bf16[45,64,128]{2,1,0:T(8,128)(2,1)S(1)}, u32[]{:S(2)}, u32[]{:S(2)}) %collective-permute-start.15) | collective-permute-done | bytes 737312 | tf_op jit(solution)/shard_map/ppermute | solution.py:96
  111.5 3.0 %collective-permute-start.21 = (bf16[16,64,128]{2,1,0:T(8,128)(2,1)S(1)}, bf16[16,64,128]{2,1,0:T(8,128)(2,1)S(1)}, u32[]{:S(2)}, u32[]{:S(2)}) collective-permute-start(bf16[16,64,128]{2,1,0:T(8,128)(2,1)S(1)} %get-tuple-element.126), channel_id=1, source_target_pairs={{0,16},{2,18},{4,20},{6,22},{1,17},{3,19},{5,21},{7,23},{8,24},{10... | collective-permute-start | bytes 786440 | tf_op jit(solution)/shard_map/ppermute | solution.py:96
  114.5 5.1 %collective-permute-done.21.refs_5_ = bf16[16,64,128]{2,1,0:T(8,128)(2,1)S(1)} collective-permute-done((bf16[16,64,128]{2,1,0:T(8,128)(2,1)S(1)}, bf16[16,64,128]{2,1,0:T(8,128)(2,1)S(1)}, u32[]{:S(2)}, u32[]{:S(2)}) %collective-permute-start.21) | collective-permute-done | bytes 262176 | tf_op jit(solution)/shard_map/ppermute | solution.py:96
  124.7 2.7 %collective-permute-start.26 = (bf16[19,64,128]{2,1,0:T(8,128)(2,1)S(1)}, bf16[19,64,128]{2,1,0:T(8,128)(2,1)S(1)}, u32[]{:S(2)}, u32[]{:S(2)}) collective-permute-start(bf16[19,64,128]{2,1,0:T(8,128)(2,1)S(1)} %get-tuple-element.139), channel_id=1, source_target_pairs={{0,24},{2,26},{4,28},{6,30},{1,25},{3,27},{5,29},{7,31},{8,16},{10... | collective-permute-start | bytes 933896 | tf_op jit(solution)/shard_map/ppermute | solution.py:96
  131.1 3.7 %collective-permute-done.26.refs_4_ = bf16[19,64,128]{2,1,0:T(8,128)(2,1)S(1)} collective-permute-done((bf16[19,64,128]{2,1,0:T(8,128)(2,1)S(1)}, bf16[19,64,128]{2,1,0:T(8,128)(2,1)S(1)}, u32[]{:S(2)}, u32[]{:S(2)}) %collective-permute-start.26) | collective-permute-done | bytes 311328 | tf_op jit(solution)/shard_map/ppermute | solution.py:96
  134.8 2.4 %collective-permute-done.27.refs_5_ = bf16[19,64,128]{2,1,0:T(8,128)(2,1)S(1)} collective-permute-done((bf16[19,64,128]{2,1,0:T(8,128)(2,1)S(1)}, bf16[19,64,128]{2,1,0:T(8,128)(2,1)S(1)}, u32[]{:S(2)}, u32[]{:S(2)}) %collective-permute-start.27) | collective-permute-done | bytes 311328 | tf_op jit(solution)/shard_map/ppermute | solution.py:96
  143.6 2.9 %collective-permute-done.30.got = bf16[37,32,128]{2,1,0:T(8,128)(2,1)S(1)} collective-permute-done((bf16[37,32,128]{2,1,0:T(8,128)(2,1)S(1)}, bf16[37,32,128]{2,1,0:T(8,128)(2,1)S(1)}, u32[]{:S(2)}, u32[]{:S(2)}) %collective-permute-start.30) | collective-permute-done | bytes 303136 | tf_op jit(solution)/shard_map/ppermute | solution.py:96
  147.1 8.4 %collective-permute-start.31 = (f32[37,16,128]{2,1,0:T(8,128)S(1)}, f32[37,16,128]{2,1,0:T(8,128)S(1)}, u32[]{:S(2)}, u32[]{:S(2)}) collective-permute-start(f32[37,16,128]{2,1,0:T(8,128)S(1)} %get-tuple-element.159), channel_id=1, source_target_pairs={{0,2},{2,0},{4,6},{6,4},{1,3},{3,1},{5,7},{7,5},{8,10},{10,8},{12,... | collective-permute-start | bytes 909320 | tf_op jit(solution)/shard_map/ppermute | solution.py:96
  (116 shorter events, 53.9 us)
Async XLA Ops:
  16.1 15.8 %collective-permute-start.3 = (bf16[256,1280]{1,0:T(8,128)(2,1)}, bf16[256,1280]{1,0:T(8,128)(2,1)}, u32[]{:S(2)}, u32[]{:S(2)}) collective-permute-start(bf16[256,1280]{1,0:T(8,128)(2,1)} %get-tuple-element.93), channel_id=1, source_target_pairs={{0,2},{2,0},{4,6},{6,4},{1,3},{3,1},{5,7},{7,5},{8,10},{10,8},{12,... | collective-permute-start | bytes 1966088 | tf_op jit(solution)/shard_map/ppermute | solution.py:96
  16.6 15.3 %collective-permute-start.1 = (bf16[256,1024]{1,0:T(8,128)(2,1)}, bf16[256,1024]{1,0:T(8,128)(2,1)}, u32[]{:S(2)}, u32[]{:S(2)}) collective-permute-start(bf16[256,1024]{1,0:T(8,128)(2,1)} %get-tuple-element.92), channel_id=1, source_target_pairs={{0,1},{2,3},{4,5},{6,7},{1,0},{3,2},{5,4},{7,6},{8,9},{10,11},{12,... | collective-permute-start | bytes 1572872 | tf_op jit(solution)/shard_map/ppermute | solution.py:96
  33.6 15.4 %collective-permute-start.4 = (bf16[256,1024]{1,0:T(8,128)(2,1)S(1)}, bf16[256,1024]{1,0:T(8,128)(2,1)S(1)}, u32[]{:S(2)}, u32[]{:S(2)}) collective-permute-start(bf16[256,1024]{1,0:T(8,128)(2,1)S(1)} %multiply_convert_fusion.3.two), channel_id=1, source_target_pairs={{0,2},{2,0},{4,6},{6,4},{1,3},{3,1},{5,7},{7,5},{8,10},{10,8},{12,... | collective-permute-start | bytes 1572872 | tf_op jit(solution)/shard_map/ppermute | solution.py:96
  41.8 7.2 %collective-permute-start.5 = (bf16[256,1152]{1,0:T(8,128)(2,1)S(1)}, bf16[256,1152]{1,0:T(8,128)(2,1)S(1)}, u32[]{:S(2)}, u32[]{:S(2)}) collective-permute-start(bf16[256,1152]{1,0:T(8,128)(2,1)S(1)} %slice_select_fusion.2), channel_id=1, source_target_pairs={{0,2},{2,0},{4,6},{6,4},{1,3},{3,1},{5,7},{7,5},{8,10},{10,8},{12,... | collective-permute-start | bytes 1769480 | tf_op jit(solution)/shard_map/ppermute | solution.py:96
  42.0 7.0 %collective-permute-start.6 = (bf16[256,1152]{1,0:T(8,128)(2,1)S(1)}, bf16[256,1152]{1,0:T(8,128)(2,1)S(1)}, u32[]{:S(2)}, u32[]{:S(2)}) collective-permute-start(bf16[256,1152]{1,0:T(8,128)(2,1)S(1)} %slice_select_fusion.1), channel_id=1, source_target_pairs={{0,2},{2,0},{4,6},{6,4},{1,3},{3,1},{5,7},{7,5},{8,10},{10,8},{12,... | collective-permute-start | bytes 1769480 | tf_op jit(solution)/shard_map/ppermute | solution.py:96
  46.3 15.3 %collective-permute-start.12 = (bf16[256,1024]{1,0:T(8,128)(2,1)S(1)}, bf16[256,1024]{1,0:T(8,128)(2,1)S(1)}, u32[]{:S(2)}, u32[]{:S(2)}) collective-permute-start(bf16[256,1024]{1,0:T(8,128)(2,1)S(1)} %fusion.1.part), channel_id=1, source_target_pairs={{0,1},{2,3},{4,5},{6,7},{1,0},{3,2},{5,4},{7,6},{8,9},{10,11},{12,... | collective-permute-start | bytes 1572872 | tf_op jit(solution)/shard_map/ppermute | solution.py:96
  54.8 22.2 %collective-permute-start.11 = (bf16[48,64,128]{2,1,0:T(8,128)(2,1)S(1)}, bf16[48,64,128]{2,1,0:T(8,128)(2,1)S(1)}, u32[]{:S(2)}, u32[]{:S(2)}) collective-permute-start(bf16[48,64,128]{2,1,0:T(8,128)(2,1)S(1)} %get-tuple-element.100), channel_id=1, source_target_pairs={{0,24},{2,26},{4,28},{6,30},{1,25},{3,27},{5,29},{7,31},{8,16},{10... | collective-permute-start | bytes 2359304 | tf_op jit(solution)/shard_map/ppermute | solution.py:96
  62.6 10.9 %collective-permute-start.13 = (f32[8,512]{1,0:T(8,128)S(1)}, f32[8,512]{1,0:T(8,128)S(1)}, u32[]{:S(2)}, u32[]{:S(2)}) collective-permute-start(f32[8,512]{1,0:T(8,128)S(1)} %shard_map.191), channel_id=1, source_target_pairs={{2,0},{4,2},{6,4},{8,6},{10,8},{12,10},{14,12},{16,14},{18,16},{20... | collective-permute-start | bytes 49160 | tf_op jit(solution)/shard_map/ppermute | solution.py:102
  65.3 23.7 %collective-permute-start.8 = (bf16[56,64,128]{2,1,0:T(8,128)(2,1)S(1)}, bf16[56,64,128]{2,1,0:T(8,128)(2,1)S(1)}, u32[]{:S(2)}, u32[]{:S(2)}) collective-permute-start(bf16[56,64,128]{2,1,0:T(8,128)(2,1)S(1)} %get-tuple-element.97), channel_id=1, source_target_pairs={{0,32},{2,34},{4,36},{6,38},{1,33},{3,35},{5,37},{7,39},{8,40},{10... | collective-permute-start | bytes 2752520 | tf_op jit(solution)/shard_map/ppermute | solution.py:96
  69.3 21.8 %collective-permute-start.9 = (bf16[56,64,128]{2,1,0:T(8,128)(2,1)S(1)}, bf16[56,64,128]{2,1,0:T(8,128)(2,1)S(1)}, u32[]{:S(2)}, u32[]{:S(2)}) collective-permute-start(bf16[56,64,128]{2,1,0:T(8,128)(2,1)S(1)} %get-tuple-element.98), channel_id=1, source_target_pairs={{0,96},{2,98},{4,100},{6,102},{1,97},{3,99},{5,101},{7,103},{8,104... | collective-permute-start | bytes 2752520 | tf_op jit(solution)/shard_map/ppermute | solution.py:96
  71.2 20.3 %collective-permute-start.10 = (bf16[56,64,128]{2,1,0:T(8,128)(2,1)S(1)}, bf16[56,64,128]{2,1,0:T(8,128)(2,1)S(1)}, u32[]{:S(2)}, u32[]{:S(2)}) collective-permute-start(bf16[56,64,128]{2,1,0:T(8,128)(2,1)S(1)} %get-tuple-element.99), channel_id=1, source_target_pairs={{0,8},{2,10},{4,12},{6,14},{1,9},{3,11},{5,13},{7,15},{8,0},{10,2}... | collective-permute-start | bytes 2752520 | tf_op jit(solution)/shard_map/ppermute | solution.py:96
  75.1 16.4 %collective-permute-start.14 = (bf16[7,256,256]{2,1,0:T(8,128)(2,1)S(1)}, bf16[7,256,256]{2,1,0:T(8,128)(2,1)S(1)}, u32[]{:S(2)}, u32[]{:S(2)}) collective-permute-start(bf16[7,256,256]{2,1,0:T(8,128)(2,1)S(1)} %get-tuple-element.115), channel_id=1, source_target_pairs={{0,2},{2,0},{4,6},{6,4},{1,3},{3,1},{5,7},{7,5},{8,10},{10,8},{12,... | collective-permute-start | bytes 2752520 | tf_op jit(solution)/shard_map/ppermute | solution.py:96
  77.1 25.3 %collective-permute-start.16 = (bf16[2,256,1024]{2,1,0:T(8,128)(2,1)S(1)}, bf16[2,256,1024]{2,1,0:T(8,128)(2,1)S(1)}, u32[]{:S(2)}, u32[]{:S(2)}) collective-permute-start(bf16[2,256,1024]{2,1,0:T(8,128)(2,1)S(1)} %get-tuple-element.120), channel_id=1, source_target_pairs={{0,1},{2,3},{4,5},{6,7},{1,0},{3,2},{5,4},{7,6},{8,9},{10,11},{12,... | collective-permute-start | bytes 3145736 | tf_op jit(solution)/shard_map/ppermute | solution.py:96
  95.9 15.6 %collective-permute-start.15 = (bf16[45,64,128]{2,1,0:T(8,128)(2,1)S(1)}, bf16[45,64,128]{2,1,0:T(8,128)(2,1)S(1)}, u32[]{:S(2)}, u32[]{:S(2)}) collective-permute-start(bf16[45,64,128]{2,1,0:T(8,128)(2,1)S(1)} %get-tuple-element.119), channel_id=1, source_target_pairs={{0,32},{2,34},{4,36},{6,38},{1,33},{3,35},{5,37},{7,39},{8,40},{10... | collective-permute-start | bytes 2211848 | tf_op jit(solution)/shard_map/ppermute | solution.py:96
  96.1 23.5 %collective-permute-start.17 = (bf16[45,64,128]{2,1,0:T(8,128)(2,1)S(1)}, bf16[45,64,128]{2,1,0:T(8,128)(2,1)S(1)}, u32[]{:S(2)}, u32[]{:S(2)}) collective-permute-start(bf16[45,64,128]{2,1,0:T(8,128)(2,1)S(1)} %get-tuple-element.122), channel_id=1, source_target_pairs={{0,96},{2,98},{4,100},{6,102},{1,97},{3,99},{5,101},{7,103},{8,104... | collective-permute-start | bytes 2211848 | tf_op jit(solution)/shard_map/ppermute | solution.py:96
  97.6 22.1 %collective-permute-start.20 = (bf16[44,64,128]{2,1,0:T(8,128)(2,1)S(1)}, bf16[44,64,128]{2,1,0:T(8,128)(2,1)S(1)}, u32[]{:S(2)}, u32[]{:S(2)}) collective-permute-start(bf16[44,64,128]{2,1,0:T(8,128)(2,1)S(1)} %get-tuple-element.125), channel_id=1, source_target_pairs={{0,24},{2,26},{4,28},{6,30},{1,25},{3,27},{5,29},{7,31},{8,16},{10... | collective-permute-start | bytes 2162696 | tf_op jit(solution)/shard_map/ppermute | solution.py:96
  100.3 19.3 %collective-permute-start.19 = (bf16[40,64,128]{2,1,0:T(8,128)(2,1)S(1)}, bf16[40,64,128]{2,1,0:T(8,128)(2,1)S(1)}, u32[]{:S(2)}, u32[]{:S(2)}) collective-permute-start(bf16[40,64,128]{2,1,0:T(8,128)(2,1)S(1)} %get-tuple-element.124), channel_id=1, source_target_pairs={{0,8},{2,10},{4,12},{6,14},{1,9},{3,11},{5,13},{7,15},{8,0},{10,2}... | collective-permute-start | bytes 1966088 | tf_op jit(solution)/shard_map/ppermute | solution.py:96
  102.3 17.3 %collective-permute-start.18 = (bf16[17,64,128]{2,1,0:T(8,128)(2,1)S(1)}, bf16[17,64,128]{2,1,0:T(8,128)(2,1)S(1)}, u32[]{:S(2)}, u32[]{:S(2)}) collective-permute-start(bf16[17,64,128]{2,1,0:T(8,128)(2,1)S(1)} %get-tuple-element.123), channel_id=1, source_target_pairs={{0,64},{2,66},{4,68},{6,70},{1,65},{3,67},{5,69},{7,71},{8,72},{10... | collective-permute-start | bytes 835592 | tf_op jit(solution)/shard_map/ppermute | solution.py:96
  111.5 8.1 %collective-permute-start.21 = (bf16[16,64,128]{2,1,0:T(8,128)(2,1)S(1)}, bf16[16,64,128]{2,1,0:T(8,128)(2,1)S(1)}, u32[]{:S(2)}, u32[]{:S(2)}) collective-permute-start(bf16[16,64,128]{2,1,0:T(8,128)(2,1)S(1)} %get-tuple-element.126), channel_id=1, source_target_pairs={{0,16},{2,18},{4,20},{6,22},{1,17},{3,19},{5,21},{7,23},{8,24},{10... | collective-permute-start | bytes 786440 | tf_op jit(solution)/shard_map/ppermute | solution.py:96
  121.5 9.6 %collective-permute-start.23 = (bf16[17,64,128]{2,1,0:T(8,128)(2,1)S(1)}, bf16[17,64,128]{2,1,0:T(8,128)(2,1)S(1)}, u32[]{:S(2)}, u32[]{:S(2)}) collective-permute-start(bf16[17,64,128]{2,1,0:T(8,128)(2,1)S(1)} %get-tuple-element.136), channel_id=1, source_target_pairs={{0,96},{2,98},{4,100},{6,102},{1,97},{3,99},{5,101},{7,103},{8,104... | collective-permute-start | bytes 835592 | tf_op jit(solution)/shard_map/ppermute | solution.py:96
  122.7 8.5 %collective-permute-start.24 = (bf16[17,64,128]{2,1,0:T(8,128)(2,1)S(1)}, bf16[17,64,128]{2,1,0:T(8,128)(2,1)S(1)}, u32[]{:S(2)}, u32[]{:S(2)}) collective-permute-start(bf16[17,64,128]{2,1,0:T(8,128)(2,1)S(1)} %get-tuple-element.137), channel_id=1, source_target_pairs={{0,64},{2,66},{4,68},{6,70},{1,65},{3,67},{5,69},{7,71},{8,72},{10... | collective-permute-start | bytes 835592 | tf_op jit(solution)/shard_map/ppermute | solution.py:96
  124.7 10.1 %collective-permute-start.26 = (bf16[19,64,128]{2,1,0:T(8,128)(2,1)S(1)}, bf16[19,64,128]{2,1,0:T(8,128)(2,1)S(1)}, u32[]{:S(2)}, u32[]{:S(2)}) collective-permute-start(bf16[19,64,128]{2,1,0:T(8,128)(2,1)S(1)} %get-tuple-element.139), channel_id=1, source_target_pairs={{0,24},{2,26},{4,28},{6,30},{1,25},{3,27},{5,29},{7,31},{8,16},{10... | collective-permute-start | bytes 933896 | tf_op jit(solution)/shard_map/ppermute | solution.py:96
  127.4 9.8 %collective-permute-start.27 = (bf16[19,64,128]{2,1,0:T(8,128)(2,1)S(1)}, bf16[19,64,128]{2,1,0:T(8,128)(2,1)S(1)}, u32[]{:S(2)}, u32[]{:S(2)}) collective-permute-start(bf16[19,64,128]{2,1,0:T(8,128)(2,1)S(1)} %get-tuple-element.140), channel_id=1, source_target_pairs={{0,16},{2,18},{4,20},{6,22},{1,17},{3,19},{5,21},{7,23},{8,24},{10... | collective-permute-start | bytes 933896 | tf_op jit(solution)/shard_map/ppermute | solution.py:96
  147.1 9.6 %collective-permute-start.31 = (f32[37,16,128]{2,1,0:T(8,128)S(1)}, f32[37,16,128]{2,1,0:T(8,128)S(1)}, u32[]{:S(2)}, u32[]{:S(2)}) collective-permute-start(f32[37,16,128]{2,1,0:T(8,128)S(1)} %get-tuple-element.159), channel_id=1, source_target_pairs={{0,2},{2,0},{4,6},{6,4},{1,3},{3,1},{5,7},{7,5},{8,10},{10,8},{12,... | collective-permute-start | bytes 909320 | tf_op jit(solution)/shard_map/ppermute | solution.py:96
  (30 other events, 198.3 us)

commit v3 on v2

v3 whole, which is shorter than its diff:
```python
import functools

import jax
import jax.numpy as jnp
from jax import lax
from jax.experimental import pallas as pl
from jax.experimental.pallas import tpu as pltpu
from jax.sharding import PartitionSpec as P

EPS = 1e-05
AXES = ("seq", "tensor")
BF16 = jnp.bfloat16
F32 = jnp.float32


def device_pairs(move):
    def number(y, z, x, core):
        return ((((y % 4) * 4 + z % 4) * 2 + x % 2) * 2 + core) * 2 + (x % 4) // 2

    return [
        (number(y, z, x, core), number(*move(y, z, x, core)))
        for y in range(4)
        for z in range(4)
        for x in range(4)
        for core in range(2)
    ]


ACROSS = device_pairs(lambda y, z, x, core: (y, z, (x + 2) % 4, core))
BESIDE = device_pairs(lambda y, z, x, core: (y, z, x ^ 1, core))
SKEW = device_pairs(lambda y, z, x, core: (y, z, (x ^ 1) ^ 2, core))
CORES = device_pairs(lambda y, z, x, core: (y, z, x, 1 - core))


def peer(at, pairing):
    return (at ^ 1, 3 - at, at ^ 2)[pairing]


FIRST = [
    device_pairs(
        functools.partial(
            lambda pairing, y, z, x, core: (y, peer(z, pairing), x, core)
            if core
            else (peer(y, pairing), z, x, core),
            pairing,
        )
    )
    for pairing in range(3)
]
SECOND = [
    device_pairs(
        functools.partial(
            lambda pairing, y, z, x, core: (peer(y, pairing), z, x, core)
            if core
            else (y, peer(z, pairing), x, core),
            pairing,
        )
    )
    for pairing in range(3)
]
WIDE_COLUMNS = 1152
WIDE_TILES = 27
WIDE = (14, 13)
NARROW = 8
BLOCK = (64, 128)
LONG = 3 * 10**10
SHORT = 8 * 10**9
TILES = WIDE_TILES + NARROW
WIDE_PIECE = (1, 0, None)
WIDE_BLOCKS = (4 * WIDE[1], 4 * WIDE[0], 0)
ROUND_ONE = tuple(count + 4 * NARROW + 1 for count in WIDE_BLOCKS)


def swap(value, pairs):
    return lax.ppermute(value, AXES, pairs)


def from_behind(value, axis, steps):
    count = lax.axis_size(axis)
    leading, last = (max(0, -steps), min(count, count - steps))
    return lax.ppermute(value, axis, [(source, source + steps) for source in range(leading, last)])


def norm_scale(values):
    return lax.rsqrt(jnp.mean(values * values, axis=1, keepdims=True) + EPS)


def norm_backward(out_grad_rows, values, scale_rows, gain):
    scaled = out_grad_rows * gain
    inner = jnp.mean(scaled * values, axis=1, keepdims=True)
    return scale_rows * (scaled - values * scale_rows * scale_rows * inner)


def like(shape, dtype):
    return jax.ShapeDtypeStruct(shape, dtype)


def call(body, *, scalars, operands, outs, scratch=(), where=pltpu.VMEM, flops=0):
    whole = pl.BlockSpec(memory_space=pltpu.VMEM)
    return pl.pallas_call(
        body,
        out_shape=tuple(outs),
        in_specs=[pl.BlockSpec(memory_space=pltpu.SMEM)] + [pl.BlockSpec(memory_space=where)] * len(operands),
        out_specs=tuple(whole for _ in outs),
        scratch_shapes=list(scratch),
        compiler_params=pltpu.CompilerParams(vmem_limit_bytes=16 * 2**20),
        cost_estimate=pl.CostEstimate(flops=flops, bytes_accessed=0, transcendentals=0),
    )(scalars, *operands)


def dot(left, right):
    return jnp.dot(left, right, preferred_element_type=F32)


def dot_rows(left, right):
    return lax.dot_general(left, right, (((1,), (1,)), ((), ())), preferred_element_type=F32)


def row_numbers(shape, first=0):
    return lax.broadcasted_iota(jnp.int32, shape, 0) + first


def valid_rows(offset, lag, shape):
    row = row_numbers(shape)
    return jnp.where((offset <= row) & (offset > row - lag), 0.0, 1.0)


def linked_rows(offset, shape, first, count):
    return jnp.where((row_numbers(shape, first) < offset) & (offset < count), 0.0, 1.0)


def tail_kernel(scalars, tokens, gain, weight, tail, token_rows, gain_row, b_weight, x_weight, done):
    rows = tokens.shape[0]
    copies = [
        pltpu.make_async_copy(source, target, done.at[at])
        for at, (source, target) in enumerate(
            (
                (tokens.at[pl.ds(rows - 16, 16)], token_rows),
                (gain, gain_row),
                (weight.at[0], b_weight),
                (weight.at[2], x_weight),
            )
        )
    ]
    for copy in copies:
        copy.start()
    for copy in copies:
        copy.wait()
    values = token_rows[...].astype(F32)
    normed = (values * norm_scale(values) * gain_row[...]).astype(BF16)
    gated = (dot(normed, b_weight[...]) * dot(normed, x_weight[...])).astype(BF16).astype(F32)
    tail[...] = (gated * linked_rows(scalars[4], gated.shape, rows - 16, rows)).astype(BF16)


def project_kernel(scalars, tokens, gain, weight, normed, parts, gated):
    values = tokens[...].astype(F32)
    normed[...] = (values * norm_scale(values) * gain[...]).astype(BF16)
    for k in range(3):
        parts[k] = dot(normed[...], weight[k])
    gated[...] = (parts[0] * parts[2]).astype(BF16)


def behind(gated, incoming, lag):
    moved = pltpu.roll(gated, lag, 0)
    row = row_numbers(gated.shape)
    for at in range(lag):
        moved = jnp.where(row == at, incoming[16 - lag + at : 17 - lag + at], moved)
    return moved


def mix_kernel(scalars, gated, incoming, parts, taps, weight, conv, ymix, branch):
    values = gated[...].astype(F32)
    before = incoming[...].astype(F32)
    total = taps[0:1] * values
    for lag in (1, 2):
        total = total + taps[lag : lag + 1] * behind(values, before, lag) * valid_rows(
            scalars[4], lag, values.shape
        )
    conv[...] = total
    ymix[...] = (parts[1] * total).astype(BF16)
    branch[...] = dot(ymix[...], weight[...]).astype(BF16)


def away_half(value, core):
    half = value.shape[-1] // 2
    return jnp.where(core == 0, value[..., half:], value[..., :half])


def hidden_kernel(scalars, cot, weight, out):
    for at in range(0, weight.shape[0], 256):
        out[:, at : at + 256] = dot_rows(cot[...], weight[at : at + 256])


def down_kernel(scalars, hidden, weight, out):
    out[...] = dot(hidden[...], weight[...]).astype(BF16)


def feed_kernel(
    scalars,
    tokens,
    branch,
    other,
    gain,
    gate,
    up,
    hidden_grad,
    normed_one,
    ymix,
    resid,
    normed,
    hidden,
    gate_back,
    up_back,
    part,
    shared,
):
    resid[...] = tokens[...].astype(F32) + (branch[...].astype(F32) + other[...].astype(F32))
    normed[...] = (resid[...] * norm_scale(resid[...]) * gain[...]).astype(BF16)
    values = normed[...]
    for at in range(0, gate.shape[1], 256):
        columns = slice(at, at + 256)
        gate_act, up_act = dot(values, gate[:, columns]), dot(values, up[:, columns])
        back = hidden_grad[:, columns]
        sigmoid_gate = jax.nn.sigmoid(gate_act)
        swish = gate_act * sigmoid_gate
        hidden[:, columns] = (swish * up_act).astype(BF16)
        up_back[:, columns] = (back * swish).astype(BF16)
        slope = sigmoid_gate * (1.0 + gate_act * (1.0 - sigmoid_gate))
        gate_back[:, columns] = (back * up_act * slope).astype(BF16)
    part[...] = (dot_rows(gate_back[...], gate[...]) + dot_rows(up_back[...], up[...])).astype(BF16)
    away = pl.ds(pl.multiple_of((1 - scalars[3]) * WIDE_COLUMNS, 128), WIDE_COLUMNS)
    for k, value in enumerate((hidden, gate_back, up_back)):
        shared[:, k * WIDE_COLUMNS : (k + 1) * WIDE_COLUMNS] = value[:, away]
    width, at = normed.shape[1], 3 * WIDE_COLUMNS
    shared[:, at : at + width] = values
    shared[:, at + width : at + 2 * width] = normed_one[...]
    shared[:, at + 2 * width :] = away_half(ymix[...], scalars[3])


def second_norm(part, other, resid, gain, cot):
    back = part.astype(F32) + other.astype(F32)
    scale = norm_scale(resid)
    return back, scale, cot.astype(F32) + norm_backward(back, resid, scale, gain)


def edge_kernel(scalars, part, other, resid, gain, cot, weight, parts, taps, edge):
    top = slice(0, 16)
    _, _, grad = second_norm(part[top], other[top], resid[top], gain[...], cot[top])
    conv_back = dot_rows(grad.astype(BF16), weight[...]) * parts[1, top]
    one = conv_back * valid_rows(scalars[4], 1, conv_back.shape) * taps[1:2]
    two = conv_back * valid_rows(scalars[4], 2, conv_back.shape) * taps[2:3]
    row = row_numbers((8, conv_back.shape[1]))
    edge[...] = jnp.where(row == 6, two[0:1], 0.0) + jnp.where(row == 7, one[0:1] + two[1:2], 0.0)


def middle_kernel(
    scalars, part, other, resid, gain, cot, weight, parts, taps, conv, gated, incoming, grad, low, gain_grad, c_back, gated_back, tap_grads
):
    back, scale, resid_grad = second_norm(part[...], other[...], resid[...], gain[...], cot[...])
    gain_grad[...] = jnp.sum(back * resid[...] * scale, axis=0, keepdims=True)
    grad[...] = resid_grad
    low[...] = resid_grad.astype(BF16)
    ymix_back = dot_rows(low[...], weight[...])
    c_back[...] = (ymix_back * conv[...]).astype(BF16)
    conv_back = ymix_back * parts[1]
    values, before = gated[...].astype(F32), incoming[...].astype(F32)
    rows = values.shape[0]
    tap_grads[0:1] = jnp.sum(conv_back * values, axis=0, keepdims=True)
    total = conv_back * taps[0:1]
    row = row_numbers(values.shape)
    for lag in (1, 2):
        term = conv_back * valid_rows(scalars[4], lag, values.shape)
        tap_grads[lag : lag + 1] = jnp.sum(term * behind(values, before, lag), axis=0, keepdims=True)
        moved = pltpu.roll(term * taps[lag : lag + 1], rows - lag, 0)
        total = total + jnp.where(row < rows - lag, moved, 0.0)
    gated_back[...] = total


def last_kernel(
    scalars,
    gated_back,
    returned,
    parts,
    c_back,
    weight,
    tokens,
    gain_two_grad,
    tap_grads,
    resid_low,
    backs,
    shared,
    part,
    small,
):
    rows = gated_back.shape[0]
    links = linked_rows(scalars[4], returned.shape, rows - 8, rows)
    end = gated_back[rows - 8 :] + returned[...] * links
    total = jnp.concatenate([gated_back[: rows - 8], end], 0)
    backs[0] = (total * parts[2]).astype(BF16)
    backs[1] = c_back[...]
    backs[2] = (total * parts[0]).astype(BF16)
    for k in range(3):
        shared[4 + k] = away_half(backs[k], scalars[3])
    for at in range(4):
        shared[at] = resid_low[:, at * 256 : at * 256 + 256]
    grad = dot_rows(backs[0], weight[0]) + dot_rows(backs[1], weight[1]) + dot_rows(backs[2], weight[2])
    part[...] = grad.astype(BF16)
    values = tokens[...].astype(F32)
    gain_grad = jnp.sum(grad * values * norm_scale(values), axis=0, keepdims=True)
    for at in range(8):
        lanes = slice(at * 128, at * 128 + 128)
        small[at : at + 1] = gain_grad[:, lanes]
        small[8 + at : 9 + at] = gain_two_grad[:, lanes]
    for lag in range(3):
        for at in range(4):
            row = 16 + 4 * lag + at
            small[row : row + 1] = tap_grads[lag : lag + 1, at * 128 : at * 128 + 128]
    small[28:32] = jnp.zeros((4, 128), F32)


def fill_transposed(left, own, other):
    for at in range(0, own.shape[1], 256):
        left[at : at + 256, :256] = own[:, at : at + 256].T
        left[at : at + 256, 256:] = other[:, at : at + 256].T


def chunk_rows(left, core, chunk):
    wide, slim = jnp.where(core == 0, 256, 64), jnp.where(core == 0, 64, 256)
    return jnp.concatenate(
        [left[pl.ds(pl.multiple_of(chunk * wide + at * slim, 64), 64)] for at in range(4)], 0
    )


def store_blocks(value, target, base, tiles, tile):
    value = value.astype(BF16)
    for chunk in range(4):
        for column in range(value.shape[1] // 128):
            target[base + chunk * tiles + tile + column] = value[
                chunk * 64 : chunk * 64 + 64, column * 128 : column * 128 + 128
            ]


def wide_runs(kind):
    at, end = (0, WIDE[0]) if kind == 0 else (WIDE[0], WIDE_TILES)
    first = at
    while at < end:
        matrix, tile = divmod(at, WIDE_COLUMNS // 128)
        count = min(2, WIDE_COLUMNS // 128 - tile, end - at)
        yield matrix, tile * 128, count * 128, at - first
        at += count


def wide_kernel(scalars, two, cot, cot_other, *refs):
    own, shared, sends, keeps = refs[:3], refs[3], refs[4:6], refs[6:8]
    left_two, left_cot = refs[8:]
    fill_transposed(left_cot, cot, cot_other)
    fill_transposed(left_two, two, shared.at[:, 3 * WIDE_COLUMNS : 3 * WIDE_COLUMNS + two.shape[1]])
    at, core = scalars[0], scalars[3]
    for kind in range(2):
        first, second = peer(at, kind), peer(at, 1 - kind)
        chunks = (at, second, first, peer(first, 1 - kind))
        for slot, chunk in enumerate(chunks):
            target = keeps[kind] if slot < 2 else sends[kind]
            rows = {}
            for matrix, column, width, tile in wide_runs(kind):
                if (matrix == 0) not in rows:
                    rows[matrix == 0] = chunk_rows(left_cot if matrix == 0 else left_two, core, chunk)
                left = rows[matrix == 0]
                mine = pl.ds(pl.multiple_of(core * WIDE_COLUMNS + column, 128), width)
                away = matrix * WIDE_COLUMNS + column
                value = dot(left[:, :256], own[matrix][:, mine])
                value = value + dot(left[:, 256:], shared[:, away : away + width])
                store_blocks(value, target, (slot % 2) * 4 * WIDE[kind], WIDE[kind], tile)


def narrow_kernel(scalars, one, shared, low, late_other, backs, ymix, out, left_one, left_low):
    width = one.shape[1]
    first = 3 * WIDE_COLUMNS + width
    one_other, ymix_other = shared.at[:, first : first + width], shared.at[:, first + width :]
    for at in range(0, width, 256):
        left_one[at : at + 256, :256] = one[:, at : at + 256].T
        left_one[at : at + 256, 256:] = one_other[:, at : at + 256].T
        left_low[at : at + 256, :256] = low[:, at : at + 256].T
        left_low[at : at + 256, 256:] = late_other[at // 256].T
    mine = pl.ds(pl.multiple_of(scalars[3] * 256, 256), 256)
    for slot in range(4):
        chunk = peer(scalars[0], slot) if slot < 3 else scalars[0]
        for kind in range(4):
            left, own, other = (
                (left_one, backs[kind, :, mine], late_other[4 + kind])
                if kind < 3
                else (left_low, ymix[:, mine], ymix_other[...])
            )
            rows = chunk_rows(left, scalars[3], chunk)
            value = dot(rows[:, :256], own) + dot(rows[:, 256:], other)
            store_blocks(value, out.at[slot], 0, NARROW, 2 * kind)


def split_small(value, target, at):
    high = value.astype(BF16)
    target[at, :32] = high
    target[at, 32:] = (value - high.astype(F32)).astype(BF16)


def join_small(source, at):
    return source[at, :32].astype(F32) + source[at, 32:].astype(F32)


def rounded_small(value):
    high = value.astype(BF16)
    return high.astype(F32) + (value - high.astype(F32)).astype(BF16).astype(F32)


def sum_small(value, gots, bases):
    near, far, cross = (join_small(got, base) for got, base in zip(gots, bases))
    return (rounded_small(value) + cross) + (near + far)


def first_kernel(scalars, *refs):
    gots, keeps, (narrow, small), sends, wide_keeps = refs[:2], refs[2:4], refs[4:6], refs[6:9], refs[9:]
    for pairing in range(3):
        base = WIDE_BLOCKS[pairing]
        sends[pairing][base : base + 4 * NARROW] = narrow[pairing]
        split_small(small[...], sends[pairing], base + 4 * NARROW)
    for kind in range(2):
        half = 4 * WIDE[kind]
        for chunk in range(4):
            at = slice(chunk * WIDE[kind], (chunk + 1) * WIDE[kind])
            after = slice(half + chunk * WIDE[kind], half + (chunk + 1) * WIDE[kind])
            wide_keeps[kind][at] = (keeps[kind][at].astype(F32) + gots[kind][at].astype(F32)).astype(BF16)
            sends[1 - kind][at] = (keeps[kind][after].astype(F32) + gots[kind][after].astype(F32)).astype(BF16)


def second_kernel(scalars, *refs):
    gots, wide_in, (narrow, small), sends, (keep, new_small) = refs[:3], refs[3:5], refs[5:7], refs[7:10], refs[10:]

    def fill(chunk, target):
        tile = 0
        for kind in range(2):
            at = pl.ds(chunk * WIDE[kind], WIDE[kind])
            value = wide_in[kind][at].astype(F32) + gots[1 - kind][at].astype(F32)
            target[tile : tile + WIDE[kind]] = value.astype(BF16)
            tile += WIDE[kind]
        value = narrow[3, pl.ds(chunk * NARROW, NARROW)].astype(F32)
        for pairing in range(3):
            value = value + gots[pairing][pl.ds(WIDE_BLOCKS[pairing] + chunk * NARROW, NARROW)].astype(F32)
        target[tile : tile + NARROW] = value.astype(BF16)

    value = sum_small(small[...], gots, [count - 1 for count in ROUND_ONE])
    new_small[...] = value
    for pairing in range(3):
        fill(peer(scalars[1], pairing), sends[pairing])
        split_small(value, sends[pairing], TILES)
    fill(scalars[1], keep)


def third_kernel(scalars, *refs):
    gots, (kept, small), (send, keep, gain_sum) = refs[:3], refs[3:5], refs[5:]
    here = scalars[2]
    for first in range(0, TILES, 7):
        at = slice(first, first + 7)
        value = kept[at].astype(F32)
        for got in gots:
            value = value + got[at].astype(F32)
        zero, one = value[:, :32], value[:, 32:]
        keep[at] = jnp.where(here == 0, zero, one)
        send[at] = jnp.where(here == 0, one, zero).astype(BF16)
    value = sum_small(small[...], gots, [TILES] * 3)
    high = value.astype(BF16)
    low = (value - high.astype(F32)).astype(BF16)
    send[TILES] = high
    send[TILES + 1] = low
    gain_sum[...] = high[:8].astype(F32) + low[:8].astype(F32)
    keep[TILES] = high.astype(F32)
    keep[TILES + 1] = low.astype(F32)


def cores_kernel(scalars, keep, across, skew, got, mine, away):
    core = scalars[3]
    total = keep[:TILES] + got[:TILES].astype(F32)
    zero, one = total[:, :16], total[:, 16:]
    mine[:TILES] = jnp.where(core == 0, zero, one)
    away[:TILES] = jnp.where(core == 0, one, zero)
    here = keep[TILES] + keep[TILES + 1]
    there = got[TILES].astype(F32) + got[TILES + 1].astype(F32)
    both = here + there
    gain = (here[:8] + across[...]) + (there[:8] + skew[...])
    for target in (mine, away):
        target[TILES, :8] = gain
        target[TILES, 8:] = both[8:16]
        target[TILES + 1] = both[16:]


def outputs_kernel(scalars, mine, got, down, gate, up, inner, out, gain_one, gain_two, taps):
    core = scalars[3]

    def place(target, tile, column, columns):
        zero, one = jnp.where(core == 0, mine[tile], got[tile]), jnp.where(core == 0, got[tile], mine[tile])
        target[:, column : column + 128] = zero
        target[:, columns + column : columns + column + 128] = one

    for matrix, target in enumerate((down, gate, up)):
        for tile in range(WIDE_COLUMNS // 128):
            place(target, matrix * (WIDE_COLUMNS // 128) + tile, tile * 128, WIDE_COLUMNS)
    for kind in range(4):
        for column in range(2):
            place(inner.at[kind] if kind < 3 else out, WIDE_TILES + 2 * kind + column, column * 128, 256)
    gains = mine[TILES] + got[TILES]
    rest = mine[TILES + 1] + got[TILES + 1]
    for at in range(8):
        lanes = slice(at * 128, at * 128 + 128)
        gain_one[:, lanes] = gains[at : at + 1]
        gain_two[:, lanes] = gains[8 + at : 9 + at]
    for lag in range(3):
        for at in range(4):
            row = 4 * lag + at
            taps[lag : lag + 1, at * 128 : at * 128 + 128] = rest[row : row + 1]


def swap_round(sends, pairings):
    return [swap(value, pairs) for value, pairs in zip(sends, pairings)]


def blocks(counts):
    return [like((count, *BLOCK), BF16) for count in counts]


def on_device(
    tokens,
    starts,
    gain_one,
    in_weight,
    conv_weight,
    out_weight,
    gain_two,
    gate_weight,
    up_weight,
    down_weight,
    cotangent,
):
    at = lax.axis_index("seq")
    core = at % 2
    y, z = at // 16, (at // 4) % 4
    scalars = jnp.stack(
        [jnp.where(core == 0, y, z), jnp.where(core == 0, z, y), (at // 2) % 2, core, starts[0]]
    ).astype(jnp.int32)
    run = functools.partial(call, scalars=scalars)
    rows, width = tokens.shape
    channels = conv_weight.shape[1]
    in_parts = in_weight.transpose(1, 0, 2)
    gain_one_row, gain_two_row = gain_one.reshape(1, -1), gain_two.reshape(1, -1)

    def share(value):
        return swap(value, CORES)

    tail = run(
        tail_kernel,
        operands=[tokens, gain_one_row, in_parts],
        outs=[like((16, channels), BF16)],
        scratch=[
            pltpu.VMEM((16, width), BF16),
            pltpu.VMEM((1, width), F32),
            pltpu.VMEM((width, channels), BF16),
            pltpu.VMEM((width, channels), BF16),
            pltpu.SemaphoreType.DMA((4,)),
        ],
        where=pltpu.HBM,
    )[0]
    incoming = from_behind(tail, "seq", 1)
    cotangent_other = share(cotangent)
    incoming, cotangent_other = lax.optimization_barrier((incoming, cotangent_other))
    normed_one, parts, gated = run(
        project_kernel,
        operands=[tokens, gain_one_row, in_parts],
        outs=[like((rows, width), BF16), like((3, rows, channels), F32), like((rows, channels), BF16)],
    )
    conv, ymix, branch = run(
        mix_kernel,
        operands=[gated, incoming, parts, conv_weight, out_weight],
        outs=[
            like((rows, channels), F32),
            like((rows, channels), BF16),
            like((rows, width), BF16),
        ],
    )
    branch, cotangent_late = lax.optimization_barrier((branch, cotangent))
    branch_other = swap(branch, ACROSS)
    units = gate_weight.shape[1]
    hidden_grad = run(
        hidden_kernel,
        operands=[cotangent_late, down_weight],
        outs=[like((rows, units), F32)],
        flops=LONG,
    )[0]
    branch_other, hidden_grad = lax.optimization_barrier((branch_other, hidden_grad))
    resid, normed_two, hidden, gate_back, up_back, norm_two_part, late_shared = run(
        feed_kernel,
        operands=[tokens, branch, branch_other, gain_two_row, gate_weight, up_weight, hidden_grad]
        + [normed_one, ymix],
        outs=[like((rows, width), F32), like((rows, width), BF16)]
        + [like((rows, units), BF16)] * 3
        + [like((rows, width), BF16), like((rows, 3 * WIDE_COLUMNS + 2 * width + channels // 2), BF16)],
    )
    norm_two_other = swap(norm_two_part, ACROSS)
    shared_other = share(late_shared)
    results = run(
        wide_kernel,
        operands=[normed_two, cotangent, cotangent_other, hidden, gate_back, up_back, shared_other],
        outs=blocks([8 * count for count in WIDE] * 2),
        scratch=[pltpu.VMEM((width, 2 * rows), BF16)] * 2,
    )
    sends, keeps = list(results[:2]), list(results[2:])
    down_part = run(down_kernel, operands=[hidden, down_weight], outs=[like((rows, width), BF16)])[0]
    norm_two_other, keeps[1], down_part = lax.optimization_barrier((norm_two_other, keeps[1], down_part))
    gots = swap_round(sends, FIRST)
    down_other = swap(down_part, ACROSS)

    edge_operands = [norm_two_part, norm_two_other, resid, gain_two_row, cotangent, out_weight, parts, conv_weight]
    edge = run(edge_kernel, operands=edge_operands, outs=[like((8, channels), F32)])[0]
    returned = from_behind(edge, "seq", -1)
    resid_grad, resid_low, gain_two_grad, c_back, gated_back, tap_grads = run(
        middle_kernel,
        operands=edge_operands + [conv, gated, incoming],
        outs=[
            like((rows, width), F32),
            like((rows, width), BF16),
            like((1, width), F32),
            like((rows, channels), BF16),
            like((rows, channels), F32),
            like((3, channels), F32),
        ],
        flops=SHORT,
    )
    backs, shared, norm_one_part, small = run(
        last_kernel,
        operands=[gated_back, returned, parts, c_back, in_parts, tokens, gain_two_grad, tap_grads]
        + [resid_low],
        outs=[
            like((3, rows, channels), BF16),
            like((7, rows, 256), BF16),
            like((rows, width), BF16),
            like((32, 128), F32),
        ],
    )
    narrow = run(
        narrow_kernel,
        operands=[normed_one, shared_other, resid_low, share(shared), backs, ymix],
        outs=[like((4, 4 * NARROW, *BLOCK), BF16)],
        scratch=[pltpu.VMEM((width, 2 * rows), BF16)] * 2,
    )[0]
    gots[0], gots[1], narrow, down_other = lax.optimization_barrier((gots[0], gots[1], narrow, down_other))
    results = run(
        first_kernel,
        operands=gots + keeps + [narrow, small],
        outs=blocks(ROUND_ONE) + blocks([4 * count for count in WIDE]),
    )
    sends, keeps = list(results[:3]), list(results[3:])
    gots = swap_round(sends, FIRST)
    norm_one_other = swap(norm_one_part, ACROSS)
    gots[0], norm_one_other = lax.optimization_barrier((gots[0], norm_one_other))
    results = run(
        second_kernel,
        operands=gots + keeps + [narrow, small],
        outs=blocks([TILES + 1] * 3 + [TILES]) + [like((32, 128), F32)],
    )
    sends, keep, small = list(results[:3]), results[3], results[4]
    gots = swap_round(sends, SECOND)
    beside, kept, gain_sum = run(
        third_kernel,
        operands=gots + [keep, small],
        outs=[like((TILES + 2, 32, 128), BF16), like((TILES + 2, 32, 128), F32), like((8, 128), F32)],
    )
    gots = [swap(gain_sum, ACROSS), swap(gain_sum, SKEW), swap(beside, BESIDE)]
    mixed = (resid + (down_part.astype(F32) + down_other.astype(F32))).astype(BF16)
    inputs = tokens.astype(F32)
    norm_one_back = norm_one_part.astype(F32) + norm_one_other.astype(F32)
    tokens_grad = resid_grad + norm_backward(norm_one_back, inputs, norm_scale(inputs), gain_one)
    gots[0], mixed, tokens_grad = lax.optimization_barrier((gots[0], mixed, tokens_grad))
    mine, away = run(
        cores_kernel,
        operands=[kept] + gots,
        outs=[like((TILES + 2, 16, 128), F32)] * 2,
    )
    down_g, gate_g, up_g, in_g, out_g, gain_one_g, gain_two_g, conv_g = run(
        outputs_kernel,
        operands=[mine, swap(away, CORES)],
        outs=[like((16, 2 * WIDE_COLUMNS), F32)] * 3
        + [like((3, 16, channels), F32), like((16, channels), F32)]
        + [like((1, width), F32)] * 2
        + [like((3, channels), F32)],
    )
    in_g, gain_one_g, gain_two_g = in_g.transpose(1, 0, 2), gain_one_g.reshape(-1), gain_two_g.reshape(-1)
    return (mixed, tokens_grad, gain_one_g, in_g, conv_g, out_g.T, gain_two_g, gate_g, up_g, down_g.T)


def solution(mesh):
    return jax.shard_map(
        on_device,
        mesh=mesh,
        in_specs=(
            P("seq", None),
            P("seq"),
            P(),
            P(None, None, "tensor"),
            P(None, "tensor"),
            P("tensor", None),
            P(),
            P(None, "tensor"),
            P(None, "tensor"),
            P("tensor", None),
            P("seq", None),
        ),
        out_specs=(
            P("seq", None),
            P("seq", None),
            P(),
            P("seq", None, "tensor"),
            P(None, "tensor"),
            P("tensor", "seq"),
            P(),
            P("seq", "tensor"),
            P("seq", "tensor"),
            P("tensor", "seq"),
        ),
        check_vma=False,
    )
```

time: 158 us -> 142 us (0.90)
  starting transfers between devices: 58.9 us -> 40.5 us
  matrix products: 13.5 us -> 0 us
  waiting for transfers between devices: 48.5 us -> 60.5 us
  Pallas kernels: 23.9 us -> 32.7 us
  other arithmetic: 5.61 us -> 2.85 us
  local copies, waits for them, and re-layouts: 6 us -> 3.77 us
    ppermute x30 -> x19, starting transfers between devices: 51.5 us -> 35.2 us  [swap(): return lax.ppermute(value, AXES, pairs)]
    dot_general x6 -> x0, matrix products: 13.5 us -> none  [the longest x1 4.03 us: on_device(): gate_act = jnp.dot(normed_two, gate_weight, preferred_element_type=F32)]
    ppermute x30 -> x19, waiting for transfers between devices: 48.5 us -> 59.5 us  [swap(): return lax.ppermute(value, AXES, pairs)]
    pallas_call x12 -> x16, Pallas kernels: 23.9 us -> 32.7 us  [call(): pl.pallas_call(body, out_shape=tuple(outs), in_specs=[pl.BlockSpec(memory...]
    unnamed x44 -> x30, local copies, waits for them, and re-layouts: 5.92 us -> 3.69 us
    ppermute x2, starting transfers between devices: 7.35 us -> 5.37 us  [from_behind(): lax.ppermute(value, axis, [(source, source + steps) for source in range(l...]
  transfers between devices with their start and end apart: 32 -> 21, of which waited for: 15 -> 13; matrix products, arithmetic and copies ran while one was open for 11% -> 2% of each run, Pallas kernels for 11% -> 14%
where the time goes in v3:
time: 142 us
  waiting for transfers between devices  60.5 us (43%)
  starting transfers between devices  40.5 us (29%)
  Pallas kernels  32.7 us (23%)
  local copies, waits for them, and re-layouts  3.77 us (3%)
  other arithmetic  2.85 us (2%)
  between operations  1.62 us (1%)
    ppermute x19, waiting for transfers between devices, swap(): return lax.ppermute(value, AXES, pairs)  59.5 us
    ppermute x19, starting transfers between devices, swap(): return lax.ppermute(value, AXES, pairs)  35.2 us
    pallas_call x16, Pallas kernels, call(): pl.pallas_call(body, out_shape=tuple(outs), in_specs=[pl.BlockSpec(memory...  32.7 us
    ppermute x2, starting transfers between devices, from_behind(): lax.ppermute(value, axis, [(source, source + steps) for source in range(l...  5.37 us
    unnamed x30, local copies, waits for them, and re-layouts  3.69 us
  transfers between devices with their start and end apart: 21, of which 13 were waited for; matrix products, arithmetic and copies ran while one was open for 2% of the time, Pallas kernels for 14%

profile of v3, /device:TPU:1, one launch (start us, length us, event | category | flops | bytes accessed | tf_op | source)
XLA Modules:
  0.0 141.9 jit_solution(842177574044255924)
XLA Ops:
  7.8 3.3 %collective-permute-start = (bf16[16,512]{1,0:T(8,128)(2,1)S(1)}, bf16[16,512]{1,0:T(8,128)(2,1)S(1)}, u32[]{:S(2)}, u32[]{:S(2)}) collective-permute-start(bf16[16,512]{1,0:T(8,128)(2,1)S(1)} %shard_map.187), channel_id=1, source_target_pairs={{0,2},{2,4},{4,6},{6,8},{8,10},{10,12},{12,14},{14,16},{16,18},{18... | collective-permute-start | bytes 49160 | tf_op jit(solution)/shard_map/ppermute | solution.py:81
  14.0 2.5 %collective-permute-start.2 = (bf16[256,1024]{1,0:T(8,128)(2,1)S(1)}, bf16[256,1024]{1,0:T(8,128)(2,1)S(1)}, u32[]{:S(2)}, u32[]{:S(2)}) collective-permute-start(bf16[256,1024]{1,0:T(8,128)(2,1)S(1)} %get-tuple-element.82.branch), channel_id=1, source_target_pairs={{0,1},{2,3},{4,5},{6,7},{1,0},{3,2},{5,4},{7,6},{8,9},{10,11},{12,... | collective-permute-start | bytes 1572872 | tf_op jit(solution)/shard_map/ppermute | solution.py:75
  18.5 10.5 %collective-permute-done.2.other = bf16[256,1024]{1,0:T(8,128)(2,1)S(1)} collective-permute-done((bf16[256,1024]{1,0:T(8,128)(2,1)S(1)}, bf16[256,1024]{1,0:T(8,128)(2,1)S(1)}, u32[]{:S(2)}, u32[]{:S(2)}) %collective-permute-start.2) | collective-permute-done | bytes 524320 | tf_op jit(solution)/shard_map/ppermute | solution.py:75
  29.0 6.6 %shard_map.190 = (f32[256,1024]{1,0:T(8,128)S(1)}, bf16[256,1024]{1,0:T(8,128)(2,1)S(1)}, bf16[256,2304]{1,0:T(8,128)(2,1)S(1)}, bf16[256,2304]{1,0:T(8,128)(2,1...) custom-call(s32[5]{0:T(128)S(1)} %stack.19.scalars, ...), custom_call_target="tpu_custom_call" | custom-call | tf_op jit(solution)/shard_map/pallas_call | solution.py:100
  36.1 3.0 %collective-permute-start.6 = (bf16[256,1024]{1,0:T(8,128)(2,1)S(1)}, bf16[256,1024]{1,0:T(8,128)(2,1)S(1)}, u32[]{:S(2)}, u32[]{:S(2)}) collective-permute-start(bf16[256,1024]{1,0:T(8,128)(2,1)S(1)} %get-tuple-element.96.part), channel_id=1, source_target_pairs={{0,1},{2,3},{4,5},{6,7},{1,0},{3,2},{5,4},{7,6},{8,9},{10,11},{12,... | collective-permute-start | bytes 1572872 | tf_op jit(solution)/shard_map/ppermute | solution.py:75
  41.1 5.4 %shard_map.191 = (bf16[112,64,128]{2,1,0:T(8,128)(2,1)S(1)}, bf16[104,64,128]{2,1,0:T(8,128)(2,1)S(1)}, bf16[112,64,128]{2,1,0:T(8,128)(2,1)S(1)}, bf16[104,64,128]{2,1,0:T(8,128)(2,1)S(1)}) custom-call(s32[5]{0:T(128)S(1)} %stack.19.scalars, bf16[256,1024]{1,0:T(8,128)(2,1)S(1)} %get-tuple-element.88.two, bf16[256,1024]{1,0:T(8,128)(2,1)S(1)} %copy-done.6, ...), custom_call_target="tpu_custom_call" | custom-call | tf_op jit(solution)/shard_map/pallas_call | solution.py:100
  46.5 2.3 %collective-permute-start.4 = (bf16[112,64,128]{2,1,0:T(8,128)(2,1)S(1)}, bf16[112,64,128]{2,1,0:T(8,128)(2,1)S(1)}, u32[]{:S(2)}, u32[]{:S(2)}) collective-permute-start(bf16[112,64,128]{2,1,0:T(8,128)(2,1)S(1)} %get-tuple-element.94), channel_id=1, source_target_pairs={{0,32},{2,10},{4,36},{6,14},{1,33},{3,11},{5,37},{7,15},{8,40},{10... | collective-permute-start | bytes 5505032 | tf_op jit(solution)/shard_map/ppermute | solution.py:75
  48.8 2.3 %collective-permute-start.5 = (bf16[104,64,128]{2,1,0:T(8,128)(2,1)S(1)}, bf16[104,64,128]{2,1,0:T(8,128)(2,1)S(1)}, u32[]{:S(2)}, u32[]{:S(2)}) collective-permute-start(bf16[104,64,128]{2,1,0:T(8,128)(2,1)S(1)} %get-tuple-element.95), channel_id=1, source_target_pairs={{0,96},{2,26},{4,100},{6,30},{1,97},{3,27},{5,101},{7,31},{8,104},... | collective-permute-start | bytes 5111816 | tf_op jit(solution)/shard_map/ppermute | solution.py:75
  56.1 2.2 %shard_map.193 = (f32[256,1024]{1,0:T(8,128)S(1)}, bf16[256,1024]{1,0:T(8,128)(2,1)S(1)}, f32[1,1024]{1,0:T(1,128)S(1)}, bf16[256,512]{1,0:T(8,128)(2,1)S(1)}, f...) custom-call(s32[5]{0:T(128)S(1)} %stack.19.scalars, bf16[256,1024]{1,0:T(8,128)(2,1)S(1)} %get-tuple-element.96.part, ...), custom_call_target="tpu_custom_call" | custom-call | flops 8000000000 | tf_op jit(solution)/shard_map/pallas_call | solution.py:100
  61.1 2.7 %collective-permute-start.9 = (bf16[256,1024]{1,0:T(8,128)(2,1)S(1)}, bf16[256,1024]{1,0:T(8,128)(2,1)S(1)}, u32[]{:S(2)}, u32[]{:S(2)}) collective-permute-start(bf16[256,1024]{1,0:T(8,128)(2,1)S(1)} %shard_map.192), channel_id=1, source_target_pairs={{0,1},{2,3},{4,5},{6,7},{1,0},{3,2},{5,4},{7,6},{8,9},{10,11},{12,... | collective-permute-start | bytes 1572872 | tf_op jit(solution)/shard_map/ppermute | solution.py:75
  63.9 2.3 %shard_map.196.refs_4_.refs_5_ = bf16[4,32,64,128]{3,2,1,0:T(8,128)(2,1)S(1)} custom-call(s32[5]{0:T(128)S(1)} %stack.19.scalars, bf16[256,1024]{1,0:T(8,128)(2,1)S(1)} %get-tuple-element.86.normed_one.one, bf16[256,5760]{1,0:T(8,128)(2,1)S(1)} %collective-permute-done.3.refs_3_.shared, bf16[256,1024]{1,0:T(8,128)(2,1)S(1)} %get-tuple-element.101.resid_low.low, ...), custom_call_target="tpu_custom_call" | custom-call | tf_op jit(solution)/shard_map/pallas_call | solution.py:100
  66.2 9.6 %collective-permute-done.9 = bf16[256,1024]{1,0:T(8,128)(2,1)S(1)} collective-permute-done((bf16[256,1024]{1,0:T(8,128)(2,1)S(1)}, bf16[256,1024]{1,0:T(8,128)(2,1)S(1)}, u32[]{:S(2)}, u32[]{:S(2)}) %collective-permute-start.9) | collective-permute-done | bytes 524320 | tf_op jit(solution)/shard_map/ppermute | solution.py:75
  77.3 2.8 %collective-permute-start.12 = (bf16[89,64,128]{2,1,0:T(8,128)(2,1)S(1)}, bf16[89,64,128]{2,1,0:T(8,128)(2,1)S(1)}, u32[]{:S(2)}, u32[]{:S(2)}) collective-permute-start(bf16[89,64,128]{2,1,0:T(8,128)(2,1)S(1)} %get-tuple-element.118), channel_id=1, source_target_pairs={{0,96},{2,26},{4,100},{6,30},{1,97},{3,27},{5,101},{7,31},{8,104},... | collective-permute-start | bytes 4374536 | tf_op jit(solution)/shard_map/ppermute | solution.py:75
  81.4 2.5 %collective-permute-start.11 = (bf16[256,1024]{1,0:T(8,128)(2,1)S(1)}, bf16[256,1024]{1,0:T(8,128)(2,1)S(1)}, u32[]{:S(2)}, u32[]{:S(2)}) collective-permute-start(bf16[256,1024]{1,0:T(8,128)(2,1)S(1)} %get-tuple-element.116), channel_id=1, source_target_pairs={{0,1},{2,3},{4,5},{6,7},{1,0},{3,2},{5,4},{7,6},{8,9},{10,11},{12,... | collective-permute-start | bytes 1572872 | tf_op jit(solution)/shard_map/ppermute | solution.py:75
  83.9 9.3 %collective-permute-done.11 = bf16[256,1024]{1,0:T(8,128)(2,1)S(1)} collective-permute-done((bf16[256,1024]{1,0:T(8,128)(2,1)S(1)}, bf16[256,1024]{1,0:T(8,128)(2,1)S(1)}, u32[]{:S(2)}, u32[]{:S(2)}) %collective-permute-start.11) | collective-permute-done | bytes 524320 | tf_op jit(solution)/shard_map/ppermute | solution.py:75
  93.2 4.5 %collective-permute-done.10.refs_0_ = bf16[85,64,128]{2,1,0:T(8,128)(2,1)S(1)} collective-permute-done((bf16[85,64,128]{2,1,0:T(8,128)(2,1)S(1)}, bf16[85,64,128]{2,1,0:T(8,128)(2,1)S(1)}, u32[]{:S(2)}, u32[]{:S(2)}) %collective-permute-start.10) | collective-permute-done | bytes 1392672 | tf_op jit(solution)/shard_map/ppermute | solution.py:75
  97.8 5.6 %collective-permute-done.13.refs_2_ = bf16[33,64,128]{2,1,0:T(8,128)(2,1)S(1)} collective-permute-done((bf16[33,64,128]{2,1,0:T(8,128)(2,1)S(1)}, bf16[33,64,128]{2,1,0:T(8,128)(2,1)S(1)}, u32[]{:S(2)}, u32[]{:S(2)}) %collective-permute-start.13) | collective-permute-done | bytes 540704 | tf_op jit(solution)/shard_map/ppermute | solution.py:75
  104.6 2.3 %collective-permute-start.14 = (bf16[36,64,128]{2,1,0:T(8,128)(2,1)S(1)}, bf16[36,64,128]{2,1,0:T(8,128)(2,1)S(1)}, u32[]{:S(2)}, u32[]{:S(2)}) collective-permute-start(bf16[36,64,128]{2,1,0:T(8,128)(2,1)S(1)} %get-tuple-element.122), channel_id=1, source_target_pairs={{0,8},{2,34},{4,12},{6,38},{1,9},{3,35},{5,13},{7,39},{8,0},{10,42... | collective-permute-start | bytes 1769480 | tf_op jit(solution)/shard_map/ppermute | solution.py:75
  111.6 2.9 %collective-permute-done.14.refs_0_ = bf16[36,64,128]{2,1,0:T(8,128)(2,1)S(1)} collective-permute-done((bf16[36,64,128]{2,1,0:T(8,128)(2,1)S(1)}, bf16[36,64,128]{2,1,0:T(8,128)(2,1)S(1)}, u32[]{:S(2)}, u32[]{:S(2)}) %collective-permute-start.14) | collective-permute-done | bytes 589856 | tf_op jit(solution)/shard_map/ppermute | solution.py:75
  114.5 7.7 %collective-permute-done.15.refs_1_ = bf16[36,64,128]{2,1,0:T(8,128)(2,1)S(1)} collective-permute-done((bf16[36,64,128]{2,1,0:T(8,128)(2,1)S(1)}, bf16[36,64,128]{2,1,0:T(8,128)(2,1)S(1)}, u32[]{:S(2)}, u32[]{:S(2)}) %collective-permute-start.15) | collective-permute-done | bytes 589856 | tf_op jit(solution)/shard_map/ppermute | solution.py:75
  124.8 2.6 %collective-permute-start.17 = (f32[8,128]{1,0:T(8,128)S(1)}, f32[8,128]{1,0:T(8,128)S(1)}, u32[]{:S(2)}, u32[]{:S(2)}) collective-permute-start(f32[8,128]{1,0:T(8,128)S(1)} %get-tuple-element.127), channel_id=1, source_target_pairs={{0,1},{2,3},{4,5},{6,7},{1,0},{3,2},{5,4},{7,6},{8,9},{10,11},{12,... | collective-permute-start | bytes 12296 | tf_op jit(solution)/shard_map/ppermute | solution.py:75
  129.2 2.2 %collective-permute-done.18.skew = f32[8,128]{1,0:T(8,128)S(1)} collective-permute-done((f32[8,128]{1,0:T(8,128)S(1)}, f32[8,128]{1,0:T(8,128)S(1)}, u32[]{:S(2)}, u32[]{:S(2)}) %collective-permute-start.18) | collective-permute-done | bytes 4128 | tf_op jit(solution)/shard_map/ppermute | solution.py:75
  131.4 2.1 %collective-permute-done.19.got = bf16[37,32,128]{2,1,0:T(8,128)(2,1)S(1)} collective-permute-done((bf16[37,32,128]{2,1,0:T(8,128)(2,1)S(1)}, bf16[37,32,128]{2,1,0:T(8,128)(2,1)S(1)}, u32[]{:S(2)}, u32[]{:S(2)}) %collective-permute-start.19) | collective-permute-done | bytes 303136 | tf_op jit(solution)/shard_map/ppermute | solution.py:75
  134.2 5.1 %collective-permute-start.20 = (f32[37,16,128]{2,1,0:T(8,128)S(1)}, f32[37,16,128]{2,1,0:T(8,128)S(1)}, u32[]{:S(2)}, u32[]{:S(2)}) collective-permute-start(f32[37,16,128]{2,1,0:T(8,128)S(1)} %get-tuple-element.137), channel_id=1, source_target_pairs={{0,2},{2,0},{4,6},{6,4},{1,3},{3,1},{5,7},{7,5},{8,10},{10,8},{12,... | collective-permute-start | bytes 909320 | tf_op jit(solution)/shard_map/ppermute | solution.py:75
  (71 shorter events, 37.8 us)
Async XLA Ops:
  0.6 12.1 %collective-permute-start.1 = (bf16[256,1024]{1,0:T(8,128)(2,1)}, bf16[256,1024]{1,0:T(8,128)(2,1)S(1)}, u32[]{:S(2)}, u32[]{:S(2)}) collective-permute-start(bf16[256,1024]{1,0:T(8,128)(2,1)} %cot.6), channel_id=1, source_target_pairs={{0,2},{2,0},{4,6},{6,4},{1,3},{3,1},{5,7},{7,5},{8,10},{10,8},{12,... | collective-permute-start | bytes 1572872 | tf_op jit(solution)/shard_map/ppermute | solution.py:75
  7.8 5.0 %collective-permute-start = (bf16[16,512]{1,0:T(8,128)(2,1)S(1)}, bf16[16,512]{1,0:T(8,128)(2,1)S(1)}, u32[]{:S(2)}, u32[]{:S(2)}) collective-permute-start(bf16[16,512]{1,0:T(8,128)(2,1)S(1)} %shard_map.187), channel_id=1, source_target_pairs={{0,2},{2,4},{4,6},{6,8},{8,10},{10,12},{12,14},{14,16},{16,18},{18... | collective-permute-start | bytes 49160 | tf_op jit(solution)/shard_map/ppermute | solution.py:81
  14.0 15.0 %slice-start = ((s8[4718592]{0:T(1024)(128)(4,1)}), s8[4194304]{0:T(1024)(128)(4,1)S(1)}, s32[]{:S(2)}) async-start(s8[4718592]{0:T(1024)(128)(4,1)} %bitcast.15), calls=%async_computation | async-start | bytes 8388608
  14.0 15.0 %slice-start.2 = ((s8[4718592]{0:T(1024)(128)(4,1)}), s8[4194304]{0:T(1024)(128)(4,1)S(1)}, s32[]{:S(2)}) async-start(s8[4718592]{0:T(1024)(128)(4,1)} %bitcast.17), calls=%async_computation.2 | async-start | bytes 8388608
  14.0 14.9 %collective-permute-start.2 = (bf16[256,1024]{1,0:T(8,128)(2,1)S(1)}, bf16[256,1024]{1,0:T(8,128)(2,1)S(1)}, u32[]{:S(2)}, u32[]{:S(2)}) collective-permute-start(bf16[256,1024]{1,0:T(8,128)(2,1)S(1)} %get-tuple-element.82.branch), channel_id=1, source_target_pairs={{0,1},{2,3},{4,5},{6,7},{1,0},{3,2},{5,4},{7,6},{8,9},{10,11},{12,... | collective-permute-start | bytes 1572872 | tf_op jit(solution)/shard_map/ppermute | solution.py:75
  35.7 5.5 %collective-permute-start.3 = (bf16[256,5760]{1,0:T(8,128)(2,1)S(1)}, bf16[256,5760]{1,0:T(8,128)(2,1)S(1)}, u32[]{:S(2)}, u32[]{:S(2)}) collective-permute-start(bf16[256,5760]{1,0:T(8,128)(2,1)S(1)} %get-tuple-element.93), channel_id=1, source_target_pairs={{0,2},{2,0},{4,6},{6,4},{1,3},{3,1},{5,7},{7,5},{8,10},{10,8},{12,... | collective-permute-start | bytes 8847368 | tf_op jit(solution)/shard_map/ppermute | solution.py:75
  36.1 16.9 %collective-permute-start.6 = (bf16[256,1024]{1,0:T(8,128)(2,1)S(1)}, bf16[256,1024]{1,0:T(8,128)(2,1)S(1)}, u32[]{:S(2)}, u32[]{:S(2)}) collective-permute-start(bf16[256,1024]{1,0:T(8,128)(2,1)S(1)} %get-tuple-element.96.part), channel_id=1, source_target_pairs={{0,1},{2,3},{4,5},{6,7},{1,0},{3,2},{5,4},{7,6},{8,9},{10,11},{12,... | collective-permute-start | bytes 1572872 | tf_op jit(solution)/shard_map/ppermute | solution.py:75
  46.5 29.3 %collective-permute-start.4 = (bf16[112,64,128]{2,1,0:T(8,128)(2,1)S(1)}, bf16[112,64,128]{2,1,0:T(8,128)(2,1)S(1)}, u32[]{:S(2)}, u32[]{:S(2)}) collective-permute-start(bf16[112,64,128]{2,1,0:T(8,128)(2,1)S(1)} %get-tuple-element.94), channel_id=1, source_target_pairs={{0,32},{2,10},{4,36},{6,14},{1,33},{3,11},{5,37},{7,15},{8,40},{10... | collective-permute-start | bytes 5505032 | tf_op jit(solution)/shard_map/ppermute | solution.py:75
  48.8 27.0 %collective-permute-start.5 = (bf16[104,64,128]{2,1,0:T(8,128)(2,1)S(1)}, bf16[104,64,128]{2,1,0:T(8,128)(2,1)S(1)}, u32[]{:S(2)}, u32[]{:S(2)}) collective-permute-start(bf16[104,64,128]{2,1,0:T(8,128)(2,1)S(1)} %get-tuple-element.95), channel_id=1, source_target_pairs={{0,96},{2,26},{4,100},{6,30},{1,97},{3,27},{5,101},{7,31},{8,104},... | collective-permute-start | bytes 5111816 | tf_op jit(solution)/shard_map/ppermute | solution.py:75
  54.0 5.4 %collective-permute-start.7 = (f32[8,512]{1,0:T(8,128)S(1)}, f32[8,512]{1,0:T(8,128)S(1)}, u32[]{:S(2)}, u32[]{:S(2)}) collective-permute-start(f32[8,512]{1,0:T(8,128)S(1)} %shard_map.194), channel_id=1, source_target_pairs={{2,0},{4,2},{6,4},{8,6},{10,8},{12,10},{14,12},{16,14},{18,16},{20... | collective-permute-start | bytes 49160 | tf_op jit(solution)/shard_map/ppermute | solution.py:81
  61.0 2.8 %collective-permute-start.8 = (bf16[7,256,256]{2,1,0:T(8,128)(2,1)S(1)}, bf16[7,256,256]{2,1,0:T(8,128)(2,1)S(1)}, u32[]{:S(2)}, u32[]{:S(2)}) collective-permute-start(bf16[7,256,256]{2,1,0:T(8,128)(2,1)S(1)} %get-tuple-element.106), channel_id=1, source_target_pairs={{0,2},{2,0},{4,6},{6,4},{1,3},{3,1},{5,7},{7,5},{8,10},{10,8},{12,... | collective-permute-start | bytes 2752520 | tf_op jit(solution)/shard_map/ppermute | solution.py:75
  61.1 14.7 %collective-permute-start.9 = (bf16[256,1024]{1,0:T(8,128)(2,1)S(1)}, bf16[256,1024]{1,0:T(8,128)(2,1)S(1)}, u32[]{:S(2)}, u32[]{:S(2)}) collective-permute-start(bf16[256,1024]{1,0:T(8,128)(2,1)S(1)} %shard_map.192), channel_id=1, source_target_pairs={{0,1},{2,3},{4,5},{6,7},{1,0},{3,2},{5,4},{7,6},{8,9},{10,11},{12,... | collective-permute-start | bytes 1572872 | tf_op jit(solution)/shard_map/ppermute | solution.py:75
  77.3 26.1 %collective-permute-start.12 = (bf16[89,64,128]{2,1,0:T(8,128)(2,1)S(1)}, bf16[89,64,128]{2,1,0:T(8,128)(2,1)S(1)}, u32[]{:S(2)}, u32[]{:S(2)}) collective-permute-start(bf16[89,64,128]{2,1,0:T(8,128)(2,1)S(1)} %get-tuple-element.118), channel_id=1, source_target_pairs={{0,96},{2,26},{4,100},{6,30},{1,97},{3,27},{5,101},{7,31},{8,104},... | collective-permute-start | bytes 4374536 | tf_op jit(solution)/shard_map/ppermute | solution.py:75
  80.1 17.6 %collective-permute-start.10 = (bf16[85,64,128]{2,1,0:T(8,128)(2,1)S(1)}, bf16[85,64,128]{2,1,0:T(8,128)(2,1)S(1)}, u32[]{:S(2)}, u32[]{:S(2)}) collective-permute-start(bf16[85,64,128]{2,1,0:T(8,128)(2,1)S(1)} %get-tuple-element.115), channel_id=1, source_target_pairs={{0,32},{2,10},{4,36},{6,14},{1,33},{3,11},{5,37},{7,15},{8,40},{10... | collective-permute-start | bytes 4177928 | tf_op jit(solution)/shard_map/ppermute | solution.py:75
  80.3 23.1 %collective-permute-start.13 = (bf16[33,64,128]{2,1,0:T(8,128)(2,1)S(1)}, bf16[33,64,128]{2,1,0:T(8,128)(2,1)S(1)}, u32[]{:S(2)}, u32[]{:S(2)}) collective-permute-start(bf16[33,64,128]{2,1,0:T(8,128)(2,1)S(1)} %get-tuple-element.119), channel_id=1, source_target_pairs={{0,64},{2,18},{4,68},{6,22},{1,65},{3,19},{5,69},{7,23},{8,72},{10... | collective-permute-start | bytes 1622024 | tf_op jit(solution)/shard_map/ppermute | solution.py:75
  81.4 11.8 %collective-permute-start.11 = (bf16[256,1024]{1,0:T(8,128)(2,1)S(1)}, bf16[256,1024]{1,0:T(8,128)(2,1)S(1)}, u32[]{:S(2)}, u32[]{:S(2)}) collective-permute-start(bf16[256,1024]{1,0:T(8,128)(2,1)S(1)} %get-tuple-element.116), channel_id=1, source_target_pairs={{0,1},{2,3},{4,5},{6,7},{1,0},{3,2},{5,4},{7,6},{8,9},{10,11},{12,... | collective-permute-start | bytes 1572872 | tf_op jit(solution)/shard_map/ppermute | solution.py:75
  104.6 9.9 %collective-permute-start.14 = (bf16[36,64,128]{2,1,0:T(8,128)(2,1)S(1)}, bf16[36,64,128]{2,1,0:T(8,128)(2,1)S(1)}, u32[]{:S(2)}, u32[]{:S(2)}) collective-permute-start(bf16[36,64,128]{2,1,0:T(8,128)(2,1)S(1)} %get-tuple-element.122), channel_id=1, source_target_pairs={{0,8},{2,34},{4,12},{6,38},{1,9},{3,35},{5,13},{7,39},{8,0},{10,42... | collective-permute-start | bytes 1769480 | tf_op jit(solution)/shard_map/ppermute | solution.py:75
  106.9 15.3 %collective-permute-start.15 = (bf16[36,64,128]{2,1,0:T(8,128)(2,1)S(1)}, bf16[36,64,128]{2,1,0:T(8,128)(2,1)S(1)}, u32[]{:S(2)}, u32[]{:S(2)}) collective-permute-start(bf16[36,64,128]{2,1,0:T(8,128)(2,1)S(1)} %get-tuple-element.123), channel_id=1, source_target_pairs={{0,24},{2,98},{4,28},{6,102},{1,25},{3,99},{5,29},{7,103},{8,16},{... | collective-permute-start | bytes 1769480 | tf_op jit(solution)/shard_map/ppermute | solution.py:75
  109.0 15.0 %collective-permute-start.16 = (bf16[36,64,128]{2,1,0:T(8,128)(2,1)S(1)}, bf16[36,64,128]{2,1,0:T(8,128)(2,1)S(1)}, u32[]{:S(2)}, u32[]{:S(2)}) collective-permute-start(bf16[36,64,128]{2,1,0:T(8,128)(2,1)S(1)} %get-tuple-element.124), channel_id=1, source_target_pairs={{0,16},{2,66},{4,20},{6,70},{1,17},{3,67},{5,21},{7,71},{8,24},{10... | collective-permute-start | bytes 1769480 | tf_op jit(solution)/shard_map/ppermute | solution.py:75
  111.2 16.7 %copy-start.8 = (f32[1024]{0:T(1024)S(1)}, f32[1024]{0:T(1024)}, u32[]{:S(2)}) copy-start(f32[1024]{0:T(1024)} %param.13) | copy-start | bytes 12292
  124.8 4.4 %collective-permute-start.17 = (f32[8,128]{1,0:T(8,128)S(1)}, f32[8,128]{1,0:T(8,128)S(1)}, u32[]{:S(2)}, u32[]{:S(2)}) collective-permute-start(f32[8,128]{1,0:T(8,128)S(1)} %get-tuple-element.127), channel_id=1, source_target_pairs={{0,1},{2,3},{4,5},{6,7},{1,0},{3,2},{5,4},{7,6},{8,9},{10,11},{12,... | collective-permute-start | bytes 12296 | tf_op jit(solution)/shard_map/ppermute | solution.py:75
  127.5 4.0 %collective-permute-start.18 = (f32[8,128]{1,0:T(8,128)S(1)}, f32[8,128]{1,0:T(8,128)S(1)}, u32[]{:S(2)}, u32[]{:S(2)}) collective-permute-start(f32[8,128]{1,0:T(8,128)S(1)} %get-tuple-element.127), channel_id=1, source_target_pairs={{0,5},{2,7},{4,1},{6,3},{1,4},{3,6},{5,0},{7,2},{8,13},{10,15},{12... | collective-permute-start | bytes 12296 | tf_op jit(solution)/shard_map/ppermute | solution.py:75
  127.9 5.7 %collective-permute-start.19 = (bf16[37,32,128]{2,1,0:T(8,128)(2,1)S(1)}, bf16[37,32,128]{2,1,0:T(8,128)(2,1)S(1)}, u32[]{:S(2)}, u32[]{:S(2)}) collective-permute-start(bf16[37,32,128]{2,1,0:T(8,128)(2,1)S(1)} %get-tuple-element.135), channel_id=1, source_target_pairs={{0,4},{2,6},{4,0},{6,2},{1,5},{3,7},{5,1},{7,3},{8,12},{10,14},{12... | collective-permute-start | bytes 909320 | tf_op jit(solution)/shard_map/ppermute | solution.py:75
  134.2 6.4 %collective-permute-start.20 = (f32[37,16,128]{2,1,0:T(8,128)S(1)}, f32[37,16,128]{2,1,0:T(8,128)S(1)}, u32[]{:S(2)}, u32[]{:S(2)}) collective-permute-start(f32[37,16,128]{2,1,0:T(8,128)S(1)} %get-tuple-element.137), channel_id=1, source_target_pairs={{0,2},{2,0},{4,6},{6,4},{1,3},{3,1},{5,7},{7,5},{8,10},{10,8},{12,... | collective-permute-start | bytes 909320 | tf_op jit(solution)/shard_map/ppermute | solution.py:75
  (12 other events, 86.2 us)

commit v4 on v3

--- a/solution.py
+++ b/solution.py
@@ -28,7 +28,7 @@
 
 ACROSS = device_pairs(lambda y, z, x, core: (y, z, (x + 2) % 4, core))
 BESIDE = device_pairs(lambda y, z, x, core: (y, z, x ^ 1, core))
-SKEW = device_pairs(lambda y, z, x, core: (y, z, (x ^ 1) ^ 2, core))
+NEAREST = device_pairs(lambda y, z, x, core: (y, z, 3 - x, core))
 CORES = device_pairs(lambda y, z, x, core: (y, z, x, 1 - core))
 
 
@@ -95,7 +95,7 @@
     return jax.ShapeDtypeStruct(shape, dtype)
 
 
-def call(body, *, scalars, operands, outs, scratch=(), where=pltpu.VMEM, flops=0):
+def call(body, *, scalars, operands, outs, scratch=(), where=pltpu.VMEM, flops=0, room=16):
     whole = pl.BlockSpec(memory_space=pltpu.VMEM)
     return pl.pallas_call(
         body,
@@ -103,7 +103,7 @@
         in_specs=[pl.BlockSpec(memory_space=pltpu.SMEM)] + [pl.BlockSpec(memory_space=where)] * len(operands),
         out_specs=tuple(whole for _ in outs),
         scratch_shapes=list(scratch),
-        compiler_params=pltpu.CompilerParams(vmem_limit_bytes=16 * 2**20),
+        compiler_params=pltpu.CompilerParams(vmem_limit_bytes=room * 2**20),
         cost_estimate=pl.CostEstimate(flops=flops, bytes_accessed=0, transcendentals=0),
     )(scalars, *operands)
 
@@ -152,11 +152,20 @@
     tail[...] = (gated * linked_rows(scalars[4], gated.shape, rows - 16, rows)).astype(BF16)
 
 
-def project_kernel(scalars, tokens, gain, weight, normed, parts, gated):
-    values = tokens[...].astype(F32)
-    normed[...] = (values * norm_scale(values) * gain[...]).astype(BF16)
+def project_kernel(scalars, tokens, gain, weight, normed, parts, gated, token_rows, gain_row, weights, done):
+    pieces = [(tokens, token_rows), (gain, gain_row)] + [(weight.at[k], weights.at[k]) for k in range(3)]
+    copies = [
+        pltpu.make_async_copy(source, target, done.at[at]) for at, (source, target) in enumerate(pieces)
+    ]
+    for copy in copies:
+        copy.start()
+    copies[0].wait()
+    copies[1].wait()
+    values = token_rows[...].astype(F32)
+    normed[...] = (values * norm_scale(values) * gain_row[...]).astype(BF16)
     for k in range(3):
-        parts[k] = dot(normed[...], weight[k])
+        copies[2 + k].wait()
+        parts[k] = dot(normed[...], weights[k])
     gated[...] = (parts[0] * parts[2]).astype(BF16)
 
 
@@ -168,7 +177,7 @@
     return moved
 
 
-def mix_kernel(scalars, gated, incoming, parts, taps, weight, conv, ymix, branch):
+def mix_kernel(scalars, gated, incoming, parts, taps, conv, ymix):
     values = gated[...].astype(F32)
     before = incoming[...].astype(F32)
     total = taps[0:1] * values
@@ -178,7 +187,6 @@
         )
     conv[...] = total
     ymix[...] = (parts[1] * total).astype(BF16)
-    branch[...] = dot(ymix[...], weight[...]).astype(BF16)
 
 
 def away_half(value, core):
@@ -195,26 +203,42 @@
     out[...] = dot(hidden[...], weight[...]).astype(BF16)
 
 
+def whole_kernel(scalars, weight, got, got_other, whole):
+    core, side = scalars[3], scalars[5]
+    half = got.shape[0]
+    low, high = jnp.where(core == 0, got[...], got_other[...]), jnp.where(core == 0, got_other[...], got[...])
+    whole[:half] = jnp.where(side == 0, weight[:half], low)
+    whole[half : 2 * half] = jnp.where(side == 0, weight[half:], high)
+    whole[2 * half : 3 * half] = jnp.where(side == 0, low, weight[:half])
+    whole[3 * half :] = jnp.where(side == 0, high, weight[half:])
+
+
 def feed_kernel(
     scalars,
     tokens,
-    branch,
-    other,
+    ymix,
+    ymix_other,
+    whole,
     gain,
     gate,
     up,
     hidden_grad,
     normed_one,
-    ymix,
     resid,
     normed,
     hidden,
     gate_back,
     up_back,
-    part,
     shared,
+    shared_early,
 ):
-    resid[...] = tokens[...].astype(F32) + (branch[...].astype(F32) + other[...].astype(F32))
+    side, channels = scalars[5], ymix.shape[1]
+    first, second = (
+        jnp.where(side == 0, ymix[...], ymix_other[...]),
+        jnp.where(side == 0, ymix_other[...], ymix[...]),
+    )
+    branch = dot(first, whole[:channels]) + dot(second, whole[channels:])
+    resid[...] = tokens[...].astype(F32) + branch
     normed[...] = (resid[...] * norm_scale(resid[...]) * gain[...]).astype(BF16)
     values = normed[...]
     for at in range(0, gate.shape[1], 256):
@@ -227,14 +251,16 @@
         up_back[:, columns] = (back * swish).astype(BF16)
         slope = sigmoid_gate * (1.0 + gate_act * (1.0 - sigmoid_gate))
         gate_back[:, columns] = (back * up_act * slope).astype(BF16)
-    part[...] = (dot_rows(gate_back[...], gate[...]) + dot_rows(up_back[...], up[...])).astype(BF16)
     away = pl.ds(pl.multiple_of((1 - scalars[3]) * WIDE_COLUMNS, 128), WIDE_COLUMNS)
     for k, value in enumerate((hidden, gate_back, up_back)):
         shared[:, k * WIDE_COLUMNS : (k + 1) * WIDE_COLUMNS] = value[:, away]
-    width, at = normed.shape[1], 3 * WIDE_COLUMNS
-    shared[:, at : at + width] = values
-    shared[:, at + width : at + 2 * width] = normed_one[...]
-    shared[:, at + 2 * width :] = away_half(ymix[...], scalars[3])
+    shared[:, 3 * WIDE_COLUMNS :] = values
+    shared_early[:, : normed.shape[1]] = normed_one[...]
+    shared_early[:, normed.shape[1] :] = away_half(ymix[...], scalars[3])
+
+
+def part_kernel(scalars, gate_back, up_back, gate, up, part):
+    part[...] = (dot_rows(gate_back[...], gate[...]) + dot_rows(up_back[...], up[...])).astype(BF16)
 
 
 def second_norm(part, other, resid, gain, cot):
@@ -290,6 +316,7 @@
     backs,
     shared,
     part,
+    gain_part,
     small,
 ):
     rows = gated_back.shape[0]
@@ -309,12 +336,13 @@
     gain_grad = jnp.sum(grad * values * norm_scale(values), axis=0, keepdims=True)
     for at in range(8):
         lanes = slice(at * 128, at * 128 + 128)
-        small[at : at + 1] = gain_grad[:, lanes]
+        gain_part[at : at + 1] = gain_grad[:, lanes]
         small[8 + at : 9 + at] = gain_two_grad[:, lanes]
     for lag in range(3):
         for at in range(4):
             row = 16 + 4 * lag + at
             small[row : row + 1] = tap_grads[lag : lag + 1, at * 128 : at * 128 + 128]
+    small[:8] = jnp.zeros((8, 128), F32)
     small[28:32] = jnp.zeros((4, 128), F32)
 
 
@@ -354,7 +382,7 @@
     own, shared, sends, keeps = refs[:3], refs[3], refs[4:6], refs[6:8]
     left_two, left_cot = refs[8:]
     fill_transposed(left_cot, cot, cot_other)
-    fill_transposed(left_two, two, shared.at[:, 3 * WIDE_COLUMNS : 3 * WIDE_COLUMNS + two.shape[1]])
+    fill_transposed(left_two, two, shared.at[:, 3 * WIDE_COLUMNS :])
     at, core = scalars[0], scalars[3]
     for kind in range(2):
         first, second = peer(at, kind), peer(at, 1 - kind)
@@ -375,8 +403,7 @@
 
 def narrow_kernel(scalars, one, shared, low, late_other, backs, ymix, out, left_one, left_low):
     width = one.shape[1]
-    first = 3 * WIDE_COLUMNS + width
-    one_other, ymix_other = shared.at[:, first : first + width], shared.at[:, first + width :]
+    one_other, ymix_other = shared.at[:, :width], shared.at[:, width:]
     for at in range(0, width, 256):
         left_one[at : at + 256, :256] = one[:, at : at + 256].T
         left_one[at : at + 256, 256:] = one_other[:, at : at + 256].T
@@ -417,11 +444,14 @@
 
 
 def first_kernel(scalars, *refs):
-    gots, keeps, (narrow, small), sends, wide_keeps = refs[:2], refs[2:4], refs[4:6], refs[6:9], refs[9:]
+    gots, keeps, (narrow, small, gain, gain_other) = refs[:2], refs[2:4], refs[4:8]
+    sends, wide_keeps, new_small = refs[8:11], refs[11:13], refs[13]
+    new_small[:8] = gain[...] + gain_other[...]
+    new_small[8:] = small[8:]
     for pairing in range(3):
         base = WIDE_BLOCKS[pairing]
         sends[pairing][base : base + 4 * NARROW] = narrow[pairing]
-        split_small(small[...], sends[pairing], base + 4 * NARROW)
+        split_small(new_small[...], sends[pairing], base + 4 * NARROW)
     for kind in range(2):
         half = 4 * WIDE[kind]
         for chunk in range(4):
@@ -455,7 +485,7 @@
 
 
 def third_kernel(scalars, *refs):
-    gots, (kept, small), (send, keep, gain_sum) = refs[:3], refs[3:5], refs[5:]
+    gots, (kept, small), (send, keep) = refs[:3], refs[3:5], refs[5:]
     here = scalars[2]
     for first in range(0, TILES, 7):
         at = slice(first, first + 7)
@@ -470,25 +500,20 @@
     low = (value - high.astype(F32)).astype(BF16)
     send[TILES] = high
     send[TILES + 1] = low
-    gain_sum[...] = high[:8].astype(F32) + low[:8].astype(F32)
     keep[TILES] = high.astype(F32)
     keep[TILES + 1] = low.astype(F32)
 
 
-def cores_kernel(scalars, keep, across, skew, got, mine, away):
+def cores_kernel(scalars, keep, got, mine, away):
     core = scalars[3]
     total = keep[:TILES] + got[:TILES].astype(F32)
     zero, one = total[:, :16], total[:, 16:]
     mine[:TILES] = jnp.where(core == 0, zero, one)
     away[:TILES] = jnp.where(core == 0, one, zero)
-    here = keep[TILES] + keep[TILES + 1]
-    there = got[TILES].astype(F32) + got[TILES + 1].astype(F32)
-    both = here + there
-    gain = (here[:8] + across[...]) + (there[:8] + skew[...])
+    small = (keep[TILES] + keep[TILES + 1]) + (got[TILES].astype(F32) + got[TILES + 1].astype(F32))
     for target in (mine, away):
-        target[TILES, :8] = gain
-        target[TILES, 8:] = both[8:16]
-        target[TILES + 1] = both[16:]
+        target[TILES] = small[:16]
+        target[TILES + 1] = small[16:]
 
 
 def outputs_kernel(scalars, mine, got, down, gate, up, inner, out, gain_one, gain_two, taps):
@@ -543,6 +568,7 @@
     y, z = at // 16, (at // 4) % 4
     scalars = jnp.stack(
         [jnp.where(core == 0, y, z), jnp.where(core == 0, z, y), (at // 2) % 2, core, starts[0]]
+        + [lax.axis_index("tensor")]
     ).astype(jnp.int32)
     run = functools.partial(call, scalars=scalars)
     rows, width = tokens.shape
@@ -553,6 +579,8 @@
     def share(value):
         return swap(value, CORES)
 
+    half = channels // 2
+    weight_got = swap(jnp.where(core == 0, out_weight[:half], out_weight[half:]), NEAREST)
     tail = run(
         tail_kernel,
         operands=[tokens, gain_one_row, in_parts],
@@ -564,6 +592,7 @@
             pltpu.VMEM((width, channels), BF16),
             pltpu.SemaphoreType.DMA((4,)),
         ],
+        room=60,
         where=pltpu.HBM,
     )[0]
     incoming = from_behind(tail, "seq", 1)
@@ -573,18 +602,22 @@
         project_kernel,
         operands=[tokens, gain_one_row, in_parts],
         outs=[like((rows, width), BF16), like((3, rows, channels), F32), like((rows, channels), BF16)],
-    )
-    conv, ymix, branch = run(
+        scratch=[
+            pltpu.VMEM((rows, width), BF16),
+            pltpu.VMEM((1, width), F32),
+            pltpu.VMEM((3, width, channels), BF16),
+            pltpu.SemaphoreType.DMA((5,)),
+        ],
+        room=50,
+        where=pltpu.HBM,
+    )
+    conv, ymix = run(
         mix_kernel,
-        operands=[gated, incoming, parts, conv_weight, out_weight],
-        outs=[
-            like((rows, channels), F32),
-            like((rows, channels), BF16),
-            like((rows, width), BF16),
-        ],
-    )
-    branch, cotangent_late = lax.optimization_barrier((branch, cotangent))
-    branch_other = swap(branch, ACROSS)
+        operands=[gated, incoming, parts, conv_weight],
+        outs=[like((rows, channels), F32), like((rows, channels), BF16)],
+    )
+    ymix, cotangent_late = lax.optimization_barrier((ymix, cotangent))
+    ymix_other = swap(ymix, ACROSS)
     units = gate_weight.shape[1]
     hidden_grad = run(
         hidden_kernel,
@@ -592,17 +625,23 @@
         outs=[like((rows, units), F32)],
         flops=LONG,
     )[0]
-    branch_other, hidden_grad = lax.optimization_barrier((branch_other, hidden_grad))
-    resid, normed_two, hidden, gate_back, up_back, norm_two_part, late_shared = run(
+    whole_weight = run(
+        whole_kernel, operands=[out_weight, weight_got, share(weight_got)], outs=[like((2 * channels, width), BF16)]
+    )[0]
+    ymix_other, hidden_grad, whole_weight = lax.optimization_barrier((ymix_other, hidden_grad, whole_weight))
+    resid, normed_two, hidden, gate_back, up_back, shared, shared_early = run(
         feed_kernel,
-        operands=[tokens, branch, branch_other, gain_two_row, gate_weight, up_weight, hidden_grad]
-        + [normed_one, ymix],
+        operands=[tokens, ymix, ymix_other, whole_weight, gain_two_row, gate_weight, up_weight, hidden_grad]
+        + [normed_one],
         outs=[like((rows, width), F32), like((rows, width), BF16)]
         + [like((rows, units), BF16)] * 3
-        + [like((rows, width), BF16), like((rows, 3 * WIDE_COLUMNS + 2 * width + channels // 2), BF16)],
-    )
+        + [like((rows, 3 * WIDE_COLUMNS + width), BF16), like((rows, width + channels // 2), BF16)],
+    )
+    shared_other = share(shared)
+    norm_two_part = run(
+        part_kernel, operands=[gate_back, up_back, gate_weight, up_weight], outs=[like((rows, width), BF16)]
+    )[0]
     norm_two_other = swap(norm_two_part, ACROSS)
-    shared_other = share(late_shared)
     results = run(
         wide_kernel,
         operands=[normed_two, cotangent, cotangent_other, hidden, gate_back, up_back, shared_other],
@@ -613,7 +652,6 @@
     down_part = run(down_kernel, operands=[hidden, down_weight], outs=[like((rows, width), BF16)])[0]
     norm_two_other, keeps[1], down_part = lax.optimization_barrier((norm_two_other, keeps[1], down_part))
     gots = swap_round(sends, FIRST)
-    down_other = swap(down_part, ACROSS)
 
     edge_operands = [norm_two_part, norm_two_other, resid, gain_two_row, cotangent, out_weight, parts, conv_weight]
     edge = run(edge_kernel, operands=edge_operands, outs=[like((8, channels), F32)])[0]
@@ -631,7 +669,7 @@
         ],
         flops=SHORT,
     )
-    backs, shared, norm_one_part, small = run(
+    backs, shared, norm_one_part, gain_part, small = run(
         last_kernel,
         operands=[gated_back, returned, parts, c_back, in_parts, tokens, gain_two_grad, tap_grads]
         + [resid_low],
@@ -639,22 +677,24 @@
             like((3, rows, channels), BF16),
             like((7, rows, 256), BF16),
             like((rows, width), BF16),
+            like((8, 128), F32),
             like((32, 128), F32),
         ],
     )
     narrow = run(
         narrow_kernel,
-        operands=[normed_one, shared_other, resid_low, share(shared), backs, ymix],
+        operands=[normed_one, share(shared_early), resid_low, share(shared), backs, ymix],
         outs=[like((4, 4 * NARROW, *BLOCK), BF16)],
         scratch=[pltpu.VMEM((width, 2 * rows), BF16)] * 2,
     )[0]
-    gots[0], gots[1], narrow, down_other = lax.optimization_barrier((gots[0], gots[1], narrow, down_other))
+    gain_other = swap(gain_part, ACROSS)
+    gots[0], gots[1], narrow, gain_other = lax.optimization_barrier((gots[0], gots[1], narrow, gain_other))
     results = run(
         first_kernel,
-        operands=gots + keeps + [narrow, small],
-        outs=blocks(ROUND_ONE) + blocks([4 * count for count in WIDE]),
-    )
-    sends, keeps = list(results[:3]), list(results[3:])
+        operands=gots + keeps + [narrow, small, gain_part, gain_other],
+        outs=blocks(ROUND_ONE) + blocks([4 * count for count in WIDE]) + [like((32, 128), F32)],
+    )
+    sends, keeps, small = list(results[:3]), list(results[3:5]), results[5]
     gots = swap_round(sends, FIRST)
     norm_one_other = swap(norm_one_part, ACROSS)
     gots[0], norm_one_other = lax.optimization_barrier((gots[0], norm_one_other))
@@ -665,20 +705,23 @@
     )
     sends, keep, small = list(results[:3]), results[3], results[4]
     gots = swap_round(sends, SECOND)
-    beside, kept, gain_sum = run(
+    small, down_part = lax.optimization_barrier((small, down_part))
+    down_other = swap(down_part, ACROSS)
+    gots[0], down_other = lax.optimization_barrier((gots[0], down_other))
+    beside, kept = run(
         third_kernel,
         operands=gots + [keep, small],
-        outs=[like((TILES + 2, 32, 128), BF16), like((TILES + 2, 32, 128), F32), like((8, 128), F32)],
-    )
-    gots = [swap(gain_sum, ACROSS), swap(gain_sum, SKEW), swap(beside, BESIDE)]
+        outs=[like((TILES + 2, 32, 128), BF16), like((TILES + 2, 32, 128), F32)],
+    )
+    beside = swap(beside, BESIDE)
     mixed = (resid + (down_part.astype(F32) + down_other.astype(F32))).astype(BF16)
     inputs = tokens.astype(F32)
     norm_one_back = norm_one_part.astype(F32) + norm_one_other.astype(F32)
     tokens_grad = resid_grad + norm_backward(norm_one_back, inputs, norm_scale(inputs), gain_one)
-    gots[0], mixed, tokens_grad = lax.optimization_barrier((gots[0], mixed, tokens_grad))
+    beside, mixed, tokens_grad = lax.optimization_barrier((beside, mixed, tokens_grad))
     mine, away = run(
         cores_kernel,
-        operands=[kept] + gots,
+        operands=[kept, beside],
         outs=[like((TILES + 2, 16, 128), F32)] * 2,
     )
     down_g, gate_g, up_g, in_g, out_g, gain_one_g, gain_two_g, conv_g = run(

time: 142 us -> 129 us (0.908)
  waiting for transfers between devices: 60.5 us -> 47.4 us
  Pallas kernels: 32.7 us -> 38.7 us
  starting transfers between devices: 40.5 us -> 36.3 us
  local copies, waits for them, and re-layouts: 3.77 us -> 0.67 us
    ppermute x19 -> x21, waiting for transfers between devices: 59.5 us -> 47 us  [swap(): return lax.ppermute(value, AXES, pairs)]
    pallas_call x16 -> x18, Pallas kernels: 32.7 us -> 38.7 us  [call(): pl.pallas_call(body, out_shape=tuple(outs), in_specs=[pl.BlockSpec(memory...]
    ppermute x19 -> x21, starting transfers between devices: 35.2 us -> 31.5 us  [swap(): return lax.ppermute(value, AXES, pairs)]
    unnamed x30 -> x26, local copies, waits for them, and re-layouts: 3.69 us -> 0.07 us
  transfers between devices with their start and end apart: 21 -> 23, of which waited for: 13 -> 12; matrix products, arithmetic and copies ran while one was open for 2% -> 4% of each run, Pallas kernels for 14% -> 22%
where the time goes in v4:
time: 129 us
  waiting for transfers between devices  47.4 us (37%)
  Pallas kernels  38.7 us (30%)
  starting transfers between devices  36.3 us (28%)
  other arithmetic  4.07 us (3%)
  between operations  1.65 us (1%)
    ppermute x21, waiting for transfers between devices, swap(): return lax.ppermute(value, AXES, pairs)  47 us
    pallas_call x18, Pallas kernels, call(): pl.pallas_call(body, out_shape=tuple(outs), in_specs=[pl.BlockSpec(memory...  38.7 us
    ppermute x21, starting transfers between devices, swap(): return lax.ppermute(value, AXES, pairs)  31.5 us
    ppermute x2, starting transfers between devices, from_behind(): lax.ppermute(value, axis, [(source, source + steps) for source in range(l...  4.76 us
  transfers between devices with their start and end apart: 23, of which 12 were waited for; matrix products, arithmetic and copies ran while one was open for 4% of the time, Pallas kernels for 22%

profile of v4, /device:TPU:1, one launch (start us, length us, event | category | flops | bytes accessed | tf_op | source)
XLA Modules:
  0.0 128.8 jit_solution(8039116696777183779)
XLA Ops:
  3.4 2.6 %collective-permute-start.3 = (bf16[256,1024]{1,0:T(8,128)(2,1)S(1)}, bf16[256,1024]{1,0:T(8,128)(2,1)S(1)}, u32[]{:S(2)}, u32[]{:S(2)}) collective-permute-start(bf16[256,1024]{1,0:T(8,128)(2,1)S(1)} %slice_select_fusion), channel_id=1, source_target_pairs={{0,5},{2,7},{4,1},{6,3},{1,4},{3,6},{5,0},{7,2},{8,13},{10,15},{12... | collective-permute-start | bytes 1572872 | tf_op jit(solution)/shard_map/ppermute | solution.py:75
  7.3 3.5 %shard_map.187 = bf16[16,512]{1,0:T(8,128)(2,1)} custom-call(s32[6]{0:T(128)} %stack.23.scalars, bf16[256,1024]{1,0:T(8,128)(2,1)} %tokens.7, f32[1,1024]{1,0:T(1,128)} %bitcast.20, bf16[3,1024,512]{2,1,0:T(8,128)(2,1)} %bitcast.13), custom_call_target="tpu_custom_call" | custom-call | tf_op jit(solution)/shard_map/pallas_call | solution.py:100
  10.8 2.1 %collective-permute-start = (bf16[16,512]{1,0:T(8,128)(2,1)}, bf16[16,512]{1,0:T(8,128)(2,1)S(1)}, u32[]{:S(2)}, u32[]{:S(2)}) collective-permute-start(bf16[16,512]{1,0:T(8,128)(2,1)} %shard_map.187), channel_id=1, source_target_pairs={{0,2},{2,4},{4,6},{6,8},{8,10},{10,12},{12,14},{14,16},{16,18},{18... | collective-permute-start | bytes 49160 | tf_op jit(solution)/shard_map/ppermute | solution.py:81
  12.9 3.5 %shard_map.186 = (bf16[256,1024]{1,0:T(8,128)(2,1)S(1)}, f32[3,256,512]{2,1,0:T(8,128)S(1)}, bf16[256,512]{1,0:T(8,128)(2,1)S(1)}) custom-call(s32[6]{0:T(128)S(1)} %copy-done.5, bf16[256,1024]{1,0:T(8,128)(2,1)S(1)} %copy-done.1, f32[1,1024]{1,0:T(1,128)S(1)} %bitcast.21, bf16[3,1024,512]{2,1,0:T(8,128)(2,1)} %bitcast.14), custom_call_target="tpu_custom_call" | custom-call | tf_op jit(solution)/shard_map/pallas_call | solution.py:100
  19.0 2.0 %shard_map.189.hidden_grad = f32[256,2304]{1,0:T(8,128)S(1)} custom-call(s32[6]{0:T(128)S(1)} %copy-done.5, bf16[256,1024]{1,0:T(8,128)(2,1)S(1)} %copy-done.4, bf16[2304,1024]{1,0:T(8,128)(2,1)S(1)} %copy-done.3), custom_call_target="tpu_custom_call" | custom-call | flops 30000001024 | tf_op jit(solution)/shard_map/pallas_call | solution.py:100
  21.9 4.6 %collective-permute-done.2.ymix_other = bf16[256,512]{1,0:T(8,128)(2,1)S(1)} collective-permute-done((bf16[256,512]{1,0:T(8,128)(2,1)S(1)}, bf16[256,512]{1,0:T(8,128)(2,1)S(1)}, u32[]{:S(2)}, u32[]{:S(2)}) %collective-permute-start.2) | collective-permute-done | bytes 262176 | tf_op jit(solution)/shard_map/ppermute | solution.py:75
  26.5 4.4 %shard_map.191 = (f32[256,1024]{1,0:T(8,128)S(1)}, bf16[256,1024]{1,0:T(8,128)(2,1)S(1)}, bf16[256,2304]{1,0:T(8,128)(2,1)S(1)}, bf16[256,2304]{1,0:T(8,128)(2,1...) custom-call(s32[6]{0:T(128)S(1)} %copy-done.5, ...), custom_call_target="tpu_custom_call" | custom-call | tf_op jit(solution)/shard_map/pallas_call | solution.py:100
  32.2 3.2 %shard_map.193.part = bf16[256,1024]{1,0:T(8,128)(2,1)S(1)} custom-call(s32[6]{0:T(128)S(1)} %copy-done.5, bf16[256,2304]{1,0:T(8,128)(2,1)S(1)} %get-tuple-element.96.refs_1_.gate_back, bf16[256,2304]{1,0:T(8,128)(2,1)S(1)} %get-tuple-element.97.refs_2_.up_back, bf16[1024,2304]{1,0:T(8,128)(2,1)S(1)} %bitcast.17, bf16[1024,2304]{1,0:T(8,128)(2,1)S(1)} %bitcast.19), custom_call_target="tpu_custom_call" | custom-call | tf_op jit(solution)/shard_map/pallas_call | solution.py:100
  36.9 5.3 %shard_map.192 = (bf16[112,64,128]{2,1,0:T(8,128)(2,1)S(1)}, bf16[104,64,128]{2,1,0:T(8,128)(2,1)S(1)}, bf16[112,64,128]{2,1,0:T(8,128)(2,1)S(1)}, bf16[104,64,128]{2,1,0:T(8,128)(2,1)S(1)}) custom-call(s32[6]{0:T(128)S(1)} %copy-done.5, bf16[256,1024]{1,0:T(8,128)(2,1)S(1)} %get-tuple-element.93.two, bf16[256,1024]{1,0:T(8,128)(2,1)S(1)} %copy-done.4, ...), custom_call_target="tpu_custom_call" | custom-call | tf_op jit(solution)/shard_map/pallas_call | solution.py:100
  44.1 2.3 %collective-permute-start.7 = (bf16[104,64,128]{2,1,0:T(8,128)(2,1)S(1)}, bf16[104,64,128]{2,1,0:T(8,128)(2,1)S(1)}, u32[]{:S(2)}, u32[]{:S(2)}) collective-permute-start(bf16[104,64,128]{2,1,0:T(8,128)(2,1)S(1)} %get-tuple-element.100), channel_id=1, source_target_pairs={{0,96},{2,26},{4,100},{6,30},{1,97},{3,27},{5,101},{7,31},{8,104},... | collective-permute-start | bytes 5111816 | tf_op jit(solution)/shard_map/ppermute | solution.py:75
  46.4 2.0 %shard_map.194 = bf16[256,1024]{1,0:T(8,128)(2,1)S(1)} custom-call(s32[6]{0:T(128)S(1)} %copy-done.5, bf16[256,2304]{1,0:T(8,128)(2,1)S(1)} %get-tuple-element.95.refs_0_.hidden, bf16[2304,1024]{1,0:T(8,128)(2,1)S(1)} %copy-done.3), custom_call_target="tpu_custom_call" | custom-call | tf_op jit(solution)/shard_map/pallas_call | solution.py:100
  48.3 2.3 %collective-permute-done.9.other = bf16[256,1024]{1,0:T(8,128)(2,1)S(1)} collective-permute-done((bf16[256,1024]{1,0:T(8,128)(2,1)S(1)}, bf16[256,1024]{1,0:T(8,128)(2,1)S(1)}, u32[]{:S(2)}, u32[]{:S(2)}) %collective-permute-start.9) | collective-permute-done | bytes 524320 | tf_op jit(solution)/shard_map/ppermute | solution.py:75
  51.6 2.7 %collective-permute-start.10 = (f32[8,512]{1,0:T(8,128)S(1)}, f32[8,512]{1,0:T(8,128)S(1)}, u32[]{:S(2)}, u32[]{:S(2)}) collective-permute-start(f32[8,512]{1,0:T(8,128)S(1)} %shard_map.196), channel_id=1, source_target_pairs={{2,0},{4,2},{6,4},{8,6},{10,8},{12,10},{14,12},{16,14},{18,16},{20... | collective-permute-start | bytes 49160 | tf_op jit(solution)/shard_map/ppermute | solution.py:81
  54.3 2.2 %shard_map.195 = (f32[256,1024]{1,0:T(8,128)S(1)}, bf16[256,1024]{1,0:T(8,128)(2,1)S(1)}, f32[1,1024]{1,0:T(1,128)S(1)}, bf16[256,512]{1,0:T(8,128)(2,1)S(1)}, f...) custom-call(s32[6]{0:T(128)S(1)} %copy-done.5, bf16[256,1024]{1,0:T(8,128)(2,1)S(1)} %shard_map.193.part, ...), custom_call_target="tpu_custom_call" | custom-call | flops 8000000000 | tf_op jit(solution)/shard_map/pallas_call | solution.py:100
  62.1 2.3 %shard_map.198.refs_4_.refs_5_ = bf16[4,32,64,128]{3,2,1,0:T(8,128)(2,1)S(1)} custom-call(s32[6]{0:T(128)S(1)} %copy-done.5, bf16[256,1024]{1,0:T(8,128)(2,1)S(1)} %get-tuple-element.92.normed_one.one, bf16[256,1280]{1,0:T(8,128)(2,1)S(1)} %collective-permute-done.8.shared, bf16[256,1024]{1,0:T(8,128)(2,1)S(1)} %get-tuple-element.106.resid_low.low, ...), custom_call_target="tpu_custom_call" | custom-call | tf_op jit(solution)/shard_map/pallas_call | solution.py:100
  66.3 2.1 %shard_map.199 = (bf16[85,64,128]{2,1,0:T(8,128)(2,1)S(1)}, bf16[89,64,128]{2,1,0:T(8,128)(2,1)S(1)}, bf16[33,64,128]{2,1,0:T(8,128)(2,1)S(1)}, bf16[56,64,128]{...) custom-call(s32[6]{0:T(128)S(1)} %copy-done.5, ...), custom_call_target="tpu_custom_call" | custom-call | tf_op jit(solution)/shard_map/pallas_call | solution.py:100
  68.4 2.6 %collective-permute-start.15 = (bf16[89,64,128]{2,1,0:T(8,128)(2,1)S(1)}, bf16[89,64,128]{2,1,0:T(8,128)(2,1)S(1)}, u32[]{:S(2)}, u32[]{:S(2)}) collective-permute-start(bf16[89,64,128]{2,1,0:T(8,128)(2,1)S(1)} %get-tuple-element.124), channel_id=1, source_target_pairs={{0,96},{2,26},{4,100},{6,30},{1,97},{3,27},{5,101},{7,31},{8,104},... | collective-permute-start | bytes 4374536 | tf_op jit(solution)/shard_map/ppermute | solution.py:75
  74.1 11.0 %collective-permute-done.14 = bf16[256,1024]{1,0:T(8,128)(2,1)S(1)} collective-permute-done((bf16[256,1024]{1,0:T(8,128)(2,1)S(1)}, bf16[256,1024]{1,0:T(8,128)(2,1)S(1)}, u32[]{:S(2)}, u32[]{:S(2)}) %collective-permute-start.14) | collective-permute-done | bytes 524320 | tf_op jit(solution)/shard_map/ppermute | solution.py:75
  85.1 3.5 %collective-permute-done.13.refs_0_ = bf16[85,64,128]{2,1,0:T(8,128)(2,1)S(1)} collective-permute-done((bf16[85,64,128]{2,1,0:T(8,128)(2,1)S(1)}, bf16[85,64,128]{2,1,0:T(8,128)(2,1)S(1)}, u32[]{:S(2)}, u32[]{:S(2)}) %collective-permute-start.13) | collective-permute-done | bytes 1392672 | tf_op jit(solution)/shard_map/ppermute | solution.py:75
  88.6 5.9 %collective-permute-done.16.refs_2_ = bf16[33,64,128]{2,1,0:T(8,128)(2,1)S(1)} collective-permute-done((bf16[33,64,128]{2,1,0:T(8,128)(2,1)S(1)}, bf16[33,64,128]{2,1,0:T(8,128)(2,1)S(1)}, u32[]{:S(2)}, u32[]{:S(2)}) %collective-permute-start.16) | collective-permute-done | bytes 540704 | tf_op jit(solution)/shard_map/ppermute | solution.py:75
  97.5 2.4 %collective-permute-start.19 = (bf16[36,64,128]{2,1,0:T(8,128)(2,1)S(1)}, bf16[36,64,128]{2,1,0:T(8,128)(2,1)S(1)}, u32[]{:S(2)}, u32[]{:S(2)}) collective-permute-start(bf16[36,64,128]{2,1,0:T(8,128)(2,1)S(1)} %get-tuple-element.134), channel_id=1, source_target_pairs={{0,24},{2,98},{4,28},{6,102},{1,25},{3,99},{5,29},{7,103},{8,16},{... | collective-permute-start | bytes 1769480 | tf_op jit(solution)/shard_map/ppermute | solution.py:75
  102.3 11.2 %collective-permute-done.18 = bf16[256,1024]{1,0:T(8,128)(2,1)S(1)} collective-permute-done((bf16[256,1024]{1,0:T(8,128)(2,1)S(1)}, bf16[256,1024]{1,0:T(8,128)(2,1)S(1)}, u32[]{:S(2)}, u32[]{:S(2)}) %collective-permute-start.18) | collective-permute-done | bytes 524320 | tf_op jit(solution)/shard_map/ppermute | solution.py:75
  119.2 2.3 %collective-permute-done.21.got = bf16[37,32,128]{2,1,0:T(8,128)(2,1)S(1)} collective-permute-done((bf16[37,32,128]{2,1,0:T(8,128)(2,1)S(1)}, bf16[37,32,128]{2,1,0:T(8,128)(2,1)S(1)}, u32[]{:S(2)}, u32[]{:S(2)}) %collective-permute-start.21) | collective-permute-done | bytes 303136 | tf_op jit(solution)/shard_map/ppermute | solution.py:75
  122.2 4.0 %collective-permute-start.22 = (f32[37,16,128]{2,1,0:T(8,128)S(1)}, f32[37,16,128]{2,1,0:T(8,128)S(1)}, u32[]{:S(2)}, u32[]{:S(2)}) collective-permute-start(f32[37,16,128]{2,1,0:T(8,128)S(1)} %get-tuple-element.147), channel_id=1, source_target_pairs={{0,2},{2,0},{4,6},{6,4},{1,3},{3,1},{5,7},{7,5},{8,10},{10,8},{12,... | collective-permute-start | bytes 909320 | tf_op jit(solution)/shard_map/ppermute | solution.py:75
  (74 shorter events, 37.2 us)
Async XLA Ops:
  0.6 15.7 %collective-permute-start.1 = (bf16[256,1024]{1,0:T(8,128)(2,1)}, bf16[256,1024]{1,0:T(8,128)(2,1)S(1)}, u32[]{:S(2)}, u32[]{:S(2)}) collective-permute-start(bf16[256,1024]{1,0:T(8,128)(2,1)} %cot.6), channel_id=1, source_target_pairs={{0,2},{2,0},{4,6},{6,4},{1,3},{3,1},{5,7},{7,5},{8,10},{10,8},{12,... | collective-permute-start | bytes 1572872 | tf_op jit(solution)/shard_map/ppermute | solution.py:75
  3.4 15.4 %collective-permute-start.3 = (bf16[256,1024]{1,0:T(8,128)(2,1)S(1)}, bf16[256,1024]{1,0:T(8,128)(2,1)S(1)}, u32[]{:S(2)}, u32[]{:S(2)}) collective-permute-start(bf16[256,1024]{1,0:T(8,128)(2,1)S(1)} %slice_select_fusion), channel_id=1, source_target_pairs={{0,5},{2,7},{4,1},{6,3},{1,4},{3,6},{5,0},{7,2},{8,13},{10,15},{12... | collective-permute-start | bytes 1572872 | tf_op jit(solution)/shard_map/ppermute | solution.py:75
  10.8 5.6 %collective-permute-start = (bf16[16,512]{1,0:T(8,128)(2,1)}, bf16[16,512]{1,0:T(8,128)(2,1)S(1)}, u32[]{:S(2)}, u32[]{:S(2)}) collective-permute-start(bf16[16,512]{1,0:T(8,128)(2,1)} %shard_map.187), channel_id=1, source_target_pairs={{0,2},{2,4},{4,6},{6,8},{8,10},{10,12},{12,14},{14,16},{16,18},{18... | collective-permute-start | bytes 49160 | tf_op jit(solution)/shard_map/ppermute | solution.py:81
  17.3 9.2 %slice-start = ((s8[4718592]{0:T(1024)(128)(4,1)}), s8[4194304]{0:T(1024)(128)(4,1)S(1)}, s32[]{:S(2)}) async-start(s8[4718592]{0:T(1024)(128)(4,1)} %bitcast.16), calls=%async_computation | async-start | bytes 8388608
  17.3 9.1 %collective-permute-start.2 = (bf16[256,512]{1,0:T(8,128)(2,1)S(1)}, bf16[256,512]{1,0:T(8,128)(2,1)S(1)}, u32[]{:S(2)}, u32[]{:S(2)}) collective-permute-start(bf16[256,512]{1,0:T(8,128)(2,1)S(1)} %get-tuple-element.87.ymix), channel_id=1, source_target_pairs={{0,1},{2,3},{4,5},{6,7},{1,0},{3,2},{5,4},{7,6},{8,9},{10,11},{12,... | collective-permute-start | bytes 786440 | tf_op jit(solution)/shard_map/ppermute | solution.py:75
  18.8 2.3 %collective-permute-start.4 = (bf16[256,1024]{1,0:T(8,128)(2,1)S(1)}, bf16[256,1024]{1,0:T(8,128)(2,1)S(1)}, u32[]{:S(2)}, u32[]{:S(2)}) collective-permute-start(bf16[256,1024]{1,0:T(8,128)(2,1)S(1)} %collective-permute-done.3.got), channel_id=1, source_target_pairs={{0,2},{2,0},{4,6},{6,4},{1,3},{3,1},{5,7},{7,5},{8,10},{10,8},{12,... | collective-permute-start | bytes 1572872 | tf_op jit(solution)/shard_map/ppermute | solution.py:75
  30.9 6.0 %collective-permute-start.5 = (bf16[256,4480]{1,0:T(8,128)(2,1)S(1)}, bf16[256,4480]{1,0:T(8,128)(2,1)S(1)}, u32[]{:S(2)}, u32[]{:S(2)}) collective-permute-start(bf16[256,4480]{1,0:T(8,128)(2,1)S(1)} %get-tuple-element.98), channel_id=1, source_target_pairs={{0,2},{2,0},{4,6},{6,4},{1,3},{3,1},{5,7},{7,5},{8,10},{10,8},{12,... | collective-permute-start | bytes 6881288 | tf_op jit(solution)/shard_map/ppermute | solution.py:75
  35.3 15.3 %collective-permute-start.9 = (bf16[256,1024]{1,0:T(8,128)(2,1)S(1)}, bf16[256,1024]{1,0:T(8,128)(2,1)S(1)}, u32[]{:S(2)}, u32[]{:S(2)}) collective-permute-start(bf16[256,1024]{1,0:T(8,128)(2,1)S(1)} %shard_map.193.part), channel_id=1, source_target_pairs={{0,1},{2,3},{4,5},{6,7},{1,0},{3,2},{5,4},{7,6},{8,9},{10,11},{12,... | collective-permute-start | bytes 1572872 | tf_op jit(solution)/shard_map/ppermute | solution.py:75
  42.3 24.0 %collective-permute-start.6 = (bf16[112,64,128]{2,1,0:T(8,128)(2,1)S(1)}, bf16[112,64,128]{2,1,0:T(8,128)(2,1)S(1)}, u32[]{:S(2)}, u32[]{:S(2)}) collective-permute-start(bf16[112,64,128]{2,1,0:T(8,128)(2,1)S(1)} %get-tuple-element.99), channel_id=1, source_target_pairs={{0,32},{2,10},{4,36},{6,14},{1,33},{3,11},{5,37},{7,15},{8,40},{10... | collective-permute-start | bytes 5505032 | tf_op jit(solution)/shard_map/ppermute | solution.py:75
  44.1 22.2 %collective-permute-start.7 = (bf16[104,64,128]{2,1,0:T(8,128)(2,1)S(1)}, bf16[104,64,128]{2,1,0:T(8,128)(2,1)S(1)}, u32[]{:S(2)}, u32[]{:S(2)}) collective-permute-start(bf16[104,64,128]{2,1,0:T(8,128)(2,1)S(1)} %get-tuple-element.100), channel_id=1, source_target_pairs={{0,96},{2,26},{4,100},{6,30},{1,97},{3,27},{5,101},{7,31},{8,104},... | collective-permute-start | bytes 5111816 | tf_op jit(solution)/shard_map/ppermute | solution.py:75
  51.6 5.4 %collective-permute-start.10 = (f32[8,512]{1,0:T(8,128)S(1)}, f32[8,512]{1,0:T(8,128)S(1)}, u32[]{:S(2)}, u32[]{:S(2)}) collective-permute-start(f32[8,512]{1,0:T(8,128)S(1)} %shard_map.196), channel_id=1, source_target_pairs={{2,0},{4,2},{6,4},{8,6},{10,8},{12,10},{14,12},{16,14},{18,16},{20... | collective-permute-start | bytes 49160 | tf_op jit(solution)/shard_map/ppermute | solution.py:81
  58.6 3.5 %collective-permute-start.11 = (bf16[7,256,256]{2,1,0:T(8,128)(2,1)S(1)}, bf16[7,256,256]{2,1,0:T(8,128)(2,1)S(1)}, u32[]{:S(2)}, u32[]{:S(2)}) collective-permute-start(bf16[7,256,256]{2,1,0:T(8,128)(2,1)S(1)} %get-tuple-element.111), channel_id=1, source_target_pairs={{0,2},{2,0},{4,6},{6,4},{1,3},{3,1},{5,7},{7,5},{8,10},{10,8},{12,... | collective-permute-start | bytes 2752520 | tf_op jit(solution)/shard_map/ppermute | solution.py:75
  58.7 3.4 %collective-permute-start.8 = (bf16[256,1280]{1,0:T(8,128)(2,1)S(1)}, bf16[256,1280]{1,0:T(8,128)(2,1)S(1)}, u32[]{:S(2)}, u32[]{:S(2)}) collective-permute-start(bf16[256,1280]{1,0:T(8,128)(2,1)S(1)} %get-tuple-element.101), channel_id=1, source_target_pairs={{0,2},{2,0},{4,6},{6,4},{1,3},{3,1},{5,7},{7,5},{8,10},{10,8},{12,... | collective-permute-start | bytes 1966088 | tf_op jit(solution)/shard_map/ppermute | solution.py:75
  59.2 5.2 %collective-permute-start.12 = (f32[8,128]{1,0:T(8,128)S(1)}, f32[8,128]{1,0:T(8,128)S(1)}, u32[]{:S(2)}, u32[]{:S(2)}) collective-permute-start(f32[8,128]{1,0:T(8,128)S(1)} %get-tuple-element.113.refs_6_), channel_id=1, source_target_pairs={{0,1},{2,3},{4,5},{6,7},{1,0},{3,2},{5,4},{7,6},{8,9},{10,11},{12,... | collective-permute-start | bytes 12296 | tf_op jit(solution)/shard_map/ppermute | solution.py:75
  68.4 26.1 %collective-permute-start.15 = (bf16[89,64,128]{2,1,0:T(8,128)(2,1)S(1)}, bf16[89,64,128]{2,1,0:T(8,128)(2,1)S(1)}, u32[]{:S(2)}, u32[]{:S(2)}) collective-permute-start(bf16[89,64,128]{2,1,0:T(8,128)(2,1)S(1)} %get-tuple-element.124), channel_id=1, source_target_pairs={{0,96},{2,26},{4,100},{6,30},{1,97},{3,27},{5,101},{7,31},{8,104},... | collective-permute-start | bytes 4374536 | tf_op jit(solution)/shard_map/ppermute | solution.py:75
  71.0 17.6 %collective-permute-start.13 = (bf16[85,64,128]{2,1,0:T(8,128)(2,1)S(1)}, bf16[85,64,128]{2,1,0:T(8,128)(2,1)S(1)}, u32[]{:S(2)}, u32[]{:S(2)}) collective-permute-start(bf16[85,64,128]{2,1,0:T(8,128)(2,1)S(1)} %get-tuple-element.121), channel_id=1, source_target_pairs={{0,32},{2,10},{4,36},{6,14},{1,33},{3,11},{5,37},{7,15},{8,40},{10... | collective-permute-start | bytes 4177928 | tf_op jit(solution)/shard_map/ppermute | solution.py:75
  71.0 23.5 %collective-permute-start.16 = (bf16[33,64,128]{2,1,0:T(8,128)(2,1)S(1)}, bf16[33,64,128]{2,1,0:T(8,128)(2,1)S(1)}, u32[]{:S(2)}, u32[]{:S(2)}) collective-permute-start(bf16[33,64,128]{2,1,0:T(8,128)(2,1)S(1)} %get-tuple-element.125), channel_id=1, source_target_pairs={{0,64},{2,18},{4,68},{6,22},{1,65},{3,19},{5,69},{7,23},{8,72},{10... | collective-permute-start | bytes 1622024 | tf_op jit(solution)/shard_map/ppermute | solution.py:75
  72.5 12.6 %collective-permute-start.14 = (bf16[256,1024]{1,0:T(8,128)(2,1)S(1)}, bf16[256,1024]{1,0:T(8,128)(2,1)S(1)}, u32[]{:S(2)}, u32[]{:S(2)}) collective-permute-start(bf16[256,1024]{1,0:T(8,128)(2,1)S(1)} %get-tuple-element.122), channel_id=1, source_target_pairs={{0,1},{2,3},{4,5},{6,7},{1,0},{3,2},{5,4},{7,6},{8,9},{10,11},{12,... | collective-permute-start | bytes 1572872 | tf_op jit(solution)/shard_map/ppermute | solution.py:75
  95.7 17.8 %collective-permute-start.17 = (bf16[36,64,128]{2,1,0:T(8,128)(2,1)S(1)}, bf16[36,64,128]{2,1,0:T(8,128)(2,1)S(1)}, u32[]{:S(2)}, u32[]{:S(2)}) collective-permute-start(bf16[36,64,128]{2,1,0:T(8,128)(2,1)S(1)} %get-tuple-element.129), channel_id=1, source_target_pairs={{0,8},{2,34},{4,12},{6,38},{1,9},{3,35},{5,13},{7,39},{8,0},{10,42... | collective-permute-start | bytes 1769480 | tf_op jit(solution)/shard_map/ppermute | solution.py:75
  97.5 16.0 %collective-permute-start.19 = (bf16[36,64,128]{2,1,0:T(8,128)(2,1)S(1)}, bf16[36,64,128]{2,1,0:T(8,128)(2,1)S(1)}, u32[]{:S(2)}, u32[]{:S(2)}) collective-permute-start(bf16[36,64,128]{2,1,0:T(8,128)(2,1)S(1)} %get-tuple-element.134), channel_id=1, source_target_pairs={{0,24},{2,98},{4,28},{6,102},{1,25},{3,99},{5,29},{7,103},{8,16},{... | collective-permute-start | bytes 1769480 | tf_op jit(solution)/shard_map/ppermute | solution.py:75
  99.9 15.0 %collective-permute-start.20 = (bf16[36,64,128]{2,1,0:T(8,128)(2,1)S(1)}, bf16[36,64,128]{2,1,0:T(8,128)(2,1)S(1)}, u32[]{:S(2)}, u32[]{:S(2)}) collective-permute-start(bf16[36,64,128]{2,1,0:T(8,128)(2,1)S(1)} %get-tuple-element.135), channel_id=1, source_target_pairs={{0,16},{2,66},{4,20},{6,70},{1,17},{3,67},{5,21},{7,71},{8,24},{10... | collective-permute-start | bytes 1769480 | tf_op jit(solution)/shard_map/ppermute | solution.py:75
  101.0 12.5 %collective-permute-start.18 = (bf16[256,1024]{1,0:T(8,128)(2,1)S(1)}, bf16[256,1024]{1,0:T(8,128)(2,1)S(1)}, u32[]{:S(2)}, u32[]{:S(2)}) collective-permute-start(bf16[256,1024]{1,0:T(8,128)(2,1)S(1)} %shard_map.194), channel_id=1, source_target_pairs={{0,1},{2,3},{4,5},{6,7},{1,0},{3,2},{5,4},{7,6},{8,9},{10,11},{12,... | collective-permute-start | bytes 1572872 | tf_op jit(solution)/shard_map/ppermute | solution.py:75
  115.8 5.7 %collective-permute-start.21 = (bf16[37,32,128]{2,1,0:T(8,128)(2,1)S(1)}, bf16[37,32,128]{2,1,0:T(8,128)(2,1)S(1)}, u32[]{:S(2)}, u32[]{:S(2)}) collective-permute-start(bf16[37,32,128]{2,1,0:T(8,128)(2,1)S(1)} %get-tuple-element.138), channel_id=1, source_target_pairs={{0,4},{2,6},{4,0},{6,2},{1,5},{3,7},{5,1},{7,3},{8,12},{10,14},{12... | collective-permute-start | bytes 909320 | tf_op jit(solution)/shard_map/ppermute | solution.py:75
  122.2 5.2 %collective-permute-start.22 = (f32[37,16,128]{2,1,0:T(8,128)S(1)}, f32[37,16,128]{2,1,0:T(8,128)S(1)}, u32[]{:S(2)}, u32[]{:S(2)}) collective-permute-start(f32[37,16,128]{2,1,0:T(8,128)S(1)} %get-tuple-element.147), channel_id=1, source_target_pairs={{0,2},{2,0},{4,6},{6,4},{1,3},{3,1},{5,7},{7,5},{8,10},{10,8},{12,... | collective-permute-start | bytes 909320 | tf_op jit(solution)/shard_map/ppermute | solution.py:75
  (12 other events, 70.4 us)

commit v5 on v4

--- a/solution.py
+++ b/solution.py
@@ -95,17 +95,37 @@
     return jax.ShapeDtypeStruct(shape, dtype)
 
 
-def call(body, *, scalars, operands, outs, scratch=(), where=pltpu.VMEM, flops=0, room=16):
+def positions(offset):
+    at = lax.axis_index("seq")
+    y, z, core = at // 16, (at // 4) % 4, at % 2
+    first, second = jnp.where(core == 0, y, z), jnp.where(core == 0, z, y)
+    return first, second, (at // 2) % 2, core, offset, lax.axis_index("tensor")
+
+
+def call(body, *, operands, outs, scratch=(), offset=None, flops=0, aliases=None, where=pltpu.VMEM, scalar=None):
     whole = pl.BlockSpec(memory_space=pltpu.VMEM)
+    specs = [pl.BlockSpec(memory_space=where)] * len(operands)
+    if scalar is not None:
+        operands, specs = [scalar, *operands], [pl.BlockSpec(memory_space=pltpu.SMEM), *specs]
+
+    def kernel(*refs):
+        if offset is None:
+            body(positions(None), *refs)
+        else:
+            body(positions(refs[0][0:1, 0:1]), *refs[1:])
+
+    if offset is not None:
+        operands, specs = [offset, *operands], [whole, *specs]
     return pl.pallas_call(
-        body,
+        kernel,
         out_shape=tuple(outs),
-        in_specs=[pl.BlockSpec(memory_space=pltpu.SMEM)] + [pl.BlockSpec(memory_space=where)] * len(operands),
+        in_specs=specs,
         out_specs=tuple(whole for _ in outs),
         scratch_shapes=list(scratch),
-        compiler_params=pltpu.CompilerParams(vmem_limit_bytes=room * 2**20),
+        input_output_aliases=aliases or {},
+        compiler_params=pltpu.CompilerParams(vmem_limit_bytes=16 * 2**20),
         cost_estimate=pl.CostEstimate(flops=flops, bytes_accessed=0, transcendentals=0),
-    )(scalars, *operands)
+    )(*operands)
 
 
 def dot(left, right):
@@ -129,42 +149,42 @@
     return jnp.where((row_numbers(shape, first) < offset) & (offset < count), 0.0, 1.0)
 
 
-def tail_kernel(scalars, tokens, gain, weight, tail, token_rows, gain_row, b_weight, x_weight, done):
-    rows = tokens.shape[0]
-    copies = [
-        pltpu.make_async_copy(source, target, done.at[at])
-        for at, (source, target) in enumerate(
-            (
-                (tokens.at[pl.ds(rows - 16, 16)], token_rows),
-                (gain, gain_row),
-                (weight.at[0], b_weight),
-                (weight.at[2], x_weight),
-            )
-        )
-    ]
-    for copy in copies:
-        copy.start()
-    for copy in copies:
-        copy.wait()
-    values = token_rows[...].astype(F32)
-    normed = (values * norm_scale(values) * gain_row[...]).astype(BF16)
-    gated = (dot(normed, b_weight[...]) * dot(normed, x_weight[...])).astype(BF16).astype(F32)
-    tail[...] = (gated * linked_rows(scalars[4], gated.shape, rows - 16, rows)).astype(BF16)
-
-
-def project_kernel(scalars, tokens, gain, weight, normed, parts, gated, token_rows, gain_row, weights, done):
-    pieces = [(tokens, token_rows), (gain, gain_row)] + [(weight.at[k], weights.at[k]) for k in range(3)]
+def half_kernel(scalars, weight, half, done):
+    rows = half.shape[0]
+    copy = pltpu.make_async_copy(weight.at[pl.ds(pl.multiple_of(scalars[3] * rows, 16), rows)], half, done)
+    copy.start()
+    copy.wait()
+
+
+def load_kernel(scalars, starts, tokens, gain, weight, tail, token_rows, gain_row, weights, offset, done):
+    rows, depth = tokens.shape[0], weight.shape[1] // 4
+    pieces = [(gain, gain_row)]
+    pieces += [(tokens.at[pl.ds(at, 128)], token_rows.at[pl.ds(at, 128)]) for at in (rows - 128, 0)]
+    for k in (0, 2, 1):
+        for at in range(0, weight.shape[1], depth):
+            pieces.append((weight.at[k, pl.ds(at, depth)], weights.at[k, pl.ds(at, depth)]))
     copies = [
         pltpu.make_async_copy(source, target, done.at[at]) for at, (source, target) in enumerate(pieces)
     ]
     for copy in copies:
         copy.start()
-    copies[0].wait()
-    copies[1].wait()
-    values = token_rows[...].astype(F32)
-    normed[...] = (values * norm_scale(values) * gain_row[...]).astype(BF16)
+    for copy in copies[:2]:
+        copy.wait()
+    offset[...] = jnp.full(offset.shape, starts[0], jnp.int32)
+    values = token_rows[rows - 16 :].astype(F32)
+    normed = (values * norm_scale(values) * gain_row[...]).astype(BF16)
+    for copy in copies[2:11]:
+        copy.wait()
+    gated = (dot(normed, weights[0]) * dot(normed, weights[2])).astype(BF16).astype(F32)
+    tail[...] = (gated * linked_rows(starts[0], gated.shape, rows - 16, rows)).astype(BF16)
+    for copy in copies[11:]:
+        copy.wait()
+
+
+def project_kernel(scalars, tokens, gain, weights, normed, parts, gated):
+    values = tokens[...].astype(F32)
+    normed[...] = (values * norm_scale(values) * gain[...]).astype(BF16)
     for k in range(3):
-        copies[2 + k].wait()
         parts[k] = dot(normed[...], weights[k])
     gated[...] = (parts[0] * parts[2]).astype(BF16)
 
@@ -378,30 +398,36 @@
         at += count
 
 
-def wide_kernel(scalars, two, cot, cot_other, *refs):
-    own, shared, sends, keeps = refs[:3], refs[3], refs[4:6], refs[6:8]
-    left_two, left_cot = refs[8:]
+def wide_piece(scalars, kind, lefts, own, shared, send, keep):
+    at, core = scalars[0], scalars[3]
+    first, second = peer(at, kind), peer(at, 1 - kind)
+    chunks = (at, second, first, peer(first, 1 - kind))
+    for slot, chunk in enumerate(chunks):
+        target = keep if slot < 2 else send
+        rows = {}
+        for matrix, column, width, tile in wide_runs(kind):
+            if (matrix == 0) not in rows:
+                rows[matrix == 0] = chunk_rows(lefts[matrix], core, chunk)
+            left = rows[matrix == 0]
+            mine = pl.ds(pl.multiple_of(core * WIDE_COLUMNS + column, 128), width)
+            away = matrix * WIDE_COLUMNS + column
+            value = dot(left[:, :256], own[matrix][:, mine])
+            value = value + dot(left[:, 256:], shared[:, away : away + width])
+            store_blocks(value, target, (slot % 2) * 4 * WIDE[kind], WIDE[kind], tile)
+
+
+def wide_first_kernel(scalars, two, cot, cot_other, hidden, gate_back, shared, send, keep, left_two, left_cot):
     fill_transposed(left_cot, cot, cot_other)
     fill_transposed(left_two, two, shared.at[:, 3 * WIDE_COLUMNS :])
-    at, core = scalars[0], scalars[3]
-    for kind in range(2):
-        first, second = peer(at, kind), peer(at, 1 - kind)
-        chunks = (at, second, first, peer(first, 1 - kind))
-        for slot, chunk in enumerate(chunks):
-            target = keeps[kind] if slot < 2 else sends[kind]
-            rows = {}
-            for matrix, column, width, tile in wide_runs(kind):
-                if (matrix == 0) not in rows:
-                    rows[matrix == 0] = chunk_rows(left_cot if matrix == 0 else left_two, core, chunk)
-                left = rows[matrix == 0]
-                mine = pl.ds(pl.multiple_of(core * WIDE_COLUMNS + column, 128), width)
-                away = matrix * WIDE_COLUMNS + column
-                value = dot(left[:, :256], own[matrix][:, mine])
-                value = value + dot(left[:, 256:], shared[:, away : away + width])
-                store_blocks(value, target, (slot % 2) * 4 * WIDE[kind], WIDE[kind], tile)
-
-
-def narrow_kernel(scalars, one, shared, low, late_other, backs, ymix, out, left_one, left_low):
+    wide_piece(scalars, 0, (left_cot, left_two), (hidden, gate_back), shared, send, keep)
+
+
+def wide_second_kernel(scalars, left_two, gate_back, up_back, shared, send, keep):
+    wide_piece(scalars, 1, (None, left_two, left_two), (None, gate_back, up_back), shared, send, keep)
+
+
+def narrow_kernel(scalars, one, shared, low, late_other, backs, ymix, *refs):
+    outs, (left_one, left_low) = refs[:4], refs[4:]
     width = one.shape[1]
     one_other, ymix_other = shared.at[:, :width], shared.at[:, width:]
     for at in range(0, width, 256):
@@ -420,7 +446,7 @@
             )
             rows = chunk_rows(left, scalars[3], chunk)
             value = dot(rows[:, :256], own) + dot(rows[:, 256:], other)
-            store_blocks(value, out.at[slot], 0, NARROW, 2 * kind)
+            store_blocks(value, outs[slot], WIDE_BLOCKS[slot] if slot < 3 else 0, NARROW, 2 * kind)
 
 
 def split_small(value, target, at):
@@ -444,14 +470,12 @@
 
 
 def first_kernel(scalars, *refs):
-    gots, keeps, (narrow, small, gain, gain_other) = refs[:2], refs[2:4], refs[4:8]
-    sends, wide_keeps, new_small = refs[8:11], refs[11:13], refs[13]
+    gots, keeps, (small, gain, gain_other) = refs[:2], refs[2:4], refs[4:7]
+    sends, wide_keeps, new_small = refs[10:13], refs[13:15], refs[15]
     new_small[:8] = gain[...] + gain_other[...]
     new_small[8:] = small[8:]
     for pairing in range(3):
-        base = WIDE_BLOCKS[pairing]
-        sends[pairing][base : base + 4 * NARROW] = narrow[pairing]
-        split_small(new_small[...], sends[pairing], base + 4 * NARROW)
+        split_small(new_small[...], sends[pairing], ROUND_ONE[pairing] - 1)
     for kind in range(2):
         half = 4 * WIDE[kind]
         for chunk in range(4):
@@ -471,7 +495,7 @@
             value = wide_in[kind][at].astype(F32) + gots[1 - kind][at].astype(F32)
             target[tile : tile + WIDE[kind]] = value.astype(BF16)
             tile += WIDE[kind]
-        value = narrow[3, pl.ds(chunk * NARROW, NARROW)].astype(F32)
+        value = narrow[pl.ds(chunk * NARROW, NARROW)].astype(F32)
         for pairing in range(3):
             value = value + gots[pairing][pl.ds(WIDE_BLOCKS[pairing] + chunk * NARROW, NARROW)].astype(F32)
         target[tile : tile + NARROW] = value.astype(BF16)
@@ -563,14 +587,8 @@
     down_weight,
     cotangent,
 ):
-    at = lax.axis_index("seq")
-    core = at % 2
-    y, z = at // 16, (at // 4) % 4
-    scalars = jnp.stack(
-        [jnp.where(core == 0, y, z), jnp.where(core == 0, z, y), (at // 2) % 2, core, starts[0]]
-        + [lax.axis_index("tensor")]
-    ).astype(jnp.int32)
-    run = functools.partial(call, scalars=scalars)
+    core = lax.axis_index("seq") % 2
+    run = call
     rows, width = tokens.shape
     channels = conv_weight.shape[1]
     in_parts = in_weight.transpose(1, 0, 2)
@@ -580,39 +598,41 @@
         return swap(value, CORES)
 
     half = channels // 2
-    weight_got = swap(jnp.where(core == 0, out_weight[:half], out_weight[half:]), NEAREST)
-    tail = run(
-        tail_kernel,
-        operands=[tokens, gain_one_row, in_parts],
-        outs=[like((16, channels), BF16)],
-        scratch=[
-            pltpu.VMEM((16, width), BF16),
-            pltpu.VMEM((1, width), F32),
-            pltpu.VMEM((width, channels), BF16),
-            pltpu.VMEM((width, channels), BF16),
-            pltpu.SemaphoreType.DMA((4,)),
-        ],
-        room=60,
+    whole_half = run(
+        half_kernel,
+        operands=[pltpu.with_memory_space_constraint(out_weight, pltpu.HBM)],
+        outs=[like((half, width), BF16)],
+        scratch=[pltpu.SemaphoreType.DMA],
         where=pltpu.HBM,
     )[0]
+    weight_got = swap(whole_half, NEAREST)
+    tail, tokens_here, gain_here, weights_here, offset = run(
+        load_kernel,
+        operands=[
+            pltpu.with_memory_space_constraint(value, pltpu.HBM) for value in (tokens, gain_one_row, in_parts)
+        ],
+        scalar=starts,
+        outs=[
+            like((16, channels), BF16),
+            like((rows, width), BF16),
+            like((1, width), F32),
+            like((3, width, channels), BF16),
+            like((8, 128), jnp.int32),
+        ],
+        scratch=[pltpu.SemaphoreType.DMA((15,))],
+        where=pltpu.HBM,
+    )
     incoming = from_behind(tail, "seq", 1)
     cotangent_other = share(cotangent)
     incoming, cotangent_other = lax.optimization_barrier((incoming, cotangent_other))
     normed_one, parts, gated = run(
         project_kernel,
-        operands=[tokens, gain_one_row, in_parts],
+        operands=[tokens_here, gain_here, weights_here],
         outs=[like((rows, width), BF16), like((3, rows, channels), F32), like((rows, channels), BF16)],
-        scratch=[
-            pltpu.VMEM((rows, width), BF16),
-            pltpu.VMEM((1, width), F32),
-            pltpu.VMEM((3, width, channels), BF16),
-            pltpu.SemaphoreType.DMA((5,)),
-        ],
-        room=50,
-        where=pltpu.HBM,
     )
     conv, ymix = run(
         mix_kernel,
+        offset=offset,
         operands=[gated, incoming, parts, conv_weight],
         outs=[like((rows, channels), F32), like((rows, channels), BF16)],
     )
@@ -642,22 +662,31 @@
         part_kernel, operands=[gate_back, up_back, gate_weight, up_weight], outs=[like((rows, width), BF16)]
     )[0]
     norm_two_other = swap(norm_two_part, ACROSS)
-    results = run(
-        wide_kernel,
-        operands=[normed_two, cotangent, cotangent_other, hidden, gate_back, up_back, shared_other],
-        outs=blocks([8 * count for count in WIDE] * 2),
-        scratch=[pltpu.VMEM((width, 2 * rows), BF16)] * 2,
-    )
-    sends, keeps = list(results[:2]), list(results[2:])
+    first_send, first_keep, left_two = run(
+        wide_first_kernel,
+        operands=[normed_two, cotangent, cotangent_other, hidden, gate_back, shared_other],
+        outs=blocks([8 * WIDE[0]] * 2) + [like((width, 2 * rows), BF16)],
+        scratch=[pltpu.VMEM((width, 2 * rows), BF16)],
+    )
+    second_send, second_keep = run(
+        wide_second_kernel,
+        operands=[left_two, gate_back, up_back, shared_other],
+        outs=blocks([8 * WIDE[1]] * 2),
+    )
+    sends, keeps = [first_send, second_send], [first_keep, second_keep]
     down_part = run(down_kernel, operands=[hidden, down_weight], outs=[like((rows, width), BF16)])[0]
-    norm_two_other, keeps[1], down_part = lax.optimization_barrier((norm_two_other, keeps[1], down_part))
+    early_other = share(shared_early)
+    norm_two_other, keeps[1], down_part, early_other = lax.optimization_barrier(
+        (norm_two_other, keeps[1], down_part, early_other)
+    )
     gots = swap_round(sends, FIRST)
 
     edge_operands = [norm_two_part, norm_two_other, resid, gain_two_row, cotangent, out_weight, parts, conv_weight]
-    edge = run(edge_kernel, operands=edge_operands, outs=[like((8, channels), F32)])[0]
+    edge = run(edge_kernel, offset=offset, operands=edge_operands, outs=[like((8, channels), F32)])[0]
     returned = from_behind(edge, "seq", -1)
     resid_grad, resid_low, gain_two_grad, c_back, gated_back, tap_grads = run(
         middle_kernel,
+        offset=offset,
         operands=edge_operands + [conv, gated, incoming],
         outs=[
             like((rows, width), F32),
@@ -671,6 +700,7 @@
     )
     backs, shared, norm_one_part, gain_part, small = run(
         last_kernel,
+        offset=offset,
         operands=[gated_back, returned, parts, c_back, in_parts, tokens, gain_two_grad, tap_grads]
         + [resid_low],
         outs=[
@@ -681,17 +711,18 @@
             like((32, 128), F32),
         ],
     )
-    narrow = run(
+    *sends, narrow = run(
         narrow_kernel,
-        operands=[normed_one, share(shared_early), resid_low, share(shared), backs, ymix],
-        outs=[like((4, 4 * NARROW, *BLOCK), BF16)],
+        operands=[normed_one, early_other, resid_low, share(shared), backs, ymix],
+        outs=blocks(ROUND_ONE) + blocks([4 * NARROW]),
         scratch=[pltpu.VMEM((width, 2 * rows), BF16)] * 2,
-    )[0]
+    )
     gain_other = swap(gain_part, ACROSS)
     gots[0], gots[1], narrow, gain_other = lax.optimization_barrier((gots[0], gots[1], narrow, gain_other))
     results = run(
         first_kernel,
-        operands=gots + keeps + [narrow, small, gain_part, gain_other],
+        operands=gots + keeps + [small, gain_part, gain_other] + sends,
+        aliases={7: 0, 8: 1, 9: 2},
         outs=blocks(ROUND_ONE) + blocks([4 * count for count in WIDE]) + [like((32, 128), F32)],
     )
     sends, keeps, small = list(results[:3]), list(results[3:5]), results[5]

time: 129 us -> 125 us (0.969)
  Pallas kernels: 38.7 us -> 27.8 us
  waiting for transfers between devices: 47.4 us -> 52.4 us
  starting transfers between devices: 36.3 us -> 38.9 us
    pallas_call x18 -> x20, Pallas kernels: 38.7 us -> 27.8 us  [call(): pl.pallas_call(kernel, out_shape=tuple(outs), in_specs=specs, out_specs=t...]
    ppermute x21, waiting for transfers between devices: 47 us -> 51.6 us  [swap(): return lax.ppermute(value, AXES, pairs)]
    ppermute x21, starting transfers between devices: 31.5 us -> 34.1 us  [swap(): return lax.ppermute(value, AXES, pairs)]
  transfers between devices with their start and end apart: 23 -> 23, of which waited for: 12 -> 13; matrix products, arithmetic and copies ran while one was open for 4% -> 2% of each run, Pallas kernels for 22% -> 17%
where the time goes in v5:
time: 125 us; the launch traced here: 124 us
  waiting for transfers between devices  52.4 us (42%)
  starting transfers between devices  38.9 us (31%)
  Pallas kernels  27.8 us (22%)
  other arithmetic  2.84 us (2%)
  between operations  1.62 us (1%)
    ppermute x21, waiting for transfers between devices, swap(): return lax.ppermute(value, AXES, pairs)  51.6 us
    ppermute x21, starting transfers between devices, swap(): return lax.ppermute(value, AXES, pairs)  34.1 us
    pallas_call x20, Pallas kernels, call(): pl.pallas_call(kernel, out_shape=tuple(outs), in_specs=specs, out_specs=t...  27.8 us
    ppermute x2, starting transfers between devices, from_behind(): lax.ppermute(value, axis, [(source, source + steps) for source in range(l...  4.83 us
  transfers between devices with their start and end apart: 23, of which 13 were waited for; matrix products, arithmetic and copies ran while one was open for 2% of the time, Pallas kernels for 17%

profile of v5, /device:TPU:1, one launch (start us, length us, event | category | flops | bytes accessed | tf_op | source)
XLA Modules:
  0.0 124.3 jit_solution(9453905428489285044)
XLA Ops:
  3.2 2.6 %collective-permute-start.3 = (bf16[256,1024]{1,0:T(8,128)(2,1)S(1)}, bf16[256,1024]{1,0:T(8,128)(2,1)S(1)}, u32[]{:S(2)}, u32[]{:S(2)}) collective-permute-start(bf16[256,1024]{1,0:T(8,128)(2,1)S(1)} %shard_map.190), channel_id=1, source_target_pairs={{0,5},{2,7},{4,1},{6,3},{1,4},{3,6},{5,0},{7,2},{8,13},{10,15},{12... | collective-permute-start | bytes 1572872 | tf_op jit(solution)/shard_map/ppermute | solution.py:75
  6.5 2.2 %shard_map.186 = (bf16[16,512]{1,0:T(8,128)(2,1)S(1)}, bf16[256,1024]{1,0:T(8,128)(2,1)S(1)}, f32[1,1024]{1,0:T(1,128)S(1)}, bf16[3,1024,512]{2,1,0:T(8,128)(2,1)S(1)}, s32[8,128]{1,0:T(8,128)S(1)}) custom-call(s32[1]{0:T(128)S(6)} %copy.27.refs_0_, bf16[256,1024]{1,0:T(8,128)(2,1)} %refs_6_.7, f32[1,1024]{1,0:T(1,128)} %bitcast.17, ...), custom_call_target="tpu_custom_call" | custom-call | tf_op jit(solution)/shard_map/pallas_call | solution.py:119
  8.7 2.0 %collective-permute-start = (bf16[16,512]{1,0:T(8,128)(2,1)S(1)}, bf16[16,512]{1,0:T(8,128)(2,1)S(1)}, u32[]{:S(2)}, u32[]{:S(2)}) collective-permute-start(bf16[16,512]{1,0:T(8,128)(2,1)S(1)} %get-tuple-element.99), channel_id=1, source_target_pairs={{0,2},{2,4},{4,6},{6,8},{8,10},{10,12},{12,14},{14,16},{16,18},{18... | collective-permute-start | bytes 49160 | tf_op jit(solution)/shard_map/ppermute | solution.py:81
  14.0 9.6 %collective-permute-done.3.refs_1_ = bf16[256,1024]{1,0:T(8,128)(2,1)S(1)} collective-permute-done((bf16[256,1024]{1,0:T(8,128)(2,1)S(1)}, bf16[256,1024]{1,0:T(8,128)(2,1)S(1)}, u32[]{:S(2)}, u32[]{:S(2)}) %collective-permute-start.3) | collective-permute-done | bytes 524320 | tf_op jit(solution)/shard_map/ppermute | solution.py:75
  26.9 3.9 %shard_map.192 = (f32[256,1024]{1,0:T(8,128)S(1)}, bf16[256,1024]{1,0:T(8,128)(2,1)S(1)}, bf16[256,2304]{1,0:T(8,128)(2,1)S(1)}, bf16[256,2304]{1,0:T(8,128)(2,1...) custom-call(bf16[256,1024]{1,0:T(8,128)(2,1)S(1)} %copy-done, ...), custom_call_target="tpu_custom_call" | custom-call | tf_op jit(solution)/shard_map/pallas_call | solution.py:119
  31.4 2.6 %shard_map.195.refs_1_ = bf16[256,1024]{1,0:T(8,128)(2,1)S(1)} custom-call(bf16[256,2304]{1,0:T(8,128)(2,1)S(1)} %get-tuple-element.112.refs_4_.refs_1_.refs_0_, bf16[256,2304]{1,0:T(8,128)(2,1)S(1)} %get-tuple-element.116.refs_2_.refs_1_, bf16[1024,2304]{1,0:T(8,128)(2,1)S(1)} %bitcast.9, bf16[1024,2304]{1,0:T(8,128)(2,1)S(1)} %bitcast.11), custom_call_target="tpu_custom_call" | custom-call | tf_op jit(solution)/shard_map/pallas_call | solution.py:119
  34.1 1.8 %collective-permute-start.8 = (bf16[256,1024]{1,0:T(8,128)(2,1)S(1)}, bf16[256,1024]{1,0:T(8,128)(2,1)S(1)}, u32[]{:S(2)}, u32[]{:S(2)}) collective-permute-start(bf16[256,1024]{1,0:T(8,128)(2,1)S(1)} %shard_map.195.refs_1_), channel_id=1, source_target_pairs={{0,1},{2,3},{4,5},{6,7},{1,0},{3,2},{5,4},{7,6},{8,9},{10,11},{12,... | collective-permute-start | bytes 1572872 | tf_op jit(solution)/shard_map/ppermute | solution.py:75
  35.9 2.8 %shard_map.193 = (bf16[112,64,128]{2,1,0:T(8,128)(2,1)S(1)}, bf16[112,64,128]{2,1,0:T(8,128)(2,1)S(1)}, bf16[1024,512]{1,0:T(8,128)(2,1)S(1)}) custom-call(bf16[256,1024]{1,0:T(8,128)(2,1)S(1)} %get-tuple-element.109.refs_0_, bf16[256,1024]{1,0:T(8,128)(2,1)S(1)} %copy-done.4, bf16[256,1024]{1,0:T(8,128)(2,1)S(1)} %collective-permute-done.1.refs_2_, ...), custom_call_target="tpu_custom_call" | custom-call | tf_op jit(solution)/shard_map/pallas_call | solution.py:119
  38.7 1.8 %collective-permute-start.6 = (bf16[112,64,128]{2,1,0:T(8,128)(2,1)S(1)}, bf16[112,64,128]{2,1,0:T(8,128)(2,1)S(1)}, u32[]{:S(2)}, u32[]{:S(2)}) collective-permute-start(bf16[112,64,128]{2,1,0:T(8,128)(2,1)S(1)} %get-tuple-element.114), channel_id=1, source_target_pairs={{0,32},{2,10},{4,36},{6,14},{1,33},{3,11},{5,37},{7,15},{8,40},{10... | collective-permute-start | bytes 5505032 | tf_op jit(solution)/shard_map/ppermute | solution.py:75
  40.4 2.1 %shard_map.194 = (bf16[104,64,128]{2,1,0:T(8,128)(2,1)S(1)}, bf16[104,64,128]{2,1,0:T(8,128)(2,1)S(1)}) custom-call(bf16[1024,512]{1,0:T(8,128)(2,1)S(1)} %get-tuple-element.115.refs_0_, bf16[256,2304]{1,0:T(8,128)(2,1)S(1)} %get-tuple-element.112.refs_4_.refs_1_.refs_0_, bf16[256,2304]{1,0:T(8,128)(2,1)S(1)} %get-tuple-element.116.refs_2_.refs_1_, ...), custom_call_target="tpu_custom_call" | custom-call | tf_op jit(solution)/shard_map/pallas_call | solution.py:119
  42.6 2.3 %collective-permute-start.7 = (bf16[104,64,128]{2,1,0:T(8,128)(2,1)S(1)}, bf16[104,64,128]{2,1,0:T(8,128)(2,1)S(1)}, u32[]{:S(2)}, u32[]{:S(2)}) collective-permute-start(bf16[104,64,128]{2,1,0:T(8,128)(2,1)S(1)} %get-tuple-element.117), channel_id=1, source_target_pairs={{0,96},{2,26},{4,100},{6,30},{1,97},{3,27},{5,101},{7,31},{8,104},... | collective-permute-start | bytes 5111816 | tf_op jit(solution)/shard_map/ppermute | solution.py:75
  46.3 3.0 %collective-permute-done.8.refs_2_ = bf16[256,1024]{1,0:T(8,128)(2,1)S(1)} collective-permute-done((bf16[256,1024]{1,0:T(8,128)(2,1)S(1)}, bf16[256,1024]{1,0:T(8,128)(2,1)S(1)}, u32[]{:S(2)}, u32[]{:S(2)}) %collective-permute-start.8) | collective-permute-done | bytes 524320 | tf_op jit(solution)/shard_map/ppermute | solution.py:75
  49.8 2.8 %collective-permute-start.10 = (f32[8,512]{1,0:T(8,128)S(1)}, f32[8,512]{1,0:T(8,128)S(1)}, u32[]{:S(2)}, u32[]{:S(2)}) collective-permute-start(f32[8,512]{1,0:T(8,128)S(1)} %shard_map.198), channel_id=1, source_target_pairs={{2,0},{4,2},{6,4},{8,6},{10,8},{12,10},{14,12},{16,14},{18,16},{20... | collective-permute-start | bytes 49160 | tf_op jit(solution)/shard_map/ppermute | solution.py:81
  56.3 2.8 %collective-permute-start.12 = (f32[8,128]{1,0:T(8,128)S(1)}, f32[8,128]{1,0:T(8,128)S(1)}, u32[]{:S(2)}, u32[]{:S(2)}) collective-permute-start(f32[8,128]{1,0:T(8,128)S(1)} %get-tuple-element.132.refs_5_), channel_id=1, source_target_pairs={{0,1},{2,3},{4,5},{6,7},{1,0},{3,2},{5,4},{7,6},{8,9},{10,11},{12,... | collective-permute-start | bytes 12296 | tf_op jit(solution)/shard_map/ppermute | solution.py:75
  60.9 3.6 %collective-permute-done.7.refs_1_ = bf16[104,64,128]{2,1,0:T(8,128)(2,1)S(1)} collective-permute-done((bf16[104,64,128]{2,1,0:T(8,128)(2,1)S(1)}, bf16[104,64,128]{2,1,0:T(8,128)(2,1)S(1)}, u32[]{:S(2)}, u32[]{:S(2)}) %collective-permute-start.7) | collective-permute-done | bytes 1703968 | tf_op jit(solution)/shard_map/ppermute | solution.py:75
  66.0 2.6 %collective-permute-start.15 = (bf16[89,64,128]{2,1,0:T(8,128)(2,1)S(1)}, bf16[89,64,128]{2,1,0:T(8,128)(2,1)S(1)}, u32[]{:S(2)}, u32[]{:S(2)}) collective-permute-start(bf16[89,64,128]{2,1,0:T(8,128)(2,1)S(1)} %get-tuple-element.145), channel_id=1, source_target_pairs={{0,96},{2,26},{4,100},{6,30},{1,97},{3,27},{5,101},{7,31},{8,104},... | collective-permute-start | bytes 4374536 | tf_op jit(solution)/shard_map/ppermute | solution.py:75
  71.5 12.7 %collective-permute-done.14 = bf16[256,1024]{1,0:T(8,128)(2,1)S(1)} collective-permute-done((bf16[256,1024]{1,0:T(8,128)(2,1)S(1)}, bf16[256,1024]{1,0:T(8,128)(2,1)S(1)}, u32[]{:S(2)}, u32[]{:S(2)}) %collective-permute-start.14) | collective-permute-done | bytes 524320 | tf_op jit(solution)/shard_map/ppermute | solution.py:75
  84.2 2.0 %collective-permute-done.13.refs_0_ = bf16[85,64,128]{2,1,0:T(8,128)(2,1)S(1)} collective-permute-done((bf16[85,64,128]{2,1,0:T(8,128)(2,1)S(1)}, bf16[85,64,128]{2,1,0:T(8,128)(2,1)S(1)}, u32[]{:S(2)}, u32[]{:S(2)}) %collective-permute-start.13) | collective-permute-done | bytes 1392672 | tf_op jit(solution)/shard_map/ppermute | solution.py:75
  86.2 5.8 %collective-permute-done.16.refs_2_ = bf16[33,64,128]{2,1,0:T(8,128)(2,1)S(1)} collective-permute-done((bf16[33,64,128]{2,1,0:T(8,128)(2,1)S(1)}, bf16[33,64,128]{2,1,0:T(8,128)(2,1)S(1)}, u32[]{:S(2)}, u32[]{:S(2)}) %collective-permute-start.16) | collective-permute-done | bytes 540704 | tf_op jit(solution)/shard_map/ppermute | solution.py:75
  93.6 2.0 %collective-permute-start.19 = (bf16[36,64,128]{2,1,0:T(8,128)(2,1)S(1)}, bf16[36,64,128]{2,1,0:T(8,128)(2,1)S(1)}, u32[]{:S(2)}, u32[]{:S(2)}) collective-permute-start(bf16[36,64,128]{2,1,0:T(8,128)(2,1)S(1)} %get-tuple-element.156), channel_id=1, source_target_pairs={{0,24},{2,98},{4,28},{6,102},{1,25},{3,99},{5,29},{7,103},{8,16},{... | collective-permute-start | bytes 1769480 | tf_op jit(solution)/shard_map/ppermute | solution.py:75
  96.7 1.8 %collective-permute-start.18 = (bf16[256,1024]{1,0:T(8,128)(2,1)S(1)}, bf16[256,1024]{1,0:T(8,128)(2,1)S(1)}, u32[]{:S(2)}, u32[]{:S(2)}) collective-permute-start(bf16[256,1024]{1,0:T(8,128)(2,1)S(1)} %shard_map.196), channel_id=1, source_target_pairs={{0,1},{2,3},{4,5},{6,7},{1,0},{3,2},{5,4},{7,6},{8,9},{10,11},{12,... | collective-permute-start | bytes 1572872 | tf_op jit(solution)/shard_map/ppermute | solution.py:75
  98.9 8.8 %collective-permute-done.18 = bf16[256,1024]{1,0:T(8,128)(2,1)S(1)} collective-permute-done((bf16[256,1024]{1,0:T(8,128)(2,1)S(1)}, bf16[256,1024]{1,0:T(8,128)(2,1)S(1)}, u32[]{:S(2)}, u32[]{:S(2)}) %collective-permute-start.18) | collective-permute-done | bytes 524320 | tf_op jit(solution)/shard_map/ppermute | solution.py:75
  108.8 1.8 %collective-permute-done.20.refs_2_ = bf16[36,64,128]{2,1,0:T(8,128)(2,1)S(1)} collective-permute-done((bf16[36,64,128]{2,1,0:T(8,128)(2,1)S(1)}, bf16[36,64,128]{2,1,0:T(8,128)(2,1)S(1)}, u32[]{:S(2)}, u32[]{:S(2)}) %collective-permute-start.20) | collective-permute-done | bytes 589856 | tf_op jit(solution)/shard_map/ppermute | solution.py:75
  116.9 5.4 %collective-permute-start.22 = (f32[37,16,128]{2,1,0:T(8,128)S(1)}, f32[37,16,128]{2,1,0:T(8,128)S(1)}, u32[]{:S(2)}, u32[]{:S(2)}) collective-permute-start(f32[37,16,128]{2,1,0:T(8,128)S(1)} %get-tuple-element.169), channel_id=1, source_target_pairs={{0,2},{2,0},{4,6},{6,4},{1,3},{3,1},{5,7},{7,5},{8,10},{10,8},{12,... | collective-permute-start | bytes 909320 | tf_op jit(solution)/shard_map/ppermute | solution.py:75
  (72 shorter events, 33.8 us)
Async XLA Ops:
  0.6 11.3 %collective-permute-start.1 = (bf16[256,1024]{1,0:T(8,128)(2,1)}, bf16[256,1024]{1,0:T(8,128)(2,1)S(1)}, u32[]{:S(2)}, u32[]{:S(2)}) collective-permute-start(bf16[256,1024]{1,0:T(8,128)(2,1)} %refs_5_.5), channel_id=1, source_target_pairs={{0,2},{2,0},{4,6},{6,4},{1,3},{3,1},{5,7},{7,5},{8,10},{10,8},{12,... | collective-permute-start | bytes 1572872 | tf_op jit(solution)/shard_map/ppermute | solution.py:75
  3.2 20.4 %collective-permute-start.3 = (bf16[256,1024]{1,0:T(8,128)(2,1)S(1)}, bf16[256,1024]{1,0:T(8,128)(2,1)S(1)}, u32[]{:S(2)}, u32[]{:S(2)}) collective-permute-start(bf16[256,1024]{1,0:T(8,128)(2,1)S(1)} %shard_map.190), channel_id=1, source_target_pairs={{0,5},{2,7},{4,1},{6,3},{1,4},{3,6},{5,0},{7,2},{8,13},{10,15},{12... | collective-permute-start | bytes 1572872 | tf_op jit(solution)/shard_map/ppermute | solution.py:75
  8.7 3.2 %collective-permute-start = (bf16[16,512]{1,0:T(8,128)(2,1)S(1)}, bf16[16,512]{1,0:T(8,128)(2,1)S(1)}, u32[]{:S(2)}, u32[]{:S(2)}) collective-permute-start(bf16[16,512]{1,0:T(8,128)(2,1)S(1)} %get-tuple-element.99), channel_id=1, source_target_pairs={{0,2},{2,4},{4,6},{6,8},{8,10},{10,12},{12,14},{14,16},{16,18},{18... | collective-permute-start | bytes 49160 | tf_op jit(solution)/shard_map/ppermute | solution.py:81
  12.5 13.8 %slice-start = ((s8[4718592]{0:T(1024)(128)(4,1)}), s8[4194304]{0:T(1024)(128)(4,1)S(1)}, s32[]{:S(2)}) async-start(s8[4718592]{0:T(1024)(128)(4,1)} %bitcast.8), calls=%async_computation | async-start | bytes 8388608
  12.6 13.7 %collective-permute-start.2 = (bf16[256,512]{1,0:T(8,128)(2,1)S(1)}, bf16[256,512]{1,0:T(8,128)(2,1)S(1)}, u32[]{:S(2)}, u32[]{:S(2)}) collective-permute-start(bf16[256,512]{1,0:T(8,128)(2,1)S(1)} %get-tuple-element.103.refs_1_.refs_5_), channel_id=1, source_target_pairs={{0,1},{2,3},{4,5},{6,7},{1,0},{3,2},{5,4},{7,6},{8,9},{10,11},{12,... | collective-permute-start | bytes 786440 | tf_op jit(solution)/shard_map/ppermute | solution.py:75
  23.6 2.4 %collective-permute-start.4 = (bf16[256,1024]{1,0:T(8,128)(2,1)S(1)}, bf16[256,1024]{1,0:T(8,128)(2,1)S(1)}, u32[]{:S(2)}, u32[]{:S(2)}) collective-permute-start(bf16[256,1024]{1,0:T(8,128)(2,1)S(1)} %collective-permute-done.3.refs_1_), channel_id=1, source_target_pairs={{0,2},{2,0},{4,6},{6,4},{1,3},{3,1},{5,7},{7,5},{8,10},{10,8},{12,... | collective-permute-start | bytes 1572872 | tf_op jit(solution)/shard_map/ppermute | solution.py:75
  30.8 5.1 %collective-permute-start.5 = (bf16[256,4480]{1,0:T(8,128)(2,1)S(1)}, bf16[256,4480]{1,0:T(8,128)(2,1)S(1)}, u32[]{:S(2)}, u32[]{:S(2)}) collective-permute-start(bf16[256,4480]{1,0:T(8,128)(2,1)S(1)} %get-tuple-element.113), channel_id=1, source_target_pairs={{0,2},{2,0},{4,6},{6,4},{1,3},{3,1},{5,7},{7,5},{8,10},{10,8},{12,... | collective-permute-start | bytes 6881288 | tf_op jit(solution)/shard_map/ppermute | solution.py:75
  31.0 18.3 %collective-permute-start.9 = (bf16[256,1280]{1,0:T(8,128)(2,1)S(1)}, bf16[256,1280]{1,0:T(8,128)(2,1)S(1)}, u32[]{:S(2)}, u32[]{:S(2)}) collective-permute-start(bf16[256,1280]{1,0:T(8,128)(2,1)S(1)} %get-tuple-element.119), channel_id=1, source_target_pairs={{0,2},{2,0},{4,6},{6,4},{1,3},{3,1},{5,7},{7,5},{8,10},{10,8},{12,... | collective-permute-start | bytes 1966088 | tf_op jit(solution)/shard_map/ppermute | solution.py:75
  34.1 15.3 %collective-permute-start.8 = (bf16[256,1024]{1,0:T(8,128)(2,1)S(1)}, bf16[256,1024]{1,0:T(8,128)(2,1)S(1)}, u32[]{:S(2)}, u32[]{:S(2)}) collective-permute-start(bf16[256,1024]{1,0:T(8,128)(2,1)S(1)} %shard_map.195.refs_1_), channel_id=1, source_target_pairs={{0,1},{2,3},{4,5},{6,7},{1,0},{3,2},{5,4},{7,6},{8,9},{10,11},{12,... | collective-permute-start | bytes 1572872 | tf_op jit(solution)/shard_map/ppermute | solution.py:75
  38.7 25.9 %collective-permute-start.6 = (bf16[112,64,128]{2,1,0:T(8,128)(2,1)S(1)}, bf16[112,64,128]{2,1,0:T(8,128)(2,1)S(1)}, u32[]{:S(2)}, u32[]{:S(2)}) collective-permute-start(bf16[112,64,128]{2,1,0:T(8,128)(2,1)S(1)} %get-tuple-element.114), channel_id=1, source_target_pairs={{0,32},{2,10},{4,36},{6,14},{1,33},{3,11},{5,37},{7,15},{8,40},{10... | collective-permute-start | bytes 5505032 | tf_op jit(solution)/shard_map/ppermute | solution.py:75
  42.6 22.0 %collective-permute-start.7 = (bf16[104,64,128]{2,1,0:T(8,128)(2,1)S(1)}, bf16[104,64,128]{2,1,0:T(8,128)(2,1)S(1)}, u32[]{:S(2)}, u32[]{:S(2)}) collective-permute-start(bf16[104,64,128]{2,1,0:T(8,128)(2,1)S(1)} %get-tuple-element.117), channel_id=1, source_target_pairs={{0,96},{2,26},{4,100},{6,30},{1,97},{3,27},{5,101},{7,31},{8,104},... | collective-permute-start | bytes 5111816 | tf_op jit(solution)/shard_map/ppermute | solution.py:75
  49.8 5.4 %collective-permute-start.10 = (f32[8,512]{1,0:T(8,128)S(1)}, f32[8,512]{1,0:T(8,128)S(1)}, u32[]{:S(2)}, u32[]{:S(2)}) collective-permute-start(f32[8,512]{1,0:T(8,128)S(1)} %shard_map.198), channel_id=1, source_target_pairs={{2,0},{4,2},{6,4},{8,6},{10,8},{12,10},{14,12},{16,14},{18,16},{20... | collective-permute-start | bytes 49160 | tf_op jit(solution)/shard_map/ppermute | solution.py:81
  56.3 2.9 %collective-permute-start.11 = (bf16[7,256,256]{2,1,0:T(8,128)(2,1)S(1)}, bf16[7,256,256]{2,1,0:T(8,128)(2,1)S(1)}, u32[]{:S(2)}, u32[]{:S(2)}) collective-permute-start(bf16[7,256,256]{2,1,0:T(8,128)(2,1)S(1)} %get-tuple-element.129), channel_id=1, source_target_pairs={{0,2},{2,0},{4,6},{6,4},{1,3},{3,1},{5,7},{7,5},{8,10},{10,8},{12,... | collective-permute-start | bytes 2752520 | tf_op jit(solution)/shard_map/ppermute | solution.py:75
  56.3 4.5 %collective-permute-start.12 = (f32[8,128]{1,0:T(8,128)S(1)}, f32[8,128]{1,0:T(8,128)S(1)}, u32[]{:S(2)}, u32[]{:S(2)}) collective-permute-start(f32[8,128]{1,0:T(8,128)S(1)} %get-tuple-element.132.refs_5_), channel_id=1, source_target_pairs={{0,1},{2,3},{4,5},{6,7},{1,0},{3,2},{5,4},{7,6},{8,9},{10,11},{12,... | collective-permute-start | bytes 12296 | tf_op jit(solution)/shard_map/ppermute | solution.py:75
  66.0 26.0 %collective-permute-start.15 = (bf16[89,64,128]{2,1,0:T(8,128)(2,1)S(1)}, bf16[89,64,128]{2,1,0:T(8,128)(2,1)S(1)}, u32[]{:S(2)}, u32[]{:S(2)}) collective-permute-start(bf16[89,64,128]{2,1,0:T(8,128)(2,1)S(1)} %get-tuple-element.145), channel_id=1, source_target_pairs={{0,96},{2,26},{4,100},{6,30},{1,97},{3,27},{5,101},{7,31},{8,104},... | collective-permute-start | bytes 4374536 | tf_op jit(solution)/shard_map/ppermute | solution.py:75
  68.6 17.6 %collective-permute-start.13 = (bf16[85,64,128]{2,1,0:T(8,128)(2,1)S(1)}, bf16[85,64,128]{2,1,0:T(8,128)(2,1)S(1)}, u32[]{:S(2)}, u32[]{:S(2)}) collective-permute-start(bf16[85,64,128]{2,1,0:T(8,128)(2,1)S(1)} %get-tuple-element.142), channel_id=1, source_target_pairs={{0,32},{2,10},{4,36},{6,14},{1,33},{3,11},{5,37},{7,15},{8,40},{10... | collective-permute-start | bytes 4177928 | tf_op jit(solution)/shard_map/ppermute | solution.py:75
  68.6 23.4 %collective-permute-start.16 = (bf16[33,64,128]{2,1,0:T(8,128)(2,1)S(1)}, bf16[33,64,128]{2,1,0:T(8,128)(2,1)S(1)}, u32[]{:S(2)}, u32[]{:S(2)}) collective-permute-start(bf16[33,64,128]{2,1,0:T(8,128)(2,1)S(1)} %get-tuple-element.146), channel_id=1, source_target_pairs={{0,64},{2,18},{4,68},{6,22},{1,65},{3,19},{5,69},{7,23},{8,72},{10... | collective-permute-start | bytes 1622024 | tf_op jit(solution)/shard_map/ppermute | solution.py:75
  70.1 14.1 %collective-permute-start.14 = (bf16[256,1024]{1,0:T(8,128)(2,1)S(1)}, bf16[256,1024]{1,0:T(8,128)(2,1)S(1)}, u32[]{:S(2)}, u32[]{:S(2)}) collective-permute-start(bf16[256,1024]{1,0:T(8,128)(2,1)S(1)} %get-tuple-element.143), channel_id=1, source_target_pairs={{0,1},{2,3},{4,5},{6,7},{1,0},{3,2},{5,4},{7,6},{8,9},{10,11},{12,... | collective-permute-start | bytes 1572872 | tf_op jit(solution)/shard_map/ppermute | solution.py:75
  92.7 15.0 %collective-permute-start.17 = (bf16[36,64,128]{2,1,0:T(8,128)(2,1)S(1)}, bf16[36,64,128]{2,1,0:T(8,128)(2,1)S(1)}, u32[]{:S(2)}, u32[]{:S(2)}) collective-permute-start(bf16[36,64,128]{2,1,0:T(8,128)(2,1)S(1)} %get-tuple-element.151), channel_id=1, source_target_pairs={{0,8},{2,34},{4,12},{6,38},{1,9},{3,35},{5,13},{7,39},{8,0},{10,42... | collective-permute-start | bytes 1769480 | tf_op jit(solution)/shard_map/ppermute | solution.py:75
  93.6 15.2 %collective-permute-start.19 = (bf16[36,64,128]{2,1,0:T(8,128)(2,1)S(1)}, bf16[36,64,128]{2,1,0:T(8,128)(2,1)S(1)}, u32[]{:S(2)}, u32[]{:S(2)}) collective-permute-start(bf16[36,64,128]{2,1,0:T(8,128)(2,1)S(1)} %get-tuple-element.156), channel_id=1, source_target_pairs={{0,24},{2,98},{4,28},{6,102},{1,25},{3,99},{5,29},{7,103},{8,16},{... | collective-permute-start | bytes 1769480 | tf_op jit(solution)/shard_map/ppermute | solution.py:75
  95.7 15.0 %collective-permute-start.20 = (bf16[36,64,128]{2,1,0:T(8,128)(2,1)S(1)}, bf16[36,64,128]{2,1,0:T(8,128)(2,1)S(1)}, u32[]{:S(2)}, u32[]{:S(2)}) collective-permute-start(bf16[36,64,128]{2,1,0:T(8,128)(2,1)S(1)} %get-tuple-element.157), channel_id=1, source_target_pairs={{0,16},{2,66},{4,20},{6,70},{1,17},{3,67},{5,21},{7,71},{8,24},{10... | collective-permute-start | bytes 1769480 | tf_op jit(solution)/shard_map/ppermute | solution.py:75
  96.7 10.9 %collective-permute-start.18 = (bf16[256,1024]{1,0:T(8,128)(2,1)S(1)}, bf16[256,1024]{1,0:T(8,128)(2,1)S(1)}, u32[]{:S(2)}, u32[]{:S(2)}) collective-permute-start(bf16[256,1024]{1,0:T(8,128)(2,1)S(1)} %shard_map.196), channel_id=1, source_target_pairs={{0,1},{2,3},{4,5},{6,7},{1,0},{3,2},{5,4},{7,6},{8,9},{10,11},{12,... | collective-permute-start | bytes 1572872 | tf_op jit(solution)/shard_map/ppermute | solution.py:75
  111.0 5.8 %collective-permute-start.21 = (bf16[37,32,128]{2,1,0:T(8,128)(2,1)S(1)}, bf16[37,32,128]{2,1,0:T(8,128)(2,1)S(1)}, u32[]{:S(2)}, u32[]{:S(2)}) collective-permute-start(bf16[37,32,128]{2,1,0:T(8,128)(2,1)S(1)} %get-tuple-element.160), channel_id=1, source_target_pairs={{0,4},{2,6},{4,0},{6,2},{1,5},{3,7},{5,1},{7,3},{8,12},{10,14},{12... | collective-permute-start | bytes 909320 | tf_op jit(solution)/shard_map/ppermute | solution.py:75
  116.9 6.6 %collective-permute-start.22 = (f32[37,16,128]{2,1,0:T(8,128)S(1)}, f32[37,16,128]{2,1,0:T(8,128)S(1)}, u32[]{:S(2)}, u32[]{:S(2)}) collective-permute-start(f32[37,16,128]{2,1,0:T(8,128)S(1)} %get-tuple-element.169), channel_id=1, source_target_pairs={{0,2},{2,0},{4,6},{6,4},{1,3},{3,1},{5,7},{7,5},{8,10},{10,8},{12,... | collective-permute-start | bytes 909320 | tf_op jit(solution)/shard_map/ppermute | solution.py:75
  (11 other events, 97.6 us)

commit v6 on v5

--- a/solution.py
+++ b/solution.py
@@ -28,7 +28,6 @@
 
 ACROSS = device_pairs(lambda y, z, x, core: (y, z, (x + 2) % 4, core))
 BESIDE = device_pairs(lambda y, z, x, core: (y, z, x ^ 1, core))
-NEAREST = device_pairs(lambda y, z, x, core: (y, z, 3 - x, core))
 CORES = device_pairs(lambda y, z, x, core: (y, z, x, 1 - core))
 
 
@@ -66,7 +65,6 @@
 LONG = 3 * 10**10
 SHORT = 8 * 10**9
 TILES = WIDE_TILES + NARROW
-WIDE_PIECE = (1, 0, None)
 WIDE_BLOCKS = (4 * WIDE[1], 4 * WIDE[0], 0)
 ROUND_ONE = tuple(count + 4 * NARROW + 1 for count in WIDE_BLOCKS)
 
@@ -99,7 +97,7 @@
     at = lax.axis_index("seq")
     y, z, core = at // 16, (at // 4) % 4, at % 2
     first, second = jnp.where(core == 0, y, z), jnp.where(core == 0, z, y)
-    return first, second, (at // 2) % 2, core, offset, lax.axis_index("tensor")
+    return first, second, (at // 2) % 2, core, offset
 
 
 def call(body, *, operands, outs, scratch=(), offset=None, flops=0, aliases=None, where=pltpu.VMEM, scalar=None):
@@ -147,13 +145,6 @@
 
 def linked_rows(offset, shape, first, count):
     return jnp.where((row_numbers(shape, first) < offset) & (offset < count), 0.0, 1.0)
-
-
-def half_kernel(scalars, weight, half, done):
-    rows = half.shape[0]
-    copy = pltpu.make_async_copy(weight.at[pl.ds(pl.multiple_of(scalars[3] * rows, 16), rows)], half, done)
-    copy.start()
-    copy.wait()
 
 
 def load_kernel(scalars, starts, tokens, gain, weight, tail, token_rows, gain_row, weights, offset, done):
@@ -197,7 +188,7 @@
     return moved
 
 
-def mix_kernel(scalars, gated, incoming, parts, taps, conv, ymix):
+def mix_kernel(scalars, gated, incoming, parts, taps, weight, conv, ymix, branch):
     values = gated[...].astype(F32)
     before = incoming[...].astype(F32)
     total = taps[0:1] * values
@@ -207,6 +198,7 @@
         )
     conv[...] = total
     ymix[...] = (parts[1] * total).astype(BF16)
+    branch[...] = dot(ymix[...], weight[...]).astype(BF16)
 
 
 def away_half(value, core):
@@ -223,27 +215,17 @@
     out[...] = dot(hidden[...], weight[...]).astype(BF16)
 
 
-def whole_kernel(scalars, weight, got, got_other, whole):
-    core, side = scalars[3], scalars[5]
-    half = got.shape[0]
-    low, high = jnp.where(core == 0, got[...], got_other[...]), jnp.where(core == 0, got_other[...], got[...])
-    whole[:half] = jnp.where(side == 0, weight[:half], low)
-    whole[half : 2 * half] = jnp.where(side == 0, weight[half:], high)
-    whole[2 * half : 3 * half] = jnp.where(side == 0, low, weight[:half])
-    whole[3 * half :] = jnp.where(side == 0, high, weight[half:])
-
-
 def feed_kernel(
     scalars,
     tokens,
-    ymix,
-    ymix_other,
-    whole,
+    branch,
+    other,
     gain,
     gate,
     up,
     hidden_grad,
     normed_one,
+    ymix,
     resid,
     normed,
     hidden,
@@ -252,13 +234,7 @@
     shared,
     shared_early,
 ):
-    side, channels = scalars[5], ymix.shape[1]
-    first, second = (
-        jnp.where(side == 0, ymix[...], ymix_other[...]),
-        jnp.where(side == 0, ymix_other[...], ymix[...]),
-    )
-    branch = dot(first, whole[:channels]) + dot(second, whole[channels:])
-    resid[...] = tokens[...].astype(F32) + branch
+    resid[...] = tokens[...].astype(F32) + (branch[...].astype(F32) + other[...].astype(F32))
     normed[...] = (resid[...] * norm_scale(resid[...]) * gain[...]).astype(BF16)
     values = normed[...]
     for at in range(0, gate.shape[1], 256):
@@ -427,7 +403,11 @@
 
 
 def narrow_kernel(scalars, one, shared, low, late_other, backs, ymix, *refs):
-    outs, (left_one, left_low) = refs[:4], refs[4:]
+    (small, gain, gain_other), outs, (new_small, left_one, left_low) = refs[:3], refs[3:7], refs[7:]
+    new_small[:8] = gain[...] + gain_other[...]
+    new_small[8:] = small[8:]
+    for pairing in range(3):
+        split_small(new_small[...], outs[pairing], ROUND_ONE[pairing] - 1)
     width = one.shape[1]
     one_other, ymix_other = shared.at[:, :width], shared.at[:, width:]
     for at in range(0, width, 256):
@@ -464,18 +444,17 @@
     return high.astype(F32) + (value - high.astype(F32)).astype(BF16).astype(F32)
 
 
-def sum_small(value, gots, bases):
-    near, far, cross = (join_small(got, base) for got, base in zip(gots, bases))
+def sum_small(value, near, far, cross):
     return (rounded_small(value) + cross) + (near + far)
 
 
+def far_kernel(scalars, mine, got, total, small):
+    total[...] = mine[...].astype(F32) + got[: 4 * NARROW].astype(F32)
+    small[...] = join_small(got, 4 * NARROW)
+
+
 def first_kernel(scalars, *refs):
-    gots, keeps, (small, gain, gain_other) = refs[:2], refs[2:4], refs[4:7]
-    sends, wide_keeps, new_small = refs[10:13], refs[13:15], refs[15]
-    new_small[:8] = gain[...] + gain_other[...]
-    new_small[8:] = small[8:]
-    for pairing in range(3):
-        split_small(new_small[...], sends[pairing], ROUND_ONE[pairing] - 1)
+    gots, keeps, sends, wide_keeps = refs[:2], refs[2:4], refs[6:8], refs[8:]
     for kind in range(2):
         half = 4 * WIDE[kind]
         for chunk in range(4):
@@ -486,7 +465,8 @@
 
 
 def second_kernel(scalars, *refs):
-    gots, wide_in, (narrow, small), sends, (keep, new_small) = refs[:3], refs[3:5], refs[5:7], refs[7:10], refs[10:]
+    gots, wide_in, (narrow, small, cross) = refs[:2], refs[2:4], refs[4:7]
+    sends, (keep, new_small) = refs[7:10], refs[10:]
 
     def fill(chunk, target):
         tile = 0
@@ -495,12 +475,13 @@
             value = wide_in[kind][at].astype(F32) + gots[1 - kind][at].astype(F32)
             target[tile : tile + WIDE[kind]] = value.astype(BF16)
             tile += WIDE[kind]
-        value = narrow[pl.ds(chunk * NARROW, NARROW)].astype(F32)
-        for pairing in range(3):
+        value = narrow[pl.ds(chunk * NARROW, NARROW)]
+        for pairing in range(2):
             value = value + gots[pairing][pl.ds(WIDE_BLOCKS[pairing] + chunk * NARROW, NARROW)].astype(F32)
         target[tile : tile + NARROW] = value.astype(BF16)
 
-    value = sum_small(small[...], gots, [count - 1 for count in ROUND_ONE])
+    near, far = (join_small(got, count - 1) for got, count in zip(gots, ROUND_ONE))
+    value = sum_small(small[...], near, far, cross[...])
     new_small[...] = value
     for pairing in range(3):
         fill(peer(scalars[1], pairing), sends[pairing])
@@ -519,7 +500,7 @@
         zero, one = value[:, :32], value[:, 32:]
         keep[at] = jnp.where(here == 0, zero, one)
         send[at] = jnp.where(here == 0, one, zero).astype(BF16)
-    value = sum_small(small[...], gots, [TILES] * 3)
+    value = sum_small(small[...], *(join_small(got, TILES) for got in gots))
     high = value.astype(BF16)
     low = (value - high.astype(F32)).astype(BF16)
     send[TILES] = high
@@ -597,15 +578,6 @@
     def share(value):
         return swap(value, CORES)
 
-    half = channels // 2
-    whole_half = run(
-        half_kernel,
-        operands=[pltpu.with_memory_space_constraint(out_weight, pltpu.HBM)],
-        outs=[like((half, width), BF16)],
-        scratch=[pltpu.SemaphoreType.DMA],
-        where=pltpu.HBM,
-    )[0]
-    weight_got = swap(whole_half, NEAREST)
     tail, tokens_here, gain_here, weights_here, offset = run(
         load_kernel,
         operands=[
@@ -630,14 +602,14 @@
         operands=[tokens_here, gain_here, weights_here],
         outs=[like((rows, width), BF16), like((3, rows, channels), F32), like((rows, channels), BF16)],
     )
-    conv, ymix = run(
+    conv, ymix, branch = run(
         mix_kernel,
         offset=offset,
-        operands=[gated, incoming, parts, conv_weight],
-        outs=[like((rows, channels), F32), like((rows, channels), BF16)],
-    )
-    ymix, cotangent_late = lax.optimization_barrier((ymix, cotangent))
-    ymix_other = swap(ymix, ACROSS)
+        operands=[gated, incoming, parts, conv_weight, out_weight],
+        outs=[like((rows, channels), F32), like((rows, channels), BF16), like((rows, width), BF16)],
+    )
+    branch, cotangent_late = lax.optimization_barrier((branch, cotangent))
+    branch_other = swap(branch, ACROSS)
     units = gate_weight.shape[1]
     hidden_grad = run(
         hidden_kernel,
@@ -645,14 +617,11 @@
         outs=[like((rows, units), F32)],
         flops=LONG,
     )[0]
-    whole_weight = run(
-        whole_kernel, operands=[out_weight, weight_got, share(weight_got)], outs=[like((2 * channels, width), BF16)]
-    )[0]
-    ymix_other, hidden_grad, whole_weight = lax.optimization_barrier((ymix_other, hidden_grad, whole_weight))
+    branch_other, hidden_grad = lax.optimization_barrier((branch_other, hidden_grad))
     resid, normed_two, hidden, gate_back, up_back, shared, shared_early = run(
         feed_kernel,
-        operands=[tokens, ymix, ymix_other, whole_weight, gain_two_row, gate_weight, up_weight, hidden_grad]
-        + [normed_one],
+        operands=[tokens, branch, branch_other, gain_two_row, gate_weight, up_weight, hidden_grad]
+        + [normed_one, ymix],
         outs=[like((rows, width), F32), like((rows, width), BF16)]
         + [like((rows, units), BF16)] * 3
         + [like((rows, 3 * WIDE_COLUMNS + width), BF16), like((rows, width + channels // 2), BF16)],
@@ -711,27 +680,32 @@
             like((32, 128), F32),
         ],
     )
-    *sends, narrow = run(
+    gain_other = swap(gain_part, ACROSS)
+    *sends, narrow, small = run(
         narrow_kernel,
-        operands=[normed_one, early_other, resid_low, share(shared), backs, ymix],
-        outs=blocks(ROUND_ONE) + blocks([4 * NARROW]),
+        operands=[normed_one, early_other, resid_low, share(shared), backs, ymix, small, gain_part, gain_other],
+        outs=blocks(ROUND_ONE) + blocks([4 * NARROW]) + [like((32, 128), F32)],
         scratch=[pltpu.VMEM((width, 2 * rows), BF16)] * 2,
     )
-    gain_other = swap(gain_part, ACROSS)
-    gots[0], gots[1], narrow, gain_other = lax.optimization_barrier((gots[0], gots[1], narrow, gain_other))
+    narrow, cross = run(
+        far_kernel,
+        operands=[narrow, swap(sends.pop(), FIRST[2])],
+        outs=[like((4 * NARROW, *BLOCK), F32), like((32, 128), F32)],
+        flops=LONG,
+    )
     results = run(
         first_kernel,
-        operands=gots + keeps + [small, gain_part, gain_other] + sends,
-        aliases={7: 0, 8: 1, 9: 2},
-        outs=blocks(ROUND_ONE) + blocks([4 * count for count in WIDE]) + [like((32, 128), F32)],
-    )
-    sends, keeps, small = list(results[:3]), list(results[3:5]), results[5]
+        operands=gots + keeps + sends,
+        aliases={4: 0, 5: 1},
+        outs=blocks(ROUND_ONE[:2]) + blocks([4 * count for count in WIDE]),
+    )
+    sends, keeps = list(results[:2]), list(results[2:])
     gots = swap_round(sends, FIRST)
     norm_one_other = swap(norm_one_part, ACROSS)
     gots[0], norm_one_other = lax.optimization_barrier((gots[0], norm_one_other))
     results = run(
         second_kernel,
-        operands=gots + keeps + [narrow, small],
+        operands=gots + keeps + [narrow, small, cross],
         outs=blocks([TILES + 1] * 3 + [TILES]) + [like((32, 128), F32)],
     )
     sends, keep, small = list(results[:3]), results[3], results[4]

time: 125 us -> 126 us (level)
  starting transfers between devices: 38.9 us -> 48.2 us
  waiting for transfers between devices: 52.4 us -> 47.9 us
  Pallas kernels: 27.8 us -> 25.4 us
    ppermute x21 -> x19, starting transfers between devices: 34.1 us -> 42 us  [swap(): return lax.ppermute(value, AXES, pairs)]
    ppermute x21 -> x19, waiting for transfers between devices: 51.6 us -> 46 us  [swap(): return lax.ppermute(value, AXES, pairs)]
    pallas_call x20 -> x19, Pallas kernels: 27.8 us -> 25.4 us  [call(): pl.pallas_call(kernel, out_shape=tuple(outs), in_specs=specs, out_specs=t...]
    ppermute x2, starting transfers between devices: 4.83 us -> 6.27 us  [from_behind(): lax.ppermute(value, axis, [(source, source + steps) for source in range(l...]
  transfers between devices with their start and end apart: 23 -> 21, of which waited for: 13 -> 13; matrix products, arithmetic and copies ran while one was open for 2% -> 2% of each run, Pallas kernels for 17% -> 16%
where the time goes in v6:
time: 126 us
  starting transfers between devices  48.2 us (38%)
  waiting for transfers between devices  47.9 us (38%)
  Pallas kernels  25.4 us (20%)
  other arithmetic  2.82 us (2%)
  between operations  1.63 us (1%)
    ppermute x19, waiting for transfers between devices, swap(): return lax.ppermute(value, AXES, pairs)  46 us
    ppermute x19, starting transfers between devices, swap(): return lax.ppermute(value, AXES, pairs)  42 us
    pallas_call x19, Pallas kernels, call(): pl.pallas_call(kernel, out_shape=tuple(outs), in_specs=specs, out_specs=t...  25.4 us
    ppermute x2, starting transfers between devices, from_behind(): lax.ppermute(value, axis, [(source, source + steps) for source in range(l...  6.27 us
  transfers between devices with their start and end apart: 21, of which 13 were waited for; matrix products, arithmetic and copies ran while one was open for 2% of the time, Pallas kernels for 16%

profile of v6, /device:TPU:1, one launch (start us, length us, event | category | flops | bytes accessed | tf_op | source)
XLA Modules:
  0.0 126.1 jit_solution(16361465209425625963)
XLA Ops:
  2.8 2.3 %shard_map.186 = (bf16[16,512]{1,0:T(8,128)(2,1)S(1)}, bf16[256,1024]{1,0:T(8,128)(2,1)S(1)}, f32[1,1024]{1,0:T(1,128)S(1)}, bf16[3,1024,512]{2,1,0:T(8,128)(2,1)S(1)}, s32[8,128]{1,0:T(8,128)S(1)}) custom-call(s32[1]{0:T(128)S(6)} %copy.25.refs_0_, bf16[256,1024]{1,0:T(8,128)(2,1)} %refs_6_.5, f32[1,1024]{1,0:T(1,128)} %bitcast.17, ...), custom_call_target="tpu_custom_call" | custom-call | tf_op jit(solution)/shard_map/pallas_call | solution.py:117
  5.1 3.1 %collective-permute-start = (bf16[16,512]{1,0:T(8,128)(2,1)S(1)}, bf16[16,512]{1,0:T(8,128)(2,1)S(1)}, u32[]{:S(2)}, u32[]{:S(2)}) collective-permute-start(bf16[16,512]{1,0:T(8,128)(2,1)S(1)} %get-tuple-element.96), channel_id=1, source_target_pairs={{0,2},{2,4},{4,6},{6,8},{8,10},{10,12},{12,14},{14,16},{16,18},{18... | collective-permute-start | bytes 49160 | tf_op jit(solution)/shard_map/ppermute | solution.py:79
  10.1 2.5 %collective-permute-start.2 = (bf16[256,1024]{1,0:T(8,128)(2,1)S(1)}, bf16[256,1024]{1,0:T(8,128)(2,1)S(1)}, u32[]{:S(2)}, u32[]{:S(2)}) collective-permute-start(bf16[256,1024]{1,0:T(8,128)(2,1)S(1)} %get-tuple-element.100.refs_1_), channel_id=1, source_target_pairs={{0,1},{2,3},{4,5},{6,7},{1,0},{3,2},{5,4},{7,6},{8,9},{10,11},{12,... | collective-permute-start | bytes 1572872 | tf_op jit(solution)/shard_map/ppermute | solution.py:73
  14.1 11.1 %collective-permute-done.2.refs_2_ = bf16[256,1024]{1,0:T(8,128)(2,1)S(1)} collective-permute-done((bf16[256,1024]{1,0:T(8,128)(2,1)S(1)}, bf16[256,1024]{1,0:T(8,128)(2,1)S(1)}, u32[]{:S(2)}, u32[]{:S(2)}) %collective-permute-start.2) | collective-permute-done | bytes 524320 | tf_op jit(solution)/shard_map/ppermute | solution.py:73
  25.3 3.4 %shard_map.190 = (f32[256,1024]{1,0:T(8,128)S(1)}, bf16[256,1024]{1,0:T(8,128)(2,1)S(1)}, bf16[256,2304]{1,0:T(8,128)(2,1)S(1)}, bf16[256,2304]{1,0:T(8,128)(2,1...) custom-call(bf16[256,1024]{1,0:T(8,128)(2,1)S(1)} %copy-done, ...), custom_call_target="tpu_custom_call" | custom-call | tf_op jit(solution)/shard_map/pallas_call | solution.py:117
  29.3 2.6 %shard_map.193.refs_1_ = bf16[256,1024]{1,0:T(8,128)(2,1)S(1)} custom-call(bf16[256,2304]{1,0:T(8,128)(2,1)S(1)} %get-tuple-element.109.refs_4_.refs_1_.refs_0_, bf16[256,2304]{1,0:T(8,128)(2,1)S(1)} %get-tuple-element.113.refs_2_.refs_1_, bf16[1024,2304]{1,0:T(8,128)(2,1)S(1)} %bitcast.9, bf16[1024,2304]{1,0:T(8,128)(2,1)S(1)} %bitcast.11), custom_call_target="tpu_custom_call" | custom-call | tf_op jit(solution)/shard_map/pallas_call | solution.py:117
  31.9 3.0 %collective-permute-start.6 = (bf16[256,1024]{1,0:T(8,128)(2,1)S(1)}, bf16[256,1024]{1,0:T(8,128)(2,1)S(1)}, u32[]{:S(2)}, u32[]{:S(2)}) collective-permute-start(bf16[256,1024]{1,0:T(8,128)(2,1)S(1)} %shard_map.193.refs_1_), channel_id=1, source_target_pairs={{0,1},{2,3},{4,5},{6,7},{1,0},{3,2},{5,4},{7,6},{8,9},{10,11},{12,... | collective-permute-start | bytes 1572872 | tf_op jit(solution)/shard_map/ppermute | solution.py:73
  36.3 2.8 %shard_map.191 = (bf16[112,64,128]{2,1,0:T(8,128)(2,1)S(1)}, bf16[112,64,128]{2,1,0:T(8,128)(2,1)S(1)}, bf16[1024,512]{1,0:T(8,128)(2,1)S(1)}) custom-call(bf16[256,1024]{1,0:T(8,128)(2,1)S(1)} %get-tuple-element.106.refs_0_, bf16[256,1024]{1,0:T(8,128)(2,1)S(1)} %copy-done.4, bf16[256,1024]{1,0:T(8,128)(2,1)S(1)} %collective-permute-done.1.refs_2_, ...), custom_call_target="tpu_custom_call" | custom-call | tf_op jit(solution)/shard_map/pallas_call | solution.py:117
  41.0 2.1 %shard_map.192 = (bf16[104,64,128]{2,1,0:T(8,128)(2,1)S(1)}, bf16[104,64,128]{2,1,0:T(8,128)(2,1)S(1)}) custom-call(bf16[1024,512]{1,0:T(8,128)(2,1)S(1)} %get-tuple-element.112.refs_0_, bf16[256,2304]{1,0:T(8,128)(2,1)S(1)} %get-tuple-element.109.refs_4_.refs_1_.refs_0_, bf16[256,2304]{1,0:T(8,128)(2,1)S(1)} %get-tuple-element.113.refs_2_.refs_1_, ...), custom_call_target="tpu_custom_call" | custom-call | tf_op jit(solution)/shard_map/pallas_call | solution.py:117
  43.1 2.3 %collective-permute-start.5 = (bf16[104,64,128]{2,1,0:T(8,128)(2,1)S(1)}, bf16[104,64,128]{2,1,0:T(8,128)(2,1)S(1)}, u32[]{:S(2)}, u32[]{:S(2)}) collective-permute-start(bf16[104,64,128]{2,1,0:T(8,128)(2,1)S(1)} %get-tuple-element.114), channel_id=1, source_target_pairs={{0,96},{2,26},{4,100},{6,30},{1,97},{3,27},{5,101},{7,31},{8,104},... | collective-permute-start | bytes 5111816 | tf_op jit(solution)/shard_map/ppermute | solution.py:73
  47.0 3.2 %collective-permute-start.8 = (f32[8,512]{1,0:T(8,128)S(1)}, f32[8,512]{1,0:T(8,128)S(1)}, u32[]{:S(2)}, u32[]{:S(2)}) collective-permute-start(f32[8,512]{1,0:T(8,128)S(1)} %shard_map.196), channel_id=1, source_target_pairs={{2,0},{4,2},{6,4},{8,6},{10,8},{12,10},{14,12},{16,14},{18,16},{20... | collective-permute-start | bytes 49160 | tf_op jit(solution)/shard_map/ppermute | solution.py:79
  55.1 2.8 %collective-permute-start.10 = (f32[8,128]{1,0:T(8,128)S(1)}, f32[8,128]{1,0:T(8,128)S(1)}, u32[]{:S(2)}, u32[]{:S(2)}) collective-permute-start(f32[8,128]{1,0:T(8,128)S(1)} %get-tuple-element.131.refs_7_), channel_id=1, source_target_pairs={{0,1},{2,3},{4,5},{6,7},{1,0},{3,2},{5,4},{7,6},{8,9},{10,11},{12,... | collective-permute-start | bytes 12296 | tf_op jit(solution)/shard_map/ppermute | solution.py:73
  60.9 3.4 %collective-permute-start.14 = (bf16[33,64,128]{2,1,0:T(8,128)(2,1)S(1)}, bf16[33,64,128]{2,1,0:T(8,128)(2,1)S(1)}, u32[]{:S(2)}, u32[]{:S(2)}) collective-permute-start(bf16[33,64,128]{2,1,0:T(8,128)(2,1)S(1)} %get-tuple-element.141), channel_id=1, source_target_pairs={{0,64},{2,18},{4,68},{6,22},{1,65},{3,19},{5,69},{7,23},{8,72},{10... | collective-permute-start | bytes 1622024 | tf_op jit(solution)/shard_map/ppermute | solution.py:73
  64.3 3.0 %collective-permute-start.12 = (bf16[256,1024]{1,0:T(8,128)(2,1)S(1)}, bf16[256,1024]{1,0:T(8,128)(2,1)S(1)}, u32[]{:S(2)}, u32[]{:S(2)}) collective-permute-start(bf16[256,1024]{1,0:T(8,128)(2,1)S(1)} %get-tuple-element.135), channel_id=1, source_target_pairs={{0,1},{2,3},{4,5},{6,7},{1,0},{3,2},{5,4},{7,6},{8,9},{10,11},{12,... | collective-permute-start | bytes 1572872 | tf_op jit(solution)/shard_map/ppermute | solution.py:73
  69.0 2.3 %collective-permute-done.14.refs_1_ = bf16[33,64,128]{2,1,0:T(8,128)(2,1)S(1)} collective-permute-done((bf16[33,64,128]{2,1,0:T(8,128)(2,1)S(1)}, bf16[33,64,128]{2,1,0:T(8,128)(2,1)S(1)}, u32[]{:S(2)}, u32[]{:S(2)}) %collective-permute-start.14) | collective-permute-done | bytes 540704 | tf_op jit(solution)/shard_map/ppermute | solution.py:73
  71.4 5.6 %collective-permute-done.12 = bf16[256,1024]{1,0:T(8,128)(2,1)S(1)} collective-permute-done((bf16[256,1024]{1,0:T(8,128)(2,1)S(1)}, bf16[256,1024]{1,0:T(8,128)(2,1)S(1)}, u32[]{:S(2)}, u32[]{:S(2)}) %collective-permute-start.12) | collective-permute-done | bytes 524320 | tf_op jit(solution)/shard_map/ppermute | solution.py:73
  77.0 9.2 %collective-permute-done.11.refs_0_ = bf16[85,64,128]{2,1,0:T(8,128)(2,1)S(1)} collective-permute-done((bf16[85,64,128]{2,1,0:T(8,128)(2,1)S(1)}, bf16[85,64,128]{2,1,0:T(8,128)(2,1)S(1)}, u32[]{:S(2)}, u32[]{:S(2)}) %collective-permute-start.11) | collective-permute-done | bytes 1392672 | tf_op jit(solution)/shard_map/ppermute | solution.py:73
  89.5 2.1 %collective-permute-start.17 = (bf16[36,64,128]{2,1,0:T(8,128)(2,1)S(1)}, bf16[36,64,128]{2,1,0:T(8,128)(2,1)S(1)}, u32[]{:S(2)}, u32[]{:S(2)}) collective-permute-start(bf16[36,64,128]{2,1,0:T(8,128)(2,1)S(1)} %get-tuple-element.150), channel_id=1, source_target_pairs={{0,24},{2,98},{4,28},{6,102},{1,25},{3,99},{5,29},{7,103},{8,16},{... | collective-permute-start | bytes 1769480 | tf_op jit(solution)/shard_map/ppermute | solution.py:73
  92.7 2.7 %collective-permute-start.16 = (bf16[256,1024]{1,0:T(8,128)(2,1)S(1)}, bf16[256,1024]{1,0:T(8,128)(2,1)S(1)}, u32[]{:S(2)}, u32[]{:S(2)}) collective-permute-start(bf16[256,1024]{1,0:T(8,128)(2,1)S(1)} %shard_map.194), channel_id=1, source_target_pairs={{0,1},{2,3},{4,5},{6,7},{1,0},{3,2},{5,4},{7,6},{8,9},{10,11},{12,... | collective-permute-start | bytes 1572872 | tf_op jit(solution)/shard_map/ppermute | solution.py:73
  95.8 6.4 %collective-permute-done.16 = bf16[256,1024]{1,0:T(8,128)(2,1)S(1)} collective-permute-done((bf16[256,1024]{1,0:T(8,128)(2,1)S(1)}, bf16[256,1024]{1,0:T(8,128)(2,1)S(1)}, u32[]{:S(2)}, u32[]{:S(2)}) %collective-permute-start.16) | collective-permute-done | bytes 524320 | tf_op jit(solution)/shard_map/ppermute | solution.py:73
  102.2 2.5 %collective-permute-done.17.refs_1_ = bf16[36,64,128]{2,1,0:T(8,128)(2,1)S(1)} collective-permute-done((bf16[36,64,128]{2,1,0:T(8,128)(2,1)S(1)}, bf16[36,64,128]{2,1,0:T(8,128)(2,1)S(1)}, u32[]{:S(2)}, u32[]{:S(2)}) %collective-permute-start.17) | collective-permute-done | bytes 589856 | tf_op jit(solution)/shard_map/ppermute | solution.py:73
  106.6 4.6 %collective-permute-start.19 = (bf16[37,32,128]{2,1,0:T(8,128)(2,1)S(1)}, bf16[37,32,128]{2,1,0:T(8,128)(2,1)S(1)}, u32[]{:S(2)}, u32[]{:S(2)}) collective-permute-start(bf16[37,32,128]{2,1,0:T(8,128)(2,1)S(1)} %get-tuple-element.154), channel_id=1, source_target_pairs={{0,4},{2,6},{4,0},{6,2},{1,5},{3,7},{5,1},{7,3},{8,12},{10,14},{12... | collective-permute-start | bytes 909320 | tf_op jit(solution)/shard_map/ppermute | solution.py:73
  113.6 2.1 %collective-permute-done.19.refs_1_ = bf16[37,32,128]{2,1,0:T(8,128)(2,1)S(1)} collective-permute-done((bf16[37,32,128]{2,1,0:T(8,128)(2,1)S(1)}, bf16[37,32,128]{2,1,0:T(8,128)(2,1)S(1)}, u32[]{:S(2)}, u32[]{:S(2)}) %collective-permute-start.19) | collective-permute-done | bytes 303136 | tf_op jit(solution)/shard_map/ppermute | solution.py:73
  115.8 8.3 %collective-permute-start.20 = (f32[37,16,128]{2,1,0:T(8,128)S(1)}, f32[37,16,128]{2,1,0:T(8,128)S(1)}, u32[]{:S(2)}, u32[]{:S(2)}) collective-permute-start(f32[37,16,128]{2,1,0:T(8,128)S(1)} %get-tuple-element.163), channel_id=1, source_target_pairs={{0,2},{2,0},{4,6},{6,4},{1,3},{3,1},{5,7},{7,5},{8,10},{10,8},{12,... | collective-permute-start | bytes 909320 | tf_op jit(solution)/shard_map/ppermute | solution.py:73
  (67 shorter events, 31.0 us)
Async XLA Ops:
  0.6 8.8 %collective-permute-start.1 = (bf16[256,1024]{1,0:T(8,128)(2,1)}, bf16[256,1024]{1,0:T(8,128)(2,1)S(1)}, u32[]{:S(2)}, u32[]{:S(2)}) collective-permute-start(bf16[256,1024]{1,0:T(8,128)(2,1)} %refs_5_.7), channel_id=1, source_target_pairs={{0,2},{2,0},{4,6},{6,4},{1,3},{3,1},{5,7},{7,5},{8,10},{10,8},{12,... | collective-permute-start | bytes 1572872 | tf_op jit(solution)/shard_map/ppermute | solution.py:73
  5.1 4.3 %collective-permute-start = (bf16[16,512]{1,0:T(8,128)(2,1)S(1)}, bf16[16,512]{1,0:T(8,128)(2,1)S(1)}, u32[]{:S(2)}, u32[]{:S(2)}) collective-permute-start(bf16[16,512]{1,0:T(8,128)(2,1)S(1)} %get-tuple-element.96), channel_id=1, source_target_pairs={{0,2},{2,4},{4,6},{6,8},{8,10},{10,12},{12,14},{14,16},{16,18},{18... | collective-permute-start | bytes 49160 | tf_op jit(solution)/shard_map/ppermute | solution.py:79
  10.0 15.2 %slice-start = ((s8[4718592]{0:T(1024)(128)(4,1)}), s8[4194304]{0:T(1024)(128)(4,1)S(1)}, s32[]{:S(2)}) async-start(s8[4718592]{0:T(1024)(128)(4,1)} %bitcast.8), calls=%async_computation | async-start | bytes 8388608
  10.1 15.1 %slice-start.2 = ((s8[4718592]{0:T(1024)(128)(4,1)}), s8[4194304]{0:T(1024)(128)(4,1)S(1)}, s32[]{:S(2)}) async-start(s8[4718592]{0:T(1024)(128)(4,1)} %bitcast.10), calls=%async_computation.2 | async-start | bytes 8388608
  10.1 15.1 %slice-start.1 = ((s8[4718592]{0:T(1024)(128)(4,1)}), s8[524288]{0:T(1024)(128)(4,1)S(1)}, s32[]{:S(2)}) async-start(s8[4718592]{0:T(1024)(128)(4,1)} %bitcast.8), calls=%async_computation.1 | async-start | bytes 1048576
  10.1 15.1 %collective-permute-start.2 = (bf16[256,1024]{1,0:T(8,128)(2,1)S(1)}, bf16[256,1024]{1,0:T(8,128)(2,1)S(1)}, u32[]{:S(2)}, u32[]{:S(2)}) collective-permute-start(bf16[256,1024]{1,0:T(8,128)(2,1)S(1)} %get-tuple-element.100.refs_1_), channel_id=1, source_target_pairs={{0,1},{2,3},{4,5},{6,7},{1,0},{3,2},{5,4},{7,6},{8,9},{10,11},{12,... | collective-permute-start | bytes 1572872 | tf_op jit(solution)/shard_map/ppermute | solution.py:73
  28.6 7.7 %collective-permute-start.3 = (bf16[256,4480]{1,0:T(8,128)(2,1)S(1)}, bf16[256,4480]{1,0:T(8,128)(2,1)S(1)}, u32[]{:S(2)}, u32[]{:S(2)}) collective-permute-start(bf16[256,4480]{1,0:T(8,128)(2,1)S(1)} %get-tuple-element.110), channel_id=1, source_target_pairs={{0,2},{2,0},{4,6},{6,4},{1,3},{3,1},{5,7},{7,5},{8,10},{10,8},{12,... | collective-permute-start | bytes 6881288 | tf_op jit(solution)/shard_map/ppermute | solution.py:73
  29.2 17.4 %collective-permute-start.7 = (bf16[256,1280]{1,0:T(8,128)(2,1)S(1)}, bf16[256,1280]{1,0:T(8,128)(2,1)S(1)}, u32[]{:S(2)}, u32[]{:S(2)}) collective-permute-start(bf16[256,1280]{1,0:T(8,128)(2,1)S(1)} %get-tuple-element.117), channel_id=1, source_target_pairs={{0,2},{2,0},{4,6},{6,4},{1,3},{3,1},{5,7},{7,5},{8,10},{10,8},{12,... | collective-permute-start | bytes 1966088 | tf_op jit(solution)/shard_map/ppermute | solution.py:73
  31.9 14.7 %collective-permute-start.6 = (bf16[256,1024]{1,0:T(8,128)(2,1)S(1)}, bf16[256,1024]{1,0:T(8,128)(2,1)S(1)}, u32[]{:S(2)}, u32[]{:S(2)}) collective-permute-start(bf16[256,1024]{1,0:T(8,128)(2,1)S(1)} %shard_map.193.refs_1_), channel_id=1, source_target_pairs={{0,1},{2,3},{4,5},{6,7},{1,0},{3,2},{5,4},{7,6},{8,9},{10,11},{12,... | collective-permute-start | bytes 1572872 | tf_op jit(solution)/shard_map/ppermute | solution.py:73
  39.1 28.2 %collective-permute-start.4 = (bf16[112,64,128]{2,1,0:T(8,128)(2,1)S(1)}, bf16[112,64,128]{2,1,0:T(8,128)(2,1)S(1)}, u32[]{:S(2)}, u32[]{:S(2)}) collective-permute-start(bf16[112,64,128]{2,1,0:T(8,128)(2,1)S(1)} %get-tuple-element.111), channel_id=1, source_target_pairs={{0,32},{2,10},{4,36},{6,14},{1,33},{3,11},{5,37},{7,15},{8,40},{10... | collective-permute-start | bytes 5505032 | tf_op jit(solution)/shard_map/ppermute | solution.py:73
  43.1 24.2 %collective-permute-start.5 = (bf16[104,64,128]{2,1,0:T(8,128)(2,1)S(1)}, bf16[104,64,128]{2,1,0:T(8,128)(2,1)S(1)}, u32[]{:S(2)}, u32[]{:S(2)}) collective-permute-start(bf16[104,64,128]{2,1,0:T(8,128)(2,1)S(1)} %get-tuple-element.114), channel_id=1, source_target_pairs={{0,96},{2,26},{4,100},{6,30},{1,97},{3,27},{5,101},{7,31},{8,104},... | collective-permute-start | bytes 5111816 | tf_op jit(solution)/shard_map/ppermute | solution.py:73
  47.0 6.8 %collective-permute-start.8 = (f32[8,512]{1,0:T(8,128)S(1)}, f32[8,512]{1,0:T(8,128)S(1)}, u32[]{:S(2)}, u32[]{:S(2)}) collective-permute-start(f32[8,512]{1,0:T(8,128)S(1)} %shard_map.196), channel_id=1, source_target_pairs={{2,0},{4,2},{6,4},{8,6},{10,8},{12,10},{14,12},{16,14},{18,16},{20... | collective-permute-start | bytes 49160 | tf_op jit(solution)/shard_map/ppermute | solution.py:79
  55.0 4.1 %collective-permute-start.9 = (bf16[7,256,256]{2,1,0:T(8,128)(2,1)S(1)}, bf16[7,256,256]{2,1,0:T(8,128)(2,1)S(1)}, u32[]{:S(2)}, u32[]{:S(2)}) collective-permute-start(bf16[7,256,256]{2,1,0:T(8,128)(2,1)S(1)} %get-tuple-element.128), channel_id=1, source_target_pairs={{0,2},{2,0},{4,6},{6,4},{1,3},{3,1},{5,7},{7,5},{8,10},{10,8},{12,... | collective-permute-start | bytes 2752520 | tf_op jit(solution)/shard_map/ppermute | solution.py:73
  55.1 4.0 %collective-permute-start.10 = (f32[8,128]{1,0:T(8,128)S(1)}, f32[8,128]{1,0:T(8,128)S(1)}, u32[]{:S(2)}, u32[]{:S(2)}) collective-permute-start(f32[8,128]{1,0:T(8,128)S(1)} %get-tuple-element.131.refs_7_), channel_id=1, source_target_pairs={{0,1},{2,3},{4,5},{6,7},{1,0},{3,2},{5,4},{7,6},{8,9},{10,11},{12,... | collective-permute-start | bytes 12296 | tf_op jit(solution)/shard_map/ppermute | solution.py:73
  60.9 10.4 %collective-permute-start.14 = (bf16[33,64,128]{2,1,0:T(8,128)(2,1)S(1)}, bf16[33,64,128]{2,1,0:T(8,128)(2,1)S(1)}, u32[]{:S(2)}, u32[]{:S(2)}) collective-permute-start(bf16[33,64,128]{2,1,0:T(8,128)(2,1)S(1)} %get-tuple-element.141), channel_id=1, source_target_pairs={{0,64},{2,18},{4,68},{6,22},{1,65},{3,19},{5,69},{7,23},{8,72},{10... | collective-permute-start | bytes 1622024 | tf_op jit(solution)/shard_map/ppermute | solution.py:73
  64.3 12.7 %collective-permute-start.12 = (bf16[256,1024]{1,0:T(8,128)(2,1)S(1)}, bf16[256,1024]{1,0:T(8,128)(2,1)S(1)}, u32[]{:S(2)}, u32[]{:S(2)}) collective-permute-start(bf16[256,1024]{1,0:T(8,128)(2,1)S(1)} %get-tuple-element.135), channel_id=1, source_target_pairs={{0,1},{2,3},{4,5},{6,7},{1,0},{3,2},{5,4},{7,6},{8,9},{10,11},{12,... | collective-permute-start | bytes 1572872 | tf_op jit(solution)/shard_map/ppermute | solution.py:73
  68.1 18.1 %collective-permute-start.11 = (bf16[85,64,128]{2,1,0:T(8,128)(2,1)S(1)}, bf16[85,64,128]{2,1,0:T(8,128)(2,1)S(1)}, u32[]{:S(2)}, u32[]{:S(2)}) collective-permute-start(bf16[85,64,128]{2,1,0:T(8,128)(2,1)S(1)} %get-tuple-element.134), channel_id=1, source_target_pairs={{0,32},{2,10},{4,36},{6,14},{1,33},{3,11},{5,37},{7,15},{8,40},{10... | collective-permute-start | bytes 4177928 | tf_op jit(solution)/shard_map/ppermute | solution.py:73
  68.2 19.6 %collective-permute-start.13 = (bf16[89,64,128]{2,1,0:T(8,128)(2,1)S(1)}, bf16[89,64,128]{2,1,0:T(8,128)(2,1)S(1)}, u32[]{:S(2)}, u32[]{:S(2)}) collective-permute-start(bf16[89,64,128]{2,1,0:T(8,128)(2,1)S(1)} %get-tuple-element.137), channel_id=1, source_target_pairs={{0,96},{2,26},{4,100},{6,30},{1,97},{3,27},{5,101},{7,31},{8,104},... | collective-permute-start | bytes 4374536 | tf_op jit(solution)/shard_map/ppermute | solution.py:73
  88.4 13.8 %collective-permute-start.15 = (bf16[36,64,128]{2,1,0:T(8,128)(2,1)S(1)}, bf16[36,64,128]{2,1,0:T(8,128)(2,1)S(1)}, u32[]{:S(2)}, u32[]{:S(2)}) collective-permute-start(bf16[36,64,128]{2,1,0:T(8,128)(2,1)S(1)} %get-tuple-element.145), channel_id=1, source_target_pairs={{0,8},{2,34},{4,12},{6,38},{1,9},{3,35},{5,13},{7,39},{8,0},{10,42... | collective-permute-start | bytes 1769480 | tf_op jit(solution)/shard_map/ppermute | solution.py:73
  89.5 15.3 %collective-permute-start.17 = (bf16[36,64,128]{2,1,0:T(8,128)(2,1)S(1)}, bf16[36,64,128]{2,1,0:T(8,128)(2,1)S(1)}, u32[]{:S(2)}, u32[]{:S(2)}) collective-permute-start(bf16[36,64,128]{2,1,0:T(8,128)(2,1)S(1)} %get-tuple-element.150), channel_id=1, source_target_pairs={{0,24},{2,98},{4,28},{6,102},{1,25},{3,99},{5,29},{7,103},{8,16},{... | collective-permute-start | bytes 1769480 | tf_op jit(solution)/shard_map/ppermute | solution.py:73
  91.6 14.7 %collective-permute-start.18 = (bf16[36,64,128]{2,1,0:T(8,128)(2,1)S(1)}, bf16[36,64,128]{2,1,0:T(8,128)(2,1)S(1)}, u32[]{:S(2)}, u32[]{:S(2)}) collective-permute-start(bf16[36,64,128]{2,1,0:T(8,128)(2,1)S(1)} %get-tuple-element.151), channel_id=1, source_target_pairs={{0,16},{2,66},{4,20},{6,70},{1,17},{3,67},{5,21},{7,71},{8,24},{10... | collective-permute-start | bytes 1769480 | tf_op jit(solution)/shard_map/ppermute | solution.py:73
  92.7 9.5 %collective-permute-start.16 = (bf16[256,1024]{1,0:T(8,128)(2,1)S(1)}, bf16[256,1024]{1,0:T(8,128)(2,1)S(1)}, u32[]{:S(2)}, u32[]{:S(2)}) collective-permute-start(bf16[256,1024]{1,0:T(8,128)(2,1)S(1)} %shard_map.194), channel_id=1, source_target_pairs={{0,1},{2,3},{4,5},{6,7},{1,0},{3,2},{5,4},{7,6},{8,9},{10,11},{12,... | collective-permute-start | bytes 1572872 | tf_op jit(solution)/shard_map/ppermute | solution.py:73
  106.6 9.1 %collective-permute-start.19 = (bf16[37,32,128]{2,1,0:T(8,128)(2,1)S(1)}, bf16[37,32,128]{2,1,0:T(8,128)(2,1)S(1)}, u32[]{:S(2)}, u32[]{:S(2)}) collective-permute-start(bf16[37,32,128]{2,1,0:T(8,128)(2,1)S(1)} %get-tuple-element.154), channel_id=1, source_target_pairs={{0,4},{2,6},{4,0},{6,2},{1,5},{3,7},{5,1},{7,3},{8,12},{10,14},{12... | collective-permute-start | bytes 909320 | tf_op jit(solution)/shard_map/ppermute | solution.py:73
  115.8 9.5 %collective-permute-start.20 = (f32[37,16,128]{2,1,0:T(8,128)S(1)}, f32[37,16,128]{2,1,0:T(8,128)S(1)}, u32[]{:S(2)}, u32[]{:S(2)}) collective-permute-start(f32[37,16,128]{2,1,0:T(8,128)S(1)} %get-tuple-element.163), channel_id=1, source_target_pairs={{0,2},{2,0},{4,6},{6,4},{1,3},{3,1},{5,7},{7,5},{8,10},{10,8},{12,... | collective-permute-start | bytes 909320 | tf_op jit(solution)/shard_map/ppermute | solution.py:73
  (9 other events, 77.6 us)

commit v7 on v6

--- a/solution.py
+++ b/solution.py
@@ -28,6 +28,7 @@
 
 ACROSS = device_pairs(lambda y, z, x, core: (y, z, (x + 2) % 4, core))
 BESIDE = device_pairs(lambda y, z, x, core: (y, z, x ^ 1, core))
+SKEW = device_pairs(lambda y, z, x, core: (y, z, (x ^ 1) ^ 2, core))
 CORES = device_pairs(lambda y, z, x, core: (y, z, x, 1 - core))
 
 
@@ -312,7 +313,6 @@
     backs,
     shared,
     part,
-    gain_part,
     small,
 ):
     rows = gated_back.shape[0]
@@ -332,13 +332,12 @@
     gain_grad = jnp.sum(grad * values * norm_scale(values), axis=0, keepdims=True)
     for at in range(8):
         lanes = slice(at * 128, at * 128 + 128)
-        gain_part[at : at + 1] = gain_grad[:, lanes]
+        small[at : at + 1] = gain_grad[:, lanes]
         small[8 + at : 9 + at] = gain_two_grad[:, lanes]
     for lag in range(3):
         for at in range(4):
             row = 16 + 4 * lag + at
             small[row : row + 1] = tap_grads[lag : lag + 1, at * 128 : at * 128 + 128]
-    small[:8] = jnp.zeros((8, 128), F32)
     small[28:32] = jnp.zeros((4, 128), F32)
 
 
@@ -403,11 +402,9 @@
 
 
 def narrow_kernel(scalars, one, shared, low, late_other, backs, ymix, *refs):
-    (small, gain, gain_other), outs, (new_small, left_one, left_low) = refs[:3], refs[3:7], refs[7:]
-    new_small[:8] = gain[...] + gain_other[...]
-    new_small[8:] = small[8:]
+    small, outs, (left_one, left_low) = refs[0], refs[1:5], refs[5:]
     for pairing in range(3):
-        split_small(new_small[...], outs[pairing], ROUND_ONE[pairing] - 1)
+        split_small(small[...], outs[pairing], ROUND_ONE[pairing] - 1)
     width = one.shape[1]
     one_other, ymix_other = shared.at[:, :width], shared.at[:, width:]
     for at in range(0, width, 256):
@@ -490,7 +487,7 @@
 
 
 def third_kernel(scalars, *refs):
-    gots, (kept, small), (send, keep) = refs[:3], refs[3:5], refs[5:]
+    gots, (kept, small), (send, keep, gain) = refs[:3], refs[3:5], refs[5:]
     here = scalars[2]
     for first in range(0, TILES, 7):
         at = slice(first, first + 7)
@@ -505,19 +502,32 @@
     low = (value - high.astype(F32)).astype(BF16)
     send[TILES] = high
     send[TILES + 1] = low
+    gain[...] = high[:8].astype(F32) + low[:8].astype(F32)
     keep[TILES] = high.astype(F32)
     keep[TILES + 1] = low.astype(F32)
 
 
-def cores_kernel(scalars, keep, got, mine, away):
+def finish_kernel(
+    scalars, resid, down, down_other, part, other, tokens, resid_grad, gain, mixed, tokens_grad
+):
+    mixed[...] = (resid[...] + (down[...].astype(F32) + down_other[...].astype(F32))).astype(BF16)
+    values = tokens[...].astype(F32)
+    back = part[...].astype(F32) + other[...].astype(F32)
+    tokens_grad[...] = resid_grad[...] + norm_backward(back, values, norm_scale(values), gain[...])
+
+
+def cores_kernel(scalars, keep, got, across, skew, mine, away):
     core = scalars[3]
     total = keep[:TILES] + got[:TILES].astype(F32)
     zero, one = total[:, :16], total[:, 16:]
     mine[:TILES] = jnp.where(core == 0, zero, one)
     away[:TILES] = jnp.where(core == 0, one, zero)
-    small = (keep[TILES] + keep[TILES + 1]) + (got[TILES].astype(F32) + got[TILES + 1].astype(F32))
+    here = keep[TILES] + keep[TILES + 1]
+    there = got[TILES].astype(F32) + got[TILES + 1].astype(F32)
+    small = here + there
     for target in (mine, away):
-        target[TILES] = small[:16]
+        target[TILES, :8] = (here[:8] + across[...]) + (there[:8] + skew[...])
+        target[TILES, 8:] = small[8:16]
         target[TILES + 1] = small[16:]
 
 
@@ -643,6 +653,7 @@
         outs=blocks([8 * WIDE[1]] * 2),
     )
     sends, keeps = [first_send, second_send], [first_keep, second_keep]
+    hidden, sends[1] = lax.optimization_barrier((hidden, sends[1]))
     down_part = run(down_kernel, operands=[hidden, down_weight], outs=[like((rows, width), BF16)])[0]
     early_other = share(shared_early)
     norm_two_other, keeps[1], down_part, early_other = lax.optimization_barrier(
@@ -667,7 +678,7 @@
         ],
         flops=SHORT,
     )
-    backs, shared, norm_one_part, gain_part, small = run(
+    backs, shared, norm_one_part, small = run(
         last_kernel,
         offset=offset,
         operands=[gated_back, returned, parts, c_back, in_parts, tokens, gain_two_grad, tap_grads]
@@ -676,15 +687,13 @@
             like((3, rows, channels), BF16),
             like((7, rows, 256), BF16),
             like((rows, width), BF16),
-            like((8, 128), F32),
             like((32, 128), F32),
         ],
     )
-    gain_other = swap(gain_part, ACROSS)
-    *sends, narrow, small = run(
+    *sends, narrow = run(
         narrow_kernel,
-        operands=[normed_one, early_other, resid_low, share(shared), backs, ymix, small, gain_part, gain_other],
-        outs=blocks(ROUND_ONE) + blocks([4 * NARROW]) + [like((32, 128), F32)],
+        operands=[normed_one, early_other, resid_low, share(shared), backs, ymix, small],
+        outs=blocks(ROUND_ONE) + blocks([4 * NARROW]),
         scratch=[pltpu.VMEM((width, 2 * rows), BF16)] * 2,
     )
     narrow, cross = run(
@@ -702,7 +711,7 @@
     sends, keeps = list(results[:2]), list(results[2:])
     gots = swap_round(sends, FIRST)
     norm_one_other = swap(norm_one_part, ACROSS)
-    gots[0], norm_one_other = lax.optimization_barrier((gots[0], norm_one_other))
+    down_other = swap(down_part, ACROSS)
     results = run(
         second_kernel,
         operands=gots + keeps + [narrow, small, cross],
@@ -710,23 +719,21 @@
     )
     sends, keep, small = list(results[:3]), results[3], results[4]
     gots = swap_round(sends, SECOND)
-    small, down_part = lax.optimization_barrier((small, down_part))
-    down_other = swap(down_part, ACROSS)
-    gots[0], down_other = lax.optimization_barrier((gots[0], down_other))
-    beside, kept = run(
+    mixed, tokens_grad = run(
+        finish_kernel,
+        operands=[resid, down_part, down_other, norm_one_part, norm_one_other, tokens, resid_grad, gain_one_row],
+        outs=[like((rows, width), BF16), like((rows, width), F32)],
+        flops=LONG,
+    )
+    gots[0], mixed, tokens_grad = lax.optimization_barrier((gots[0], mixed, tokens_grad))
+    beside, kept, gain = run(
         third_kernel,
         operands=gots + [keep, small],
-        outs=[like((TILES + 2, 32, 128), BF16), like((TILES + 2, 32, 128), F32)],
-    )
-    beside = swap(beside, BESIDE)
-    mixed = (resid + (down_part.astype(F32) + down_other.astype(F32))).astype(BF16)
-    inputs = tokens.astype(F32)
-    norm_one_back = norm_one_part.astype(F32) + norm_one_other.astype(F32)
-    tokens_grad = resid_grad + norm_backward(norm_one_back, inputs, norm_scale(inputs), gain_one)
-    beside, mixed, tokens_grad = lax.optimization_barrier((beside, mixed, tokens_grad))
+        outs=[like((TILES + 2, 32, 128), BF16), like((TILES + 2, 32, 128), F32), like((8, 128), F32)],
+    )
     mine, away = run(
         cores_kernel,
-        operands=[kept, beside],
+        operands=[kept, swap(beside, BESIDE), swap(gain, ACROSS), swap(gain, SKEW)],
         outs=[like((TILES + 2, 16, 128), F32)] * 2,
     )
     down_g, gate_g, up_g, in_g, out_g, gain_one_g, gain_two_g, conv_g = run(

time: 126 us -> 125 us (level)
  starting transfers between devices: 48.2 us -> 43.7 us
  waiting for transfers between devices: 47.9 us -> 52.1 us
  other arithmetic: 2.82 us -> 0.01 us
  Pallas kernels: 25.4 us -> 27.1 us
    ppermute x19 -> x20, starting transfers between devices: 42 us -> 37.4 us  [swap(): return lax.ppermute(value, AXES, pairs)]
    ppermute x19 -> x20, waiting for transfers between devices: 46 us -> 50.1 us  [swap(): return lax.ppermute(value, AXES, pairs)]
    pallas_call x19 -> x20, Pallas kernels: 25.4 us -> 27.1 us  [call(): pl.pallas_call(kernel, out_shape=tuple(outs), in_specs=specs, out_specs=t...]
    add x1 -> x0, other arithmetic: 1.38 us -> none  [on_device(): resid_grad + norm_backward(norm_one_back, inputs, norm_scale(inputs), gai...]
  transfers between devices with their start and end apart: 21 -> 22, of which waited for: 13 -> 12; matrix products, arithmetic and copies ran while one was open for 2% -> 0% of each run, Pallas kernels for 16% -> 18%
where the time goes in v7:
time: 125 us
  waiting for transfers between devices  52.1 us (42%)
  starting transfers between devices  43.7 us (35%)
  Pallas kernels  27.1 us (22%)
  between operations  1.63 us (1%)
    ppermute x20, waiting for transfers between devices, swap(): return lax.ppermute(value, AXES, pairs)  50.1 us
    ppermute x20, starting transfers between devices, swap(): return lax.ppermute(value, AXES, pairs)  37.4 us
    pallas_call x20, Pallas kernels, call(): pl.pallas_call(kernel, out_shape=tuple(outs), in_specs=specs, out_specs=t...  27.1 us
    ppermute x2, starting transfers between devices, from_behind(): lax.ppermute(value, axis, [(source, source + steps) for source in range(l...  6.27 us
  transfers between devices with their start and end apart: 22, of which 12 were waited for; matrix products, arithmetic and copies ran while one was open for 0% of the time, Pallas kernels for 18%

profile of v7, /device:TPU:1, one launch (start us, length us, event | category | flops | bytes accessed | tf_op | source)
XLA Modules:
  0.0 124.6 jit_solution(6150029787164921523)
XLA Ops:
  2.8 2.3 %shard_map.186 = (bf16[16,512]{1,0:T(8,128)(2,1)S(1)}, bf16[256,1024]{1,0:T(8,128)(2,1)S(1)}, f32[1,1024]{1,0:T(1,128)S(1)}, bf16[3,1024,512]{2,1,0:T(8,128)(2,1)S(1)}, s32[8,128]{1,0:T(8,128)S(1)}) custom-call(s32[1]{0:T(128)S(6)} %copy.25.refs_0_, bf16[256,1024]{1,0:T(8,128)(2,1)} %refs_5_.9, f32[1,1024]{1,0:T(1,128)} %bitcast.17, ...), custom_call_target="tpu_custom_call" | custom-call | tf_op jit(solution)/shard_map/pallas_call | solution.py:118
  5.1 3.1 %collective-permute-start = (bf16[16,512]{1,0:T(8,128)(2,1)S(1)}, bf16[16,512]{1,0:T(8,128)(2,1)S(1)}, u32[]{:S(2)}, u32[]{:S(2)}) collective-permute-start(bf16[16,512]{1,0:T(8,128)(2,1)S(1)} %get-tuple-element.93), channel_id=1, source_target_pairs={{0,2},{2,4},{4,6},{6,8},{8,10},{10,12},{12,14},{14,16},{16,18},{18... | collective-permute-start | bytes 49160 | tf_op jit(solution)/shard_map/ppermute | solution.py:80
  10.1 2.5 %collective-permute-start.2 = (bf16[256,1024]{1,0:T(8,128)(2,1)S(1)}, bf16[256,1024]{1,0:T(8,128)(2,1)S(1)}, u32[]{:S(2)}, u32[]{:S(2)}) collective-permute-start(bf16[256,1024]{1,0:T(8,128)(2,1)S(1)} %get-tuple-element.97.refs_1_), channel_id=1, source_target_pairs={{0,1},{2,3},{4,5},{6,7},{1,0},{3,2},{5,4},{7,6},{8,9},{10,11},{12,... | collective-permute-start | bytes 1572872 | tf_op jit(solution)/shard_map/ppermute | solution.py:74
  14.1 11.1 %collective-permute-done.2.refs_2_ = bf16[256,1024]{1,0:T(8,128)(2,1)S(1)} collective-permute-done((bf16[256,1024]{1,0:T(8,128)(2,1)S(1)}, bf16[256,1024]{1,0:T(8,128)(2,1)S(1)}, u32[]{:S(2)}, u32[]{:S(2)}) %collective-permute-start.2) | collective-permute-done | bytes 524320 | tf_op jit(solution)/shard_map/ppermute | solution.py:74
  25.3 3.4 %shard_map.190 = (f32[256,1024]{1,0:T(8,128)S(1)}, bf16[256,1024]{1,0:T(8,128)(2,1)S(1)}, bf16[256,2304]{1,0:T(8,128)(2,1)S(1)}, bf16[256,2304]{1,0:T(8,128)(2,1...) custom-call(bf16[256,1024]{1,0:T(8,128)(2,1)S(1)} %copy-done.2, ...), custom_call_target="tpu_custom_call" | custom-call | tf_op jit(solution)/shard_map/pallas_call | solution.py:118
  29.3 2.6 %shard_map.193.refs_1_ = bf16[256,1024]{1,0:T(8,128)(2,1)S(1)} custom-call(bf16[256,2304]{1,0:T(8,128)(2,1)S(1)} %get-tuple-element.106.refs_4_.refs_1_.refs_0_, bf16[256,2304]{1,0:T(8,128)(2,1)S(1)} %get-tuple-element.110.refs_2_.refs_1_, bf16[1024,2304]{1,0:T(8,128)(2,1)S(1)} %bitcast.9, bf16[1024,2304]{1,0:T(8,128)(2,1)S(1)} %bitcast.11), custom_call_target="tpu_custom_call" | custom-call | tf_op jit(solution)/shard_map/pallas_call | solution.py:118
  32.0 3.0 %collective-permute-start.6 = (bf16[256,1024]{1,0:T(8,128)(2,1)S(1)}, bf16[256,1024]{1,0:T(8,128)(2,1)S(1)}, u32[]{:S(2)}, u32[]{:S(2)}) collective-permute-start(bf16[256,1024]{1,0:T(8,128)(2,1)S(1)} %shard_map.193.refs_1_), channel_id=1, source_target_pairs={{0,1},{2,3},{4,5},{6,7},{1,0},{3,2},{5,4},{7,6},{8,9},{10,11},{12,... | collective-permute-start | bytes 1572872 | tf_op jit(solution)/shard_map/ppermute | solution.py:74
  34.9 2.8 %shard_map.191 = (bf16[112,64,128]{2,1,0:T(8,128)(2,1)S(1)}, bf16[112,64,128]{2,1,0:T(8,128)(2,1)S(1)}, bf16[1024,512]{1,0:T(8,128)(2,1)S(1)}) custom-call(bf16[256,1024]{1,0:T(8,128)(2,1)S(1)} %get-tuple-element.103.refs_0_, bf16[256,1024]{1,0:T(8,128)(2,1)S(1)} %copy-done.4, bf16[256,1024]{1,0:T(8,128)(2,1)S(1)} %collective-permute-done.1.refs_2_, ...), custom_call_target="tpu_custom_call" | custom-call | tf_op jit(solution)/shard_map/pallas_call | solution.py:118
  37.7 1.9 %collective-permute-start.4 = (bf16[112,64,128]{2,1,0:T(8,128)(2,1)S(1)}, bf16[112,64,128]{2,1,0:T(8,128)(2,1)S(1)}, u32[]{:S(2)}, u32[]{:S(2)}) collective-permute-start(bf16[112,64,128]{2,1,0:T(8,128)(2,1)S(1)} %get-tuple-element.108), channel_id=1, source_target_pairs={{0,32},{2,10},{4,36},{6,14},{1,33},{3,11},{5,37},{7,15},{8,40},{10... | collective-permute-start | bytes 5505032 | tf_op jit(solution)/shard_map/ppermute | solution.py:74
  39.6 2.1 %shard_map.192 = (bf16[104,64,128]{2,1,0:T(8,128)(2,1)S(1)}, bf16[104,64,128]{2,1,0:T(8,128)(2,1)S(1)}) custom-call(bf16[1024,512]{1,0:T(8,128)(2,1)S(1)} %get-tuple-element.109.refs_0_, bf16[256,2304]{1,0:T(8,128)(2,1)S(1)} %get-tuple-element.106.refs_4_.refs_1_.refs_0_, bf16[256,2304]{1,0:T(8,128)(2,1)S(1)} %get-tuple-element.110.refs_2_.refs_1_, ...), custom_call_target="tpu_custom_call" | custom-call | tf_op jit(solution)/shard_map/pallas_call | solution.py:118
  41.7 2.3 %collective-permute-start.5 = (bf16[104,64,128]{2,1,0:T(8,128)(2,1)S(1)}, bf16[104,64,128]{2,1,0:T(8,128)(2,1)S(1)}, u32[]{:S(2)}, u32[]{:S(2)}) collective-permute-start(bf16[104,64,128]{2,1,0:T(8,128)(2,1)S(1)} %get-tuple-element.112), channel_id=1, source_target_pairs={{0,96},{2,26},{4,100},{6,30},{1,97},{3,27},{5,101},{7,31},{8,104},... | collective-permute-start | bytes 5111816 | tf_op jit(solution)/shard_map/ppermute | solution.py:74
  47.1 3.2 %collective-permute-start.8 = (f32[8,512]{1,0:T(8,128)S(1)}, f32[8,512]{1,0:T(8,128)S(1)}, u32[]{:S(2)}, u32[]{:S(2)}) collective-permute-start(f32[8,512]{1,0:T(8,128)S(1)} %shard_map.196), channel_id=1, source_target_pairs={{2,0},{4,2},{6,4},{8,6},{10,8},{12,10},{14,12},{16,14},{18,16},{20... | collective-permute-start | bytes 49160 | tf_op jit(solution)/shard_map/ppermute | solution.py:80
  51.9 2.0 %collective-permute-done.8.refs_2_ = f32[8,512]{1,0:T(8,128)S(1)} collective-permute-done((f32[8,512]{1,0:T(8,128)S(1)}, f32[8,512]{1,0:T(8,128)S(1)}, u32[]{:S(2)}, u32[]{:S(2)}) %collective-permute-start.8) | collective-permute-done | bytes 16416 | tf_op jit(solution)/shard_map/ppermute | solution.py:80
  55.1 2.5 %collective-permute-done.9.refs_3_ = bf16[7,256,256]{2,1,0:T(8,128)(2,1)S(1)} collective-permute-done((bf16[7,256,256]{2,1,0:T(8,128)(2,1)S(1)}, bf16[7,256,256]{2,1,0:T(8,128)(2,1)S(1)}, u32[]{:S(2)}, u32[]{:S(2)}) %collective-permute-start.9) | collective-permute-done | bytes 917536 | tf_op jit(solution)/shard_map/ppermute | solution.py:74
  59.3 3.4 %collective-permute-start.12 = (bf16[33,64,128]{2,1,0:T(8,128)(2,1)S(1)}, bf16[33,64,128]{2,1,0:T(8,128)(2,1)S(1)}, u32[]{:S(2)}, u32[]{:S(2)}) collective-permute-start(bf16[33,64,128]{2,1,0:T(8,128)(2,1)S(1)} %get-tuple-element.137), channel_id=1, source_target_pairs={{0,64},{2,18},{4,68},{6,22},{1,65},{3,19},{5,69},{7,23},{8,72},{10... | collective-permute-start | bytes 1622024 | tf_op jit(solution)/shard_map/ppermute | solution.py:74
  62.7 2.7 %collective-permute-start.14 = (bf16[256,1024]{1,0:T(8,128)(2,1)S(1)}, bf16[256,1024]{1,0:T(8,128)(2,1)S(1)}, u32[]{:S(2)}, u32[]{:S(2)}) collective-permute-start(bf16[256,1024]{1,0:T(8,128)(2,1)S(1)} %shard_map.194.refs_1_), channel_id=1, source_target_pairs={{0,1},{2,3},{4,5},{6,7},{1,0},{3,2},{5,4},{7,6},{8,9},{10,11},{12,... | collective-permute-start | bytes 1572872 | tf_op jit(solution)/shard_map/ppermute | solution.py:74
  67.3 2.4 %collective-permute-done.12.refs_1_ = bf16[33,64,128]{2,1,0:T(8,128)(2,1)S(1)} collective-permute-done((bf16[33,64,128]{2,1,0:T(8,128)(2,1)S(1)}, bf16[33,64,128]{2,1,0:T(8,128)(2,1)S(1)}, u32[]{:S(2)}, u32[]{:S(2)}) %collective-permute-start.12) | collective-permute-done | bytes 540704 | tf_op jit(solution)/shard_map/ppermute | solution.py:74
  69.8 14.8 %collective-permute-done.10.refs_0_ = bf16[85,64,128]{2,1,0:T(8,128)(2,1)S(1)} collective-permute-done((bf16[85,64,128]{2,1,0:T(8,128)(2,1)S(1)}, bf16[85,64,128]{2,1,0:T(8,128)(2,1)S(1)}, u32[]{:S(2)}, u32[]{:S(2)}) %collective-permute-start.10) | collective-permute-done | bytes 1392672 | tf_op jit(solution)/shard_map/ppermute | solution.py:74
  88.1 1.9 %collective-permute-start.16 = (bf16[36,64,128]{2,1,0:T(8,128)(2,1)S(1)}, bf16[36,64,128]{2,1,0:T(8,128)(2,1)S(1)}, u32[]{:S(2)}, u32[]{:S(2)}) collective-permute-start(bf16[36,64,128]{2,1,0:T(8,128)(2,1)S(1)} %get-tuple-element.149), channel_id=1, source_target_pairs={{0,24},{2,98},{4,28},{6,102},{1,25},{3,99},{5,29},{7,103},{8,16},{... | collective-permute-start | bytes 1769480 | tf_op jit(solution)/shard_map/ppermute | solution.py:74
  92.6 3.0 %collective-permute-done.13.refs_0_ = bf16[36,64,128]{2,1,0:T(8,128)(2,1)S(1)} collective-permute-done((bf16[36,64,128]{2,1,0:T(8,128)(2,1)S(1)}, bf16[36,64,128]{2,1,0:T(8,128)(2,1)S(1)}, u32[]{:S(2)}, u32[]{:S(2)}) %collective-permute-start.13) | collective-permute-done | bytes 589856 | tf_op jit(solution)/shard_map/ppermute | solution.py:74
  95.6 7.6 %collective-permute-done.16.refs_1_ = bf16[36,64,128]{2,1,0:T(8,128)(2,1)S(1)} collective-permute-done((bf16[36,64,128]{2,1,0:T(8,128)(2,1)S(1)}, bf16[36,64,128]{2,1,0:T(8,128)(2,1)S(1)}, u32[]{:S(2)}, u32[]{:S(2)}) %collective-permute-start.16) | collective-permute-done | bytes 589856 | tf_op jit(solution)/shard_map/ppermute | solution.py:74
  104.7 4.7 %collective-permute-start.18 = (bf16[37,32,128]{2,1,0:T(8,128)(2,1)S(1)}, bf16[37,32,128]{2,1,0:T(8,128)(2,1)S(1)}, u32[]{:S(2)}, u32[]{:S(2)}) collective-permute-start(bf16[37,32,128]{2,1,0:T(8,128)(2,1)S(1)} %get-tuple-element.154), channel_id=1, source_target_pairs={{0,4},{2,6},{4,0},{6,2},{1,5},{3,7},{5,1},{7,3},{8,12},{10,14},{12... | collective-permute-start | bytes 909320 | tf_op jit(solution)/shard_map/ppermute | solution.py:74
  111.9 3.6 %collective-permute-done.19.refs_2_ = f32[8,128]{1,0:T(8,128)S(1)} collective-permute-done((f32[8,128]{1,0:T(8,128)S(1)}, f32[8,128]{1,0:T(8,128)S(1)}, u32[]{:S(2)}, u32[]{:S(2)}) %collective-permute-start.19) | collective-permute-done | bytes 4128 | tf_op jit(solution)/shard_map/ppermute | solution.py:74
  115.7 6.9 %collective-permute-start.21 = (f32[37,16,128]{2,1,0:T(8,128)S(1)}, f32[37,16,128]{2,1,0:T(8,128)S(1)}, u32[]{:S(2)}, u32[]{:S(2)}) collective-permute-start(f32[37,16,128]{2,1,0:T(8,128)S(1)} %get-tuple-element.157), channel_id=1, source_target_pairs={{0,2},{2,0},{4,6},{6,4},{1,3},{3,1},{5,7},{7,5},{8,10},{10,8},{12,... | collective-permute-start | bytes 909320 | tf_op jit(solution)/shard_map/ppermute | solution.py:74
  (66 shorter events, 27.3 us)
Async XLA Ops:
  0.6 8.8 %collective-permute-start.1 = (bf16[256,1024]{1,0:T(8,128)(2,1)}, bf16[256,1024]{1,0:T(8,128)(2,1)S(1)}, u32[]{:S(2)}, u32[]{:S(2)}) collective-permute-start(bf16[256,1024]{1,0:T(8,128)(2,1)} %refs_5_.8), channel_id=1, source_target_pairs={{0,2},{2,0},{4,6},{6,4},{1,3},{3,1},{5,7},{7,5},{8,10},{10,8},{12,... | collective-permute-start | bytes 1572872 | tf_op jit(solution)/shard_map/ppermute | solution.py:74
  5.1 4.3 %collective-permute-start = (bf16[16,512]{1,0:T(8,128)(2,1)S(1)}, bf16[16,512]{1,0:T(8,128)(2,1)S(1)}, u32[]{:S(2)}, u32[]{:S(2)}) collective-permute-start(bf16[16,512]{1,0:T(8,128)(2,1)S(1)} %get-tuple-element.93), channel_id=1, source_target_pairs={{0,2},{2,4},{4,6},{6,8},{8,10},{10,12},{12,14},{14,16},{16,18},{18... | collective-permute-start | bytes 49160 | tf_op jit(solution)/shard_map/ppermute | solution.py:80
  10.1 15.2 %slice-start = ((s8[4718592]{0:T(1024)(128)(4,1)}), s8[4194304]{0:T(1024)(128)(4,1)S(1)}, s32[]{:S(2)}) async-start(s8[4718592]{0:T(1024)(128)(4,1)} %bitcast.8), calls=%async_computation | async-start | bytes 8388608
  10.1 15.1 %slice-start.2 = ((s8[4718592]{0:T(1024)(128)(4,1)}), s8[4194304]{0:T(1024)(128)(4,1)S(1)}, s32[]{:S(2)}) async-start(s8[4718592]{0:T(1024)(128)(4,1)} %bitcast.10), calls=%async_computation.2 | async-start | bytes 8388608
  10.1 15.1 %collective-permute-start.2 = (bf16[256,1024]{1,0:T(8,128)(2,1)S(1)}, bf16[256,1024]{1,0:T(8,128)(2,1)S(1)}, u32[]{:S(2)}, u32[]{:S(2)}) collective-permute-start(bf16[256,1024]{1,0:T(8,128)(2,1)S(1)} %get-tuple-element.97.refs_1_), channel_id=1, source_target_pairs={{0,1},{2,3},{4,5},{6,7},{1,0},{3,2},{5,4},{7,6},{8,9},{10,11},{12,... | collective-permute-start | bytes 1572872 | tf_op jit(solution)/shard_map/ppermute | solution.py:74
  28.6 6.3 %collective-permute-start.3 = (bf16[256,4480]{1,0:T(8,128)(2,1)S(1)}, bf16[256,4480]{1,0:T(8,128)(2,1)S(1)}, u32[]{:S(2)}, u32[]{:S(2)}) collective-permute-start(bf16[256,4480]{1,0:T(8,128)(2,1)S(1)} %get-tuple-element.107), channel_id=1, source_target_pairs={{0,2},{2,0},{4,6},{6,4},{1,3},{3,1},{5,7},{7,5},{8,10},{10,8},{12,... | collective-permute-start | bytes 6881288 | tf_op jit(solution)/shard_map/ppermute | solution.py:74
  29.2 17.4 %collective-permute-start.7 = (bf16[256,1280]{1,0:T(8,128)(2,1)S(1)}, bf16[256,1280]{1,0:T(8,128)(2,1)S(1)}, u32[]{:S(2)}, u32[]{:S(2)}) collective-permute-start(bf16[256,1280]{1,0:T(8,128)(2,1)S(1)} %get-tuple-element.116), channel_id=1, source_target_pairs={{0,2},{2,0},{4,6},{6,4},{1,3},{3,1},{5,7},{7,5},{8,10},{10,8},{12,... | collective-permute-start | bytes 1966088 | tf_op jit(solution)/shard_map/ppermute | solution.py:74
  32.0 14.7 %collective-permute-start.6 = (bf16[256,1024]{1,0:T(8,128)(2,1)S(1)}, bf16[256,1024]{1,0:T(8,128)(2,1)S(1)}, u32[]{:S(2)}, u32[]{:S(2)}) collective-permute-start(bf16[256,1024]{1,0:T(8,128)(2,1)S(1)} %shard_map.193.refs_1_), channel_id=1, source_target_pairs={{0,1},{2,3},{4,5},{6,7},{1,0},{3,2},{5,4},{7,6},{8,9},{10,11},{12,... | collective-permute-start | bytes 1572872 | tf_op jit(solution)/shard_map/ppermute | solution.py:74
  37.7 28.0 %collective-permute-start.4 = (bf16[112,64,128]{2,1,0:T(8,128)(2,1)S(1)}, bf16[112,64,128]{2,1,0:T(8,128)(2,1)S(1)}, u32[]{:S(2)}, u32[]{:S(2)}) collective-permute-start(bf16[112,64,128]{2,1,0:T(8,128)(2,1)S(1)} %get-tuple-element.108), channel_id=1, source_target_pairs={{0,32},{2,10},{4,36},{6,14},{1,33},{3,11},{5,37},{7,15},{8,40},{10... | collective-permute-start | bytes 5505032 | tf_op jit(solution)/shard_map/ppermute | solution.py:74
  41.7 23.9 %collective-permute-start.5 = (bf16[104,64,128]{2,1,0:T(8,128)(2,1)S(1)}, bf16[104,64,128]{2,1,0:T(8,128)(2,1)S(1)}, u32[]{:S(2)}, u32[]{:S(2)}) collective-permute-start(bf16[104,64,128]{2,1,0:T(8,128)(2,1)S(1)} %get-tuple-element.112), channel_id=1, source_target_pairs={{0,96},{2,26},{4,100},{6,30},{1,97},{3,27},{5,101},{7,31},{8,104},... | collective-permute-start | bytes 5111816 | tf_op jit(solution)/shard_map/ppermute | solution.py:74
  47.1 6.8 %collective-permute-start.8 = (f32[8,512]{1,0:T(8,128)S(1)}, f32[8,512]{1,0:T(8,128)S(1)}, u32[]{:S(2)}, u32[]{:S(2)}) collective-permute-start(f32[8,512]{1,0:T(8,128)S(1)} %shard_map.196), channel_id=1, source_target_pairs={{2,0},{4,2},{6,4},{8,6},{10,8},{12,10},{14,12},{16,14},{18,16},{20... | collective-permute-start | bytes 49160 | tf_op jit(solution)/shard_map/ppermute | solution.py:80
  55.0 2.6 %collective-permute-start.9 = (bf16[7,256,256]{2,1,0:T(8,128)(2,1)S(1)}, bf16[7,256,256]{2,1,0:T(8,128)(2,1)S(1)}, u32[]{:S(2)}, u32[]{:S(2)}) collective-permute-start(bf16[7,256,256]{2,1,0:T(8,128)(2,1)S(1)} %get-tuple-element.127), channel_id=1, source_target_pairs={{0,2},{2,0},{4,6},{6,4},{1,3},{3,1},{5,7},{7,5},{8,10},{10,8},{12,... | collective-permute-start | bytes 2752520 | tf_op jit(solution)/shard_map/ppermute | solution.py:74
  59.3 10.4 %collective-permute-start.12 = (bf16[33,64,128]{2,1,0:T(8,128)(2,1)S(1)}, bf16[33,64,128]{2,1,0:T(8,128)(2,1)S(1)}, u32[]{:S(2)}, u32[]{:S(2)}) collective-permute-start(bf16[33,64,128]{2,1,0:T(8,128)(2,1)S(1)} %get-tuple-element.137), channel_id=1, source_target_pairs={{0,64},{2,18},{4,68},{6,22},{1,65},{3,19},{5,69},{7,23},{8,72},{10... | collective-permute-start | bytes 1622024 | tf_op jit(solution)/shard_map/ppermute | solution.py:74
  62.7 28.2 %collective-permute-start.14 = (bf16[256,1024]{1,0:T(8,128)(2,1)S(1)}, bf16[256,1024]{1,0:T(8,128)(2,1)S(1)}, u32[]{:S(2)}, u32[]{:S(2)}) collective-permute-start(bf16[256,1024]{1,0:T(8,128)(2,1)S(1)} %shard_map.194.refs_1_), channel_id=1, source_target_pairs={{0,1},{2,3},{4,5},{6,7},{1,0},{3,2},{5,4},{7,6},{8,9},{10,11},{12,... | collective-permute-start | bytes 1572872 | tf_op jit(solution)/shard_map/ppermute | solution.py:74
  65.4 25.4 %collective-permute-start.15 = (bf16[256,1024]{1,0:T(8,128)(2,1)S(1)}, bf16[256,1024]{1,0:T(8,128)(2,1)S(1)}, u32[]{:S(2)}, u32[]{:S(2)}) collective-permute-start(bf16[256,1024]{1,0:T(8,128)(2,1)S(1)} %get-tuple-element.142.refs_3_), channel_id=1, source_target_pairs={{0,1},{2,3},{4,5},{6,7},{1,0},{3,2},{5,4},{7,6},{8,9},{10,11},{12,... | collective-permute-start | bytes 1572872 | tf_op jit(solution)/shard_map/ppermute | solution.py:74
  66.4 18.2 %collective-permute-start.10 = (bf16[85,64,128]{2,1,0:T(8,128)(2,1)S(1)}, bf16[85,64,128]{2,1,0:T(8,128)(2,1)S(1)}, u32[]{:S(2)}, u32[]{:S(2)}) collective-permute-start(bf16[85,64,128]{2,1,0:T(8,128)(2,1)S(1)} %get-tuple-element.132), channel_id=1, source_target_pairs={{0,32},{2,10},{4,36},{6,14},{1,33},{3,11},{5,37},{7,15},{8,40},{10... | collective-permute-start | bytes 4177928 | tf_op jit(solution)/shard_map/ppermute | solution.py:74
  66.5 19.6 %collective-permute-start.11 = (bf16[89,64,128]{2,1,0:T(8,128)(2,1)S(1)}, bf16[89,64,128]{2,1,0:T(8,128)(2,1)S(1)}, u32[]{:S(2)}, u32[]{:S(2)}) collective-permute-start(bf16[89,64,128]{2,1,0:T(8,128)(2,1)S(1)} %get-tuple-element.133), channel_id=1, source_target_pairs={{0,96},{2,26},{4,100},{6,30},{1,97},{3,27},{5,101},{7,31},{8,104},... | collective-permute-start | bytes 4374536 | tf_op jit(solution)/shard_map/ppermute | solution.py:74
  86.7 8.8 %collective-permute-start.13 = (bf16[36,64,128]{2,1,0:T(8,128)(2,1)S(1)}, bf16[36,64,128]{2,1,0:T(8,128)(2,1)S(1)}, u32[]{:S(2)}, u32[]{:S(2)}) collective-permute-start(bf16[36,64,128]{2,1,0:T(8,128)(2,1)S(1)} %get-tuple-element.140), channel_id=1, source_target_pairs={{0,8},{2,34},{4,12},{6,38},{1,9},{3,35},{5,13},{7,39},{8,0},{10,42... | collective-permute-start | bytes 1769480 | tf_op jit(solution)/shard_map/ppermute | solution.py:74
  88.1 15.1 %collective-permute-start.16 = (bf16[36,64,128]{2,1,0:T(8,128)(2,1)S(1)}, bf16[36,64,128]{2,1,0:T(8,128)(2,1)S(1)}, u32[]{:S(2)}, u32[]{:S(2)}) collective-permute-start(bf16[36,64,128]{2,1,0:T(8,128)(2,1)S(1)} %get-tuple-element.149), channel_id=1, source_target_pairs={{0,24},{2,98},{4,28},{6,102},{1,25},{3,99},{5,29},{7,103},{8,16},{... | collective-permute-start | bytes 1769480 | tf_op jit(solution)/shard_map/ppermute | solution.py:74
  90.0 14.4 %collective-permute-start.17 = (bf16[36,64,128]{2,1,0:T(8,128)(2,1)S(1)}, bf16[36,64,128]{2,1,0:T(8,128)(2,1)S(1)}, u32[]{:S(2)}, u32[]{:S(2)}) collective-permute-start(bf16[36,64,128]{2,1,0:T(8,128)(2,1)S(1)} %get-tuple-element.150), channel_id=1, source_target_pairs={{0,16},{2,66},{4,20},{6,70},{1,17},{3,67},{5,21},{7,71},{8,24},{10... | collective-permute-start | bytes 1769480 | tf_op jit(solution)/shard_map/ppermute | solution.py:74
  104.7 10.8 %collective-permute-start.18 = (bf16[37,32,128]{2,1,0:T(8,128)(2,1)S(1)}, bf16[37,32,128]{2,1,0:T(8,128)(2,1)S(1)}, u32[]{:S(2)}, u32[]{:S(2)}) collective-permute-start(bf16[37,32,128]{2,1,0:T(8,128)(2,1)S(1)} %get-tuple-element.154), channel_id=1, source_target_pairs={{0,4},{2,6},{4,0},{6,2},{1,5},{3,7},{5,1},{7,3},{8,12},{10,14},{12... | collective-permute-start | bytes 909320 | tf_op jit(solution)/shard_map/ppermute | solution.py:74
  109.5 6.1 %collective-permute-start.19 = (f32[8,128]{1,0:T(8,128)S(1)}, f32[8,128]{1,0:T(8,128)S(1)}, u32[]{:S(2)}, u32[]{:S(2)}) collective-permute-start(f32[8,128]{1,0:T(8,128)S(1)} %get-tuple-element.155), channel_id=1, source_target_pairs={{0,1},{2,3},{4,5},{6,7},{1,0},{3,2},{5,4},{7,6},{8,9},{10,11},{12,... | collective-permute-start | bytes 12296 | tf_op jit(solution)/shard_map/ppermute | solution.py:74
  111.3 4.2 %collective-permute-start.20 = (f32[8,128]{1,0:T(8,128)S(1)}, f32[8,128]{1,0:T(8,128)S(1)}, u32[]{:S(2)}, u32[]{:S(2)}) collective-permute-start(f32[8,128]{1,0:T(8,128)S(1)} %get-tuple-element.155), channel_id=1, source_target_pairs={{0,5},{2,7},{4,1},{6,3},{1,4},{3,6},{5,0},{7,2},{8,13},{10,15},{12... | collective-permute-start | bytes 12296 | tf_op jit(solution)/shard_map/ppermute | solution.py:74
  115.7 8.1 %collective-permute-start.21 = (f32[37,16,128]{2,1,0:T(8,128)S(1)}, f32[37,16,128]{2,1,0:T(8,128)S(1)}, u32[]{:S(2)}, u32[]{:S(2)}) collective-permute-start(f32[37,16,128]{2,1,0:T(8,128)S(1)} %get-tuple-element.157), channel_id=1, source_target_pairs={{0,2},{2,0},{4,6},{6,4},{1,3},{3,1},{5,7},{7,5},{8,10},{10,8},{12,... | collective-permute-start | bytes 909320 | tf_op jit(solution)/shard_map/ppermute | solution.py:74
  (10 other events, 89.8 us)

commit v8 on v6

--- a/solution.py
+++ b/solution.py
@@ -509,6 +509,15 @@
     keep[TILES + 1] = low.astype(F32)
 
 
+def finish_kernel(
+    scalars, resid, down, down_other, part, other, tokens, resid_grad, gain, mixed, tokens_grad
+):
+    mixed[...] = (resid[...] + (down[...].astype(F32) + down_other[...].astype(F32))).astype(BF16)
+    values = tokens[...].astype(F32)
+    back = part[...].astype(F32) + other[...].astype(F32)
+    tokens_grad[...] = resid_grad[...] + norm_backward(back, values, norm_scale(values), gain[...])
+
+
 def cores_kernel(scalars, keep, got, mine, away):
     core = scalars[3]
     total = keep[:TILES] + got[:TILES].astype(F32)
@@ -643,6 +652,7 @@
         outs=blocks([8 * WIDE[1]] * 2),
     )
     sends, keeps = [first_send, second_send], [first_keep, second_keep]
+    hidden, sends[1] = lax.optimization_barrier((hidden, sends[1]))
     down_part = run(down_kernel, operands=[hidden, down_weight], outs=[like((rows, width), BF16)])[0]
     early_other = share(shared_early)
     norm_two_other, keeps[1], down_part, early_other = lax.optimization_barrier(
@@ -687,12 +697,7 @@
         outs=blocks(ROUND_ONE) + blocks([4 * NARROW]) + [like((32, 128), F32)],
         scratch=[pltpu.VMEM((width, 2 * rows), BF16)] * 2,
     )
-    narrow, cross = run(
-        far_kernel,
-        operands=[narrow, swap(sends.pop(), FIRST[2])],
-        outs=[like((4 * NARROW, *BLOCK), F32), like((32, 128), F32)],
-        flops=LONG,
-    )
+    far_send = sends.pop()
     results = run(
         first_kernel,
         operands=gots + keeps + sends,
@@ -700,9 +705,15 @@
         outs=blocks(ROUND_ONE[:2]) + blocks([4 * count for count in WIDE]),
     )
     sends, keeps = list(results[:2]), list(results[2:])
+    keeps[0], far_send = lax.optimization_barrier((keeps[0], far_send))
+    narrow, cross = run(
+        far_kernel,
+        operands=[narrow, swap(far_send, FIRST[2])],
+        outs=[like((4 * NARROW, *BLOCK), F32), like((32, 128), F32)],
+    )
     gots = swap_round(sends, FIRST)
+    down_other = swap(down_part, ACROSS)
     norm_one_other = swap(norm_one_part, ACROSS)
-    gots[0], norm_one_other = lax.optimization_barrier((gots[0], norm_one_other))
     results = run(
         second_kernel,
         operands=gots + keeps + [narrow, small, cross],
@@ -710,20 +721,19 @@
     )
     sends, keep, small = list(results[:3]), results[3], results[4]
     gots = swap_round(sends, SECOND)
-    small, down_part = lax.optimization_barrier((small, down_part))
-    down_other = swap(down_part, ACROSS)
-    gots[0], down_other = lax.optimization_barrier((gots[0], down_other))
+    mixed, tokens_grad = run(
+        finish_kernel,
+        operands=[resid, down_part, down_other, norm_one_part, norm_one_other, tokens, resid_grad, gain_one_row],
+        outs=[like((rows, width), BF16), like((rows, width), F32)],
+        flops=LONG,
+    )
+    gots[0], mixed, tokens_grad = lax.optimization_barrier((gots[0], mixed, tokens_grad))
     beside, kept = run(
         third_kernel,
         operands=gots + [keep, small],
         outs=[like((TILES + 2, 32, 128), BF16), like((TILES + 2, 32, 128), F32)],
     )
     beside = swap(beside, BESIDE)
-    mixed = (resid + (down_part.astype(F32) + down_other.astype(F32))).astype(BF16)
-    inputs = tokens.astype(F32)
-    norm_one_back = norm_one_part.astype(F32) + norm_one_other.astype(F32)
-    tokens_grad = resid_grad + norm_backward(norm_one_back, inputs, norm_scale(inputs), gain_one)
-    beside, mixed, tokens_grad = lax.optimization_barrier((beside, mixed, tokens_grad))
     mine, away = run(
         cores_kernel,
         operands=[kept, beside],

time: 126 us -> 123 us (0.976)
  starting transfers between devices: 48.2 us -> 39 us
  waiting for transfers between devices: 47.9 us -> 55.4 us
  other arithmetic: 2.82 us -> 0.01 us
  Pallas kernels: 25.4 us -> 27.1 us
    ppermute x19, starting transfers between devices: 42 us -> 32.7 us  [swap(): return lax.ppermute(value, AXES, pairs)]
    ppermute x19, waiting for transfers between devices: 46 us -> 53.4 us  [swap(): return lax.ppermute(value, AXES, pairs)]
    pallas_call x19 -> x20, Pallas kernels: 25.4 us -> 27.1 us  [call(): pl.pallas_call(kernel, out_shape=tuple(outs), in_specs=specs, out_specs=t...]
    add x1 -> x0, other arithmetic: 1.38 us -> none  [on_device(): resid_grad + norm_backward(norm_one_back, inputs, norm_scale(inputs), gai...]
  transfers between devices with their start and end apart: 21 -> 21, of which waited for: 13 -> 11; matrix products, arithmetic and copies ran while one was open for 2% -> 0% of each run, Pallas kernels for 16% -> 17%
where the time goes in v8:
time: 123 us
  waiting for transfers between devices  55.4 us (45%)
  starting transfers between devices  39 us (32%)
  Pallas kernels  27.1 us (22%)
  between operations  1.64 us (1%)
    ppermute x19, waiting for transfers between devices, swap(): return lax.ppermute(value, AXES, pairs)  53.4 us
    ppermute x19, starting transfers between devices, swap(): return lax.ppermute(value, AXES, pairs)  32.7 us
    pallas_call x20, Pallas kernels, call(): pl.pallas_call(kernel, out_shape=tuple(outs), in_specs=specs, out_specs=t...  27.1 us
    ppermute x2, starting transfers between devices, from_behind(): lax.ppermute(value, axis, [(source, source + steps) for source in range(l...  6.27 us
  transfers between devices with their start and end apart: 21, of which 11 were waited for; matrix products, arithmetic and copies ran while one was open for 0% of the time, Pallas kernels for 17%

profile of v8, /device:TPU:1, one launch (start us, length us, event | category | flops | bytes accessed | tf_op | source)
XLA Modules:
  0.0 123.2 jit_solution(8355759804362259128)
XLA Ops:
  2.8 2.3 %shard_map.186 = (bf16[16,512]{1,0:T(8,128)(2,1)S(1)}, bf16[256,1024]{1,0:T(8,128)(2,1)S(1)}, f32[1,1024]{1,0:T(1,128)S(1)}, bf16[3,1024,512]{2,1,0:T(8,128)(2,1)S(1)}, s32[8,128]{1,0:T(8,128)S(1)}) custom-call(s32[1]{0:T(128)S(6)} %copy.25.refs_0_, bf16[256,1024]{1,0:T(8,128)(2,1)} %refs_5_.9, f32[1,1024]{1,0:T(1,128)} %bitcast.17, ...), custom_call_target="tpu_custom_call" | custom-call | tf_op jit(solution)/shard_map/pallas_call | solution.py:117
  5.1 3.1 %collective-permute-start = (bf16[16,512]{1,0:T(8,128)(2,1)S(1)}, bf16[16,512]{1,0:T(8,128)(2,1)S(1)}, u32[]{:S(2)}, u32[]{:S(2)}) collective-permute-start(bf16[16,512]{1,0:T(8,128)(2,1)S(1)} %get-tuple-element.96), channel_id=1, source_target_pairs={{0,2},{2,4},{4,6},{6,8},{8,10},{10,12},{12,14},{14,16},{16,18},{18... | collective-permute-start | bytes 49160 | tf_op jit(solution)/shard_map/ppermute | solution.py:79
  10.1 2.5 %collective-permute-start.2 = (bf16[256,1024]{1,0:T(8,128)(2,1)S(1)}, bf16[256,1024]{1,0:T(8,128)(2,1)S(1)}, u32[]{:S(2)}, u32[]{:S(2)}) collective-permute-start(bf16[256,1024]{1,0:T(8,128)(2,1)S(1)} %get-tuple-element.100.refs_1_), channel_id=1, source_target_pairs={{0,1},{2,3},{4,5},{6,7},{1,0},{3,2},{5,4},{7,6},{8,9},{10,11},{12,... | collective-permute-start | bytes 1572872 | tf_op jit(solution)/shard_map/ppermute | solution.py:73
  14.1 11.1 %collective-permute-done.2.refs_2_ = bf16[256,1024]{1,0:T(8,128)(2,1)S(1)} collective-permute-done((bf16[256,1024]{1,0:T(8,128)(2,1)S(1)}, bf16[256,1024]{1,0:T(8,128)(2,1)S(1)}, u32[]{:S(2)}, u32[]{:S(2)}) %collective-permute-start.2) | collective-permute-done | bytes 524320 | tf_op jit(solution)/shard_map/ppermute | solution.py:73
  25.3 3.4 %shard_map.190 = (f32[256,1024]{1,0:T(8,128)S(1)}, bf16[256,1024]{1,0:T(8,128)(2,1)S(1)}, bf16[256,2304]{1,0:T(8,128)(2,1)S(1)}, bf16[256,2304]{1,0:T(8,128)(2,1...) custom-call(bf16[256,1024]{1,0:T(8,128)(2,1)S(1)} %copy-done.2, ...), custom_call_target="tpu_custom_call" | custom-call | tf_op jit(solution)/shard_map/pallas_call | solution.py:117
  29.3 2.6 %shard_map.193.refs_1_ = bf16[256,1024]{1,0:T(8,128)(2,1)S(1)} custom-call(bf16[256,2304]{1,0:T(8,128)(2,1)S(1)} %get-tuple-element.109.refs_4_.refs_1_.refs_0_, bf16[256,2304]{1,0:T(8,128)(2,1)S(1)} %get-tuple-element.113.refs_2_.refs_1_, bf16[1024,2304]{1,0:T(8,128)(2,1)S(1)} %bitcast.9, bf16[1024,2304]{1,0:T(8,128)(2,1)S(1)} %bitcast.11), custom_call_target="tpu_custom_call" | custom-call | tf_op jit(solution)/shard_map/pallas_call | solution.py:117
  31.9 3.0 %collective-permute-start.6 = (bf16[256,1024]{1,0:T(8,128)(2,1)S(1)}, bf16[256,1024]{1,0:T(8,128)(2,1)S(1)}, u32[]{:S(2)}, u32[]{:S(2)}) collective-permute-start(bf16[256,1024]{1,0:T(8,128)(2,1)S(1)} %shard_map.193.refs_1_), channel_id=1, source_target_pairs={{0,1},{2,3},{4,5},{6,7},{1,0},{3,2},{5,4},{7,6},{8,9},{10,11},{12,... | collective-permute-start | bytes 1572872 | tf_op jit(solution)/shard_map/ppermute | solution.py:73
  34.9 2.8 %shard_map.191 = (bf16[112,64,128]{2,1,0:T(8,128)(2,1)S(1)}, bf16[112,64,128]{2,1,0:T(8,128)(2,1)S(1)}, bf16[1024,512]{1,0:T(8,128)(2,1)S(1)}) custom-call(bf16[256,1024]{1,0:T(8,128)(2,1)S(1)} %get-tuple-element.106.refs_0_, bf16[256,1024]{1,0:T(8,128)(2,1)S(1)} %copy-done.4, bf16[256,1024]{1,0:T(8,128)(2,1)S(1)} %collective-permute-done.1.refs_2_, ...), custom_call_target="tpu_custom_call" | custom-call | tf_op jit(solution)/shard_map/pallas_call | solution.py:117
  37.7 1.9 %collective-permute-start.4 = (bf16[112,64,128]{2,1,0:T(8,128)(2,1)S(1)}, bf16[112,64,128]{2,1,0:T(8,128)(2,1)S(1)}, u32[]{:S(2)}, u32[]{:S(2)}) collective-permute-start(bf16[112,64,128]{2,1,0:T(8,128)(2,1)S(1)} %get-tuple-element.111), channel_id=1, source_target_pairs={{0,32},{2,10},{4,36},{6,14},{1,33},{3,11},{5,37},{7,15},{8,40},{10... | collective-permute-start | bytes 5505032 | tf_op jit(solution)/shard_map/ppermute | solution.py:73
  39.6 2.1 %shard_map.192 = (bf16[104,64,128]{2,1,0:T(8,128)(2,1)S(1)}, bf16[104,64,128]{2,1,0:T(8,128)(2,1)S(1)}) custom-call(bf16[1024,512]{1,0:T(8,128)(2,1)S(1)} %get-tuple-element.112.refs_0_, bf16[256,2304]{1,0:T(8,128)(2,1)S(1)} %get-tuple-element.109.refs_4_.refs_1_.refs_0_, bf16[256,2304]{1,0:T(8,128)(2,1)S(1)} %get-tuple-element.113.refs_2_.refs_1_, ...), custom_call_target="tpu_custom_call" | custom-call | tf_op jit(solution)/shard_map/pallas_call | solution.py:117
  41.7 2.3 %collective-permute-start.5 = (bf16[104,64,128]{2,1,0:T(8,128)(2,1)S(1)}, bf16[104,64,128]{2,1,0:T(8,128)(2,1)S(1)}, u32[]{:S(2)}, u32[]{:S(2)}) collective-permute-start(bf16[104,64,128]{2,1,0:T(8,128)(2,1)S(1)} %get-tuple-element.115), channel_id=1, source_target_pairs={{0,96},{2,26},{4,100},{6,30},{1,97},{3,27},{5,101},{7,31},{8,104},... | collective-permute-start | bytes 5111816 | tf_op jit(solution)/shard_map/ppermute | solution.py:73
  47.0 3.2 %collective-permute-start.8 = (f32[8,512]{1,0:T(8,128)S(1)}, f32[8,512]{1,0:T(8,128)S(1)}, u32[]{:S(2)}, u32[]{:S(2)}) collective-permute-start(f32[8,512]{1,0:T(8,128)S(1)} %shard_map.196), channel_id=1, source_target_pairs={{2,0},{4,2},{6,4},{8,6},{10,8},{12,10},{14,12},{16,14},{18,16},{20... | collective-permute-start | bytes 49160 | tf_op jit(solution)/shard_map/ppermute | solution.py:79
  51.9 2.0 %collective-permute-done.8.refs_2_ = f32[8,512]{1,0:T(8,128)S(1)} collective-permute-done((f32[8,512]{1,0:T(8,128)S(1)}, f32[8,512]{1,0:T(8,128)S(1)}, u32[]{:S(2)}, u32[]{:S(2)}) %collective-permute-start.8) | collective-permute-done | bytes 16416 | tf_op jit(solution)/shard_map/ppermute | solution.py:79
  55.1 2.8 %collective-permute-start.10 = (f32[8,128]{1,0:T(8,128)S(1)}, f32[8,128]{1,0:T(8,128)S(1)}, u32[]{:S(2)}, u32[]{:S(2)}) collective-permute-start(f32[8,128]{1,0:T(8,128)S(1)} %get-tuple-element.133.refs_7_), channel_id=1, source_target_pairs={{0,1},{2,3},{4,5},{6,7},{1,0},{3,2},{5,4},{7,6},{8,9},{10,11},{12,... | collective-permute-start | bytes 12296 | tf_op jit(solution)/shard_map/ppermute | solution.py:73
  60.8 3.1 %collective-permute-done.5.refs_1_ = bf16[104,64,128]{2,1,0:T(8,128)(2,1)S(1)} collective-permute-done((bf16[104,64,128]{2,1,0:T(8,128)(2,1)S(1)}, bf16[104,64,128]{2,1,0:T(8,128)(2,1)S(1)}, u32[]{:S(2)}, u32[]{:S(2)}) %collective-permute-start.5) | collective-permute-done | bytes 1703968 | tf_op jit(solution)/shard_map/ppermute | solution.py:73
  64.8 2.3 %collective-permute-start.12 = (bf16[89,64,128]{2,1,0:T(8,128)(2,1)S(1)}, bf16[89,64,128]{2,1,0:T(8,128)(2,1)S(1)}, u32[]{:S(2)}, u32[]{:S(2)}) collective-permute-start(bf16[89,64,128]{2,1,0:T(8,128)(2,1)S(1)} %get-tuple-element.137), channel_id=1, source_target_pairs={{0,96},{2,26},{4,100},{6,30},{1,97},{3,27},{5,101},{7,31},{8,104},... | collective-permute-start | bytes 4374536 | tf_op jit(solution)/shard_map/ppermute | solution.py:73
  71.7 19.0 %collective-permute-done.13.refs_1_ = bf16[33,64,128]{2,1,0:T(8,128)(2,1)S(1)} collective-permute-done((bf16[33,64,128]{2,1,0:T(8,128)(2,1)S(1)}, bf16[33,64,128]{2,1,0:T(8,128)(2,1)S(1)}, u32[]{:S(2)}, u32[]{:S(2)}) %collective-permute-start.13) | collective-permute-done | bytes 540704 | tf_op jit(solution)/shard_map/ppermute | solution.py:73
  92.5 1.9 %collective-permute-start.17 = (bf16[36,64,128]{2,1,0:T(8,128)(2,1)S(1)}, bf16[36,64,128]{2,1,0:T(8,128)(2,1)S(1)}, u32[]{:S(2)}, u32[]{:S(2)}) collective-permute-start(bf16[36,64,128]{2,1,0:T(8,128)(2,1)S(1)} %get-tuple-element.156), channel_id=1, source_target_pairs={{0,24},{2,98},{4,28},{6,102},{1,25},{3,99},{5,29},{7,103},{8,16},{... | collective-permute-start | bytes 1769480 | tf_op jit(solution)/shard_map/ppermute | solution.py:73
  95.4 1.7 %shard_map.202 = (bf16[256,1024]{1,0:T(8,128)(2,1)}, f32[256,1024]{1,0:T(8,128)}) custom-call(f32[256,1024]{1,0:T(8,128)S(1)} %get-tuple-element.123.refs_3_.refs_0_, bf16[256,1024]{1,0:T(8,128)(2,1)S(1)} %shard_map.194.refs_1_, bf16[256,1024]{1,0:T(8,128)(2,1)S(1)} %collective-permute-done.15.refs_2_, bf16[256,1024]{1,0:T(8,128)(2,1)S(1)} %get-tuple-element.149.refs_3_, ...), custom_call_target="tpu_custom_call" | custom-call | flops 30000001024 | tf_op jit(solution)/shard_map/pallas_call | solution.py:117
  97.2 3.4 %collective-permute-done.14.refs_0_ = bf16[36,64,128]{2,1,0:T(8,128)(2,1)S(1)} collective-permute-done((bf16[36,64,128]{2,1,0:T(8,128)(2,1)S(1)}, bf16[36,64,128]{2,1,0:T(8,128)(2,1)S(1)}, u32[]{:S(2)}, u32[]{:S(2)}) %collective-permute-start.14) | collective-permute-done | bytes 589856 | tf_op jit(solution)/shard_map/ppermute | solution.py:73
  100.5 7.0 %collective-permute-done.17.refs_1_ = bf16[36,64,128]{2,1,0:T(8,128)(2,1)S(1)} collective-permute-done((bf16[36,64,128]{2,1,0:T(8,128)(2,1)S(1)}, bf16[36,64,128]{2,1,0:T(8,128)(2,1)S(1)}, u32[]{:S(2)}, u32[]{:S(2)}) %collective-permute-start.17) | collective-permute-done | bytes 589856 | tf_op jit(solution)/shard_map/ppermute | solution.py:73
  107.5 1.7 %collective-permute-done.18.refs_2_ = bf16[36,64,128]{2,1,0:T(8,128)(2,1)S(1)} collective-permute-done((bf16[36,64,128]{2,1,0:T(8,128)(2,1)S(1)}, bf16[36,64,128]{2,1,0:T(8,128)(2,1)S(1)}, u32[]{:S(2)}, u32[]{:S(2)}) %collective-permute-start.18) | collective-permute-done | bytes 589856 | tf_op jit(solution)/shard_map/ppermute | solution.py:73
  111.0 4.4 %collective-permute-done.19.refs_1_ = bf16[37,32,128]{2,1,0:T(8,128)(2,1)S(1)} collective-permute-done((bf16[37,32,128]{2,1,0:T(8,128)(2,1)S(1)}, bf16[37,32,128]{2,1,0:T(8,128)(2,1)S(1)}, u32[]{:S(2)}, u32[]{:S(2)}) %collective-permute-start.19) | collective-permute-done | bytes 303136 | tf_op jit(solution)/shard_map/ppermute | solution.py:73
  115.5 5.7 %collective-permute-start.20 = (f32[37,16,128]{2,1,0:T(8,128)S(1)}, f32[37,16,128]{2,1,0:T(8,128)S(1)}, u32[]{:S(2)}, u32[]{:S(2)}) collective-permute-start(f32[37,16,128]{2,1,0:T(8,128)S(1)} %get-tuple-element.163), channel_id=1, source_target_pairs={{0,2},{2,0},{4,6},{6,4},{1,3},{3,1},{5,7},{7,5},{8,10},{10,8},{12,... | collective-permute-start | bytes 909320 | tf_op jit(solution)/shard_map/ppermute | solution.py:73
  (64 shorter events, 26.2 us)
Async XLA Ops:
  0.6 8.8 %collective-permute-start.1 = (bf16[256,1024]{1,0:T(8,128)(2,1)}, bf16[256,1024]{1,0:T(8,128)(2,1)S(1)}, u32[]{:S(2)}, u32[]{:S(2)}) collective-permute-start(bf16[256,1024]{1,0:T(8,128)(2,1)} %refs_5_.8), channel_id=1, source_target_pairs={{0,2},{2,0},{4,6},{6,4},{1,3},{3,1},{5,7},{7,5},{8,10},{10,8},{12,... | collective-permute-start | bytes 1572872 | tf_op jit(solution)/shard_map/ppermute | solution.py:73
  5.1 4.3 %collective-permute-start = (bf16[16,512]{1,0:T(8,128)(2,1)S(1)}, bf16[16,512]{1,0:T(8,128)(2,1)S(1)}, u32[]{:S(2)}, u32[]{:S(2)}) collective-permute-start(bf16[16,512]{1,0:T(8,128)(2,1)S(1)} %get-tuple-element.96), channel_id=1, source_target_pairs={{0,2},{2,4},{4,6},{6,8},{8,10},{10,12},{12,14},{14,16},{16,18},{18... | collective-permute-start | bytes 49160 | tf_op jit(solution)/shard_map/ppermute | solution.py:79
  10.1 15.2 %slice-start = ((s8[4718592]{0:T(1024)(128)(4,1)}), s8[4194304]{0:T(1024)(128)(4,1)S(1)}, s32[]{:S(2)}) async-start(s8[4718592]{0:T(1024)(128)(4,1)} %bitcast.8), calls=%async_computation | async-start | bytes 8388608
  10.1 15.1 %slice-start.2 = ((s8[4718592]{0:T(1024)(128)(4,1)}), s8[4194304]{0:T(1024)(128)(4,1)S(1)}, s32[]{:S(2)}) async-start(s8[4718592]{0:T(1024)(128)(4,1)} %bitcast.10), calls=%async_computation.2 | async-start | bytes 8388608
  10.1 15.1 %slice-start.1 = ((s8[4718592]{0:T(1024)(128)(4,1)}), s8[524288]{0:T(1024)(128)(4,1)S(1)}, s32[]{:S(2)}) async-start(s8[4718592]{0:T(1024)(128)(4,1)} %bitcast.8), calls=%async_computation.1 | async-start | bytes 1048576
  10.1 15.1 %collective-permute-start.2 = (bf16[256,1024]{1,0:T(8,128)(2,1)S(1)}, bf16[256,1024]{1,0:T(8,128)(2,1)S(1)}, u32[]{:S(2)}, u32[]{:S(2)}) collective-permute-start(bf16[256,1024]{1,0:T(8,128)(2,1)S(1)} %get-tuple-element.100.refs_1_), channel_id=1, source_target_pairs={{0,1},{2,3},{4,5},{6,7},{1,0},{3,2},{5,4},{7,6},{8,9},{10,11},{12,... | collective-permute-start | bytes 1572872 | tf_op jit(solution)/shard_map/ppermute | solution.py:73
  28.6 6.3 %collective-permute-start.3 = (bf16[256,4480]{1,0:T(8,128)(2,1)S(1)}, bf16[256,4480]{1,0:T(8,128)(2,1)S(1)}, u32[]{:S(2)}, u32[]{:S(2)}) collective-permute-start(bf16[256,4480]{1,0:T(8,128)(2,1)S(1)} %get-tuple-element.110), channel_id=1, source_target_pairs={{0,2},{2,0},{4,6},{6,4},{1,3},{3,1},{5,7},{7,5},{8,10},{10,8},{12,... | collective-permute-start | bytes 6881288 | tf_op jit(solution)/shard_map/ppermute | solution.py:73
  29.2 17.4 %collective-permute-start.7 = (bf16[256,1280]{1,0:T(8,128)(2,1)S(1)}, bf16[256,1280]{1,0:T(8,128)(2,1)S(1)}, u32[]{:S(2)}, u32[]{:S(2)}) collective-permute-start(bf16[256,1280]{1,0:T(8,128)(2,1)S(1)} %get-tuple-element.119), channel_id=1, source_target_pairs={{0,2},{2,0},{4,6},{6,4},{1,3},{3,1},{5,7},{7,5},{8,10},{10,8},{12,... | collective-permute-start | bytes 1966088 | tf_op jit(solution)/shard_map/ppermute | solution.py:73
  31.9 14.7 %collective-permute-start.6 = (bf16[256,1024]{1,0:T(8,128)(2,1)S(1)}, bf16[256,1024]{1,0:T(8,128)(2,1)S(1)}, u32[]{:S(2)}, u32[]{:S(2)}) collective-permute-start(bf16[256,1024]{1,0:T(8,128)(2,1)S(1)} %shard_map.193.refs_1_), channel_id=1, source_target_pairs={{0,1},{2,3},{4,5},{6,7},{1,0},{3,2},{5,4},{7,6},{8,9},{10,11},{12,... | collective-permute-start | bytes 1572872 | tf_op jit(solution)/shard_map/ppermute | solution.py:73
  37.7 26.3 %collective-permute-start.4 = (bf16[112,64,128]{2,1,0:T(8,128)(2,1)S(1)}, bf16[112,64,128]{2,1,0:T(8,128)(2,1)S(1)}, u32[]{:S(2)}, u32[]{:S(2)}) collective-permute-start(bf16[112,64,128]{2,1,0:T(8,128)(2,1)S(1)} %get-tuple-element.111), channel_id=1, source_target_pairs={{0,32},{2,10},{4,36},{6,14},{1,33},{3,11},{5,37},{7,15},{8,40},{10... | collective-permute-start | bytes 5505032 | tf_op jit(solution)/shard_map/ppermute | solution.py:73
  41.7 22.3 %collective-permute-start.5 = (bf16[104,64,128]{2,1,0:T(8,128)(2,1)S(1)}, bf16[104,64,128]{2,1,0:T(8,128)(2,1)S(1)}, u32[]{:S(2)}, u32[]{:S(2)}) collective-permute-start(bf16[104,64,128]{2,1,0:T(8,128)(2,1)S(1)} %get-tuple-element.115), channel_id=1, source_target_pairs={{0,96},{2,26},{4,100},{6,30},{1,97},{3,27},{5,101},{7,31},{8,104},... | collective-permute-start | bytes 5111816 | tf_op jit(solution)/shard_map/ppermute | solution.py:73
  47.0 6.8 %collective-permute-start.8 = (f32[8,512]{1,0:T(8,128)S(1)}, f32[8,512]{1,0:T(8,128)S(1)}, u32[]{:S(2)}, u32[]{:S(2)}) collective-permute-start(f32[8,512]{1,0:T(8,128)S(1)} %shard_map.196), channel_id=1, source_target_pairs={{2,0},{4,2},{6,4},{8,6},{10,8},{12,10},{14,12},{16,14},{18,16},{20... | collective-permute-start | bytes 49160 | tf_op jit(solution)/shard_map/ppermute | solution.py:79
  55.0 4.1 %collective-permute-start.9 = (bf16[7,256,256]{2,1,0:T(8,128)(2,1)S(1)}, bf16[7,256,256]{2,1,0:T(8,128)(2,1)S(1)}, u32[]{:S(2)}, u32[]{:S(2)}) collective-permute-start(bf16[7,256,256]{2,1,0:T(8,128)(2,1)S(1)} %get-tuple-element.130), channel_id=1, source_target_pairs={{0,2},{2,0},{4,6},{6,4},{1,3},{3,1},{5,7},{7,5},{8,10},{10,8},{12,... | collective-permute-start | bytes 2752520 | tf_op jit(solution)/shard_map/ppermute | solution.py:73
  55.1 4.0 %collective-permute-start.10 = (f32[8,128]{1,0:T(8,128)S(1)}, f32[8,128]{1,0:T(8,128)S(1)}, u32[]{:S(2)}, u32[]{:S(2)}) collective-permute-start(f32[8,128]{1,0:T(8,128)S(1)} %get-tuple-element.133.refs_7_), channel_id=1, source_target_pairs={{0,1},{2,3},{4,5},{6,7},{1,0},{3,2},{5,4},{7,6},{8,9},{10,11},{12,... | collective-permute-start | bytes 12296 | tf_op jit(solution)/shard_map/ppermute | solution.py:73
  64.8 26.0 %collective-permute-start.12 = (bf16[89,64,128]{2,1,0:T(8,128)(2,1)S(1)}, bf16[89,64,128]{2,1,0:T(8,128)(2,1)S(1)}, u32[]{:S(2)}, u32[]{:S(2)}) collective-permute-start(bf16[89,64,128]{2,1,0:T(8,128)(2,1)S(1)} %get-tuple-element.137), channel_id=1, source_target_pairs={{0,96},{2,26},{4,100},{6,30},{1,97},{3,27},{5,101},{7,31},{8,104},... | collective-permute-start | bytes 4374536 | tf_op jit(solution)/shard_map/ppermute | solution.py:73
  67.1 23.7 %collective-permute-start.11 = (bf16[85,64,128]{2,1,0:T(8,128)(2,1)S(1)}, bf16[85,64,128]{2,1,0:T(8,128)(2,1)S(1)}, u32[]{:S(2)}, u32[]{:S(2)}) collective-permute-start(bf16[85,64,128]{2,1,0:T(8,128)(2,1)S(1)} %get-tuple-element.136), channel_id=1, source_target_pairs={{0,32},{2,10},{4,36},{6,14},{1,33},{3,11},{5,37},{7,15},{8,40},{10... | collective-permute-start | bytes 4177928 | tf_op jit(solution)/shard_map/ppermute | solution.py:73
  67.1 23.6 %collective-permute-start.13 = (bf16[33,64,128]{2,1,0:T(8,128)(2,1)S(1)}, bf16[33,64,128]{2,1,0:T(8,128)(2,1)S(1)}, u32[]{:S(2)}, u32[]{:S(2)}) collective-permute-start(bf16[33,64,128]{2,1,0:T(8,128)(2,1)S(1)} %get-tuple-element.143), channel_id=1, source_target_pairs={{0,64},{2,18},{4,68},{6,22},{1,65},{3,19},{5,69},{7,23},{8,72},{10... | collective-permute-start | bytes 1622024 | tf_op jit(solution)/shard_map/ppermute | solution.py:73
  68.7 26.7 %collective-permute-start.15 = (bf16[256,1024]{1,0:T(8,128)(2,1)S(1)}, bf16[256,1024]{1,0:T(8,128)(2,1)S(1)}, u32[]{:S(2)}, u32[]{:S(2)}) collective-permute-start(bf16[256,1024]{1,0:T(8,128)(2,1)S(1)} %shard_map.194.refs_1_), channel_id=1, source_target_pairs={{0,1},{2,3},{4,5},{6,7},{1,0},{3,2},{5,4},{7,6},{8,9},{10,11},{12,... | collective-permute-start | bytes 1572872 | tf_op jit(solution)/shard_map/ppermute | solution.py:73
  70.0 25.4 %collective-permute-start.16 = (bf16[256,1024]{1,0:T(8,128)(2,1)S(1)}, bf16[256,1024]{1,0:T(8,128)(2,1)S(1)}, u32[]{:S(2)}, u32[]{:S(2)}) collective-permute-start(bf16[256,1024]{1,0:T(8,128)(2,1)S(1)} %get-tuple-element.149.refs_3_), channel_id=1, source_target_pairs={{0,1},{2,3},{4,5},{6,7},{1,0},{3,2},{5,4},{7,6},{8,9},{10,11},{12,... | collective-permute-start | bytes 1572872 | tf_op jit(solution)/shard_map/ppermute | solution.py:73
  91.4 9.1 %collective-permute-start.14 = (bf16[36,64,128]{2,1,0:T(8,128)(2,1)S(1)}, bf16[36,64,128]{2,1,0:T(8,128)(2,1)S(1)}, u32[]{:S(2)}, u32[]{:S(2)}) collective-permute-start(bf16[36,64,128]{2,1,0:T(8,128)(2,1)S(1)} %get-tuple-element.147), channel_id=1, source_target_pairs={{0,8},{2,34},{4,12},{6,38},{1,9},{3,35},{5,13},{7,39},{8,0},{10,42... | collective-permute-start | bytes 1769480 | tf_op jit(solution)/shard_map/ppermute | solution.py:73
  92.5 15.1 %collective-permute-start.17 = (bf16[36,64,128]{2,1,0:T(8,128)(2,1)S(1)}, bf16[36,64,128]{2,1,0:T(8,128)(2,1)S(1)}, u32[]{:S(2)}, u32[]{:S(2)}) collective-permute-start(bf16[36,64,128]{2,1,0:T(8,128)(2,1)S(1)} %get-tuple-element.156), channel_id=1, source_target_pairs={{0,24},{2,98},{4,28},{6,102},{1,25},{3,99},{5,29},{7,103},{8,16},{... | collective-permute-start | bytes 1769480 | tf_op jit(solution)/shard_map/ppermute | solution.py:73
  94.4 14.9 %collective-permute-start.18 = (bf16[36,64,128]{2,1,0:T(8,128)(2,1)S(1)}, bf16[36,64,128]{2,1,0:T(8,128)(2,1)S(1)}, u32[]{:S(2)}, u32[]{:S(2)}) collective-permute-start(bf16[36,64,128]{2,1,0:T(8,128)(2,1)S(1)} %get-tuple-element.157), channel_id=1, source_target_pairs={{0,16},{2,66},{4,20},{6,70},{1,17},{3,67},{5,21},{7,71},{8,24},{10... | collective-permute-start | bytes 1769480 | tf_op jit(solution)/shard_map/ppermute | solution.py:73
  109.6 5.7 %collective-permute-start.19 = (bf16[37,32,128]{2,1,0:T(8,128)(2,1)S(1)}, bf16[37,32,128]{2,1,0:T(8,128)(2,1)S(1)}, u32[]{:S(2)}, u32[]{:S(2)}) collective-permute-start(bf16[37,32,128]{2,1,0:T(8,128)(2,1)S(1)} %get-tuple-element.161), channel_id=1, source_target_pairs={{0,4},{2,6},{4,0},{6,2},{1,5},{3,7},{5,1},{7,3},{8,12},{10,14},{12... | collective-permute-start | bytes 909320 | tf_op jit(solution)/shard_map/ppermute | solution.py:73
  115.5 6.9 %collective-permute-start.20 = (f32[37,16,128]{2,1,0:T(8,128)S(1)}, f32[37,16,128]{2,1,0:T(8,128)S(1)}, u32[]{:S(2)}, u32[]{:S(2)}) collective-permute-start(f32[37,16,128]{2,1,0:T(8,128)S(1)} %get-tuple-element.163), channel_id=1, source_target_pairs={{0,2},{2,0},{4,6},{6,4},{1,3},{3,1},{5,7},{7,5},{8,10},{10,8},{12,... | collective-permute-start | bytes 909320 | tf_op jit(solution)/shard_map/ppermute | solution.py:73
  (9 other events, 74.6 us)

commit v9 on v8

--- a/solution.py
+++ b/solution.py
@@ -28,6 +28,7 @@
 
 ACROSS = device_pairs(lambda y, z, x, core: (y, z, (x + 2) % 4, core))
 BESIDE = device_pairs(lambda y, z, x, core: (y, z, x ^ 1, core))
+BESIDE_OTHER = device_pairs(lambda y, z, x, core: (y, z, x ^ 1, 1 - core))
 CORES = device_pairs(lambda y, z, x, core: (y, z, x, 1 - core))
 
 
@@ -490,23 +491,29 @@
 
 
 def third_kernel(scalars, *refs):
-    gots, (kept, small), (send, keep) = refs[:3], refs[3:5], refs[5:]
-    here = scalars[2]
+    gots, (kept, small), (mine, away, near, far, new_small) = refs[:3], refs[3:5], refs[5:]
+    here, core = scalars[2], scalars[3]
     for first in range(0, TILES, 7):
         at = slice(first, first + 7)
         value = kept[at].astype(F32)
         for got in gots:
             value = value + got[at].astype(F32)
         zero, one = value[:, :32], value[:, 32:]
-        keep[at] = jnp.where(here == 0, zero, one)
-        send[at] = jnp.where(here == 0, one, zero).astype(BF16)
+        stay, leave = jnp.where(here == 0, zero, one), jnp.where(here == 0, one, zero)
+        mine[at] = jnp.where(core == 0, stay[:, :16], stay[:, 16:])
+        away[at] = jnp.where(core == 0, stay[:, 16:], stay[:, :16])
+        near[at] = jnp.where(core == 0, leave[:, :16], leave[:, 16:]).astype(BF16)
+        far[at] = jnp.where(core == 0, leave[:, 16:], leave[:, :16]).astype(BF16)
     value = sum_small(small[...], *(join_small(got, TILES) for got in gots))
     high = value.astype(BF16)
     low = (value - high.astype(F32)).astype(BF16)
-    send[TILES] = high
-    send[TILES + 1] = low
-    keep[TILES] = high.astype(F32)
-    keep[TILES + 1] = low.astype(F32)
+    new_small[...] = high.astype(F32) + low.astype(F32)
+    for at in range(2):
+        rows = slice(16 * at, 16 * at + 16)
+        away[TILES + at] = new_small[rows]
+        for target in (near, far):
+            target[TILES + at] = high[rows]
+            target[TILES + 2 + at] = low[rows]
 
 
 def finish_kernel(
@@ -518,25 +525,14 @@
     tokens_grad[...] = resid_grad[...] + norm_backward(back, values, norm_scale(values), gain[...])
 
 
-def cores_kernel(scalars, keep, got, mine, away):
+def outputs_kernel(scalars, mine, away, near, far, small, down, gate, up, inner, out, gain_one, gain_two, taps):
     core = scalars[3]
-    total = keep[:TILES] + got[:TILES].astype(F32)
-    zero, one = total[:, :16], total[:, 16:]
-    mine[:TILES] = jnp.where(core == 0, zero, one)
-    away[:TILES] = jnp.where(core == 0, one, zero)
-    small = (keep[TILES] + keep[TILES + 1]) + (got[TILES].astype(F32) + got[TILES + 1].astype(F32))
-    for target in (mine, away):
-        target[TILES] = small[:16]
-        target[TILES + 1] = small[16:]
-
-
-def outputs_kernel(scalars, mine, got, down, gate, up, inner, out, gain_one, gain_two, taps):
-    core = scalars[3]
 
     def place(target, tile, column, columns):
-        zero, one = jnp.where(core == 0, mine[tile], got[tile]), jnp.where(core == 0, got[tile], mine[tile])
-        target[:, column : column + 128] = zero
-        target[:, columns + column : columns + column + 128] = one
+        own = mine[tile] + near[tile].astype(F32)
+        other = away[tile] + far[tile].astype(F32)
+        target[:, column : column + 128] = jnp.where(core == 0, own, other)
+        target[:, columns + column : columns + column + 128] = jnp.where(core == 0, other, own)
 
     for matrix, target in enumerate((down, gate, up)):
         for tile in range(WIDE_COLUMNS // 128):
@@ -544,8 +540,12 @@
     for kind in range(4):
         for column in range(2):
             place(inner.at[kind] if kind < 3 else out, WIDE_TILES + 2 * kind + column, column * 128, 256)
-    gains = mine[TILES] + got[TILES]
-    rest = mine[TILES + 1] + got[TILES + 1]
+    sums = []
+    for at in range(2):
+        own = small[16 * at : 16 * at + 16] + (near[TILES + at].astype(F32) + near[TILES + 2 + at].astype(F32))
+        other = away[TILES + at] + (far[TILES + at].astype(F32) + far[TILES + 2 + at].astype(F32))
+        sums.append(own + other)
+    gains, rest = sums
     for at in range(8):
         lanes = slice(at * 128, at * 128 + 128)
         gain_one[:, lanes] = gains[at : at + 1]
@@ -728,20 +728,16 @@
         flops=LONG,
     )
     gots[0], mixed, tokens_grad = lax.optimization_barrier((gots[0], mixed, tokens_grad))
-    beside, kept = run(
+    mine, away, near, far, small = run(
         third_kernel,
         operands=gots + [keep, small],
-        outs=[like((TILES + 2, 32, 128), BF16), like((TILES + 2, 32, 128), F32)],
-    )
-    beside = swap(beside, BESIDE)
-    mine, away = run(
-        cores_kernel,
-        operands=[kept, beside],
-        outs=[like((TILES + 2, 16, 128), F32)] * 2,
+        outs=[like((TILES, 16, 128), F32), like((TILES + 2, 16, 128), F32)]
+        + [like((TILES + 4, 16, 128), BF16)] * 2
+        + [like((32, 128), F32)],
     )
     down_g, gate_g, up_g, in_g, out_g, gain_one_g, gain_two_g, conv_g = run(
         outputs_kernel,
-        operands=[mine, swap(away, CORES)],
+        operands=[mine, swap(away, CORES), swap(near, BESIDE), swap(far, BESIDE_OTHER), small],
         outs=[like((16, 2 * WIDE_COLUMNS), F32)] * 3
         + [like((3, 16, channels), F32), like((16, channels), F32)]
         + [like((1, width), F32)] * 2

time: 123 us -> 125 us (1.016)
  waiting for transfers between devices: 55.4 us -> 57.3 us
    ppermute x19 -> x20, waiting for transfers between devices: 53.4 us -> 55.4 us  [swap(): return lax.ppermute(value, AXES, pairs)]
    ppermute x19 -> x20, starting transfers between devices: 32.7 us -> 31.9 us  [swap(): return lax.ppermute(value, AXES, pairs)]
    pallas_call x20 -> x19, Pallas kernels: 27.1 us -> 27.2 us  [call(): pl.pallas_call(kernel, out_shape=tuple(outs), in_specs=specs, out_specs=t...]
  transfers between devices with their start and end apart: 21 -> 22, of which waited for: 11 -> 11; matrix products, arithmetic and copies ran while one was open for 0% -> 0% of each run, Pallas kernels for 17% -> 17%
where the time goes in v9:
time: 125 us; the launch traced here: 124 us
  waiting for transfers between devices  57.3 us (46%)
  starting transfers between devices  38.2 us (31%)
  Pallas kernels  27.2 us (22%)
  between operations  1.64 us (1%)
    ppermute x20, waiting for transfers between devices, swap(): return lax.ppermute(value, AXES, pairs)  55.4 us
    ppermute x20, starting transfers between devices, swap(): return lax.ppermute(value, AXES, pairs)  31.9 us
    pallas_call x19, Pallas kernels, call(): pl.pallas_call(kernel, out_shape=tuple(outs), in_specs=specs, out_specs=t...  27.2 us
    ppermute x2, starting transfers between devices, from_behind(): lax.ppermute(value, axis, [(source, source + steps) for source in range(l...  6.27 us
  transfers between devices with their start and end apart: 22, of which 11 were waited for; matrix products, arithmetic and copies ran while one was open for 0% of the time, Pallas kernels for 17%

profile of v9, /device:TPU:1, one launch (start us, length us, event | category | flops | bytes accessed | tf_op | source)
XLA Modules:
  0.0 124.4 jit_solution(11485406917694850217)
XLA Ops:
  2.8 2.3 %shard_map.186 = (bf16[16,512]{1,0:T(8,128)(2,1)S(1)}, bf16[256,1024]{1,0:T(8,128)(2,1)S(1)}, f32[1,1024]{1,0:T(1,128)S(1)}, bf16[3,1024,512]{2,1,0:T(8,128)(2,1)S(1)}, s32[8,128]{1,0:T(8,128)S(1)}) custom-call(s32[1]{0:T(128)S(6)} %copy.25.refs_0_, bf16[256,1024]{1,0:T(8,128)(2,1)} %refs_5_.9, f32[1,1024]{1,0:T(1,128)} %bitcast.17, ...), custom_call_target="tpu_custom_call" | custom-call | tf_op jit(solution)/shard_map/pallas_call | solution.py:118
  5.1 3.1 %collective-permute-start = (bf16[16,512]{1,0:T(8,128)(2,1)S(1)}, bf16[16,512]{1,0:T(8,128)(2,1)S(1)}, u32[]{:S(2)}, u32[]{:S(2)}) collective-permute-start(bf16[16,512]{1,0:T(8,128)(2,1)S(1)} %get-tuple-element.97), channel_id=1, source_target_pairs={{0,2},{2,4},{4,6},{6,8},{8,10},{10,12},{12,14},{14,16},{16,18},{18... | collective-permute-start | bytes 49160 | tf_op jit(solution)/shard_map/ppermute | solution.py:80
  10.1 2.5 %collective-permute-start.2 = (bf16[256,1024]{1,0:T(8,128)(2,1)S(1)}, bf16[256,1024]{1,0:T(8,128)(2,1)S(1)}, u32[]{:S(2)}, u32[]{:S(2)}) collective-permute-start(bf16[256,1024]{1,0:T(8,128)(2,1)S(1)} %get-tuple-element.101.refs_1_), channel_id=1, source_target_pairs={{0,1},{2,3},{4,5},{6,7},{1,0},{3,2},{5,4},{7,6},{8,9},{10,11},{12,... | collective-permute-start | bytes 1572872 | tf_op jit(solution)/shard_map/ppermute | solution.py:74
  14.1 11.1 %collective-permute-done.2.refs_2_ = bf16[256,1024]{1,0:T(8,128)(2,1)S(1)} collective-permute-done((bf16[256,1024]{1,0:T(8,128)(2,1)S(1)}, bf16[256,1024]{1,0:T(8,128)(2,1)S(1)}, u32[]{:S(2)}, u32[]{:S(2)}) %collective-permute-start.2) | collective-permute-done | bytes 524320 | tf_op jit(solution)/shard_map/ppermute | solution.py:74
  25.3 3.4 %shard_map.190 = (f32[256,1024]{1,0:T(8,128)S(1)}, bf16[256,1024]{1,0:T(8,128)(2,1)S(1)}, bf16[256,2304]{1,0:T(8,128)(2,1)S(1)}, bf16[256,2304]{1,0:T(8,128)(2,1...) custom-call(bf16[256,1024]{1,0:T(8,128)(2,1)S(1)} %copy-done.2, ...), custom_call_target="tpu_custom_call" | custom-call | tf_op jit(solution)/shard_map/pallas_call | solution.py:118
  29.3 2.6 %shard_map.193.refs_1_ = bf16[256,1024]{1,0:T(8,128)(2,1)S(1)} custom-call(bf16[256,2304]{1,0:T(8,128)(2,1)S(1)} %get-tuple-element.110.refs_4_.refs_1_.refs_0_, bf16[256,2304]{1,0:T(8,128)(2,1)S(1)} %get-tuple-element.114.refs_2_.refs_1_, bf16[1024,2304]{1,0:T(8,128)(2,1)S(1)} %bitcast.9, bf16[1024,2304]{1,0:T(8,128)(2,1)S(1)} %bitcast.11), custom_call_target="tpu_custom_call" | custom-call | tf_op jit(solution)/shard_map/pallas_call | solution.py:118
  31.9 3.0 %collective-permute-start.6 = (bf16[256,1024]{1,0:T(8,128)(2,1)S(1)}, bf16[256,1024]{1,0:T(8,128)(2,1)S(1)}, u32[]{:S(2)}, u32[]{:S(2)}) collective-permute-start(bf16[256,1024]{1,0:T(8,128)(2,1)S(1)} %shard_map.193.refs_1_), channel_id=1, source_target_pairs={{0,1},{2,3},{4,5},{6,7},{1,0},{3,2},{5,4},{7,6},{8,9},{10,11},{12,... | collective-permute-start | bytes 1572872 | tf_op jit(solution)/shard_map/ppermute | solution.py:74
  34.9 2.8 %shard_map.191 = (bf16[112,64,128]{2,1,0:T(8,128)(2,1)S(1)}, bf16[112,64,128]{2,1,0:T(8,128)(2,1)S(1)}, bf16[1024,512]{1,0:T(8,128)(2,1)S(1)}) custom-call(bf16[256,1024]{1,0:T(8,128)(2,1)S(1)} %get-tuple-element.107.refs_0_, bf16[256,1024]{1,0:T(8,128)(2,1)S(1)} %copy-done.4, bf16[256,1024]{1,0:T(8,128)(2,1)S(1)} %collective-permute-done.1.refs_2_, ...), custom_call_target="tpu_custom_call" | custom-call | tf_op jit(solution)/shard_map/pallas_call | solution.py:118
  37.7 1.9 %collective-permute-start.4 = (bf16[112,64,128]{2,1,0:T(8,128)(2,1)S(1)}, bf16[112,64,128]{2,1,0:T(8,128)(2,1)S(1)}, u32[]{:S(2)}, u32[]{:S(2)}) collective-permute-start(bf16[112,64,128]{2,1,0:T(8,128)(2,1)S(1)} %get-tuple-element.112), channel_id=1, source_target_pairs={{0,32},{2,10},{4,36},{6,14},{1,33},{3,11},{5,37},{7,15},{8,40},{10... | collective-permute-start | bytes 5505032 | tf_op jit(solution)/shard_map/ppermute | solution.py:74
  39.6 2.1 %shard_map.192 = (bf16[104,64,128]{2,1,0:T(8,128)(2,1)S(1)}, bf16[104,64,128]{2,1,0:T(8,128)(2,1)S(1)}) custom-call(bf16[1024,512]{1,0:T(8,128)(2,1)S(1)} %get-tuple-element.113.refs_0_, bf16[256,2304]{1,0:T(8,128)(2,1)S(1)} %get-tuple-element.110.refs_4_.refs_1_.refs_0_, bf16[256,2304]{1,0:T(8,128)(2,1)S(1)} %get-tuple-element.114.refs_2_.refs_1_, ...), custom_call_target="tpu_custom_call" | custom-call | tf_op jit(solution)/shard_map/pallas_call | solution.py:118
  41.7 2.3 %collective-permute-start.5 = (bf16[104,64,128]{2,1,0:T(8,128)(2,1)S(1)}, bf16[104,64,128]{2,1,0:T(8,128)(2,1)S(1)}, u32[]{:S(2)}, u32[]{:S(2)}) collective-permute-start(bf16[104,64,128]{2,1,0:T(8,128)(2,1)S(1)} %get-tuple-element.116), channel_id=1, source_target_pairs={{0,96},{2,26},{4,100},{6,30},{1,97},{3,27},{5,101},{7,31},{8,104},... | collective-permute-start | bytes 5111816 | tf_op jit(solution)/shard_map/ppermute | solution.py:74
  47.0 3.2 %collective-permute-start.8 = (f32[8,512]{1,0:T(8,128)S(1)}, f32[8,512]{1,0:T(8,128)S(1)}, u32[]{:S(2)}, u32[]{:S(2)}) collective-permute-start(f32[8,512]{1,0:T(8,128)S(1)} %shard_map.196), channel_id=1, source_target_pairs={{2,0},{4,2},{6,4},{8,6},{10,8},{12,10},{14,12},{16,14},{18,16},{20... | collective-permute-start | bytes 49160 | tf_op jit(solution)/shard_map/ppermute | solution.py:80
  51.9 2.0 %collective-permute-done.8.refs_2_ = f32[8,512]{1,0:T(8,128)S(1)} collective-permute-done((f32[8,512]{1,0:T(8,128)S(1)}, f32[8,512]{1,0:T(8,128)S(1)}, u32[]{:S(2)}, u32[]{:S(2)}) %collective-permute-start.8) | collective-permute-done | bytes 16416 | tf_op jit(solution)/shard_map/ppermute | solution.py:80
  55.1 2.8 %collective-permute-start.10 = (f32[8,128]{1,0:T(8,128)S(1)}, f32[8,128]{1,0:T(8,128)S(1)}, u32[]{:S(2)}, u32[]{:S(2)}) collective-permute-start(f32[8,128]{1,0:T(8,128)S(1)} %get-tuple-element.134.refs_7_), channel_id=1, source_target_pairs={{0,1},{2,3},{4,5},{6,7},{1,0},{3,2},{5,4},{7,6},{8,9},{10,11},{12,... | collective-permute-start | bytes 12296 | tf_op jit(solution)/shard_map/ppermute | solution.py:74
  60.8 3.1 %collective-permute-done.5.refs_1_ = bf16[104,64,128]{2,1,0:T(8,128)(2,1)S(1)} collective-permute-done((bf16[104,64,128]{2,1,0:T(8,128)(2,1)S(1)}, bf16[104,64,128]{2,1,0:T(8,128)(2,1)S(1)}, u32[]{:S(2)}, u32[]{:S(2)}) %collective-permute-start.5) | collective-permute-done | bytes 1703968 | tf_op jit(solution)/shard_map/ppermute | solution.py:74
  64.8 2.3 %collective-permute-start.12 = (bf16[89,64,128]{2,1,0:T(8,128)(2,1)S(1)}, bf16[89,64,128]{2,1,0:T(8,128)(2,1)S(1)}, u32[]{:S(2)}, u32[]{:S(2)}) collective-permute-start(bf16[89,64,128]{2,1,0:T(8,128)(2,1)S(1)} %get-tuple-element.138), channel_id=1, source_target_pairs={{0,96},{2,26},{4,100},{6,30},{1,97},{3,27},{5,101},{7,31},{8,104},... | collective-permute-start | bytes 4374536 | tf_op jit(solution)/shard_map/ppermute | solution.py:74
  71.7 19.0 %collective-permute-done.13.refs_1_ = bf16[33,64,128]{2,1,0:T(8,128)(2,1)S(1)} collective-permute-done((bf16[33,64,128]{2,1,0:T(8,128)(2,1)S(1)}, bf16[33,64,128]{2,1,0:T(8,128)(2,1)S(1)}, u32[]{:S(2)}, u32[]{:S(2)}) %collective-permute-start.13) | collective-permute-done | bytes 540704 | tf_op jit(solution)/shard_map/ppermute | solution.py:74
  92.5 1.9 %collective-permute-start.17 = (bf16[36,64,128]{2,1,0:T(8,128)(2,1)S(1)}, bf16[36,64,128]{2,1,0:T(8,128)(2,1)S(1)}, u32[]{:S(2)}, u32[]{:S(2)}) collective-permute-start(bf16[36,64,128]{2,1,0:T(8,128)(2,1)S(1)} %get-tuple-element.157), channel_id=1, source_target_pairs={{0,24},{2,98},{4,28},{6,102},{1,25},{3,99},{5,29},{7,103},{8,16},{... | collective-permute-start | bytes 1769480 | tf_op jit(solution)/shard_map/ppermute | solution.py:74
  97.2 3.4 %collective-permute-done.14.refs_0_ = bf16[36,64,128]{2,1,0:T(8,128)(2,1)S(1)} collective-permute-done((bf16[36,64,128]{2,1,0:T(8,128)(2,1)S(1)}, bf16[36,64,128]{2,1,0:T(8,128)(2,1)S(1)}, u32[]{:S(2)}, u32[]{:S(2)}) %collective-permute-start.14) | collective-permute-done | bytes 589856 | tf_op jit(solution)/shard_map/ppermute | solution.py:74
  100.5 7.0 %collective-permute-done.17.refs_1_ = bf16[36,64,128]{2,1,0:T(8,128)(2,1)S(1)} collective-permute-done((bf16[36,64,128]{2,1,0:T(8,128)(2,1)S(1)}, bf16[36,64,128]{2,1,0:T(8,128)(2,1)S(1)}, u32[]{:S(2)}, u32[]{:S(2)}) %collective-permute-start.17) | collective-permute-done | bytes 589856 | tf_op jit(solution)/shard_map/ppermute | solution.py:74
  107.5 1.7 %collective-permute-done.18.refs_2_ = bf16[36,64,128]{2,1,0:T(8,128)(2,1)S(1)} collective-permute-done((bf16[36,64,128]{2,1,0:T(8,128)(2,1)S(1)}, bf16[36,64,128]{2,1,0:T(8,128)(2,1)S(1)}, u32[]{:S(2)}, u32[]{:S(2)}) %collective-permute-start.18) | collective-permute-done | bytes 589856 | tf_op jit(solution)/shard_map/ppermute | solution.py:74
  109.8 4.5 %collective-permute-start.19 = (f32[37,16,128]{2,1,0:T(8,128)S(1)}, f32[37,16,128]{2,1,0:T(8,128)S(1)}, u32[]{:S(2)}, u32[]{:S(2)}) collective-permute-start(f32[37,16,128]{2,1,0:T(8,128)S(1)} %get-tuple-element.162), channel_id=1, source_target_pairs={{0,2},{2,0},{4,6},{6,4},{1,3},{3,1},{5,7},{7,5},{8,10},{10,8},{12,... | collective-permute-start | bytes 909320 | tf_op jit(solution)/shard_map/ppermute | solution.py:74
  116.0 3.9 %collective-permute-done.20.refs_2_ = bf16[39,16,128]{2,1,0:T(8,128)(2,1)S(1)} collective-permute-done((bf16[39,16,128]{2,1,0:T(8,128)(2,1)S(1)}, bf16[39,16,128]{2,1,0:T(8,128)(2,1)S(1)}, u32[]{:S(2)}, u32[]{:S(2)}) %collective-permute-start.20) | collective-permute-done | bytes 159776 | tf_op jit(solution)/shard_map/ppermute | solution.py:74
  120.0 3.6 %collective-permute-done.21.refs_3_ = bf16[39,16,128]{2,1,0:T(8,128)(2,1)S(1)} collective-permute-done((bf16[39,16,128]{2,1,0:T(8,128)(2,1)S(1)}, bf16[39,16,128]{2,1,0:T(8,128)(2,1)S(1)}, u32[]{:S(2)}, u32[]{:S(2)}) %collective-permute-start.21) | collective-permute-done | bytes 159776 | tf_op jit(solution)/shard_map/ppermute | solution.py:74
  (65 shorter events, 27.2 us)
Async XLA Ops:
  0.6 8.8 %collective-permute-start.1 = (bf16[256,1024]{1,0:T(8,128)(2,1)}, bf16[256,1024]{1,0:T(8,128)(2,1)S(1)}, u32[]{:S(2)}, u32[]{:S(2)}) collective-permute-start(bf16[256,1024]{1,0:T(8,128)(2,1)} %refs_5_.8), channel_id=1, source_target_pairs={{0,2},{2,0},{4,6},{6,4},{1,3},{3,1},{5,7},{7,5},{8,10},{10,8},{12,... | collective-permute-start | bytes 1572872 | tf_op jit(solution)/shard_map/ppermute | solution.py:74
  5.1 4.3 %collective-permute-start = (bf16[16,512]{1,0:T(8,128)(2,1)S(1)}, bf16[16,512]{1,0:T(8,128)(2,1)S(1)}, u32[]{:S(2)}, u32[]{:S(2)}) collective-permute-start(bf16[16,512]{1,0:T(8,128)(2,1)S(1)} %get-tuple-element.97), channel_id=1, source_target_pairs={{0,2},{2,4},{4,6},{6,8},{8,10},{10,12},{12,14},{14,16},{16,18},{18... | collective-permute-start | bytes 49160 | tf_op jit(solution)/shard_map/ppermute | solution.py:80
  10.1 15.2 %slice-start = ((s8[4718592]{0:T(1024)(128)(4,1)}), s8[4194304]{0:T(1024)(128)(4,1)S(1)}, s32[]{:S(2)}) async-start(s8[4718592]{0:T(1024)(128)(4,1)} %bitcast.8), calls=%async_computation | async-start | bytes 8388608
  10.1 15.1 %slice-start.2 = ((s8[4718592]{0:T(1024)(128)(4,1)}), s8[4194304]{0:T(1024)(128)(4,1)S(1)}, s32[]{:S(2)}) async-start(s8[4718592]{0:T(1024)(128)(4,1)} %bitcast.10), calls=%async_computation.2 | async-start | bytes 8388608
  10.1 15.1 %collective-permute-start.2 = (bf16[256,1024]{1,0:T(8,128)(2,1)S(1)}, bf16[256,1024]{1,0:T(8,128)(2,1)S(1)}, u32[]{:S(2)}, u32[]{:S(2)}) collective-permute-start(bf16[256,1024]{1,0:T(8,128)(2,1)S(1)} %get-tuple-element.101.refs_1_), channel_id=1, source_target_pairs={{0,1},{2,3},{4,5},{6,7},{1,0},{3,2},{5,4},{7,6},{8,9},{10,11},{12,... | collective-permute-start | bytes 1572872 | tf_op jit(solution)/shard_map/ppermute | solution.py:74
  28.6 6.3 %collective-permute-start.3 = (bf16[256,4480]{1,0:T(8,128)(2,1)S(1)}, bf16[256,4480]{1,0:T(8,128)(2,1)S(1)}, u32[]{:S(2)}, u32[]{:S(2)}) collective-permute-start(bf16[256,4480]{1,0:T(8,128)(2,1)S(1)} %get-tuple-element.111), channel_id=1, source_target_pairs={{0,2},{2,0},{4,6},{6,4},{1,3},{3,1},{5,7},{7,5},{8,10},{10,8},{12,... | collective-permute-start | bytes 6881288 | tf_op jit(solution)/shard_map/ppermute | solution.py:74
  29.2 17.4 %collective-permute-start.7 = (bf16[256,1280]{1,0:T(8,128)(2,1)S(1)}, bf16[256,1280]{1,0:T(8,128)(2,1)S(1)}, u32[]{:S(2)}, u32[]{:S(2)}) collective-permute-start(bf16[256,1280]{1,0:T(8,128)(2,1)S(1)} %get-tuple-element.120), channel_id=1, source_target_pairs={{0,2},{2,0},{4,6},{6,4},{1,3},{3,1},{5,7},{7,5},{8,10},{10,8},{12,... | collective-permute-start | bytes 1966088 | tf_op jit(solution)/shard_map/ppermute | solution.py:74
  31.9 14.7 %collective-permute-start.6 = (bf16[256,1024]{1,0:T(8,128)(2,1)S(1)}, bf16[256,1024]{1,0:T(8,128)(2,1)S(1)}, u32[]{:S(2)}, u32[]{:S(2)}) collective-permute-start(bf16[256,1024]{1,0:T(8,128)(2,1)S(1)} %shard_map.193.refs_1_), channel_id=1, source_target_pairs={{0,1},{2,3},{4,5},{6,7},{1,0},{3,2},{5,4},{7,6},{8,9},{10,11},{12,... | collective-permute-start | bytes 1572872 | tf_op jit(solution)/shard_map/ppermute | solution.py:74
  37.7 26.3 %collective-permute-start.4 = (bf16[112,64,128]{2,1,0:T(8,128)(2,1)S(1)}, bf16[112,64,128]{2,1,0:T(8,128)(2,1)S(1)}, u32[]{:S(2)}, u32[]{:S(2)}) collective-permute-start(bf16[112,64,128]{2,1,0:T(8,128)(2,1)S(1)} %get-tuple-element.112), channel_id=1, source_target_pairs={{0,32},{2,10},{4,36},{6,14},{1,33},{3,11},{5,37},{7,15},{8,40},{10... | collective-permute-start | bytes 5505032 | tf_op jit(solution)/shard_map/ppermute | solution.py:74
  41.7 22.3 %collective-permute-start.5 = (bf16[104,64,128]{2,1,0:T(8,128)(2,1)S(1)}, bf16[104,64,128]{2,1,0:T(8,128)(2,1)S(1)}, u32[]{:S(2)}, u32[]{:S(2)}) collective-permute-start(bf16[104,64,128]{2,1,0:T(8,128)(2,1)S(1)} %get-tuple-element.116), channel_id=1, source_target_pairs={{0,96},{2,26},{4,100},{6,30},{1,97},{3,27},{5,101},{7,31},{8,104},... | collective-permute-start | bytes 5111816 | tf_op jit(solution)/shard_map/ppermute | solution.py:74
  47.0 6.8 %collective-permute-start.8 = (f32[8,512]{1,0:T(8,128)S(1)}, f32[8,512]{1,0:T(8,128)S(1)}, u32[]{:S(2)}, u32[]{:S(2)}) collective-permute-start(f32[8,512]{1,0:T(8,128)S(1)} %shard_map.196), channel_id=1, source_target_pairs={{2,0},{4,2},{6,4},{8,6},{10,8},{12,10},{14,12},{16,14},{18,16},{20... | collective-permute-start | bytes 49160 | tf_op jit(solution)/shard_map/ppermute | solution.py:80
  55.0 4.1 %collective-permute-start.9 = (bf16[7,256,256]{2,1,0:T(8,128)(2,1)S(1)}, bf16[7,256,256]{2,1,0:T(8,128)(2,1)S(1)}, u32[]{:S(2)}, u32[]{:S(2)}) collective-permute-start(bf16[7,256,256]{2,1,0:T(8,128)(2,1)S(1)} %get-tuple-element.131), channel_id=1, source_target_pairs={{0,2},{2,0},{4,6},{6,4},{1,3},{3,1},{5,7},{7,5},{8,10},{10,8},{12,... | collective-permute-start | bytes 2752520 | tf_op jit(solution)/shard_map/ppermute | solution.py:74
  55.1 4.0 %collective-permute-start.10 = (f32[8,128]{1,0:T(8,128)S(1)}, f32[8,128]{1,0:T(8,128)S(1)}, u32[]{:S(2)}, u32[]{:S(2)}) collective-permute-start(f32[8,128]{1,0:T(8,128)S(1)} %get-tuple-element.134.refs_7_), channel_id=1, source_target_pairs={{0,1},{2,3},{4,5},{6,7},{1,0},{3,2},{5,4},{7,6},{8,9},{10,11},{12,... | collective-permute-start | bytes 12296 | tf_op jit(solution)/shard_map/ppermute | solution.py:74
  64.8 26.0 %collective-permute-start.12 = (bf16[89,64,128]{2,1,0:T(8,128)(2,1)S(1)}, bf16[89,64,128]{2,1,0:T(8,128)(2,1)S(1)}, u32[]{:S(2)}, u32[]{:S(2)}) collective-permute-start(bf16[89,64,128]{2,1,0:T(8,128)(2,1)S(1)} %get-tuple-element.138), channel_id=1, source_target_pairs={{0,96},{2,26},{4,100},{6,30},{1,97},{3,27},{5,101},{7,31},{8,104},... | collective-permute-start | bytes 4374536 | tf_op jit(solution)/shard_map/ppermute | solution.py:74
  67.1 23.7 %collective-permute-start.11 = (bf16[85,64,128]{2,1,0:T(8,128)(2,1)S(1)}, bf16[85,64,128]{2,1,0:T(8,128)(2,1)S(1)}, u32[]{:S(2)}, u32[]{:S(2)}) collective-permute-start(bf16[85,64,128]{2,1,0:T(8,128)(2,1)S(1)} %get-tuple-element.137), channel_id=1, source_target_pairs={{0,32},{2,10},{4,36},{6,14},{1,33},{3,11},{5,37},{7,15},{8,40},{10... | collective-permute-start | bytes 4177928 | tf_op jit(solution)/shard_map/ppermute | solution.py:74
  67.1 23.6 %collective-permute-start.13 = (bf16[33,64,128]{2,1,0:T(8,128)(2,1)S(1)}, bf16[33,64,128]{2,1,0:T(8,128)(2,1)S(1)}, u32[]{:S(2)}, u32[]{:S(2)}) collective-permute-start(bf16[33,64,128]{2,1,0:T(8,128)(2,1)S(1)} %get-tuple-element.144), channel_id=1, source_target_pairs={{0,64},{2,18},{4,68},{6,22},{1,65},{3,19},{5,69},{7,23},{8,72},{10... | collective-permute-start | bytes 1622024 | tf_op jit(solution)/shard_map/ppermute | solution.py:74
  68.7 26.7 %collective-permute-start.15 = (bf16[256,1024]{1,0:T(8,128)(2,1)S(1)}, bf16[256,1024]{1,0:T(8,128)(2,1)S(1)}, u32[]{:S(2)}, u32[]{:S(2)}) collective-permute-start(bf16[256,1024]{1,0:T(8,128)(2,1)S(1)} %shard_map.194.refs_1_), channel_id=1, source_target_pairs={{0,1},{2,3},{4,5},{6,7},{1,0},{3,2},{5,4},{7,6},{8,9},{10,11},{12,... | collective-permute-start | bytes 1572872 | tf_op jit(solution)/shard_map/ppermute | solution.py:74
  70.0 25.4 %collective-permute-start.16 = (bf16[256,1024]{1,0:T(8,128)(2,1)S(1)}, bf16[256,1024]{1,0:T(8,128)(2,1)S(1)}, u32[]{:S(2)}, u32[]{:S(2)}) collective-permute-start(bf16[256,1024]{1,0:T(8,128)(2,1)S(1)} %get-tuple-element.150.refs_3_), channel_id=1, source_target_pairs={{0,1},{2,3},{4,5},{6,7},{1,0},{3,2},{5,4},{7,6},{8,9},{10,11},{12,... | collective-permute-start | bytes 1572872 | tf_op jit(solution)/shard_map/ppermute | solution.py:74
  91.4 9.1 %collective-permute-start.14 = (bf16[36,64,128]{2,1,0:T(8,128)(2,1)S(1)}, bf16[36,64,128]{2,1,0:T(8,128)(2,1)S(1)}, u32[]{:S(2)}, u32[]{:S(2)}) collective-permute-start(bf16[36,64,128]{2,1,0:T(8,128)(2,1)S(1)} %get-tuple-element.148), channel_id=1, source_target_pairs={{0,8},{2,34},{4,12},{6,38},{1,9},{3,35},{5,13},{7,39},{8,0},{10,42... | collective-permute-start | bytes 1769480 | tf_op jit(solution)/shard_map/ppermute | solution.py:74
  92.5 15.1 %collective-permute-start.17 = (bf16[36,64,128]{2,1,0:T(8,128)(2,1)S(1)}, bf16[36,64,128]{2,1,0:T(8,128)(2,1)S(1)}, u32[]{:S(2)}, u32[]{:S(2)}) collective-permute-start(bf16[36,64,128]{2,1,0:T(8,128)(2,1)S(1)} %get-tuple-element.157), channel_id=1, source_target_pairs={{0,24},{2,98},{4,28},{6,102},{1,25},{3,99},{5,29},{7,103},{8,16},{... | collective-permute-start | bytes 1769480 | tf_op jit(solution)/shard_map/ppermute | solution.py:74
  94.4 14.9 %collective-permute-start.18 = (bf16[36,64,128]{2,1,0:T(8,128)(2,1)S(1)}, bf16[36,64,128]{2,1,0:T(8,128)(2,1)S(1)}, u32[]{:S(2)}, u32[]{:S(2)}) collective-permute-start(bf16[36,64,128]{2,1,0:T(8,128)(2,1)S(1)} %get-tuple-element.158), channel_id=1, source_target_pairs={{0,16},{2,66},{4,20},{6,70},{1,17},{3,67},{5,21},{7,71},{8,24},{10... | collective-permute-start | bytes 1769480 | tf_op jit(solution)/shard_map/ppermute | solution.py:74
  109.8 13.8 %collective-permute-start.19 = (f32[37,16,128]{2,1,0:T(8,128)S(1)}, f32[37,16,128]{2,1,0:T(8,128)S(1)}, u32[]{:S(2)}, u32[]{:S(2)}) collective-permute-start(f32[37,16,128]{2,1,0:T(8,128)S(1)} %get-tuple-element.162), channel_id=1, source_target_pairs={{0,2},{2,0},{4,6},{6,4},{1,3},{3,1},{5,7},{7,5},{8,10},{10,8},{12,... | collective-permute-start | bytes 909320 | tf_op jit(solution)/shard_map/ppermute | solution.py:74
  114.3 5.7 %collective-permute-start.20 = (bf16[39,16,128]{2,1,0:T(8,128)(2,1)S(1)}, bf16[39,16,128]{2,1,0:T(8,128)(2,1)S(1)}, u32[]{:S(2)}, u32[]{:S(2)}) collective-permute-start(bf16[39,16,128]{2,1,0:T(8,128)(2,1)S(1)} %get-tuple-element.163), channel_id=1, source_target_pairs={{0,4},{2,6},{4,0},{6,2},{1,5},{3,7},{5,1},{7,3},{8,12},{10,14},{12... | collective-permute-start | bytes 479240 | tf_op jit(solution)/shard_map/ppermute | solution.py:74
  115.3 8.3 %collective-permute-start.21 = (bf16[39,16,128]{2,1,0:T(8,128)(2,1)S(1)}, bf16[39,16,128]{2,1,0:T(8,128)(2,1)S(1)}, u32[]{:S(2)}, u32[]{:S(2)}) collective-permute-start(bf16[39,16,128]{2,1,0:T(8,128)(2,1)S(1)} %get-tuple-element.164), channel_id=1, source_target_pairs={{0,6},{2,4},{4,2},{6,0},{1,7},{3,5},{5,3},{7,1},{8,14},{10,12},{12... | collective-permute-start | bytes 479240 | tf_op jit(solution)/shard_map/ppermute | solution.py:74
  (10 other events, 89.7 us)

commit v10 on v9

--- a/solution.py
+++ b/solution.py
@@ -65,6 +65,7 @@
 BLOCK = (64, 128)
 LONG = 3 * 10**10
 SHORT = 8 * 10**9
+MIDDLE = 12 * 10**9
 TILES = WIDE_TILES + NARROW
 WIDE_BLOCKS = (4 * WIDE[1], 4 * WIDE[0], 0)
 ROUND_ONE = tuple(count + 4 * NARROW + 1 for count in WIDE_BLOCKS)
@@ -501,7 +502,7 @@
         zero, one = value[:, :32], value[:, 32:]
         stay, leave = jnp.where(here == 0, zero, one), jnp.where(here == 0, one, zero)
         mine[at] = jnp.where(core == 0, stay[:, :16], stay[:, 16:])
-        away[at] = jnp.where(core == 0, stay[:, 16:], stay[:, :16])
+        away[at] = jnp.where(core == 0, stay[:, 16:], stay[:, :16]).astype(BF16)
         near[at] = jnp.where(core == 0, leave[:, :16], leave[:, 16:]).astype(BF16)
         far[at] = jnp.where(core == 0, leave[:, 16:], leave[:, :16]).astype(BF16)
     value = sum_small(small[...], *(join_small(got, TILES) for got in gots))
@@ -510,10 +511,11 @@
     new_small[...] = high.astype(F32) + low.astype(F32)
     for at in range(2):
         rows = slice(16 * at, 16 * at + 16)
-        away[TILES + at] = new_small[rows]
-        for target in (near, far):
+        for target in (away, near, far):
             target[TILES + at] = high[rows]
             target[TILES + 2 + at] = low[rows]
+    for target in (near, far):
+        target[TILES + 4] = jnp.zeros((16, 128), BF16)
 
 
 def finish_kernel(
@@ -530,7 +532,7 @@
 
     def place(target, tile, column, columns):
         own = mine[tile] + near[tile].astype(F32)
-        other = away[tile] + far[tile].astype(F32)
+        other = away[tile].astype(F32) + far[tile].astype(F32)
         target[:, column : column + 128] = jnp.where(core == 0, own, other)
         target[:, columns + column : columns + column + 128] = jnp.where(core == 0, other, own)
 
@@ -542,9 +544,8 @@
             place(inner.at[kind] if kind < 3 else out, WIDE_TILES + 2 * kind + column, column * 128, 256)
     sums = []
     for at in range(2):
-        own = small[16 * at : 16 * at + 16] + (near[TILES + at].astype(F32) + near[TILES + 2 + at].astype(F32))
-        other = away[TILES + at] + (far[TILES + at].astype(F32) + far[TILES + 2 + at].astype(F32))
-        sums.append(own + other)
+        came = [part[TILES + at].astype(F32) + part[TILES + 2 + at].astype(F32) for part in (near, away, far)]
+        sums.append((small[16 * at : 16 * at + 16] + came[0]) + (came[1] + came[2]))
     gains, rest = sums
     for at in range(8):
         lanes = slice(at * 128, at * 128 + 128)
@@ -710,6 +711,7 @@
         far_kernel,
         operands=[narrow, swap(far_send, FIRST[2])],
         outs=[like((4 * NARROW, *BLOCK), F32), like((32, 128), F32)],
+        flops=MIDDLE,
     )
     gots = swap_round(sends, FIRST)
     down_other = swap(down_part, ACROSS)
@@ -731,8 +733,8 @@
     mine, away, near, far, small = run(
         third_kernel,
         operands=gots + [keep, small],
-        outs=[like((TILES, 16, 128), F32), like((TILES + 2, 16, 128), F32)]
-        + [like((TILES + 4, 16, 128), BF16)] * 2
+        outs=[like((TILES, 16, 128), F32), like((TILES + 4, 16, 128), BF16)]
+        + [like((TILES + 5, 16, 128), BF16)] * 2
         + [like((32, 128), F32)],
     )
     down_g, gate_g, up_g, in_g, out_g, gain_one_g, gain_two_g, conv_g = run(

time: 125 us -> 123 us (0.984)
  starting transfers between devices: 38.2 us -> 36.8 us
    ppermute x20, starting transfers between devices: 31.9 us -> 30.5 us  [swap(): return lax.ppermute(value, AXES, pairs)]
  transfers between devices with their start and end apart: 22 -> 22, of which waited for: 11 -> 13; matrix products, arithmetic and copies ran while one was open for 0% -> 0% of each run, Pallas kernels for 17% -> 17%
where the time goes in v10:
time: 123 us
  waiting for transfers between devices  57 us (46%)
  starting transfers between devices  36.8 us (30%)
  Pallas kernels  27.1 us (22%)
  between operations  1.62 us (1%)
    ppermute x20, waiting for transfers between devices, swap(): return lax.ppermute(value, AXES, pairs)  55 us
    ppermute x20, starting transfers between devices, swap(): return lax.ppermute(value, AXES, pairs)  30.5 us
    pallas_call x19, Pallas kernels, call(): pl.pallas_call(kernel, out_shape=tuple(outs), in_specs=specs, out_specs=t...  27.1 us
    ppermute x2, starting transfers between devices, from_behind(): lax.ppermute(value, axis, [(source, source + steps) for source in range(l...  6.27 us
  transfers between devices with their start and end apart: 22, of which 13 were waited for; matrix products, arithmetic and copies ran while one was open for 0% of the time, Pallas kernels for 17%

profile of v10, /device:TPU:1, one launch (start us, length us, event | category | flops | bytes accessed | tf_op | source)
XLA Modules:
  0.0 122.5 jit_solution(1752575925274445727)
XLA Ops:
  2.8 2.3 %shard_map.186 = (bf16[16,512]{1,0:T(8,128)(2,1)S(1)}, bf16[256,1024]{1,0:T(8,128)(2,1)S(1)}, f32[1,1024]{1,0:T(1,128)S(1)}, bf16[3,1024,512]{2,1,0:T(8,128)(2,1)S(1)}, s32[8,128]{1,0:T(8,128)S(1)}) custom-call(s32[1]{0:T(128)S(6)} %copy.25.refs_0_, bf16[256,1024]{1,0:T(8,128)(2,1)} %refs_5_.9, f32[1,1024]{1,0:T(1,128)} %bitcast.17, ...), custom_call_target="tpu_custom_call" | custom-call | tf_op jit(solution)/shard_map/pallas_call | solution.py:119
  5.1 3.1 %collective-permute-start = (bf16[16,512]{1,0:T(8,128)(2,1)S(1)}, bf16[16,512]{1,0:T(8,128)(2,1)S(1)}, u32[]{:S(2)}, u32[]{:S(2)}) collective-permute-start(bf16[16,512]{1,0:T(8,128)(2,1)S(1)} %get-tuple-element.97), channel_id=1, source_target_pairs={{0,2},{2,4},{4,6},{6,8},{8,10},{10,12},{12,14},{14,16},{16,18},{18... | collective-permute-start | bytes 49160 | tf_op jit(solution)/shard_map/ppermute | solution.py:81
  10.1 2.5 %collective-permute-start.2 = (bf16[256,1024]{1,0:T(8,128)(2,1)S(1)}, bf16[256,1024]{1,0:T(8,128)(2,1)S(1)}, u32[]{:S(2)}, u32[]{:S(2)}) collective-permute-start(bf16[256,1024]{1,0:T(8,128)(2,1)S(1)} %get-tuple-element.101.refs_1_), channel_id=1, source_target_pairs={{0,1},{2,3},{4,5},{6,7},{1,0},{3,2},{5,4},{7,6},{8,9},{10,11},{12,... | collective-permute-start | bytes 1572872 | tf_op jit(solution)/shard_map/ppermute | solution.py:75
  14.1 11.1 %collective-permute-done.2.refs_2_ = bf16[256,1024]{1,0:T(8,128)(2,1)S(1)} collective-permute-done((bf16[256,1024]{1,0:T(8,128)(2,1)S(1)}, bf16[256,1024]{1,0:T(8,128)(2,1)S(1)}, u32[]{:S(2)}, u32[]{:S(2)}) %collective-permute-start.2) | collective-permute-done | bytes 524320 | tf_op jit(solution)/shard_map/ppermute | solution.py:75
  25.3 3.4 %shard_map.190 = (f32[256,1024]{1,0:T(8,128)S(1)}, bf16[256,1024]{1,0:T(8,128)(2,1)S(1)}, bf16[256,2304]{1,0:T(8,128)(2,1)S(1)}, bf16[256,2304]{1,0:T(8,128)(2,1...) custom-call(bf16[256,1024]{1,0:T(8,128)(2,1)S(1)} %copy-done.2, ...), custom_call_target="tpu_custom_call" | custom-call | tf_op jit(solution)/shard_map/pallas_call | solution.py:119
  29.3 2.6 %shard_map.193.refs_1_ = bf16[256,1024]{1,0:T(8,128)(2,1)S(1)} custom-call(bf16[256,2304]{1,0:T(8,128)(2,1)S(1)} %get-tuple-element.110.refs_4_.refs_1_.refs_0_, bf16[256,2304]{1,0:T(8,128)(2,1)S(1)} %get-tuple-element.114.refs_2_.refs_1_, bf16[1024,2304]{1,0:T(8,128)(2,1)S(1)} %bitcast.9, bf16[1024,2304]{1,0:T(8,128)(2,1)S(1)} %bitcast.11), custom_call_target="tpu_custom_call" | custom-call | tf_op jit(solution)/shard_map/pallas_call | solution.py:119
  31.9 3.0 %collective-permute-start.6 = (bf16[256,1024]{1,0:T(8,128)(2,1)S(1)}, bf16[256,1024]{1,0:T(8,128)(2,1)S(1)}, u32[]{:S(2)}, u32[]{:S(2)}) collective-permute-start(bf16[256,1024]{1,0:T(8,128)(2,1)S(1)} %shard_map.193.refs_1_), channel_id=1, source_target_pairs={{0,1},{2,3},{4,5},{6,7},{1,0},{3,2},{5,4},{7,6},{8,9},{10,11},{12,... | collective-permute-start | bytes 1572872 | tf_op jit(solution)/shard_map/ppermute | solution.py:75
  34.9 2.8 %shard_map.191 = (bf16[112,64,128]{2,1,0:T(8,128)(2,1)S(1)}, bf16[112,64,128]{2,1,0:T(8,128)(2,1)S(1)}, bf16[1024,512]{1,0:T(8,128)(2,1)S(1)}) custom-call(bf16[256,1024]{1,0:T(8,128)(2,1)S(1)} %get-tuple-element.107.refs_0_, bf16[256,1024]{1,0:T(8,128)(2,1)S(1)} %copy-done.4, bf16[256,1024]{1,0:T(8,128)(2,1)S(1)} %collective-permute-done.1.refs_2_, ...), custom_call_target="tpu_custom_call" | custom-call | tf_op jit(solution)/shard_map/pallas_call | solution.py:119
  37.7 1.9 %collective-permute-start.4 = (bf16[112,64,128]{2,1,0:T(8,128)(2,1)S(1)}, bf16[112,64,128]{2,1,0:T(8,128)(2,1)S(1)}, u32[]{:S(2)}, u32[]{:S(2)}) collective-permute-start(bf16[112,64,128]{2,1,0:T(8,128)(2,1)S(1)} %get-tuple-element.112), channel_id=1, source_target_pairs={{0,32},{2,10},{4,36},{6,14},{1,33},{3,11},{5,37},{7,15},{8,40},{10... | collective-permute-start | bytes 5505032 | tf_op jit(solution)/shard_map/ppermute | solution.py:75
  39.6 2.1 %shard_map.192 = (bf16[104,64,128]{2,1,0:T(8,128)(2,1)S(1)}, bf16[104,64,128]{2,1,0:T(8,128)(2,1)S(1)}) custom-call(bf16[1024,512]{1,0:T(8,128)(2,1)S(1)} %get-tuple-element.113.refs_0_, bf16[256,2304]{1,0:T(8,128)(2,1)S(1)} %get-tuple-element.110.refs_4_.refs_1_.refs_0_, bf16[256,2304]{1,0:T(8,128)(2,1)S(1)} %get-tuple-element.114.refs_2_.refs_1_, ...), custom_call_target="tpu_custom_call" | custom-call | tf_op jit(solution)/shard_map/pallas_call | solution.py:119
  41.7 2.3 %collective-permute-start.5 = (bf16[104,64,128]{2,1,0:T(8,128)(2,1)S(1)}, bf16[104,64,128]{2,1,0:T(8,128)(2,1)S(1)}, u32[]{:S(2)}, u32[]{:S(2)}) collective-permute-start(bf16[104,64,128]{2,1,0:T(8,128)(2,1)S(1)} %get-tuple-element.116), channel_id=1, source_target_pairs={{0,96},{2,26},{4,100},{6,30},{1,97},{3,27},{5,101},{7,31},{8,104},... | collective-permute-start | bytes 5111816 | tf_op jit(solution)/shard_map/ppermute | solution.py:75
  47.0 3.2 %collective-permute-start.8 = (f32[8,512]{1,0:T(8,128)S(1)}, f32[8,512]{1,0:T(8,128)S(1)}, u32[]{:S(2)}, u32[]{:S(2)}) collective-permute-start(f32[8,512]{1,0:T(8,128)S(1)} %shard_map.196), channel_id=1, source_target_pairs={{2,0},{4,2},{6,4},{8,6},{10,8},{12,10},{14,12},{16,14},{18,16},{20... | collective-permute-start | bytes 49160 | tf_op jit(solution)/shard_map/ppermute | solution.py:81
  51.9 2.0 %collective-permute-done.8.refs_2_ = f32[8,512]{1,0:T(8,128)S(1)} collective-permute-done((f32[8,512]{1,0:T(8,128)S(1)}, f32[8,512]{1,0:T(8,128)S(1)}, u32[]{:S(2)}, u32[]{:S(2)}) %collective-permute-start.8) | collective-permute-done | bytes 16416 | tf_op jit(solution)/shard_map/ppermute | solution.py:81
  55.1 2.8 %collective-permute-start.10 = (f32[8,128]{1,0:T(8,128)S(1)}, f32[8,128]{1,0:T(8,128)S(1)}, u32[]{:S(2)}, u32[]{:S(2)}) collective-permute-start(f32[8,128]{1,0:T(8,128)S(1)} %get-tuple-element.134.refs_7_), channel_id=1, source_target_pairs={{0,1},{2,3},{4,5},{6,7},{1,0},{3,2},{5,4},{7,6},{8,9},{10,11},{12,... | collective-permute-start | bytes 12296 | tf_op jit(solution)/shard_map/ppermute | solution.py:75
  60.8 3.1 %collective-permute-done.5.refs_1_ = bf16[104,64,128]{2,1,0:T(8,128)(2,1)S(1)} collective-permute-done((bf16[104,64,128]{2,1,0:T(8,128)(2,1)S(1)}, bf16[104,64,128]{2,1,0:T(8,128)(2,1)S(1)}, u32[]{:S(2)}, u32[]{:S(2)}) %collective-permute-start.5) | collective-permute-done | bytes 1703968 | tf_op jit(solution)/shard_map/ppermute | solution.py:75
  64.8 2.2 %collective-permute-start.13 = (bf16[33,64,128]{2,1,0:T(8,128)(2,1)S(1)}, bf16[33,64,128]{2,1,0:T(8,128)(2,1)S(1)}, u32[]{:S(2)}, u32[]{:S(2)}) collective-permute-start(bf16[33,64,128]{2,1,0:T(8,128)(2,1)S(1)} %get-tuple-element.144), channel_id=1, source_target_pairs={{0,64},{2,18},{4,68},{6,22},{1,65},{3,19},{5,69},{7,23},{8,72},{10... | collective-permute-start | bytes 1622024 | tf_op jit(solution)/shard_map/ppermute | solution.py:75
  70.7 4.2 %collective-permute-done.13.refs_1_ = bf16[33,64,128]{2,1,0:T(8,128)(2,1)S(1)} collective-permute-done((bf16[33,64,128]{2,1,0:T(8,128)(2,1)S(1)}, bf16[33,64,128]{2,1,0:T(8,128)(2,1)S(1)}, u32[]{:S(2)}, u32[]{:S(2)}) %collective-permute-start.13) | collective-permute-done | bytes 540704 | tf_op jit(solution)/shard_map/ppermute | solution.py:75
  75.0 14.7 %collective-permute-done.11.refs_0_ = bf16[85,64,128]{2,1,0:T(8,128)(2,1)S(1)} collective-permute-done((bf16[85,64,128]{2,1,0:T(8,128)(2,1)S(1)}, bf16[85,64,128]{2,1,0:T(8,128)(2,1)S(1)}, u32[]{:S(2)}, u32[]{:S(2)}) %collective-permute-start.11) | collective-permute-done | bytes 1392672 | tf_op jit(solution)/shard_map/ppermute | solution.py:75
  92.2 1.9 %collective-permute-start.17 = (bf16[36,64,128]{2,1,0:T(8,128)(2,1)S(1)}, bf16[36,64,128]{2,1,0:T(8,128)(2,1)S(1)}, u32[]{:S(2)}, u32[]{:S(2)}) collective-permute-start(bf16[36,64,128]{2,1,0:T(8,128)(2,1)S(1)} %get-tuple-element.157), channel_id=1, source_target_pairs={{0,24},{2,98},{4,28},{6,102},{1,25},{3,99},{5,29},{7,103},{8,16},{... | collective-permute-start | bytes 1769480 | tf_op jit(solution)/shard_map/ppermute | solution.py:75
  96.8 3.4 %collective-permute-done.14.refs_0_ = bf16[36,64,128]{2,1,0:T(8,128)(2,1)S(1)} collective-permute-done((bf16[36,64,128]{2,1,0:T(8,128)(2,1)S(1)}, bf16[36,64,128]{2,1,0:T(8,128)(2,1)S(1)}, u32[]{:S(2)}, u32[]{:S(2)}) %collective-permute-start.14) | collective-permute-done | bytes 589856 | tf_op jit(solution)/shard_map/ppermute | solution.py:75
  100.2 7.0 %collective-permute-done.17.refs_1_ = bf16[36,64,128]{2,1,0:T(8,128)(2,1)S(1)} collective-permute-done((bf16[36,64,128]{2,1,0:T(8,128)(2,1)S(1)}, bf16[36,64,128]{2,1,0:T(8,128)(2,1)S(1)}, u32[]{:S(2)}, u32[]{:S(2)}) %collective-permute-start.17) | collective-permute-done | bytes 589856 | tf_op jit(solution)/shard_map/ppermute | solution.py:75
  107.2 1.7 %collective-permute-done.18.refs_2_ = bf16[36,64,128]{2,1,0:T(8,128)(2,1)S(1)} collective-permute-done((bf16[36,64,128]{2,1,0:T(8,128)(2,1)S(1)}, bf16[36,64,128]{2,1,0:T(8,128)(2,1)S(1)}, u32[]{:S(2)}, u32[]{:S(2)}) %collective-permute-start.18) | collective-permute-done | bytes 589856 | tf_op jit(solution)/shard_map/ppermute | solution.py:75
  110.7 4.5 %collective-permute-start.21 = (bf16[40,16,128]{2,1,0:T(8,128)(2,1)S(1)}, bf16[40,16,128]{2,1,0:T(8,128)(2,1)S(1)}, u32[]{:S(2)}, u32[]{:S(2)}) collective-permute-start(bf16[40,16,128]{2,1,0:T(8,128)(2,1)S(1)} %get-tuple-element.164), channel_id=1, source_target_pairs={{0,6},{2,4},{4,2},{6,0},{1,7},{3,5},{5,3},{7,1},{8,14},{10,12},{12... | collective-permute-start | bytes 491528 | tf_op jit(solution)/shard_map/ppermute | solution.py:75
  116.6 5.1 %collective-permute-done.21.refs_3_ = bf16[40,16,128]{2,1,0:T(8,128)(2,1)S(1)} collective-permute-done((bf16[40,16,128]{2,1,0:T(8,128)(2,1)S(1)}, bf16[40,16,128]{2,1,0:T(8,128)(2,1)S(1)}, u32[]{:S(2)}, u32[]{:S(2)}) %collective-permute-start.21) | collective-permute-done | bytes 163872 | tf_op jit(solution)/shard_map/ppermute | solution.py:75
  (65 shorter events, 28.0 us)
Async XLA Ops:
  0.6 8.8 %collective-permute-start.1 = (bf16[256,1024]{1,0:T(8,128)(2,1)}, bf16[256,1024]{1,0:T(8,128)(2,1)S(1)}, u32[]{:S(2)}, u32[]{:S(2)}) collective-permute-start(bf16[256,1024]{1,0:T(8,128)(2,1)} %refs_5_.8), channel_id=1, source_target_pairs={{0,2},{2,0},{4,6},{6,4},{1,3},{3,1},{5,7},{7,5},{8,10},{10,8},{12,... | collective-permute-start | bytes 1572872 | tf_op jit(solution)/shard_map/ppermute | solution.py:75
  5.1 4.3 %collective-permute-start = (bf16[16,512]{1,0:T(8,128)(2,1)S(1)}, bf16[16,512]{1,0:T(8,128)(2,1)S(1)}, u32[]{:S(2)}, u32[]{:S(2)}) collective-permute-start(bf16[16,512]{1,0:T(8,128)(2,1)S(1)} %get-tuple-element.97), channel_id=1, source_target_pairs={{0,2},{2,4},{4,6},{6,8},{8,10},{10,12},{12,14},{14,16},{16,18},{18... | collective-permute-start | bytes 49160 | tf_op jit(solution)/shard_map/ppermute | solution.py:81
  10.1 15.2 %slice-start = ((s8[4718592]{0:T(1024)(128)(4,1)}), s8[4194304]{0:T(1024)(128)(4,1)S(1)}, s32[]{:S(2)}) async-start(s8[4718592]{0:T(1024)(128)(4,1)} %bitcast.8), calls=%async_computation | async-start | bytes 8388608
  10.1 15.1 %slice-start.2 = ((s8[4718592]{0:T(1024)(128)(4,1)}), s8[4194304]{0:T(1024)(128)(4,1)S(1)}, s32[]{:S(2)}) async-start(s8[4718592]{0:T(1024)(128)(4,1)} %bitcast.10), calls=%async_computation.2 | async-start | bytes 8388608
  10.1 15.1 %collective-permute-start.2 = (bf16[256,1024]{1,0:T(8,128)(2,1)S(1)}, bf16[256,1024]{1,0:T(8,128)(2,1)S(1)}, u32[]{:S(2)}, u32[]{:S(2)}) collective-permute-start(bf16[256,1024]{1,0:T(8,128)(2,1)S(1)} %get-tuple-element.101.refs_1_), channel_id=1, source_target_pairs={{0,1},{2,3},{4,5},{6,7},{1,0},{3,2},{5,4},{7,6},{8,9},{10,11},{12,... | collective-permute-start | bytes 1572872 | tf_op jit(solution)/shard_map/ppermute | solution.py:75
  28.6 6.3 %collective-permute-start.3 = (bf16[256,4480]{1,0:T(8,128)(2,1)S(1)}, bf16[256,4480]{1,0:T(8,128)(2,1)S(1)}, u32[]{:S(2)}, u32[]{:S(2)}) collective-permute-start(bf16[256,4480]{1,0:T(8,128)(2,1)S(1)} %get-tuple-element.111), channel_id=1, source_target_pairs={{0,2},{2,0},{4,6},{6,4},{1,3},{3,1},{5,7},{7,5},{8,10},{10,8},{12,... | collective-permute-start | bytes 6881288 | tf_op jit(solution)/shard_map/ppermute | solution.py:75
  29.2 17.4 %collective-permute-start.7 = (bf16[256,1280]{1,0:T(8,128)(2,1)S(1)}, bf16[256,1280]{1,0:T(8,128)(2,1)S(1)}, u32[]{:S(2)}, u32[]{:S(2)}) collective-permute-start(bf16[256,1280]{1,0:T(8,128)(2,1)S(1)} %get-tuple-element.120), channel_id=1, source_target_pairs={{0,2},{2,0},{4,6},{6,4},{1,3},{3,1},{5,7},{7,5},{8,10},{10,8},{12,... | collective-permute-start | bytes 1966088 | tf_op jit(solution)/shard_map/ppermute | solution.py:75
  31.9 14.7 %collective-permute-start.6 = (bf16[256,1024]{1,0:T(8,128)(2,1)S(1)}, bf16[256,1024]{1,0:T(8,128)(2,1)S(1)}, u32[]{:S(2)}, u32[]{:S(2)}) collective-permute-start(bf16[256,1024]{1,0:T(8,128)(2,1)S(1)} %shard_map.193.refs_1_), channel_id=1, source_target_pairs={{0,1},{2,3},{4,5},{6,7},{1,0},{3,2},{5,4},{7,6},{8,9},{10,11},{12,... | collective-permute-start | bytes 1572872 | tf_op jit(solution)/shard_map/ppermute | solution.py:75
  37.7 26.3 %collective-permute-start.4 = (bf16[112,64,128]{2,1,0:T(8,128)(2,1)S(1)}, bf16[112,64,128]{2,1,0:T(8,128)(2,1)S(1)}, u32[]{:S(2)}, u32[]{:S(2)}) collective-permute-start(bf16[112,64,128]{2,1,0:T(8,128)(2,1)S(1)} %get-tuple-element.112), channel_id=1, source_target_pairs={{0,32},{2,10},{4,36},{6,14},{1,33},{3,11},{5,37},{7,15},{8,40},{10... | collective-permute-start | bytes 5505032 | tf_op jit(solution)/shard_map/ppermute | solution.py:75
  41.7 22.3 %collective-permute-start.5 = (bf16[104,64,128]{2,1,0:T(8,128)(2,1)S(1)}, bf16[104,64,128]{2,1,0:T(8,128)(2,1)S(1)}, u32[]{:S(2)}, u32[]{:S(2)}) collective-permute-start(bf16[104,64,128]{2,1,0:T(8,128)(2,1)S(1)} %get-tuple-element.116), channel_id=1, source_target_pairs={{0,96},{2,26},{4,100},{6,30},{1,97},{3,27},{5,101},{7,31},{8,104},... | collective-permute-start | bytes 5111816 | tf_op jit(solution)/shard_map/ppermute | solution.py:75
  47.0 6.8 %collective-permute-start.8 = (f32[8,512]{1,0:T(8,128)S(1)}, f32[8,512]{1,0:T(8,128)S(1)}, u32[]{:S(2)}, u32[]{:S(2)}) collective-permute-start(f32[8,512]{1,0:T(8,128)S(1)} %shard_map.196), channel_id=1, source_target_pairs={{2,0},{4,2},{6,4},{8,6},{10,8},{12,10},{14,12},{16,14},{18,16},{20... | collective-permute-start | bytes 49160 | tf_op jit(solution)/shard_map/ppermute | solution.py:81
  55.0 4.1 %collective-permute-start.9 = (bf16[7,256,256]{2,1,0:T(8,128)(2,1)S(1)}, bf16[7,256,256]{2,1,0:T(8,128)(2,1)S(1)}, u32[]{:S(2)}, u32[]{:S(2)}) collective-permute-start(bf16[7,256,256]{2,1,0:T(8,128)(2,1)S(1)} %get-tuple-element.131), channel_id=1, source_target_pairs={{0,2},{2,0},{4,6},{6,4},{1,3},{3,1},{5,7},{7,5},{8,10},{10,8},{12,... | collective-permute-start | bytes 2752520 | tf_op jit(solution)/shard_map/ppermute | solution.py:75
  55.1 4.0 %collective-permute-start.10 = (f32[8,128]{1,0:T(8,128)S(1)}, f32[8,128]{1,0:T(8,128)S(1)}, u32[]{:S(2)}, u32[]{:S(2)}) collective-permute-start(f32[8,128]{1,0:T(8,128)S(1)} %get-tuple-element.134.refs_7_), channel_id=1, source_target_pairs={{0,1},{2,3},{4,5},{6,7},{1,0},{3,2},{5,4},{7,6},{8,9},{10,11},{12,... | collective-permute-start | bytes 12296 | tf_op jit(solution)/shard_map/ppermute | solution.py:75
  64.8 10.1 %collective-permute-start.13 = (bf16[33,64,128]{2,1,0:T(8,128)(2,1)S(1)}, bf16[33,64,128]{2,1,0:T(8,128)(2,1)S(1)}, u32[]{:S(2)}, u32[]{:S(2)}) collective-permute-start(bf16[33,64,128]{2,1,0:T(8,128)(2,1)S(1)} %get-tuple-element.144), channel_id=1, source_target_pairs={{0,64},{2,18},{4,68},{6,22},{1,65},{3,19},{5,69},{7,23},{8,72},{10... | collective-permute-start | bytes 1622024 | tf_op jit(solution)/shard_map/ppermute | solution.py:75
  66.9 23.5 %collective-permute-start.12 = (bf16[89,64,128]{2,1,0:T(8,128)(2,1)S(1)}, bf16[89,64,128]{2,1,0:T(8,128)(2,1)S(1)}, u32[]{:S(2)}, u32[]{:S(2)}) collective-permute-start(bf16[89,64,128]{2,1,0:T(8,128)(2,1)S(1)} %get-tuple-element.138), channel_id=1, source_target_pairs={{0,96},{2,26},{4,100},{6,30},{1,97},{3,27},{5,101},{7,31},{8,104},... | collective-permute-start | bytes 4374536 | tf_op jit(solution)/shard_map/ppermute | solution.py:75
  67.6 22.1 %collective-permute-start.11 = (bf16[85,64,128]{2,1,0:T(8,128)(2,1)S(1)}, bf16[85,64,128]{2,1,0:T(8,128)(2,1)S(1)}, u32[]{:S(2)}, u32[]{:S(2)}) collective-permute-start(bf16[85,64,128]{2,1,0:T(8,128)(2,1)S(1)} %get-tuple-element.137), channel_id=1, source_target_pairs={{0,32},{2,10},{4,36},{6,14},{1,33},{3,11},{5,37},{7,15},{8,40},{10... | collective-permute-start | bytes 4177928 | tf_op jit(solution)/shard_map/ppermute | solution.py:75
  67.7 27.4 %collective-permute-start.15 = (bf16[256,1024]{1,0:T(8,128)(2,1)S(1)}, bf16[256,1024]{1,0:T(8,128)(2,1)S(1)}, u32[]{:S(2)}, u32[]{:S(2)}) collective-permute-start(bf16[256,1024]{1,0:T(8,128)(2,1)S(1)} %shard_map.194.refs_1_), channel_id=1, source_target_pairs={{0,1},{2,3},{4,5},{6,7},{1,0},{3,2},{5,4},{7,6},{8,9},{10,11},{12,... | collective-permute-start | bytes 1572872 | tf_op jit(solution)/shard_map/ppermute | solution.py:75
  68.9 26.1 %collective-permute-start.16 = (bf16[256,1024]{1,0:T(8,128)(2,1)S(1)}, bf16[256,1024]{1,0:T(8,128)(2,1)S(1)}, u32[]{:S(2)}, u32[]{:S(2)}) collective-permute-start(bf16[256,1024]{1,0:T(8,128)(2,1)S(1)} %get-tuple-element.150.refs_3_), channel_id=1, source_target_pairs={{0,1},{2,3},{4,5},{6,7},{1,0},{3,2},{5,4},{7,6},{8,9},{10,11},{12,... | collective-permute-start | bytes 1572872 | tf_op jit(solution)/shard_map/ppermute | solution.py:75
  91.1 9.1 %collective-permute-start.14 = (bf16[36,64,128]{2,1,0:T(8,128)(2,1)S(1)}, bf16[36,64,128]{2,1,0:T(8,128)(2,1)S(1)}, u32[]{:S(2)}, u32[]{:S(2)}) collective-permute-start(bf16[36,64,128]{2,1,0:T(8,128)(2,1)S(1)} %get-tuple-element.148), channel_id=1, source_target_pairs={{0,8},{2,34},{4,12},{6,38},{1,9},{3,35},{5,13},{7,39},{8,0},{10,42... | collective-permute-start | bytes 1769480 | tf_op jit(solution)/shard_map/ppermute | solution.py:75
  92.2 15.1 %collective-permute-start.17 = (bf16[36,64,128]{2,1,0:T(8,128)(2,1)S(1)}, bf16[36,64,128]{2,1,0:T(8,128)(2,1)S(1)}, u32[]{:S(2)}, u32[]{:S(2)}) collective-permute-start(bf16[36,64,128]{2,1,0:T(8,128)(2,1)S(1)} %get-tuple-element.157), channel_id=1, source_target_pairs={{0,24},{2,98},{4,28},{6,102},{1,25},{3,99},{5,29},{7,103},{8,16},{... | collective-permute-start | bytes 1769480 | tf_op jit(solution)/shard_map/ppermute | solution.py:75
  94.1 14.9 %collective-permute-start.18 = (bf16[36,64,128]{2,1,0:T(8,128)(2,1)S(1)}, bf16[36,64,128]{2,1,0:T(8,128)(2,1)S(1)}, u32[]{:S(2)}, u32[]{:S(2)}) collective-permute-start(bf16[36,64,128]{2,1,0:T(8,128)(2,1)S(1)} %get-tuple-element.158), channel_id=1, source_target_pairs={{0,16},{2,66},{4,20},{6,70},{1,17},{3,67},{5,21},{7,71},{8,24},{10... | collective-permute-start | bytes 1769480 | tf_op jit(solution)/shard_map/ppermute | solution.py:75
  109.3 7.3 %collective-permute-start.20 = (bf16[40,16,128]{2,1,0:T(8,128)(2,1)S(1)}, bf16[40,16,128]{2,1,0:T(8,128)(2,1)S(1)}, u32[]{:S(2)}, u32[]{:S(2)}) collective-permute-start(bf16[40,16,128]{2,1,0:T(8,128)(2,1)S(1)} %get-tuple-element.163), channel_id=1, source_target_pairs={{0,4},{2,6},{4,0},{6,2},{1,5},{3,7},{5,1},{7,3},{8,12},{10,14},{12... | collective-permute-start | bytes 491528 | tf_op jit(solution)/shard_map/ppermute | solution.py:75
  110.7 11.0 %collective-permute-start.21 = (bf16[40,16,128]{2,1,0:T(8,128)(2,1)S(1)}, bf16[40,16,128]{2,1,0:T(8,128)(2,1)S(1)}, u32[]{:S(2)}, u32[]{:S(2)}) collective-permute-start(bf16[40,16,128]{2,1,0:T(8,128)(2,1)S(1)} %get-tuple-element.164), channel_id=1, source_target_pairs={{0,6},{2,4},{4,2},{6,0},{1,7},{3,5},{5,3},{7,1},{8,14},{10,12},{12... | collective-permute-start | bytes 491528 | tf_op jit(solution)/shard_map/ppermute | solution.py:75
  115.2 1.4 %collective-permute-start.19 = (bf16[39,16,128]{2,1,0:T(8,128)(2,1)S(1)}, bf16[39,16,128]{2,1,0:T(8,128)(2,1)S(1)}, u32[]{:S(2)}, u32[]{:S(2)}) collective-permute-start(bf16[39,16,128]{2,1,0:T(8,128)(2,1)S(1)} %get-tuple-element.162), channel_id=1, source_target_pairs={{0,2},{2,0},{4,6},{6,4},{1,3},{3,1},{5,7},{7,5},{8,10},{10,8},{12,... | collective-permute-start | bytes 479240 | tf_op jit(solution)/shard_map/ppermute | solution.py:75
  (10 other events, 89.7 us)

commit v11 on v10

--- a/solution.py
+++ b/solution.py
@@ -60,7 +60,7 @@
 ]
 WIDE_COLUMNS = 1152
 WIDE_TILES = 27
-WIDE = (14, 13)
+WIDE = (15, 12)
 NARROW = 8
 BLOCK = (64, 128)
 LONG = 3 * 10**10
@@ -405,11 +405,7 @@
 
 
 def narrow_kernel(scalars, one, shared, low, late_other, backs, ymix, *refs):
-    (small, gain, gain_other), outs, (new_small, left_one, left_low) = refs[:3], refs[3:7], refs[7:]
-    new_small[:8] = gain[...] + gain_other[...]
-    new_small[8:] = small[8:]
-    for pairing in range(3):
-        split_small(new_small[...], outs[pairing], ROUND_ONE[pairing] - 1)
+    outs, (left_one, left_low) = refs[:4], refs[4:]
     width = one.shape[1]
     one_other, ymix_other = shared.at[:, :width], shared.at[:, width:]
     for at in range(0, width, 256):
@@ -456,7 +452,12 @@
 
 
 def first_kernel(scalars, *refs):
-    gots, keeps, sends, wide_keeps = refs[:2], refs[2:4], refs[6:8], refs[8:]
+    gots, keeps, (small, gain, gain_other) = refs[:2], refs[2:4], refs[4:7]
+    sends, wide_keeps, new_small = refs[10:13], refs[13:15], refs[15]
+    new_small[:8] = gain[...] + gain_other[...]
+    new_small[8:] = small[8:]
+    for pairing in range(3):
+        split_small(new_small[...], sends[pairing], ROUND_ONE[pairing] - 1)
     for kind in range(2):
         half = 4 * WIDE[kind]
         for chunk in range(4):
@@ -692,21 +693,20 @@
         ],
     )
     gain_other = swap(gain_part, ACROSS)
-    *sends, narrow, small = run(
+    *sends, narrow = run(
         narrow_kernel,
-        operands=[normed_one, early_other, resid_low, share(shared), backs, ymix, small, gain_part, gain_other],
-        outs=blocks(ROUND_ONE) + blocks([4 * NARROW]) + [like((32, 128), F32)],
+        operands=[normed_one, early_other, resid_low, share(shared), backs, ymix],
+        outs=blocks(ROUND_ONE) + blocks([4 * NARROW]),
         scratch=[pltpu.VMEM((width, 2 * rows), BF16)] * 2,
     )
-    far_send = sends.pop()
     results = run(
         first_kernel,
-        operands=gots + keeps + sends,
-        aliases={4: 0, 5: 1},
-        outs=blocks(ROUND_ONE[:2]) + blocks([4 * count for count in WIDE]),
-    )
-    sends, keeps = list(results[:2]), list(results[2:])
-    keeps[0], far_send = lax.optimization_barrier((keeps[0], far_send))
+        operands=gots + keeps + [small, gain_part, gain_other] + sends,
+        aliases={7: 0, 8: 1, 9: 2},
+        outs=blocks(ROUND_ONE) + blocks([4 * count for count in WIDE]) + [like((32, 128), F32)],
+    )
+    *sends, far_send = results[:3]
+    keeps, small = list(results[3:5]), results[5]
     narrow, cross = run(
         far_kernel,
         operands=[narrow, swap(far_send, FIRST[2])],

time: 123 us -> 123 us (level)
  waiting for transfers between devices: 57 us -> 55.5 us
    ppermute x20, waiting for transfers between devices: 55 us -> 53.5 us  [swap(): return lax.ppermute(value, AXES, pairs)]
  transfers between devices with their start and end apart: 22 -> 22, of which waited for: 13 -> 12; matrix products, arithmetic and copies ran while one was open for 0% -> 0% of each run, Pallas kernels for 17% -> 17%
where the time goes in v11:
time: 123 us; the launch traced here: 122 us
  waiting for transfers between devices  55.5 us (45%)
  starting transfers between devices  37.5 us (30%)
  Pallas kernels  27.8 us (23%)
  between operations  1.63 us (1%)
    ppermute x20, waiting for transfers between devices, swap(): return lax.ppermute(value, AXES, pairs)  53.5 us
    ppermute x20, starting transfers between devices, swap(): return lax.ppermute(value, AXES, pairs)  31.2 us
    pallas_call x19, Pallas kernels, call(): pl.pallas_call(kernel, out_shape=tuple(outs), in_specs=specs, out_specs=t...  27.8 us
    ppermute x2, starting transfers between devices, from_behind(): lax.ppermute(value, axis, [(source, source + steps) for source in range(l...  6.27 us
  transfers between devices with their start and end apart: 22, of which 12 were waited for; matrix products, arithmetic and copies ran while one was open for 0% of the time, Pallas kernels for 17%

profile of v11, /device:TPU:1, one launch (start us, length us, event | category | flops | bytes accessed | tf_op | source)
XLA Modules:
  0.0 122.5 jit_solution(18380817911430648258)
XLA Ops:
  2.8 2.3 %shard_map.186 = (bf16[16,512]{1,0:T(8,128)(2,1)S(1)}, bf16[256,1024]{1,0:T(8,128)(2,1)S(1)}, f32[1,1024]{1,0:T(1,128)S(1)}, bf16[3,1024,512]{2,1,0:T(8,128)(2,1)S(1)}, s32[8,128]{1,0:T(8,128)S(1)}) custom-call(s32[1]{0:T(128)S(6)} %copy.27.refs_0_, bf16[256,1024]{1,0:T(8,128)(2,1)} %refs_5_.9, f32[1,1024]{1,0:T(1,128)} %bitcast.17, ...), custom_call_target="tpu_custom_call" | custom-call | tf_op jit(solution)/shard_map/pallas_call | solution.py:119
  5.1 3.1 %collective-permute-start = (bf16[16,512]{1,0:T(8,128)(2,1)S(1)}, bf16[16,512]{1,0:T(8,128)(2,1)S(1)}, u32[]{:S(2)}, u32[]{:S(2)}) collective-permute-start(bf16[16,512]{1,0:T(8,128)(2,1)S(1)} %get-tuple-element.96), channel_id=1, source_target_pairs={{0,2},{2,4},{4,6},{6,8},{8,10},{10,12},{12,14},{14,16},{16,18},{18... | collective-permute-start | bytes 49160 | tf_op jit(solution)/shard_map/ppermute | solution.py:81
  10.1 2.5 %collective-permute-start.2 = (bf16[256,1024]{1,0:T(8,128)(2,1)S(1)}, bf16[256,1024]{1,0:T(8,128)(2,1)S(1)}, u32[]{:S(2)}, u32[]{:S(2)}) collective-permute-start(bf16[256,1024]{1,0:T(8,128)(2,1)S(1)} %get-tuple-element.100.refs_1_), channel_id=1, source_target_pairs={{0,1},{2,3},{4,5},{6,7},{1,0},{3,2},{5,4},{7,6},{8,9},{10,11},{12,... | collective-permute-start | bytes 1572872 | tf_op jit(solution)/shard_map/ppermute | solution.py:75
  14.1 11.1 %collective-permute-done.2.refs_2_ = bf16[256,1024]{1,0:T(8,128)(2,1)S(1)} collective-permute-done((bf16[256,1024]{1,0:T(8,128)(2,1)S(1)}, bf16[256,1024]{1,0:T(8,128)(2,1)S(1)}, u32[]{:S(2)}, u32[]{:S(2)}) %collective-permute-start.2) | collective-permute-done | bytes 524320 | tf_op jit(solution)/shard_map/ppermute | solution.py:75
  25.3 3.4 %shard_map.190 = (f32[256,1024]{1,0:T(8,128)S(1)}, bf16[256,1024]{1,0:T(8,128)(2,1)S(1)}, bf16[256,2304]{1,0:T(8,128)(2,1)S(1)}, bf16[256,2304]{1,0:T(8,128)(2,1...) custom-call(bf16[256,1024]{1,0:T(8,128)(2,1)S(1)} %copy-done.2, ...), custom_call_target="tpu_custom_call" | custom-call | tf_op jit(solution)/shard_map/pallas_call | solution.py:119
  29.3 2.6 %shard_map.193.refs_1_ = bf16[256,1024]{1,0:T(8,128)(2,1)S(1)} custom-call(bf16[256,2304]{1,0:T(8,128)(2,1)S(1)} %get-tuple-element.109.refs_4_.refs_1_.refs_0_, bf16[256,2304]{1,0:T(8,128)(2,1)S(1)} %get-tuple-element.113.refs_2_.refs_1_, bf16[1024,2304]{1,0:T(8,128)(2,1)S(1)} %bitcast.9, bf16[1024,2304]{1,0:T(8,128)(2,1)S(1)} %bitcast.11), custom_call_target="tpu_custom_call" | custom-call | tf_op jit(solution)/shard_map/pallas_call | solution.py:119
  31.9 3.0 %collective-permute-start.6 = (bf16[256,1024]{1,0:T(8,128)(2,1)S(1)}, bf16[256,1024]{1,0:T(8,128)(2,1)S(1)}, u32[]{:S(2)}, u32[]{:S(2)}) collective-permute-start(bf16[256,1024]{1,0:T(8,128)(2,1)S(1)} %shard_map.193.refs_1_), channel_id=1, source_target_pairs={{0,1},{2,3},{4,5},{6,7},{1,0},{3,2},{5,4},{7,6},{8,9},{10,11},{12,... | collective-permute-start | bytes 1572872 | tf_op jit(solution)/shard_map/ppermute | solution.py:75
  34.9 2.7 %shard_map.191 = (bf16[120,64,128]{2,1,0:T(8,128)(2,1)S(1)}, bf16[120,64,128]{2,1,0:T(8,128)(2,1)S(1)}, bf16[1024,512]{1,0:T(8,128)(2,1)S(1)}) custom-call(bf16[256,1024]{1,0:T(8,128)(2,1)S(1)} %get-tuple-element.106.refs_0_, bf16[256,1024]{1,0:T(8,128)(2,1)S(1)} %copy-done.4, bf16[256,1024]{1,0:T(8,128)(2,1)S(1)} %collective-permute-done.1.refs_2_, ...), custom_call_target="tpu_custom_call" | custom-call | tf_op jit(solution)/shard_map/pallas_call | solution.py:119
  37.7 1.9 %collective-permute-start.4 = (bf16[120,64,128]{2,1,0:T(8,128)(2,1)S(1)}, bf16[120,64,128]{2,1,0:T(8,128)(2,1)S(1)}, u32[]{:S(2)}, u32[]{:S(2)}) collective-permute-start(bf16[120,64,128]{2,1,0:T(8,128)(2,1)S(1)} %get-tuple-element.111), channel_id=1, source_target_pairs={{0,32},{2,10},{4,36},{6,14},{1,33},{3,11},{5,37},{7,15},{8,40},{10... | collective-permute-start | bytes 5898248 | tf_op jit(solution)/shard_map/ppermute | solution.py:75
  39.6 2.1 %shard_map.192 = (bf16[96,64,128]{2,1,0:T(8,128)(2,1)S(1)}, bf16[96,64,128]{2,1,0:T(8,128)(2,1)S(1)}) custom-call(bf16[1024,512]{1,0:T(8,128)(2,1)S(1)} %get-tuple-element.112.refs_0_, bf16[256,2304]{1,0:T(8,128)(2,1)S(1)} %get-tuple-element.109.refs_4_.refs_1_.refs_0_, bf16[256,2304]{1,0:T(8,128)(2,1)S(1)} %get-tuple-element.113.refs_2_.refs_1_, ...), custom_call_target="tpu_custom_call" | custom-call | tf_op jit(solution)/shard_map/pallas_call | solution.py:119
  41.7 2.3 %collective-permute-start.5 = (bf16[96,64,128]{2,1,0:T(8,128)(2,1)S(1)}, bf16[96,64,128]{2,1,0:T(8,128)(2,1)S(1)}, u32[]{:S(2)}, u32[]{:S(2)}) collective-permute-start(bf16[96,64,128]{2,1,0:T(8,128)(2,1)S(1)} %get-tuple-element.115), channel_id=1, source_target_pairs={{0,96},{2,26},{4,100},{6,30},{1,97},{3,27},{5,101},{7,31},{8,104},... | collective-permute-start | bytes 4718600 | tf_op jit(solution)/shard_map/ppermute | solution.py:75
  47.0 3.2 %collective-permute-start.8 = (f32[8,512]{1,0:T(8,128)S(1)}, f32[8,512]{1,0:T(8,128)S(1)}, u32[]{:S(2)}, u32[]{:S(2)}) collective-permute-start(f32[8,512]{1,0:T(8,128)S(1)} %shard_map.196), channel_id=1, source_target_pairs={{2,0},{4,2},{6,4},{8,6},{10,8},{12,10},{14,12},{16,14},{18,16},{20... | collective-permute-start | bytes 49160 | tf_op jit(solution)/shard_map/ppermute | solution.py:81
  51.9 2.0 %collective-permute-done.8.refs_2_ = f32[8,512]{1,0:T(8,128)S(1)} collective-permute-done((f32[8,512]{1,0:T(8,128)S(1)}, f32[8,512]{1,0:T(8,128)S(1)}, u32[]{:S(2)}, u32[]{:S(2)}) %collective-permute-start.8) | collective-permute-done | bytes 16416 | tf_op jit(solution)/shard_map/ppermute | solution.py:81
  55.1 2.8 %collective-permute-start.9 = (f32[8,128]{1,0:T(8,128)S(1)}, f32[8,128]{1,0:T(8,128)S(1)}, u32[]{:S(2)}, u32[]{:S(2)}) collective-permute-start(f32[8,128]{1,0:T(8,128)S(1)} %get-tuple-element.130.refs_5_), channel_id=1, source_target_pairs={{0,1},{2,3},{4,5},{6,7},{1,0},{3,2},{5,4},{7,6},{8,9},{10,11},{12,... | collective-permute-start | bytes 12296 | tf_op jit(solution)/shard_map/ppermute | solution.py:75
  59.7 2.9 %collective-permute-done.5.refs_1_ = bf16[96,64,128]{2,1,0:T(8,128)(2,1)S(1)} collective-permute-done((bf16[96,64,128]{2,1,0:T(8,128)(2,1)S(1)}, bf16[96,64,128]{2,1,0:T(8,128)(2,1)S(1)}, u32[]{:S(2)}, u32[]{:S(2)}) %collective-permute-start.5) | collective-permute-done | bytes 1572896 | tf_op jit(solution)/shard_map/ppermute | solution.py:75
  64.0 2.8 %collective-permute-start.13 = (bf16[33,64,128]{2,1,0:T(8,128)(2,1)S(1)}, bf16[33,64,128]{2,1,0:T(8,128)(2,1)S(1)}, u32[]{:S(2)}, u32[]{:S(2)}) collective-permute-start(bf16[33,64,128]{2,1,0:T(8,128)(2,1)S(1)} %get-tuple-element.142), channel_id=1, source_target_pairs={{0,64},{2,18},{4,68},{6,22},{1,65},{3,19},{5,69},{7,23},{8,72},{10... | collective-permute-start | bytes 1622024 | tf_op jit(solution)/shard_map/ppermute | solution.py:75
  70.6 3.6 %collective-permute-done.13.refs_1_ = bf16[33,64,128]{2,1,0:T(8,128)(2,1)S(1)} collective-permute-done((bf16[33,64,128]{2,1,0:T(8,128)(2,1)S(1)}, bf16[33,64,128]{2,1,0:T(8,128)(2,1)S(1)}, u32[]{:S(2)}, u32[]{:S(2)}) %collective-permute-start.13) | collective-permute-done | bytes 540704 | tf_op jit(solution)/shard_map/ppermute | solution.py:75
  74.3 14.6 %collective-permute-done.11.refs_0_ = bf16[81,64,128]{2,1,0:T(8,128)(2,1)S(1)} collective-permute-done((bf16[81,64,128]{2,1,0:T(8,128)(2,1)S(1)}, bf16[81,64,128]{2,1,0:T(8,128)(2,1)S(1)}, u32[]{:S(2)}, u32[]{:S(2)}) %collective-permute-start.11) | collective-permute-done | bytes 1327136 | tf_op jit(solution)/shard_map/ppermute | solution.py:75
  92.2 2.0 %collective-permute-start.17 = (bf16[36,64,128]{2,1,0:T(8,128)(2,1)S(1)}, bf16[36,64,128]{2,1,0:T(8,128)(2,1)S(1)}, u32[]{:S(2)}, u32[]{:S(2)}) collective-permute-start(bf16[36,64,128]{2,1,0:T(8,128)(2,1)S(1)} %get-tuple-element.155), channel_id=1, source_target_pairs={{0,24},{2,98},{4,28},{6,102},{1,25},{3,99},{5,29},{7,103},{8,16},{... | collective-permute-start | bytes 1769480 | tf_op jit(solution)/shard_map/ppermute | solution.py:75
  95.0 1.8 %shard_map.202 = (bf16[256,1024]{1,0:T(8,128)(2,1)}, f32[256,1024]{1,0:T(8,128)}) custom-call(f32[256,1024]{1,0:T(8,128)S(1)} %get-tuple-element.122.refs_3_.refs_0_, bf16[256,1024]{1,0:T(8,128)(2,1)S(1)} %shard_map.194.refs_1_, bf16[256,1024]{1,0:T(8,128)(2,1)S(1)} %collective-permute-done.15.refs_2_, bf16[256,1024]{1,0:T(8,128)(2,1)S(1)} %get-tuple-element.148.refs_3_, ...), custom_call_target="tpu_custom_call" | custom-call | flops 30000001024 | tf_op jit(solution)/shard_map/pallas_call | solution.py:119
  96.8 3.3 %collective-permute-done.14.refs_0_ = bf16[36,64,128]{2,1,0:T(8,128)(2,1)S(1)} collective-permute-done((bf16[36,64,128]{2,1,0:T(8,128)(2,1)S(1)}, bf16[36,64,128]{2,1,0:T(8,128)(2,1)S(1)}, u32[]{:S(2)}, u32[]{:S(2)}) %collective-permute-start.14) | collective-permute-done | bytes 589856 | tf_op jit(solution)/shard_map/ppermute | solution.py:75
  100.1 7.2 %collective-permute-done.17.refs_1_ = bf16[36,64,128]{2,1,0:T(8,128)(2,1)S(1)} collective-permute-done((bf16[36,64,128]{2,1,0:T(8,128)(2,1)S(1)}, bf16[36,64,128]{2,1,0:T(8,128)(2,1)S(1)}, u32[]{:S(2)}, u32[]{:S(2)}) %collective-permute-start.17) | collective-permute-done | bytes 589856 | tf_op jit(solution)/shard_map/ppermute | solution.py:75
  110.7 4.5 %collective-permute-start.21 = (bf16[40,16,128]{2,1,0:T(8,128)(2,1)S(1)}, bf16[40,16,128]{2,1,0:T(8,128)(2,1)S(1)}, u32[]{:S(2)}, u32[]{:S(2)}) collective-permute-start(bf16[40,16,128]{2,1,0:T(8,128)(2,1)S(1)} %get-tuple-element.162), channel_id=1, source_target_pairs={{0,6},{2,4},{4,2},{6,0},{1,7},{3,5},{5,3},{7,1},{8,14},{10,12},{12... | collective-permute-start | bytes 491528 | tf_op jit(solution)/shard_map/ppermute | solution.py:75
  116.5 5.1 %collective-permute-done.21.refs_3_ = bf16[40,16,128]{2,1,0:T(8,128)(2,1)S(1)} collective-permute-done((bf16[40,16,128]{2,1,0:T(8,128)(2,1)S(1)}, bf16[40,16,128]{2,1,0:T(8,128)(2,1)S(1)}, u32[]{:S(2)}, u32[]{:S(2)}) %collective-permute-start.21) | collective-permute-done | bytes 163872 | tf_op jit(solution)/shard_map/ppermute | solution.py:75
  (65 shorter events, 28.1 us)
Async XLA Ops:
  0.6 8.8 %collective-permute-start.1 = (bf16[256,1024]{1,0:T(8,128)(2,1)}, bf16[256,1024]{1,0:T(8,128)(2,1)S(1)}, u32[]{:S(2)}, u32[]{:S(2)}) collective-permute-start(bf16[256,1024]{1,0:T(8,128)(2,1)} %refs_5_.8), channel_id=1, source_target_pairs={{0,2},{2,0},{4,6},{6,4},{1,3},{3,1},{5,7},{7,5},{8,10},{10,8},{12,... | collective-permute-start | bytes 1572872 | tf_op jit(solution)/shard_map/ppermute | solution.py:75
  5.1 4.3 %collective-permute-start = (bf16[16,512]{1,0:T(8,128)(2,1)S(1)}, bf16[16,512]{1,0:T(8,128)(2,1)S(1)}, u32[]{:S(2)}, u32[]{:S(2)}) collective-permute-start(bf16[16,512]{1,0:T(8,128)(2,1)S(1)} %get-tuple-element.96), channel_id=1, source_target_pairs={{0,2},{2,4},{4,6},{6,8},{8,10},{10,12},{12,14},{14,16},{16,18},{18... | collective-permute-start | bytes 49160 | tf_op jit(solution)/shard_map/ppermute | solution.py:81
  10.0 15.2 %slice-start = ((s8[4718592]{0:T(1024)(128)(4,1)}), s8[4194304]{0:T(1024)(128)(4,1)S(1)}, s32[]{:S(2)}) async-start(s8[4718592]{0:T(1024)(128)(4,1)} %bitcast.8), calls=%async_computation | async-start | bytes 8388608
  10.1 15.1 %slice-start.2 = ((s8[4718592]{0:T(1024)(128)(4,1)}), s8[4194304]{0:T(1024)(128)(4,1)S(1)}, s32[]{:S(2)}) async-start(s8[4718592]{0:T(1024)(128)(4,1)} %bitcast.10), calls=%async_computation.2 | async-start | bytes 8388608
  10.1 15.1 %collective-permute-start.2 = (bf16[256,1024]{1,0:T(8,128)(2,1)S(1)}, bf16[256,1024]{1,0:T(8,128)(2,1)S(1)}, u32[]{:S(2)}, u32[]{:S(2)}) collective-permute-start(bf16[256,1024]{1,0:T(8,128)(2,1)S(1)} %get-tuple-element.100.refs_1_), channel_id=1, source_target_pairs={{0,1},{2,3},{4,5},{6,7},{1,0},{3,2},{5,4},{7,6},{8,9},{10,11},{12,... | collective-permute-start | bytes 1572872 | tf_op jit(solution)/shard_map/ppermute | solution.py:75
  28.6 6.3 %collective-permute-start.3 = (bf16[256,4480]{1,0:T(8,128)(2,1)S(1)}, bf16[256,4480]{1,0:T(8,128)(2,1)S(1)}, u32[]{:S(2)}, u32[]{:S(2)}) collective-permute-start(bf16[256,4480]{1,0:T(8,128)(2,1)S(1)} %get-tuple-element.110), channel_id=1, source_target_pairs={{0,2},{2,0},{4,6},{6,4},{1,3},{3,1},{5,7},{7,5},{8,10},{10,8},{12,... | collective-permute-start | bytes 6881288 | tf_op jit(solution)/shard_map/ppermute | solution.py:75
  29.2 17.4 %collective-permute-start.7 = (bf16[256,1280]{1,0:T(8,128)(2,1)S(1)}, bf16[256,1280]{1,0:T(8,128)(2,1)S(1)}, u32[]{:S(2)}, u32[]{:S(2)}) collective-permute-start(bf16[256,1280]{1,0:T(8,128)(2,1)S(1)} %get-tuple-element.119), channel_id=1, source_target_pairs={{0,2},{2,0},{4,6},{6,4},{1,3},{3,1},{5,7},{7,5},{8,10},{10,8},{12,... | collective-permute-start | bytes 1966088 | tf_op jit(solution)/shard_map/ppermute | solution.py:75
  31.9 14.7 %collective-permute-start.6 = (bf16[256,1024]{1,0:T(8,128)(2,1)S(1)}, bf16[256,1024]{1,0:T(8,128)(2,1)S(1)}, u32[]{:S(2)}, u32[]{:S(2)}) collective-permute-start(bf16[256,1024]{1,0:T(8,128)(2,1)S(1)} %shard_map.193.refs_1_), channel_id=1, source_target_pairs={{0,1},{2,3},{4,5},{6,7},{1,0},{3,2},{5,4},{7,6},{8,9},{10,11},{12,... | collective-permute-start | bytes 1572872 | tf_op jit(solution)/shard_map/ppermute | solution.py:75
  37.7 24.9 %collective-permute-start.4 = (bf16[120,64,128]{2,1,0:T(8,128)(2,1)S(1)}, bf16[120,64,128]{2,1,0:T(8,128)(2,1)S(1)}, u32[]{:S(2)}, u32[]{:S(2)}) collective-permute-start(bf16[120,64,128]{2,1,0:T(8,128)(2,1)S(1)} %get-tuple-element.111), channel_id=1, source_target_pairs={{0,32},{2,10},{4,36},{6,14},{1,33},{3,11},{5,37},{7,15},{8,40},{10... | collective-permute-start | bytes 5898248 | tf_op jit(solution)/shard_map/ppermute | solution.py:75
  41.7 20.9 %collective-permute-start.5 = (bf16[96,64,128]{2,1,0:T(8,128)(2,1)S(1)}, bf16[96,64,128]{2,1,0:T(8,128)(2,1)S(1)}, u32[]{:S(2)}, u32[]{:S(2)}) collective-permute-start(bf16[96,64,128]{2,1,0:T(8,128)(2,1)S(1)} %get-tuple-element.115), channel_id=1, source_target_pairs={{0,96},{2,26},{4,100},{6,30},{1,97},{3,27},{5,101},{7,31},{8,104},... | collective-permute-start | bytes 4718600 | tf_op jit(solution)/shard_map/ppermute | solution.py:75
  47.0 6.8 %collective-permute-start.8 = (f32[8,512]{1,0:T(8,128)S(1)}, f32[8,512]{1,0:T(8,128)S(1)}, u32[]{:S(2)}, u32[]{:S(2)}) collective-permute-start(f32[8,512]{1,0:T(8,128)S(1)} %shard_map.196), channel_id=1, source_target_pairs={{2,0},{4,2},{6,4},{8,6},{10,8},{12,10},{14,12},{16,14},{18,16},{20... | collective-permute-start | bytes 49160 | tf_op jit(solution)/shard_map/ppermute | solution.py:81
  55.0 2.9 %collective-permute-start.10 = (bf16[7,256,256]{2,1,0:T(8,128)(2,1)S(1)}, bf16[7,256,256]{2,1,0:T(8,128)(2,1)S(1)}, u32[]{:S(2)}, u32[]{:S(2)}) collective-permute-start(bf16[7,256,256]{2,1,0:T(8,128)(2,1)S(1)} %get-tuple-element.132), channel_id=1, source_target_pairs={{0,2},{2,0},{4,6},{6,4},{1,3},{3,1},{5,7},{7,5},{8,10},{10,8},{12,... | collective-permute-start | bytes 2752520 | tf_op jit(solution)/shard_map/ppermute | solution.py:75
  55.1 4.6 %collective-permute-start.9 = (f32[8,128]{1,0:T(8,128)S(1)}, f32[8,128]{1,0:T(8,128)S(1)}, u32[]{:S(2)}, u32[]{:S(2)}) collective-permute-start(f32[8,128]{1,0:T(8,128)S(1)} %get-tuple-element.130.refs_5_), channel_id=1, source_target_pairs={{0,1},{2,3},{4,5},{6,7},{1,0},{3,2},{5,4},{7,6},{8,9},{10,11},{12,... | collective-permute-start | bytes 12296 | tf_op jit(solution)/shard_map/ppermute | solution.py:75
  64.0 10.1 %collective-permute-start.13 = (bf16[33,64,128]{2,1,0:T(8,128)(2,1)S(1)}, bf16[33,64,128]{2,1,0:T(8,128)(2,1)S(1)}, u32[]{:S(2)}, u32[]{:S(2)}) collective-permute-start(bf16[33,64,128]{2,1,0:T(8,128)(2,1)S(1)} %get-tuple-element.142), channel_id=1, source_target_pairs={{0,64},{2,18},{4,68},{6,22},{1,65},{3,19},{5,69},{7,23},{8,72},{10... | collective-permute-start | bytes 1622024 | tf_op jit(solution)/shard_map/ppermute | solution.py:75
  66.9 23.6 %collective-permute-start.12 = (bf16[93,64,128]{2,1,0:T(8,128)(2,1)S(1)}, bf16[93,64,128]{2,1,0:T(8,128)(2,1)S(1)}, u32[]{:S(2)}, u32[]{:S(2)}) collective-permute-start(bf16[93,64,128]{2,1,0:T(8,128)(2,1)S(1)} %get-tuple-element.138), channel_id=1, source_target_pairs={{0,96},{2,26},{4,100},{6,30},{1,97},{3,27},{5,101},{7,31},{8,104},... | collective-permute-start | bytes 4571144 | tf_op jit(solution)/shard_map/ppermute | solution.py:75
  67.3 21.6 %collective-permute-start.11 = (bf16[81,64,128]{2,1,0:T(8,128)(2,1)S(1)}, bf16[81,64,128]{2,1,0:T(8,128)(2,1)S(1)}, u32[]{:S(2)}, u32[]{:S(2)}) collective-permute-start(bf16[81,64,128]{2,1,0:T(8,128)(2,1)S(1)} %get-tuple-element.137), channel_id=1, source_target_pairs={{0,32},{2,10},{4,36},{6,14},{1,33},{3,11},{5,37},{7,15},{8,40},{10... | collective-permute-start | bytes 3981320 | tf_op jit(solution)/shard_map/ppermute | solution.py:75
  67.6 27.4 %collective-permute-start.15 = (bf16[256,1024]{1,0:T(8,128)(2,1)S(1)}, bf16[256,1024]{1,0:T(8,128)(2,1)S(1)}, u32[]{:S(2)}, u32[]{:S(2)}) collective-permute-start(bf16[256,1024]{1,0:T(8,128)(2,1)S(1)} %shard_map.194.refs_1_), channel_id=1, source_target_pairs={{0,1},{2,3},{4,5},{6,7},{1,0},{3,2},{5,4},{7,6},{8,9},{10,11},{12,... | collective-permute-start | bytes 1572872 | tf_op jit(solution)/shard_map/ppermute | solution.py:75
  68.9 26.2 %collective-permute-start.16 = (bf16[256,1024]{1,0:T(8,128)(2,1)S(1)}, bf16[256,1024]{1,0:T(8,128)(2,1)S(1)}, u32[]{:S(2)}, u32[]{:S(2)}) collective-permute-start(bf16[256,1024]{1,0:T(8,128)(2,1)S(1)} %get-tuple-element.148.refs_3_), channel_id=1, source_target_pairs={{0,1},{2,3},{4,5},{6,7},{1,0},{3,2},{5,4},{7,6},{8,9},{10,11},{12,... | collective-permute-start | bytes 1572872 | tf_op jit(solution)/shard_map/ppermute | solution.py:75
  91.0 9.1 %collective-permute-start.14 = (bf16[36,64,128]{2,1,0:T(8,128)(2,1)S(1)}, bf16[36,64,128]{2,1,0:T(8,128)(2,1)S(1)}, u32[]{:S(2)}, u32[]{:S(2)}) collective-permute-start(bf16[36,64,128]{2,1,0:T(8,128)(2,1)S(1)} %get-tuple-element.146), channel_id=1, source_target_pairs={{0,8},{2,34},{4,12},{6,38},{1,9},{3,35},{5,13},{7,39},{8,0},{10,42... | collective-permute-start | bytes 1769480 | tf_op jit(solution)/shard_map/ppermute | solution.py:75
  92.2 15.1 %collective-permute-start.17 = (bf16[36,64,128]{2,1,0:T(8,128)(2,1)S(1)}, bf16[36,64,128]{2,1,0:T(8,128)(2,1)S(1)}, u32[]{:S(2)}, u32[]{:S(2)}) collective-permute-start(bf16[36,64,128]{2,1,0:T(8,128)(2,1)S(1)} %get-tuple-element.155), channel_id=1, source_target_pairs={{0,24},{2,98},{4,28},{6,102},{1,25},{3,99},{5,29},{7,103},{8,16},{... | collective-permute-start | bytes 1769480 | tf_op jit(solution)/shard_map/ppermute | solution.py:75
  94.1 14.8 %collective-permute-start.18 = (bf16[36,64,128]{2,1,0:T(8,128)(2,1)S(1)}, bf16[36,64,128]{2,1,0:T(8,128)(2,1)S(1)}, u32[]{:S(2)}, u32[]{:S(2)}) collective-permute-start(bf16[36,64,128]{2,1,0:T(8,128)(2,1)S(1)} %get-tuple-element.156), channel_id=1, source_target_pairs={{0,16},{2,66},{4,20},{6,70},{1,17},{3,67},{5,21},{7,71},{8,24},{10... | collective-permute-start | bytes 1769480 | tf_op jit(solution)/shard_map/ppermute | solution.py:75
  109.3 7.2 %collective-permute-start.20 = (bf16[40,16,128]{2,1,0:T(8,128)(2,1)S(1)}, bf16[40,16,128]{2,1,0:T(8,128)(2,1)S(1)}, u32[]{:S(2)}, u32[]{:S(2)}) collective-permute-start(bf16[40,16,128]{2,1,0:T(8,128)(2,1)S(1)} %get-tuple-element.161), channel_id=1, source_target_pairs={{0,4},{2,6},{4,0},{6,2},{1,5},{3,7},{5,1},{7,3},{8,12},{10,14},{12... | collective-permute-start | bytes 491528 | tf_op jit(solution)/shard_map/ppermute | solution.py:75
  110.7 11.0 %collective-permute-start.21 = (bf16[40,16,128]{2,1,0:T(8,128)(2,1)S(1)}, bf16[40,16,128]{2,1,0:T(8,128)(2,1)S(1)}, u32[]{:S(2)}, u32[]{:S(2)}) collective-permute-start(bf16[40,16,128]{2,1,0:T(8,128)(2,1)S(1)} %get-tuple-element.162), channel_id=1, source_target_pairs={{0,6},{2,4},{4,2},{6,0},{1,7},{3,5},{5,3},{7,1},{8,14},{10,12},{12... | collective-permute-start | bytes 491528 | tf_op jit(solution)/shard_map/ppermute | solution.py:75
  115.1 1.4 %collective-permute-start.19 = (bf16[39,16,128]{2,1,0:T(8,128)(2,1)S(1)}, bf16[39,16,128]{2,1,0:T(8,128)(2,1)S(1)}, u32[]{:S(2)}, u32[]{:S(2)}) collective-permute-start(bf16[39,16,128]{2,1,0:T(8,128)(2,1)S(1)} %get-tuple-element.160), channel_id=1, source_target_pairs={{0,2},{2,0},{4,6},{6,4},{1,3},{3,1},{5,7},{7,5},{8,10},{10,8},{12,... | collective-permute-start | bytes 479240 | tf_op jit(solution)/shard_map/ppermute | solution.py:75
  (10 other events, 89.7 us)

commit v12 on v10

--- a/solution.py
+++ b/solution.py
@@ -706,7 +706,7 @@
         outs=blocks(ROUND_ONE[:2]) + blocks([4 * count for count in WIDE]),
     )
     sends, keeps = list(results[:2]), list(results[2:])
-    keeps[0], far_send = lax.optimization_barrier((keeps[0], far_send))
+    keeps[0], norm_one_late, down_late = lax.optimization_barrier((keeps[0], norm_one_part, down_part))
     narrow, cross = run(
         far_kernel,
         operands=[narrow, swap(far_send, FIRST[2])],
@@ -714,8 +714,8 @@
         flops=MIDDLE,
     )
     gots = swap_round(sends, FIRST)
-    down_other = swap(down_part, ACROSS)
-    norm_one_other = swap(norm_one_part, ACROSS)
+    down_other = swap(down_late, ACROSS)
+    norm_one_other = swap(norm_one_late, ACROSS)
     results = run(
         second_kernel,
         operands=gots + keeps + [narrow, small, cross],

time: 123 us -> 119 us (0.967)
  waiting for transfers between devices: 57 us -> 50.5 us
  starting transfers between devices: 36.8 us -> 39.8 us
    ppermute x20, waiting for transfers between devices: 55 us -> 48.6 us  [swap(): return lax.ppermute(value, AXES, pairs)]
    ppermute x20, starting transfers between devices: 30.5 us -> 33.5 us  [swap(): return lax.ppermute(value, AXES, pairs)]
  transfers between devices with their start and end apart: 22 -> 22, of which waited for: 13 -> 12; matrix products, arithmetic and copies ran while one was open for 0% -> 0% of each run, Pallas kernels for 17% -> 18%
where the time goes in v12:
time: 119 us
  waiting for transfers between devices  50.5 us (42%)
  starting transfers between devices  39.8 us (33%)
  Pallas kernels  27.1 us (23%)
  between operations  1.62 us (1%)
    ppermute x20, waiting for transfers between devices, swap(): return lax.ppermute(value, AXES, pairs)  48.6 us
    ppermute x20, starting transfers between devices, swap(): return lax.ppermute(value, AXES, pairs)  33.5 us
    pallas_call x19, Pallas kernels, call(): pl.pallas_call(kernel, out_shape=tuple(outs), in_specs=specs, out_specs=t...  27.1 us
    ppermute x2, starting transfers between devices, from_behind(): lax.ppermute(value, axis, [(source, source + steps) for source in range(l...  6.27 us
  transfers between devices with their start and end apart: 22, of which 12 were waited for; matrix products, arithmetic and copies ran while one was open for 0% of the time, Pallas kernels for 18%

profile of v12, /device:TPU:1, one launch (start us, length us, event | category | flops | bytes accessed | tf_op | source)
XLA Modules:
  0.0 119.0 jit_solution(8883448516253036450)
XLA Ops:
  2.8 2.3 %shard_map.186 = (bf16[16,512]{1,0:T(8,128)(2,1)S(1)}, bf16[256,1024]{1,0:T(8,128)(2,1)S(1)}, f32[1,1024]{1,0:T(1,128)S(1)}, bf16[3,1024,512]{2,1,0:T(8,128)(2,1)S(1)}, s32[8,128]{1,0:T(8,128)S(1)}) custom-call(s32[1]{0:T(128)S(6)} %copy.25.refs_0_, bf16[256,1024]{1,0:T(8,128)(2,1)} %refs_5_.9, f32[1,1024]{1,0:T(1,128)} %bitcast.17, ...), custom_call_target="tpu_custom_call" | custom-call | tf_op jit(solution)/shard_map/pallas_call | solution.py:119
  5.1 3.1 %collective-permute-start = (bf16[16,512]{1,0:T(8,128)(2,1)S(1)}, bf16[16,512]{1,0:T(8,128)(2,1)S(1)}, u32[]{:S(2)}, u32[]{:S(2)}) collective-permute-start(bf16[16,512]{1,0:T(8,128)(2,1)S(1)} %get-tuple-element.98), channel_id=1, source_target_pairs={{0,2},{2,4},{4,6},{6,8},{8,10},{10,12},{12,14},{14,16},{16,18},{18... | collective-permute-start | bytes 49160 | tf_op jit(solution)/shard_map/ppermute | solution.py:81
  10.1 2.5 %collective-permute-start.2 = (bf16[256,1024]{1,0:T(8,128)(2,1)S(1)}, bf16[256,1024]{1,0:T(8,128)(2,1)S(1)}, u32[]{:S(2)}, u32[]{:S(2)}) collective-permute-start(bf16[256,1024]{1,0:T(8,128)(2,1)S(1)} %get-tuple-element.102.refs_1_), channel_id=1, source_target_pairs={{0,1},{2,3},{4,5},{6,7},{1,0},{3,2},{5,4},{7,6},{8,9},{10,11},{12,... | collective-permute-start | bytes 1572872 | tf_op jit(solution)/shard_map/ppermute | solution.py:75
  14.1 11.1 %collective-permute-done.2.refs_2_ = bf16[256,1024]{1,0:T(8,128)(2,1)S(1)} collective-permute-done((bf16[256,1024]{1,0:T(8,128)(2,1)S(1)}, bf16[256,1024]{1,0:T(8,128)(2,1)S(1)}, u32[]{:S(2)}, u32[]{:S(2)}) %collective-permute-start.2) | collective-permute-done | bytes 524320 | tf_op jit(solution)/shard_map/ppermute | solution.py:75
  25.3 3.4 %shard_map.190 = (f32[256,1024]{1,0:T(8,128)S(1)}, bf16[256,1024]{1,0:T(8,128)(2,1)S(1)}, bf16[256,2304]{1,0:T(8,128)(2,1)S(1)}, bf16[256,2304]{1,0:T(8,128)(2,1...) custom-call(bf16[256,1024]{1,0:T(8,128)(2,1)S(1)} %copy-done.2, ...), custom_call_target="tpu_custom_call" | custom-call | tf_op jit(solution)/shard_map/pallas_call | solution.py:119
  29.3 2.6 %shard_map.193.refs_1_ = bf16[256,1024]{1,0:T(8,128)(2,1)S(1)} custom-call(bf16[256,2304]{1,0:T(8,128)(2,1)S(1)} %get-tuple-element.111.refs_4_.refs_1_.refs_0_, bf16[256,2304]{1,0:T(8,128)(2,1)S(1)} %get-tuple-element.115.refs_2_.refs_1_, bf16[1024,2304]{1,0:T(8,128)(2,1)S(1)} %bitcast.9, bf16[1024,2304]{1,0:T(8,128)(2,1)S(1)} %bitcast.11), custom_call_target="tpu_custom_call" | custom-call | tf_op jit(solution)/shard_map/pallas_call | solution.py:119
  31.9 3.0 %collective-permute-start.6 = (bf16[256,1024]{1,0:T(8,128)(2,1)S(1)}, bf16[256,1024]{1,0:T(8,128)(2,1)S(1)}, u32[]{:S(2)}, u32[]{:S(2)}) collective-permute-start(bf16[256,1024]{1,0:T(8,128)(2,1)S(1)} %shard_map.193.refs_1_), channel_id=1, source_target_pairs={{0,1},{2,3},{4,5},{6,7},{1,0},{3,2},{5,4},{7,6},{8,9},{10,11},{12,... | collective-permute-start | bytes 1572872 | tf_op jit(solution)/shard_map/ppermute | solution.py:75
  34.9 2.8 %shard_map.191 = (bf16[112,64,128]{2,1,0:T(8,128)(2,1)S(1)}, bf16[112,64,128]{2,1,0:T(8,128)(2,1)S(1)}, bf16[1024,512]{1,0:T(8,128)(2,1)S(1)}) custom-call(bf16[256,1024]{1,0:T(8,128)(2,1)S(1)} %get-tuple-element.108.refs_0_, bf16[256,1024]{1,0:T(8,128)(2,1)S(1)} %copy-done.4, bf16[256,1024]{1,0:T(8,128)(2,1)S(1)} %collective-permute-done.1.refs_2_, ...), custom_call_target="tpu_custom_call" | custom-call | tf_op jit(solution)/shard_map/pallas_call | solution.py:119
  37.7 1.9 %collective-permute-start.4 = (bf16[112,64,128]{2,1,0:T(8,128)(2,1)S(1)}, bf16[112,64,128]{2,1,0:T(8,128)(2,1)S(1)}, u32[]{:S(2)}, u32[]{:S(2)}) collective-permute-start(bf16[112,64,128]{2,1,0:T(8,128)(2,1)S(1)} %get-tuple-element.113), channel_id=1, source_target_pairs={{0,32},{2,10},{4,36},{6,14},{1,33},{3,11},{5,37},{7,15},{8,40},{10... | collective-permute-start | bytes 5505032 | tf_op jit(solution)/shard_map/ppermute | solution.py:75
  39.6 2.1 %shard_map.192 = (bf16[104,64,128]{2,1,0:T(8,128)(2,1)S(1)}, bf16[104,64,128]{2,1,0:T(8,128)(2,1)S(1)}) custom-call(bf16[1024,512]{1,0:T(8,128)(2,1)S(1)} %get-tuple-element.114.refs_0_, bf16[256,2304]{1,0:T(8,128)(2,1)S(1)} %get-tuple-element.111.refs_4_.refs_1_.refs_0_, bf16[256,2304]{1,0:T(8,128)(2,1)S(1)} %get-tuple-element.115.refs_2_.refs_1_, ...), custom_call_target="tpu_custom_call" | custom-call | tf_op jit(solution)/shard_map/pallas_call | solution.py:119
  41.7 2.3 %collective-permute-start.5 = (bf16[104,64,128]{2,1,0:T(8,128)(2,1)S(1)}, bf16[104,64,128]{2,1,0:T(8,128)(2,1)S(1)}, u32[]{:S(2)}, u32[]{:S(2)}) collective-permute-start(bf16[104,64,128]{2,1,0:T(8,128)(2,1)S(1)} %get-tuple-element.117), channel_id=1, source_target_pairs={{0,96},{2,26},{4,100},{6,30},{1,97},{3,27},{5,101},{7,31},{8,104},... | collective-permute-start | bytes 5111816 | tf_op jit(solution)/shard_map/ppermute | solution.py:75
  47.0 3.2 %collective-permute-start.8 = (f32[8,512]{1,0:T(8,128)S(1)}, f32[8,512]{1,0:T(8,128)S(1)}, u32[]{:S(2)}, u32[]{:S(2)}) collective-permute-start(f32[8,512]{1,0:T(8,128)S(1)} %shard_map.196), channel_id=1, source_target_pairs={{2,0},{4,2},{6,4},{8,6},{10,8},{12,10},{14,12},{16,14},{18,16},{20... | collective-permute-start | bytes 49160 | tf_op jit(solution)/shard_map/ppermute | solution.py:81
  51.9 2.0 %collective-permute-done.8.refs_2_ = f32[8,512]{1,0:T(8,128)S(1)} collective-permute-done((f32[8,512]{1,0:T(8,128)S(1)}, f32[8,512]{1,0:T(8,128)S(1)}, u32[]{:S(2)}, u32[]{:S(2)}) %collective-permute-start.8) | collective-permute-done | bytes 16416 | tf_op jit(solution)/shard_map/ppermute | solution.py:81
  55.1 2.8 %collective-permute-start.10 = (f32[8,128]{1,0:T(8,128)S(1)}, f32[8,128]{1,0:T(8,128)S(1)}, u32[]{:S(2)}, u32[]{:S(2)}) collective-permute-start(f32[8,128]{1,0:T(8,128)S(1)} %get-tuple-element.135.refs_7_), channel_id=1, source_target_pairs={{0,1},{2,3},{4,5},{6,7},{1,0},{3,2},{5,4},{7,6},{8,9},{10,11},{12,... | collective-permute-start | bytes 12296 | tf_op jit(solution)/shard_map/ppermute | solution.py:75
  60.8 3.4 %collective-permute-start.13 = (bf16[33,64,128]{2,1,0:T(8,128)(2,1)S(1)}, bf16[33,64,128]{2,1,0:T(8,128)(2,1)S(1)}, u32[]{:S(2)}, u32[]{:S(2)}) collective-permute-start(bf16[33,64,128]{2,1,0:T(8,128)(2,1)S(1)} %get-tuple-element.146), channel_id=1, source_target_pairs={{0,64},{2,18},{4,68},{6,22},{1,65},{3,19},{5,69},{7,23},{8,72},{10... | collective-permute-start | bytes 1622024 | tf_op jit(solution)/shard_map/ppermute | solution.py:75
  65.0 2.1 %collective-permute-start.12 = (bf16[89,64,128]{2,1,0:T(8,128)(2,1)S(1)}, bf16[89,64,128]{2,1,0:T(8,128)(2,1)S(1)}, u32[]{:S(2)}, u32[]{:S(2)}) collective-permute-start(bf16[89,64,128]{2,1,0:T(8,128)(2,1)S(1)} %get-tuple-element.139), channel_id=1, source_target_pairs={{0,96},{2,26},{4,100},{6,30},{1,97},{3,27},{5,101},{7,31},{8,104},... | collective-permute-start | bytes 4374536 | tf_op jit(solution)/shard_map/ppermute | solution.py:75
  67.1 1.8 %collective-permute-start.15 = (bf16[256,1024]{1,0:T(8,128)(2,1)S(1)}, bf16[256,1024]{1,0:T(8,128)(2,1)S(1)}, u32[]{:S(2)}, u32[]{:S(2)}) collective-permute-start(bf16[256,1024]{1,0:T(8,128)(2,1)S(1)} %shard_map.194.refs_1_), channel_id=1, source_target_pairs={{0,1},{2,3},{4,5},{6,7},{1,0},{3,2},{5,4},{7,6},{8,9},{10,11},{12,... | collective-permute-start | bytes 1572872 | tf_op jit(solution)/shard_map/ppermute | solution.py:75
  71.4 14.8 %collective-permute-done.11.refs_0_ = bf16[85,64,128]{2,1,0:T(8,128)(2,1)S(1)} collective-permute-done((bf16[85,64,128]{2,1,0:T(8,128)(2,1)S(1)}, bf16[85,64,128]{2,1,0:T(8,128)(2,1)S(1)}, u32[]{:S(2)}, u32[]{:S(2)}) %collective-permute-start.11) | collective-permute-done | bytes 1392672 | tf_op jit(solution)/shard_map/ppermute | solution.py:75
  87.5 2.3 %collective-permute-start.14 = (bf16[36,64,128]{2,1,0:T(8,128)(2,1)S(1)}, bf16[36,64,128]{2,1,0:T(8,128)(2,1)S(1)}, u32[]{:S(2)}, u32[]{:S(2)}) collective-permute-start(bf16[36,64,128]{2,1,0:T(8,128)(2,1)S(1)} %get-tuple-element.150), channel_id=1, source_target_pairs={{0,8},{2,34},{4,12},{6,38},{1,9},{3,35},{5,13},{7,39},{8,0},{10,42... | collective-permute-start | bytes 1769480 | tf_op jit(solution)/shard_map/ppermute | solution.py:75
  89.7 1.9 %collective-permute-start.17 = (bf16[36,64,128]{2,1,0:T(8,128)(2,1)S(1)}, bf16[36,64,128]{2,1,0:T(8,128)(2,1)S(1)}, u32[]{:S(2)}, u32[]{:S(2)}) collective-permute-start(bf16[36,64,128]{2,1,0:T(8,128)(2,1)S(1)} %get-tuple-element.159), channel_id=1, source_target_pairs={{0,24},{2,98},{4,28},{6,102},{1,25},{3,99},{5,29},{7,103},{8,16},{... | collective-permute-start | bytes 1769480 | tf_op jit(solution)/shard_map/ppermute | solution.py:75
  94.4 2.9 %collective-permute-done.14.refs_0_ = bf16[36,64,128]{2,1,0:T(8,128)(2,1)S(1)} collective-permute-done((bf16[36,64,128]{2,1,0:T(8,128)(2,1)S(1)}, bf16[36,64,128]{2,1,0:T(8,128)(2,1)S(1)}, u32[]{:S(2)}, u32[]{:S(2)}) %collective-permute-start.14) | collective-permute-done | bytes 589856 | tf_op jit(solution)/shard_map/ppermute | solution.py:75
  97.3 7.5 %collective-permute-done.17.refs_1_ = bf16[36,64,128]{2,1,0:T(8,128)(2,1)S(1)} collective-permute-done((bf16[36,64,128]{2,1,0:T(8,128)(2,1)S(1)}, bf16[36,64,128]{2,1,0:T(8,128)(2,1)S(1)}, u32[]{:S(2)}, u32[]{:S(2)}) %collective-permute-start.17) | collective-permute-done | bytes 589856 | tf_op jit(solution)/shard_map/ppermute | solution.py:75
  108.2 3.6 %collective-permute-start.21 = (bf16[40,16,128]{2,1,0:T(8,128)(2,1)S(1)}, bf16[40,16,128]{2,1,0:T(8,128)(2,1)S(1)}, u32[]{:S(2)}, u32[]{:S(2)}) collective-permute-start(bf16[40,16,128]{2,1,0:T(8,128)(2,1)S(1)} %get-tuple-element.166), channel_id=1, source_target_pairs={{0,6},{2,4},{4,2},{6,0},{1,7},{3,5},{5,3},{7,1},{8,14},{10,12},{12... | collective-permute-start | bytes 491528 | tf_op jit(solution)/shard_map/ppermute | solution.py:75
  113.1 5.1 %collective-permute-done.21.refs_3_ = bf16[40,16,128]{2,1,0:T(8,128)(2,1)S(1)} collective-permute-done((bf16[40,16,128]{2,1,0:T(8,128)(2,1)S(1)}, bf16[40,16,128]{2,1,0:T(8,128)(2,1)S(1)}, u32[]{:S(2)}, u32[]{:S(2)}) %collective-permute-start.21) | collective-permute-done | bytes 163872 | tf_op jit(solution)/shard_map/ppermute | solution.py:75
  (65 shorter events, 27.2 us)
Async XLA Ops:
  0.6 8.8 %collective-permute-start.1 = (bf16[256,1024]{1,0:T(8,128)(2,1)}, bf16[256,1024]{1,0:T(8,128)(2,1)S(1)}, u32[]{:S(2)}, u32[]{:S(2)}) collective-permute-start(bf16[256,1024]{1,0:T(8,128)(2,1)} %refs_5_.8), channel_id=1, source_target_pairs={{0,2},{2,0},{4,6},{6,4},{1,3},{3,1},{5,7},{7,5},{8,10},{10,8},{12,... | collective-permute-start | bytes 1572872 | tf_op jit(solution)/shard_map/ppermute | solution.py:75
  5.1 4.3 %collective-permute-start = (bf16[16,512]{1,0:T(8,128)(2,1)S(1)}, bf16[16,512]{1,0:T(8,128)(2,1)S(1)}, u32[]{:S(2)}, u32[]{:S(2)}) collective-permute-start(bf16[16,512]{1,0:T(8,128)(2,1)S(1)} %get-tuple-element.98), channel_id=1, source_target_pairs={{0,2},{2,4},{4,6},{6,8},{8,10},{10,12},{12,14},{14,16},{16,18},{18... | collective-permute-start | bytes 49160 | tf_op jit(solution)/shard_map/ppermute | solution.py:81
  10.1 15.2 %slice-start = ((s8[4718592]{0:T(1024)(128)(4,1)}), s8[4194304]{0:T(1024)(128)(4,1)S(1)}, s32[]{:S(2)}) async-start(s8[4718592]{0:T(1024)(128)(4,1)} %bitcast.8), calls=%async_computation | async-start | bytes 8388608
  10.1 15.1 %slice-start.2 = ((s8[4718592]{0:T(1024)(128)(4,1)}), s8[4194304]{0:T(1024)(128)(4,1)S(1)}, s32[]{:S(2)}) async-start(s8[4718592]{0:T(1024)(128)(4,1)} %bitcast.10), calls=%async_computation.2 | async-start | bytes 8388608
  10.1 15.1 %collective-permute-start.2 = (bf16[256,1024]{1,0:T(8,128)(2,1)S(1)}, bf16[256,1024]{1,0:T(8,128)(2,1)S(1)}, u32[]{:S(2)}, u32[]{:S(2)}) collective-permute-start(bf16[256,1024]{1,0:T(8,128)(2,1)S(1)} %get-tuple-element.102.refs_1_), channel_id=1, source_target_pairs={{0,1},{2,3},{4,5},{6,7},{1,0},{3,2},{5,4},{7,6},{8,9},{10,11},{12,... | collective-permute-start | bytes 1572872 | tf_op jit(solution)/shard_map/ppermute | solution.py:75
  28.6 6.3 %collective-permute-start.3 = (bf16[256,4480]{1,0:T(8,128)(2,1)S(1)}, bf16[256,4480]{1,0:T(8,128)(2,1)S(1)}, u32[]{:S(2)}, u32[]{:S(2)}) collective-permute-start(bf16[256,4480]{1,0:T(8,128)(2,1)S(1)} %get-tuple-element.112), channel_id=1, source_target_pairs={{0,2},{2,0},{4,6},{6,4},{1,3},{3,1},{5,7},{7,5},{8,10},{10,8},{12,... | collective-permute-start | bytes 6881288 | tf_op jit(solution)/shard_map/ppermute | solution.py:75
  29.2 17.4 %collective-permute-start.7 = (bf16[256,1280]{1,0:T(8,128)(2,1)S(1)}, bf16[256,1280]{1,0:T(8,128)(2,1)S(1)}, u32[]{:S(2)}, u32[]{:S(2)}) collective-permute-start(bf16[256,1280]{1,0:T(8,128)(2,1)S(1)} %get-tuple-element.121), channel_id=1, source_target_pairs={{0,2},{2,0},{4,6},{6,4},{1,3},{3,1},{5,7},{7,5},{8,10},{10,8},{12,... | collective-permute-start | bytes 1966088 | tf_op jit(solution)/shard_map/ppermute | solution.py:75
  31.9 14.7 %collective-permute-start.6 = (bf16[256,1024]{1,0:T(8,128)(2,1)S(1)}, bf16[256,1024]{1,0:T(8,128)(2,1)S(1)}, u32[]{:S(2)}, u32[]{:S(2)}) collective-permute-start(bf16[256,1024]{1,0:T(8,128)(2,1)S(1)} %shard_map.193.refs_1_), channel_id=1, source_target_pairs={{0,1},{2,3},{4,5},{6,7},{1,0},{3,2},{5,4},{7,6},{8,9},{10,11},{12,... | collective-permute-start | bytes 1572872 | tf_op jit(solution)/shard_map/ppermute | solution.py:75
  37.7 26.6 %collective-permute-start.4 = (bf16[112,64,128]{2,1,0:T(8,128)(2,1)S(1)}, bf16[112,64,128]{2,1,0:T(8,128)(2,1)S(1)}, u32[]{:S(2)}, u32[]{:S(2)}) collective-permute-start(bf16[112,64,128]{2,1,0:T(8,128)(2,1)S(1)} %get-tuple-element.113), channel_id=1, source_target_pairs={{0,32},{2,10},{4,36},{6,14},{1,33},{3,11},{5,37},{7,15},{8,40},{10... | collective-permute-start | bytes 5505032 | tf_op jit(solution)/shard_map/ppermute | solution.py:75
  41.7 22.5 %collective-permute-start.5 = (bf16[104,64,128]{2,1,0:T(8,128)(2,1)S(1)}, bf16[104,64,128]{2,1,0:T(8,128)(2,1)S(1)}, u32[]{:S(2)}, u32[]{:S(2)}) collective-permute-start(bf16[104,64,128]{2,1,0:T(8,128)(2,1)S(1)} %get-tuple-element.117), channel_id=1, source_target_pairs={{0,96},{2,26},{4,100},{6,30},{1,97},{3,27},{5,101},{7,31},{8,104},... | collective-permute-start | bytes 5111816 | tf_op jit(solution)/shard_map/ppermute | solution.py:75
  47.0 6.8 %collective-permute-start.8 = (f32[8,512]{1,0:T(8,128)S(1)}, f32[8,512]{1,0:T(8,128)S(1)}, u32[]{:S(2)}, u32[]{:S(2)}) collective-permute-start(f32[8,512]{1,0:T(8,128)S(1)} %shard_map.196), channel_id=1, source_target_pairs={{2,0},{4,2},{6,4},{8,6},{10,8},{12,10},{14,12},{16,14},{18,16},{20... | collective-permute-start | bytes 49160 | tf_op jit(solution)/shard_map/ppermute | solution.py:81
  55.0 4.1 %collective-permute-start.9 = (bf16[7,256,256]{2,1,0:T(8,128)(2,1)S(1)}, bf16[7,256,256]{2,1,0:T(8,128)(2,1)S(1)}, u32[]{:S(2)}, u32[]{:S(2)}) collective-permute-start(bf16[7,256,256]{2,1,0:T(8,128)(2,1)S(1)} %get-tuple-element.132), channel_id=1, source_target_pairs={{0,2},{2,0},{4,6},{6,4},{1,3},{3,1},{5,7},{7,5},{8,10},{10,8},{12,... | collective-permute-start | bytes 2752520 | tf_op jit(solution)/shard_map/ppermute | solution.py:75
  55.1 4.0 %collective-permute-start.10 = (f32[8,128]{1,0:T(8,128)S(1)}, f32[8,128]{1,0:T(8,128)S(1)}, u32[]{:S(2)}, u32[]{:S(2)}) collective-permute-start(f32[8,128]{1,0:T(8,128)S(1)} %get-tuple-element.135.refs_7_), channel_id=1, source_target_pairs={{0,1},{2,3},{4,5},{6,7},{1,0},{3,2},{5,4},{7,6},{8,9},{10,11},{12,... | collective-permute-start | bytes 12296 | tf_op jit(solution)/shard_map/ppermute | solution.py:75
  60.8 10.5 %collective-permute-start.13 = (bf16[33,64,128]{2,1,0:T(8,128)(2,1)S(1)}, bf16[33,64,128]{2,1,0:T(8,128)(2,1)S(1)}, u32[]{:S(2)}, u32[]{:S(2)}) collective-permute-start(bf16[33,64,128]{2,1,0:T(8,128)(2,1)S(1)} %get-tuple-element.146), channel_id=1, source_target_pairs={{0,64},{2,18},{4,68},{6,22},{1,65},{3,19},{5,69},{7,23},{8,72},{10... | collective-permute-start | bytes 1622024 | tf_op jit(solution)/shard_map/ppermute | solution.py:75
  65.0 21.9 %collective-permute-start.12 = (bf16[89,64,128]{2,1,0:T(8,128)(2,1)S(1)}, bf16[89,64,128]{2,1,0:T(8,128)(2,1)S(1)}, u32[]{:S(2)}, u32[]{:S(2)}) collective-permute-start(bf16[89,64,128]{2,1,0:T(8,128)(2,1)S(1)} %get-tuple-element.139), channel_id=1, source_target_pairs={{0,96},{2,26},{4,100},{6,30},{1,97},{3,27},{5,101},{7,31},{8,104},... | collective-permute-start | bytes 4374536 | tf_op jit(solution)/shard_map/ppermute | solution.py:75
  67.1 19.1 %collective-permute-start.11 = (bf16[85,64,128]{2,1,0:T(8,128)(2,1)S(1)}, bf16[85,64,128]{2,1,0:T(8,128)(2,1)S(1)}, u32[]{:S(2)}, u32[]{:S(2)}) collective-permute-start(bf16[85,64,128]{2,1,0:T(8,128)(2,1)S(1)} %get-tuple-element.138), channel_id=1, source_target_pairs={{0,32},{2,10},{4,36},{6,14},{1,33},{3,11},{5,37},{7,15},{8,40},{10... | collective-permute-start | bytes 4177928 | tf_op jit(solution)/shard_map/ppermute | solution.py:75
  67.1 25.6 %collective-permute-start.15 = (bf16[256,1024]{1,0:T(8,128)(2,1)S(1)}, bf16[256,1024]{1,0:T(8,128)(2,1)S(1)}, u32[]{:S(2)}, u32[]{:S(2)}) collective-permute-start(bf16[256,1024]{1,0:T(8,128)(2,1)S(1)} %shard_map.194.refs_1_), channel_id=1, source_target_pairs={{0,1},{2,3},{4,5},{6,7},{1,0},{3,2},{5,4},{7,6},{8,9},{10,11},{12,... | collective-permute-start | bytes 1572872 | tf_op jit(solution)/shard_map/ppermute | solution.py:75
  68.9 23.8 %collective-permute-start.16 = (bf16[256,1024]{1,0:T(8,128)(2,1)S(1)}, bf16[256,1024]{1,0:T(8,128)(2,1)S(1)}, u32[]{:S(2)}, u32[]{:S(2)}) collective-permute-start(bf16[256,1024]{1,0:T(8,128)(2,1)S(1)} %get-tuple-element.152.refs_3_), channel_id=1, source_target_pairs={{0,1},{2,3},{4,5},{6,7},{1,0},{3,2},{5,4},{7,6},{8,9},{10,11},{12,... | collective-permute-start | bytes 1572872 | tf_op jit(solution)/shard_map/ppermute | solution.py:75
  87.5 9.8 %collective-permute-start.14 = (bf16[36,64,128]{2,1,0:T(8,128)(2,1)S(1)}, bf16[36,64,128]{2,1,0:T(8,128)(2,1)S(1)}, u32[]{:S(2)}, u32[]{:S(2)}) collective-permute-start(bf16[36,64,128]{2,1,0:T(8,128)(2,1)S(1)} %get-tuple-element.150), channel_id=1, source_target_pairs={{0,8},{2,34},{4,12},{6,38},{1,9},{3,35},{5,13},{7,39},{8,0},{10,42... | collective-permute-start | bytes 1769480 | tf_op jit(solution)/shard_map/ppermute | solution.py:75
  89.7 15.0 %collective-permute-start.17 = (bf16[36,64,128]{2,1,0:T(8,128)(2,1)S(1)}, bf16[36,64,128]{2,1,0:T(8,128)(2,1)S(1)}, u32[]{:S(2)}, u32[]{:S(2)}) collective-permute-start(bf16[36,64,128]{2,1,0:T(8,128)(2,1)S(1)} %get-tuple-element.159), channel_id=1, source_target_pairs={{0,24},{2,98},{4,28},{6,102},{1,25},{3,99},{5,29},{7,103},{8,16},{... | collective-permute-start | bytes 1769480 | tf_op jit(solution)/shard_map/ppermute | solution.py:75
  91.6 14.9 %collective-permute-start.18 = (bf16[36,64,128]{2,1,0:T(8,128)(2,1)S(1)}, bf16[36,64,128]{2,1,0:T(8,128)(2,1)S(1)}, u32[]{:S(2)}, u32[]{:S(2)}) collective-permute-start(bf16[36,64,128]{2,1,0:T(8,128)(2,1)S(1)} %get-tuple-element.160), channel_id=1, source_target_pairs={{0,16},{2,66},{4,20},{6,70},{1,17},{3,67},{5,21},{7,71},{8,24},{10... | collective-permute-start | bytes 1769480 | tf_op jit(solution)/shard_map/ppermute | solution.py:75
  106.9 6.2 %collective-permute-start.20 = (bf16[40,16,128]{2,1,0:T(8,128)(2,1)S(1)}, bf16[40,16,128]{2,1,0:T(8,128)(2,1)S(1)}, u32[]{:S(2)}, u32[]{:S(2)}) collective-permute-start(bf16[40,16,128]{2,1,0:T(8,128)(2,1)S(1)} %get-tuple-element.165), channel_id=1, source_target_pairs={{0,4},{2,6},{4,0},{6,2},{1,5},{3,7},{5,1},{7,3},{8,12},{10,14},{12... | collective-permute-start | bytes 491528 | tf_op jit(solution)/shard_map/ppermute | solution.py:75
  108.2 10.0 %collective-permute-start.21 = (bf16[40,16,128]{2,1,0:T(8,128)(2,1)S(1)}, bf16[40,16,128]{2,1,0:T(8,128)(2,1)S(1)}, u32[]{:S(2)}, u32[]{:S(2)}) collective-permute-start(bf16[40,16,128]{2,1,0:T(8,128)(2,1)S(1)} %get-tuple-element.166), channel_id=1, source_target_pairs={{0,6},{2,4},{4,2},{6,0},{1,7},{3,5},{5,3},{7,1},{8,14},{10,12},{12... | collective-permute-start | bytes 491528 | tf_op jit(solution)/shard_map/ppermute | solution.py:75
  111.7 1.4 %collective-permute-start.19 = (bf16[39,16,128]{2,1,0:T(8,128)(2,1)S(1)}, bf16[39,16,128]{2,1,0:T(8,128)(2,1)S(1)}, u32[]{:S(2)}, u32[]{:S(2)}) collective-permute-start(bf16[39,16,128]{2,1,0:T(8,128)(2,1)S(1)} %get-tuple-element.164), channel_id=1, source_target_pairs={{0,2},{2,0},{4,6},{6,4},{1,3},{3,1},{5,7},{7,5},{8,10},{10,8},{12,... | collective-permute-start | bytes 479240 | tf_op jit(solution)/shard_map/ppermute | solution.py:75
  (10 other events, 90.9 us)

commit v13 on v12

--- a/solution.py
+++ b/solution.py
@@ -605,8 +605,6 @@
         where=pltpu.HBM,
     )
     incoming = from_behind(tail, "seq", 1)
-    cotangent_other = share(cotangent)
-    incoming, cotangent_other = lax.optimization_barrier((incoming, cotangent_other))
     normed_one, parts, gated = run(
         project_kernel,
         operands=[tokens_here, gain_here, weights_here],
@@ -627,7 +625,11 @@
         outs=[like((rows, units), F32)],
         flops=LONG,
     )[0]
-    branch_other, hidden_grad = lax.optimization_barrier((branch_other, hidden_grad))
+    cotangent_late, hidden_grad = lax.optimization_barrier((cotangent_late, hidden_grad))
+    cotangent_other = share(cotangent_late)
+    branch_other, hidden_grad, cotangent_other = lax.optimization_barrier(
+        (branch_other, hidden_grad, cotangent_other)
+    )
     resid, normed_two, hidden, gate_back, up_back, shared, shared_early = run(
         feed_kernel,
         operands=[tokens, branch, branch_other, gain_two_row, gate_weight, up_weight, hidden_grad]

time: 119 us -> 119 us (level)
    ppermute x20, waiting for transfers between devices: 48.6 us -> 46.7 us  [swap(): return lax.ppermute(value, AXES, pairs)]
  transfers between devices with their start and end apart: 22 -> 22, of which waited for: 12 -> 12; matrix products, arithmetic and copies ran while one was open for 0% -> 0% of each run, Pallas kernels for 18% -> 16%
where the time goes in v13:
time: 119 us
  waiting for transfers between devices  49.7 us (42%)
  starting transfers between devices  40.3 us (34%)
  Pallas kernels  27 us (23%)
  between operations  1.62 us (1%)
    ppermute x20, waiting for transfers between devices, swap(): return lax.ppermute(value, AXES, pairs)  46.7 us
    ppermute x20, starting transfers between devices, swap(): return lax.ppermute(value, AXES, pairs)  33 us
    pallas_call x19, Pallas kernels, call(): pl.pallas_call(kernel, out_shape=tuple(outs), in_specs=specs, out_specs=t...  27 us
    ppermute x2, starting transfers between devices, from_behind(): lax.ppermute(value, axis, [(source, source + steps) for source in range(l...  7.28 us
    ppermute x2, waiting for transfers between devices, from_behind(): lax.ppermute(value, axis, [(source, source + steps) for source in range(l...  2.94 us
  transfers between devices with their start and end apart: 22, of which 12 were waited for; matrix products, arithmetic and copies ran while one was open for 0% of the time, Pallas kernels for 16%

profile of v13, /device:TPU:1, one launch (start us, length us, event | category | flops | bytes accessed | tf_op | source)
XLA Modules:
  0.0 118.7 jit_solution(13567522333949472157)
XLA Ops:
  1.3 2.3 %shard_map.186 = (bf16[16,512]{1,0:T(8,128)(2,1)S(1)}, bf16[256,1024]{1,0:T(8,128)(2,1)S(1)}, f32[1,1024]{1,0:T(1,128)S(1)}, bf16[3,1024,512]{2,1,0:T(8,128)(2,1)S(1)}, s32[8,128]{1,0:T(8,128)S(1)}) custom-call(s32[1]{0:T(128)S(6)} %copy.25.refs_0_, bf16[256,1024]{1,0:T(8,128)(2,1)} %refs_5_.9, f32[1,1024]{1,0:T(1,128)} %bitcast.17, ...), custom_call_target="tpu_custom_call" | custom-call | tf_op jit(solution)/shard_map/pallas_call | solution.py:119
  3.6 4.5 %collective-permute-start = (bf16[16,512]{1,0:T(8,128)(2,1)S(1)}, bf16[16,512]{1,0:T(8,128)(2,1)S(1)}, u32[]{:S(2)}, u32[]{:S(2)}) collective-permute-start(bf16[16,512]{1,0:T(8,128)(2,1)S(1)} %get-tuple-element.99), channel_id=1, source_target_pairs={{0,2},{2,4},{4,6},{6,8},{8,10},{10,12},{12,14},{14,16},{16,18},{18... | collective-permute-start | bytes 49160 | tf_op jit(solution)/shard_map/ppermute | solution.py:81
  10.0 2.5 %collective-permute-start.1 = (bf16[256,1024]{1,0:T(8,128)(2,1)S(1)}, bf16[256,1024]{1,0:T(8,128)(2,1)S(1)}, u32[]{:S(2)}, u32[]{:S(2)}) collective-permute-start(bf16[256,1024]{1,0:T(8,128)(2,1)S(1)} %get-tuple-element.102.refs_1_), channel_id=1, source_target_pairs={{0,1},{2,3},{4,5},{6,7},{1,0},{3,2},{5,4},{7,6},{8,9},{10,11},{12,... | collective-permute-start | bytes 1572872 | tf_op jit(solution)/shard_map/ppermute | solution.py:75
  14.1 9.9 %collective-permute-done.1.refs_2_ = bf16[256,1024]{1,0:T(8,128)(2,1)S(1)} collective-permute-done((bf16[256,1024]{1,0:T(8,128)(2,1)S(1)}, bf16[256,1024]{1,0:T(8,128)(2,1)S(1)}, u32[]{:S(2)}, u32[]{:S(2)}) %collective-permute-start.1) | collective-permute-done | bytes 524320 | tf_op jit(solution)/shard_map/ppermute | solution.py:75
  24.0 3.4 %shard_map.190 = (f32[256,1024]{1,0:T(8,128)S(1)}, bf16[256,1024]{1,0:T(8,128)(2,1)S(1)}, bf16[256,2304]{1,0:T(8,128)(2,1)S(1)}, bf16[256,2304]{1,0:T(8,128)(2,1...) custom-call(bf16[256,1024]{1,0:T(8,128)(2,1)S(1)} %copy-done.2, ...), custom_call_target="tpu_custom_call" | custom-call | tf_op jit(solution)/shard_map/pallas_call | solution.py:119
  28.0 2.6 %shard_map.193.refs_1_ = bf16[256,1024]{1,0:T(8,128)(2,1)S(1)} custom-call(bf16[256,2304]{1,0:T(8,128)(2,1)S(1)} %get-tuple-element.113.refs_4_.refs_1_.refs_0_, bf16[256,2304]{1,0:T(8,128)(2,1)S(1)} %get-tuple-element.117.refs_2_.refs_1_, bf16[1024,2304]{1,0:T(8,128)(2,1)S(1)} %bitcast.9, bf16[1024,2304]{1,0:T(8,128)(2,1)S(1)} %bitcast.11), custom_call_target="tpu_custom_call" | custom-call | tf_op jit(solution)/shard_map/pallas_call | solution.py:119
  30.6 3.3 %collective-permute-start.6 = (bf16[256,1024]{1,0:T(8,128)(2,1)S(1)}, bf16[256,1024]{1,0:T(8,128)(2,1)S(1)}, u32[]{:S(2)}, u32[]{:S(2)}) collective-permute-start(bf16[256,1024]{1,0:T(8,128)(2,1)S(1)} %shard_map.193.refs_1_), channel_id=1, source_target_pairs={{0,1},{2,3},{4,5},{6,7},{1,0},{3,2},{5,4},{7,6},{8,9},{10,11},{12,... | collective-permute-start | bytes 1572872 | tf_op jit(solution)/shard_map/ppermute | solution.py:75
  33.9 2.8 %shard_map.191 = (bf16[112,64,128]{2,1,0:T(8,128)(2,1)S(1)}, bf16[112,64,128]{2,1,0:T(8,128)(2,1)S(1)}, bf16[1024,512]{1,0:T(8,128)(2,1)S(1)}) custom-call(bf16[256,1024]{1,0:T(8,128)(2,1)S(1)} %get-tuple-element.110.refs_0_, bf16[256,1024]{1,0:T(8,128)(2,1)S(1)} %copy-done.4, bf16[256,1024]{1,0:T(8,128)(2,1)S(1)} %collective-permute-done.2.refs_2_, ...), custom_call_target="tpu_custom_call" | custom-call | tf_op jit(solution)/shard_map/pallas_call | solution.py:119
  36.7 2.8 %collective-permute-start.4 = (bf16[112,64,128]{2,1,0:T(8,128)(2,1)S(1)}, bf16[112,64,128]{2,1,0:T(8,128)(2,1)S(1)}, u32[]{:S(2)}, u32[]{:S(2)}) collective-permute-start(bf16[112,64,128]{2,1,0:T(8,128)(2,1)S(1)} %get-tuple-element.115), channel_id=1, source_target_pairs={{0,32},{2,10},{4,36},{6,14},{1,33},{3,11},{5,37},{7,15},{8,40},{10... | collective-permute-start | bytes 5505032 | tf_op jit(solution)/shard_map/ppermute | solution.py:75
  39.5 2.1 %shard_map.192 = (bf16[104,64,128]{2,1,0:T(8,128)(2,1)S(1)}, bf16[104,64,128]{2,1,0:T(8,128)(2,1)S(1)}) custom-call(bf16[1024,512]{1,0:T(8,128)(2,1)S(1)} %get-tuple-element.116.refs_0_, bf16[256,2304]{1,0:T(8,128)(2,1)S(1)} %get-tuple-element.113.refs_4_.refs_1_.refs_0_, bf16[256,2304]{1,0:T(8,128)(2,1)S(1)} %get-tuple-element.117.refs_2_.refs_1_, ...), custom_call_target="tpu_custom_call" | custom-call | tf_op jit(solution)/shard_map/pallas_call | solution.py:119
  41.6 2.3 %collective-permute-start.5 = (bf16[104,64,128]{2,1,0:T(8,128)(2,1)S(1)}, bf16[104,64,128]{2,1,0:T(8,128)(2,1)S(1)}, u32[]{:S(2)}, u32[]{:S(2)}) collective-permute-start(bf16[104,64,128]{2,1,0:T(8,128)(2,1)S(1)} %get-tuple-element.119), channel_id=1, source_target_pairs={{0,96},{2,26},{4,100},{6,30},{1,97},{3,27},{5,101},{7,31},{8,104},... | collective-permute-start | bytes 5111816 | tf_op jit(solution)/shard_map/ppermute | solution.py:75
  46.4 2.8 %collective-permute-start.8 = (f32[8,512]{1,0:T(8,128)S(1)}, f32[8,512]{1,0:T(8,128)S(1)}, u32[]{:S(2)}, u32[]{:S(2)}) collective-permute-start(f32[8,512]{1,0:T(8,128)S(1)} %shard_map.196), channel_id=1, source_target_pairs={{2,0},{4,2},{6,4},{8,6},{10,8},{12,10},{14,12},{16,14},{18,16},{20... | collective-permute-start | bytes 49160 | tf_op jit(solution)/shard_map/ppermute | solution.py:81
  50.9 2.9 %collective-permute-done.8.refs_2_ = f32[8,512]{1,0:T(8,128)S(1)} collective-permute-done((f32[8,512]{1,0:T(8,128)S(1)}, f32[8,512]{1,0:T(8,128)S(1)}, u32[]{:S(2)}, u32[]{:S(2)}) %collective-permute-start.8) | collective-permute-done | bytes 16416 | tf_op jit(solution)/shard_map/ppermute | solution.py:81
  55.0 2.8 %collective-permute-start.10 = (f32[8,128]{1,0:T(8,128)S(1)}, f32[8,128]{1,0:T(8,128)S(1)}, u32[]{:S(2)}, u32[]{:S(2)}) collective-permute-start(f32[8,128]{1,0:T(8,128)S(1)} %get-tuple-element.137.refs_7_), channel_id=1, source_target_pairs={{0,1},{2,3},{4,5},{6,7},{1,0},{3,2},{5,4},{7,6},{8,9},{10,11},{12,... | collective-permute-start | bytes 12296 | tf_op jit(solution)/shard_map/ppermute | solution.py:75
  60.8 3.4 %collective-permute-start.13 = (bf16[33,64,128]{2,1,0:T(8,128)(2,1)S(1)}, bf16[33,64,128]{2,1,0:T(8,128)(2,1)S(1)}, u32[]{:S(2)}, u32[]{:S(2)}) collective-permute-start(bf16[33,64,128]{2,1,0:T(8,128)(2,1)S(1)} %get-tuple-element.148), channel_id=1, source_target_pairs={{0,64},{2,18},{4,68},{6,22},{1,65},{3,19},{5,69},{7,23},{8,72},{10... | collective-permute-start | bytes 1622024 | tf_op jit(solution)/shard_map/ppermute | solution.py:75
  65.0 2.1 %collective-permute-start.12 = (bf16[89,64,128]{2,1,0:T(8,128)(2,1)S(1)}, bf16[89,64,128]{2,1,0:T(8,128)(2,1)S(1)}, u32[]{:S(2)}, u32[]{:S(2)}) collective-permute-start(bf16[89,64,128]{2,1,0:T(8,128)(2,1)S(1)} %get-tuple-element.141), channel_id=1, source_target_pairs={{0,96},{2,26},{4,100},{6,30},{1,97},{3,27},{5,101},{7,31},{8,104},... | collective-permute-start | bytes 4374536 | tf_op jit(solution)/shard_map/ppermute | solution.py:75
  67.0 1.8 %collective-permute-start.15 = (bf16[256,1024]{1,0:T(8,128)(2,1)S(1)}, bf16[256,1024]{1,0:T(8,128)(2,1)S(1)}, u32[]{:S(2)}, u32[]{:S(2)}) collective-permute-start(bf16[256,1024]{1,0:T(8,128)(2,1)S(1)} %shard_map.194.refs_1_), channel_id=1, source_target_pairs={{0,1},{2,3},{4,5},{6,7},{1,0},{3,2},{5,4},{7,6},{8,9},{10,11},{12,... | collective-permute-start | bytes 1572872 | tf_op jit(solution)/shard_map/ppermute | solution.py:75
  71.3 14.8 %collective-permute-done.11.refs_0_ = bf16[85,64,128]{2,1,0:T(8,128)(2,1)S(1)} collective-permute-done((bf16[85,64,128]{2,1,0:T(8,128)(2,1)S(1)}, bf16[85,64,128]{2,1,0:T(8,128)(2,1)S(1)}, u32[]{:S(2)}, u32[]{:S(2)}) %collective-permute-start.11) | collective-permute-done | bytes 1392672 | tf_op jit(solution)/shard_map/ppermute | solution.py:75
  87.4 2.0 %collective-permute-start.14 = (bf16[36,64,128]{2,1,0:T(8,128)(2,1)S(1)}, bf16[36,64,128]{2,1,0:T(8,128)(2,1)S(1)}, u32[]{:S(2)}, u32[]{:S(2)}) collective-permute-start(bf16[36,64,128]{2,1,0:T(8,128)(2,1)S(1)} %get-tuple-element.152), channel_id=1, source_target_pairs={{0,8},{2,34},{4,12},{6,38},{1,9},{3,35},{5,13},{7,39},{8,0},{10,42... | collective-permute-start | bytes 1769480 | tf_op jit(solution)/shard_map/ppermute | solution.py:75
  89.4 1.9 %collective-permute-start.17 = (bf16[36,64,128]{2,1,0:T(8,128)(2,1)S(1)}, bf16[36,64,128]{2,1,0:T(8,128)(2,1)S(1)}, u32[]{:S(2)}, u32[]{:S(2)}) collective-permute-start(bf16[36,64,128]{2,1,0:T(8,128)(2,1)S(1)} %get-tuple-element.161), channel_id=1, source_target_pairs={{0,24},{2,98},{4,28},{6,102},{1,25},{3,99},{5,29},{7,103},{8,16},{... | collective-permute-start | bytes 1769480 | tf_op jit(solution)/shard_map/ppermute | solution.py:75
  93.8 3.2 %collective-permute-done.14.refs_0_ = bf16[36,64,128]{2,1,0:T(8,128)(2,1)S(1)} collective-permute-done((bf16[36,64,128]{2,1,0:T(8,128)(2,1)S(1)}, bf16[36,64,128]{2,1,0:T(8,128)(2,1)S(1)}, u32[]{:S(2)}, u32[]{:S(2)}) %collective-permute-start.14) | collective-permute-done | bytes 589856 | tf_op jit(solution)/shard_map/ppermute | solution.py:75
  97.0 7.5 %collective-permute-done.17.refs_1_ = bf16[36,64,128]{2,1,0:T(8,128)(2,1)S(1)} collective-permute-done((bf16[36,64,128]{2,1,0:T(8,128)(2,1)S(1)}, bf16[36,64,128]{2,1,0:T(8,128)(2,1)S(1)}, u32[]{:S(2)}, u32[]{:S(2)}) %collective-permute-start.17) | collective-permute-done | bytes 589856 | tf_op jit(solution)/shard_map/ppermute | solution.py:75
  107.9 3.5 %collective-permute-start.21 = (bf16[40,16,128]{2,1,0:T(8,128)(2,1)S(1)}, bf16[40,16,128]{2,1,0:T(8,128)(2,1)S(1)}, u32[]{:S(2)}, u32[]{:S(2)}) collective-permute-start(bf16[40,16,128]{2,1,0:T(8,128)(2,1)S(1)} %get-tuple-element.168), channel_id=1, source_target_pairs={{0,6},{2,4},{4,2},{6,0},{1,7},{3,5},{5,3},{7,1},{8,14},{10,12},{12... | collective-permute-start | bytes 491528 | tf_op jit(solution)/shard_map/ppermute | solution.py:75
  112.8 5.1 %collective-permute-done.21.refs_3_ = bf16[40,16,128]{2,1,0:T(8,128)(2,1)S(1)} collective-permute-done((bf16[40,16,128]{2,1,0:T(8,128)(2,1)S(1)}, bf16[40,16,128]{2,1,0:T(8,128)(2,1)S(1)}, u32[]{:S(2)}, u32[]{:S(2)}) %collective-permute-start.21) | collective-permute-done | bytes 163872 | tf_op jit(solution)/shard_map/ppermute | solution.py:75
  (65 shorter events, 24.8 us)
Async XLA Ops:
  3.6 5.7 %collective-permute-start = (bf16[16,512]{1,0:T(8,128)(2,1)S(1)}, bf16[16,512]{1,0:T(8,128)(2,1)S(1)}, u32[]{:S(2)}, u32[]{:S(2)}) collective-permute-start(bf16[16,512]{1,0:T(8,128)(2,1)S(1)} %get-tuple-element.99), channel_id=1, source_target_pairs={{0,2},{2,4},{4,6},{6,8},{8,10},{10,12},{12,14},{14,16},{16,18},{18... | collective-permute-start | bytes 49160 | tf_op jit(solution)/shard_map/ppermute | solution.py:81
  10.0 14.0 %slice-start = ((s8[4718592]{0:T(1024)(128)(4,1)}), s8[4194304]{0:T(1024)(128)(4,1)S(1)}, s32[]{:S(2)}) async-start(s8[4718592]{0:T(1024)(128)(4,1)} %bitcast.8), calls=%async_computation | async-start | bytes 8388608
  10.0 14.0 %slice-start.2 = ((s8[4718592]{0:T(1024)(128)(4,1)}), s8[4194304]{0:T(1024)(128)(4,1)S(1)}, s32[]{:S(2)}) async-start(s8[4718592]{0:T(1024)(128)(4,1)} %bitcast.10), calls=%async_computation.2 | async-start | bytes 8388608
  10.0 13.9 %collective-permute-start.1 = (bf16[256,1024]{1,0:T(8,128)(2,1)S(1)}, bf16[256,1024]{1,0:T(8,128)(2,1)S(1)}, u32[]{:S(2)}, u32[]{:S(2)}) collective-permute-start(bf16[256,1024]{1,0:T(8,128)(2,1)S(1)} %get-tuple-element.102.refs_1_), channel_id=1, source_target_pairs={{0,1},{2,3},{4,5},{6,7},{1,0},{3,2},{5,4},{7,6},{8,9},{10,11},{12,... | collective-permute-start | bytes 1572872 | tf_op jit(solution)/shard_map/ppermute | solution.py:75
  14.0 10.0 %collective-permute-start.2 = (bf16[256,1024]{1,0:T(8,128)(2,1)S(1)}, bf16[256,1024]{1,0:T(8,128)(2,1)S(1)}, u32[]{:S(2)}, u32[]{:S(2)}) collective-permute-start(bf16[256,1024]{1,0:T(8,128)(2,1)S(1)} %copy-done.4), channel_id=1, source_target_pairs={{0,2},{2,0},{4,6},{6,4},{1,3},{3,1},{5,7},{7,5},{8,10},{10,8},{12,... | collective-permute-start | bytes 1572872 | tf_op jit(solution)/shard_map/ppermute | solution.py:75
  27.4 6.5 %collective-permute-start.3 = (bf16[256,4480]{1,0:T(8,128)(2,1)S(1)}, bf16[256,4480]{1,0:T(8,128)(2,1)S(1)}, u32[]{:S(2)}, u32[]{:S(2)}) collective-permute-start(bf16[256,4480]{1,0:T(8,128)(2,1)S(1)} %get-tuple-element.114), channel_id=1, source_target_pairs={{0,2},{2,0},{4,6},{6,4},{1,3},{3,1},{5,7},{7,5},{8,10},{10,8},{12,... | collective-permute-start | bytes 6881288 | tf_op jit(solution)/shard_map/ppermute | solution.py:75
  27.5 18.5 %collective-permute-start.7 = (bf16[256,1280]{1,0:T(8,128)(2,1)S(1)}, bf16[256,1280]{1,0:T(8,128)(2,1)S(1)}, u32[]{:S(2)}, u32[]{:S(2)}) collective-permute-start(bf16[256,1280]{1,0:T(8,128)(2,1)S(1)} %get-tuple-element.123), channel_id=1, source_target_pairs={{0,2},{2,0},{4,6},{6,4},{1,3},{3,1},{5,7},{7,5},{8,10},{10,8},{12,... | collective-permute-start | bytes 1966088 | tf_op jit(solution)/shard_map/ppermute | solution.py:75
  30.6 15.3 %collective-permute-start.6 = (bf16[256,1024]{1,0:T(8,128)(2,1)S(1)}, bf16[256,1024]{1,0:T(8,128)(2,1)S(1)}, u32[]{:S(2)}, u32[]{:S(2)}) collective-permute-start(bf16[256,1024]{1,0:T(8,128)(2,1)S(1)} %shard_map.193.refs_1_), channel_id=1, source_target_pairs={{0,1},{2,3},{4,5},{6,7},{1,0},{3,2},{5,4},{7,6},{8,9},{10,11},{12,... | collective-permute-start | bytes 1572872 | tf_op jit(solution)/shard_map/ppermute | solution.py:75
  36.7 27.4 %collective-permute-start.4 = (bf16[112,64,128]{2,1,0:T(8,128)(2,1)S(1)}, bf16[112,64,128]{2,1,0:T(8,128)(2,1)S(1)}, u32[]{:S(2)}, u32[]{:S(2)}) collective-permute-start(bf16[112,64,128]{2,1,0:T(8,128)(2,1)S(1)} %get-tuple-element.115), channel_id=1, source_target_pairs={{0,32},{2,10},{4,36},{6,14},{1,33},{3,11},{5,37},{7,15},{8,40},{10... | collective-permute-start | bytes 5505032 | tf_op jit(solution)/shard_map/ppermute | solution.py:75
  41.6 22.5 %collective-permute-start.5 = (bf16[104,64,128]{2,1,0:T(8,128)(2,1)S(1)}, bf16[104,64,128]{2,1,0:T(8,128)(2,1)S(1)}, u32[]{:S(2)}, u32[]{:S(2)}) collective-permute-start(bf16[104,64,128]{2,1,0:T(8,128)(2,1)S(1)} %get-tuple-element.119), channel_id=1, source_target_pairs={{0,96},{2,26},{4,100},{6,30},{1,97},{3,27},{5,101},{7,31},{8,104},... | collective-permute-start | bytes 5111816 | tf_op jit(solution)/shard_map/ppermute | solution.py:75
  46.4 7.4 %collective-permute-start.8 = (f32[8,512]{1,0:T(8,128)S(1)}, f32[8,512]{1,0:T(8,128)S(1)}, u32[]{:S(2)}, u32[]{:S(2)}) collective-permute-start(f32[8,512]{1,0:T(8,128)S(1)} %shard_map.196), channel_id=1, source_target_pairs={{2,0},{4,2},{6,4},{8,6},{10,8},{12,10},{14,12},{16,14},{18,16},{20... | collective-permute-start | bytes 49160 | tf_op jit(solution)/shard_map/ppermute | solution.py:81
  54.9 4.1 %collective-permute-start.9 = (bf16[7,256,256]{2,1,0:T(8,128)(2,1)S(1)}, bf16[7,256,256]{2,1,0:T(8,128)(2,1)S(1)}, u32[]{:S(2)}, u32[]{:S(2)}) collective-permute-start(bf16[7,256,256]{2,1,0:T(8,128)(2,1)S(1)} %get-tuple-element.134), channel_id=1, source_target_pairs={{0,2},{2,0},{4,6},{6,4},{1,3},{3,1},{5,7},{7,5},{8,10},{10,8},{12,... | collective-permute-start | bytes 2752520 | tf_op jit(solution)/shard_map/ppermute | solution.py:75
  55.0 4.0 %collective-permute-start.10 = (f32[8,128]{1,0:T(8,128)S(1)}, f32[8,128]{1,0:T(8,128)S(1)}, u32[]{:S(2)}, u32[]{:S(2)}) collective-permute-start(f32[8,128]{1,0:T(8,128)S(1)} %get-tuple-element.137.refs_7_), channel_id=1, source_target_pairs={{0,1},{2,3},{4,5},{6,7},{1,0},{3,2},{5,4},{7,6},{8,9},{10,11},{12,... | collective-permute-start | bytes 12296 | tf_op jit(solution)/shard_map/ppermute | solution.py:75
  60.8 10.5 %collective-permute-start.13 = (bf16[33,64,128]{2,1,0:T(8,128)(2,1)S(1)}, bf16[33,64,128]{2,1,0:T(8,128)(2,1)S(1)}, u32[]{:S(2)}, u32[]{:S(2)}) collective-permute-start(bf16[33,64,128]{2,1,0:T(8,128)(2,1)S(1)} %get-tuple-element.148), channel_id=1, source_target_pairs={{0,64},{2,18},{4,68},{6,22},{1,65},{3,19},{5,69},{7,23},{8,72},{10... | collective-permute-start | bytes 1622024 | tf_op jit(solution)/shard_map/ppermute | solution.py:75
  65.0 21.9 %collective-permute-start.12 = (bf16[89,64,128]{2,1,0:T(8,128)(2,1)S(1)}, bf16[89,64,128]{2,1,0:T(8,128)(2,1)S(1)}, u32[]{:S(2)}, u32[]{:S(2)}) collective-permute-start(bf16[89,64,128]{2,1,0:T(8,128)(2,1)S(1)} %get-tuple-element.141), channel_id=1, source_target_pairs={{0,96},{2,26},{4,100},{6,30},{1,97},{3,27},{5,101},{7,31},{8,104},... | collective-permute-start | bytes 4374536 | tf_op jit(solution)/shard_map/ppermute | solution.py:75
  67.0 19.1 %collective-permute-start.11 = (bf16[85,64,128]{2,1,0:T(8,128)(2,1)S(1)}, bf16[85,64,128]{2,1,0:T(8,128)(2,1)S(1)}, u32[]{:S(2)}, u32[]{:S(2)}) collective-permute-start(bf16[85,64,128]{2,1,0:T(8,128)(2,1)S(1)} %get-tuple-element.140), channel_id=1, source_target_pairs={{0,32},{2,10},{4,36},{6,14},{1,33},{3,11},{5,37},{7,15},{8,40},{10... | collective-permute-start | bytes 4177928 | tf_op jit(solution)/shard_map/ppermute | solution.py:75
  67.0 25.1 %collective-permute-start.15 = (bf16[256,1024]{1,0:T(8,128)(2,1)S(1)}, bf16[256,1024]{1,0:T(8,128)(2,1)S(1)}, u32[]{:S(2)}, u32[]{:S(2)}) collective-permute-start(bf16[256,1024]{1,0:T(8,128)(2,1)S(1)} %shard_map.194.refs_1_), channel_id=1, source_target_pairs={{0,1},{2,3},{4,5},{6,7},{1,0},{3,2},{5,4},{7,6},{8,9},{10,11},{12,... | collective-permute-start | bytes 1572872 | tf_op jit(solution)/shard_map/ppermute | solution.py:75
  68.8 23.3 %collective-permute-start.16 = (bf16[256,1024]{1,0:T(8,128)(2,1)S(1)}, bf16[256,1024]{1,0:T(8,128)(2,1)S(1)}, u32[]{:S(2)}, u32[]{:S(2)}) collective-permute-start(bf16[256,1024]{1,0:T(8,128)(2,1)S(1)} %get-tuple-element.154.refs_3_), channel_id=1, source_target_pairs={{0,1},{2,3},{4,5},{6,7},{1,0},{3,2},{5,4},{7,6},{8,9},{10,11},{12,... | collective-permute-start | bytes 1572872 | tf_op jit(solution)/shard_map/ppermute | solution.py:75
  87.4 9.6 %collective-permute-start.14 = (bf16[36,64,128]{2,1,0:T(8,128)(2,1)S(1)}, bf16[36,64,128]{2,1,0:T(8,128)(2,1)S(1)}, u32[]{:S(2)}, u32[]{:S(2)}) collective-permute-start(bf16[36,64,128]{2,1,0:T(8,128)(2,1)S(1)} %get-tuple-element.152), channel_id=1, source_target_pairs={{0,8},{2,34},{4,12},{6,38},{1,9},{3,35},{5,13},{7,39},{8,0},{10,42... | collective-permute-start | bytes 1769480 | tf_op jit(solution)/shard_map/ppermute | solution.py:75
  89.4 15.1 %collective-permute-start.17 = (bf16[36,64,128]{2,1,0:T(8,128)(2,1)S(1)}, bf16[36,64,128]{2,1,0:T(8,128)(2,1)S(1)}, u32[]{:S(2)}, u32[]{:S(2)}) collective-permute-start(bf16[36,64,128]{2,1,0:T(8,128)(2,1)S(1)} %get-tuple-element.161), channel_id=1, source_target_pairs={{0,24},{2,98},{4,28},{6,102},{1,25},{3,99},{5,29},{7,103},{8,16},{... | collective-permute-start | bytes 1769480 | tf_op jit(solution)/shard_map/ppermute | solution.py:75
  91.4 14.6 %collective-permute-start.18 = (bf16[36,64,128]{2,1,0:T(8,128)(2,1)S(1)}, bf16[36,64,128]{2,1,0:T(8,128)(2,1)S(1)}, u32[]{:S(2)}, u32[]{:S(2)}) collective-permute-start(bf16[36,64,128]{2,1,0:T(8,128)(2,1)S(1)} %get-tuple-element.162), channel_id=1, source_target_pairs={{0,16},{2,66},{4,20},{6,70},{1,17},{3,67},{5,21},{7,71},{8,24},{10... | collective-permute-start | bytes 1769480 | tf_op jit(solution)/shard_map/ppermute | solution.py:75
  106.3 6.5 %collective-permute-start.20 = (bf16[40,16,128]{2,1,0:T(8,128)(2,1)S(1)}, bf16[40,16,128]{2,1,0:T(8,128)(2,1)S(1)}, u32[]{:S(2)}, u32[]{:S(2)}) collective-permute-start(bf16[40,16,128]{2,1,0:T(8,128)(2,1)S(1)} %get-tuple-element.167), channel_id=1, source_target_pairs={{0,4},{2,6},{4,0},{6,2},{1,5},{3,7},{5,1},{7,3},{8,12},{10,14},{12... | collective-permute-start | bytes 491528 | tf_op jit(solution)/shard_map/ppermute | solution.py:75
  107.9 10.0 %collective-permute-start.21 = (bf16[40,16,128]{2,1,0:T(8,128)(2,1)S(1)}, bf16[40,16,128]{2,1,0:T(8,128)(2,1)S(1)}, u32[]{:S(2)}, u32[]{:S(2)}) collective-permute-start(bf16[40,16,128]{2,1,0:T(8,128)(2,1)S(1)} %get-tuple-element.168), channel_id=1, source_target_pairs={{0,6},{2,4},{4,2},{6,0},{1,7},{3,5},{5,3},{7,1},{8,14},{10,12},{12... | collective-permute-start | bytes 491528 | tf_op jit(solution)/shard_map/ppermute | solution.py:75
  111.4 1.4 %collective-permute-start.19 = (bf16[39,16,128]{2,1,0:T(8,128)(2,1)S(1)}, bf16[39,16,128]{2,1,0:T(8,128)(2,1)S(1)}, u32[]{:S(2)}, u32[]{:S(2)}) collective-permute-start(bf16[39,16,128]{2,1,0:T(8,128)(2,1)S(1)} %get-tuple-element.166), channel_id=1, source_target_pairs={{0,2},{2,0},{4,6},{6,4},{1,3},{3,1},{5,7},{7,5},{8,10},{10,8},{12,... | collective-permute-start | bytes 479240 | tf_op jit(solution)/shard_map/ppermute | solution.py:75
  (10 other events, 89.6 us)
